TPU v7x, 512 devices: a whole 4x8x8 slice. The times are simulated.
512 devices in a mesh: wave: 32 (over y, x), field: 16 (over z, core).
Axes of the slice: x: 4, y: 8, z: 8, core: 2. Of those that a mesh axis runs over, the one named last changes fastest.
Arguments:
- spectra: bfloat16 [384, 2, 640, 64], P('wave', None, None, 'field'), may hold values from -6 to 6
- legendre: bfloat16 [384, 640, 768], P('wave', None, 'field'), may hold values from -0.3125 to 0.3125
- lat_weight: float32 [768], P('field'), may hold values from 0.25 to 0.75
- wave_of_slot: int32 [384], replicated, may hold values from 0 to 639, as said below
- lat_of_row: int32 [1536], replicated, may hold values from 0 to 1535, as said below
- lon_count: int32 [768], replicated, may hold values from 16 to 3088
Outputs:
- grid_field: bfloat16 [1536, 64, 3200], P(('wave', 'field'))
- spectral_out: float32 [384, 2, 640, 64], P('wave', None, None, 'field')
Inputs may be any that keep to these rules, and one draw needn't show every extreme that they name: `wave_of_slot`: the 384 wavenumbers are distinct. `lat_of_row`: each latitude stands in exactly one row; the latitude j of row r has min(j, 1535 - j) in the block of 48 hemisphere rows numbered (r // 3) mod (16).
All inputs are finite; a program needn't handle non-finite values.
Results may differ from a plain program's by a relative error of at most 0.0081.
Values may be sent and summed in bfloat16 or wider, within the bound.
No kernel may reach another device: no remote copies, remote signals or barrier semaphores. Data moves between devices by JAX's collectives and lax.ppermute only.
A program may use at most 128 MiB of HBM per device.

v0:
```python
import math

import jax
import jax.numpy as jnp
from jax import lax
from jax.sharding import PartitionSpec as P

LONPAD = 3200


def fourier_table(wavenumbers, lon_points, padded):
    columns = lax.broadcasted_iota(jnp.int32, (wavenumbers.shape[0], padded), 1)
    phase = wavenumbers[:, None] * columns % lon_points
    angle = phase.astype(jnp.float32) * (2.0 * math.pi / lon_points.astype(jnp.float32))
    inside = columns < lon_points
    cosine = jnp.where(inside, jnp.cos(angle), 0.0)
    sine = jnp.where(inside, -jnp.sin(angle), 0.0)
    return jnp.stack([cosine, sine], axis=1).astype(jnp.bfloat16)


def shards(spectra, legendre, lat_weight, wave_of_slot, lat_of_row, lon_count):
    wave_total = lax.axis_size("wave")
    field_total = lax.axis_size("field")
    wave_id = lax.axis_index("wave")
    field_id = lax.axis_index("field")
    slot_count = spectra.shape[0]
    degrees = spectra.shape[2]
    field_cols = spectra.shape[3]
    all_fields = field_cols * field_total
    band_rows = legendre.shape[2]
    half_deg = degrees // 2
    lat_total = 2 * lon_count.shape[0]
    row_count = 2 * band_rows // wave_total
    all_waves = wave_of_slot.shape[0]
    own_waves = lax.dynamic_slice_in_dim(wave_of_slot, wave_id * slot_count, slot_count)
    parity_table = legendre.reshape(slot_count, half_deg, 2, band_rows)
    offsets = 2 * lax.broadcasted_iota(
        jnp.int32, (slot_count, half_deg, 2), 1
    ) + lax.broadcasted_iota(jnp.int32, (slot_count, half_deg, 2), 2)
    valid_rows = offsets < (degrees - own_waves)[:, None, None]
    shard_piece = lax.all_gather(spectra, "field", axis=3, tiled=True)
    width_now = shard_piece.shape[3]
    shaped = shard_piece.reshape(slot_count, 2, half_deg, 2, width_now)
    shaped = jnp.where(valid_rows[:, None, :, :, None], shaped, jnp.zeros((), jnp.bfloat16))
    parity_sums = jnp.einsum(
        "skph,sckpf->scphf", parity_table, shaped, preferred_element_type=jnp.float32
    )
    north_part = parity_sums[:, :, 0] + parity_sums[:, :, 1]
    south_part = parity_sums[:, :, 0] - parity_sums[:, :, 1]
    band_fourier = jnp.concatenate([north_part, south_part], axis=2).astype(jnp.bfloat16)
    band_first = field_id * band_rows
    field_rows = lax.dynamic_slice_in_dim(
        lat_of_row.reshape(wave_total, field_total, row_count), field_id, 1, 1
    ).reshape(wave_total * row_count)
    positions = jnp.where(
        field_rows < lat_total // 2,
        field_rows - band_first,
        band_rows + (lat_total - 1 - field_rows - band_first),
    )
    outgoing = jnp.take(band_fourier, positions, axis=2)
    arrived = lax.all_to_all(outgoing, "wave", split_axis=2, concat_axis=0, tiled=True)
    my_lats = lax.dynamic_slice_in_dim(
        lat_of_row, (wave_id * field_total + field_id) * row_count, row_count
    )
    wave_scale = 1.0 / math.sqrt(all_waves)

    def grid_row(row_item):
        coefficients, latitude = row_item
        hemisphere = jnp.minimum(latitude, lat_total - 1 - latitude)
        lon_points = lon_count[hemisphere]
        lon_table = fourier_table(wave_of_slot, lon_points, LONPAD)
        grid_line = (
            jnp.einsum("mcf,mck->fk", coefficients, lon_table, preferred_element_type=jnp.float32)
            * wave_scale
        ).astype(jnp.bfloat16)
        partner = jnp.roll(grid_line, -1, axis=0)
        product = (grid_line.astype(jnp.float32) * partner.astype(jnp.float32)).astype(jnp.bfloat16)
        analysed = jnp.einsum("fk,mck->mcf", product, lon_table, preferred_element_type=jnp.float32)
        return (
            grid_line,
            (analysed / jnp.sqrt(lon_points.astype(jnp.float32))).astype(jnp.bfloat16),
        )

    grid_field, analysed_rows = lax.map(grid_row, (jnp.moveaxis(arrived, 2, 0), my_lats))
    returned = lax.all_to_all(
        jnp.moveaxis(analysed_rows, 0, 2), "wave", split_axis=0, concat_axis=2, tiled=True
    )
    inverse_order = (
        jnp.zeros((2 * band_rows,), jnp.int32)
        .at[positions]
        .set(jnp.arange(2 * band_rows, dtype=jnp.int32))
    )
    band_order = jnp.take(returned, inverse_order, axis=2).astype(jnp.float32)
    north_part = band_order[:, :, :band_rows]
    south_part = band_order[:, :, band_rows:]
    weights = lat_weight[None, None, :, None]
    weighted = jnp.stack(
        [(north_part + south_part) * weights, (north_part - south_part) * weights], axis=2
    ).astype(jnp.bfloat16)
    partial_sum = jnp.einsum(
        "skph,scphf->sckpf", parity_table, weighted, preferred_element_type=jnp.float32
    )
    summed = lax.psum_scatter(
        partial_sum.reshape(slot_count, 2, degrees, all_fields),
        "field",
        scatter_dimension=3,
        tiled=True,
    )
    kept_rows = valid_rows.reshape(slot_count, degrees)[:, None, :, None]
    return (grid_field, jnp.where(kept_rows, summed, 0.0))


def solution(mesh):
    in_specs = (P("wave", None, None, "field"), P("wave", None, "field"), P("field"), P(), P(), P())
    out_specs = (P(("wave", "field"), None, None), P("wave", None, None, "field"))
    return jax.shard_map(shards, mesh=mesh, in_specs=in_specs, out_specs=out_specs, check_vma=False)
```

profile of v0, /device:TPU:1, one launch (start us, length us, event | category | flops | bytes accessed | tf_op | source)
XLA Modules:
  0.0 514.7 jit_solution(4811912169414130954)
XLA Ops:
  14.2 45.5 %all-gather.2.cloned.1.call-done = bf16[12,2,640,64]{2,1,0,3:T(2,128)(2,1)} async-done(((bf16[12,2,640,4]{2,1,0,3:T(2,128)(2,1)}), bf16[12,2,640,64]{2,1,0,3:T(2,128)(2,1)}) %all-gather.2.cloned.1.call-update) | async-done | bytes 1966096 | tf_op jit(solution)/shard_map/all_gather | solution.py:41
  59.7 7.5 %copy.35 = bf16[12,2,640,64]{3,2,1,0:T(8,128)(2,1)} copy(bf16[12,2,640,64]{2,1,0,3:T(2,128)(2,1)} %all-gather.2.cloned.1.call-done) | data formatting | bytes 3932160 | tf_op jit(solution)/shard_map/all_gather | solution.py:41
  67.2 8.0 %broadcast_select_fusion = bf16[12,2,320,2,64]{4,3,2,1,0:T(2,128)(2,1)S(1)} fusion(bf16[12,2,320,2,64]{4,3,2,1,0:T(2,128)(2,1)} %bitcast.97, pred[12,320,2]{2,1,0:T(8,128)(4,1)S(1)} %add_compare_fusion), kind=kLoop, calls=%fused_computation.34 | loop fusion | flops 983040 | bytes 3939840 | tf_op jit(solution)/shard_map/jit(_where)/select_n | solution.py:44
  76.9 2.3 gather_fusion
  80.9 9.3 %all-to-all-start = ((bf16[32,2,2304]{2,1,0:T(2,128)(2,1)}), bf16[32,2,2304]{2,1,0:T(2,128)(2,1)S(1)}, u32[]{:S(2)}, u32[]{:S(2)}) async-start(bf16[32,2,2304]{2,1,0:T(2,128)(2,1)} %reshape.290), calls=%async_computation | async-start | bytes 589824 | tf_op jit(solution)/shard_map/all_to_all | solution.py:61
  90.4 12.1 %all-to-all-done = bf16[32,2,2304]{2,1,0:T(2,128)(2,1)S(1)} async-done(((bf16[32,2,2304]{2,1,0:T(2,128)(2,1)}), bf16[32,2,2304]{2,1,0:T(2,128)(2,1)S(1)}, u32[]{:S(2)}, u32[]{:S(2)}) %all-to-all-start) | async-done | bytes 294944 | tf_op jit(solution)/shard_map/all_to_all | solution.py:61
  105.0 234.2 %while.12 = (s32[]{:T(128)}, bf16[3,64,3200]{2,1,0:T(8,128)(2,1)}, bf16[3,384,2,64]{1,3,2,0:T(8,128)(2,1)}, bf16[3,384,2,64]{1,3,2,0:T(8,128)(2,1)}, s32[3]{0:T(...) while((s32[]{:T(128)}, bf16[3,64,3200]{2,1,0:T(8,128)(2,1)}, ...), condition=%wide.region_1.3_spmd, body=%wide.region_0.2_spmd.sunk | while | flops 654437504 | bytes 27239484 | solution.py:84
  110.4 65.8 %select_convert_fusion.3 = (bf16[384,1,3200]{2,0,1:T(8,128)(2,1)S(1)}, bf16[384,1,3200]{2,0,1:T(8,128)(2,1)S(1)}) fusion(f32[]{:T(128)S(6)} %div.22, s32[]{:T(128)S(6)} %select_n.150, s32[384]{0:T(512)S(1)} %get-tuple-element.164, pred[]{:T(512)S(6)} %lt.156, pred[3200]{0:T(1024)(128)(4,1)S(1)} %iota_compare_fusion.2), kind=kLoop, calls=%fused_computation.8.clone.1 | loop fusion | flops 18432000 | bytes 4919945 | tf_op jit(solution)/shard_map/convert
  176.2 2.8 bitcast_dynamic-update-slice_fusion.2
  179.2 3.9 fusion.48
  188.4 65.8 %select_convert_fusion.3 = (bf16[384,1,3200]{2,0,1:T(8,128)(2,1)S(1)}, bf16[384,1,3200]{2,0,1:T(8,128)(2,1)S(1)}) fusion(f32[]{:T(128)S(6)} %div.22, s32[]{:T(128)S(6)} %select_n.150, s32[384]{0:T(512)S(1)} %get-tuple-element.164, pred[]{:T(512)S(6)} %lt.156, pred[3200]{0:T(1024)(128)(4,1)S(1)} %iota_compare_fusion.2), kind=kLoop, calls=%fused_computation.8.clone.1 | loop fusion | flops 18432000 | bytes 4919945 | tf_op jit(solution)/shard_map/convert
  254.3 2.8 bitcast_dynamic-update-slice_fusion.2
  257.3 3.9 fusion.48
  266.5 65.8 %select_convert_fusion.3 = (bf16[384,1,3200]{2,0,1:T(8,128)(2,1)S(1)}, bf16[384,1,3200]{2,0,1:T(8,128)(2,1)S(1)}) fusion(f32[]{:T(128)S(6)} %div.22, s32[]{:T(128)S(6)} %select_n.150, s32[384]{0:T(512)S(1)} %get-tuple-element.164, pred[]{:T(512)S(6)} %lt.156, pred[3200]{0:T(1024)(128)(4,1)S(1)} %iota_compare_fusion.2), kind=kLoop, calls=%fused_computation.8.clone.1 | loop fusion | flops 18432000 | bytes 4919945 | tf_op jit(solution)/shard_map/convert
  332.3 2.8 bitcast_dynamic-update-slice_fusion.2
  335.3 3.9 fusion.48
  339.2 2.1 copy.46
  342.8 4.6 all-to-all-start.1
  348.4 9.7 %all-to-all-done.1 = bf16[32,2,2304]{2,1,0:T(2,128)(2,1)S(1)} async-done(((bf16[32,2,2304]{2,1,0:T(2,128)(2,1)}), bf16[32,2,2304]{2,1,0:T(2,128)(2,1)S(1)}, u32[]{:S(2)}, u32[]{:S(2)}) %all-to-all-start.1) | async-done | bytes 294944 | tf_op jit(solution)/shard_map/all_to_all | solution.py:85
  359.0 2.3 gather_fusion.1
  361.7 3.0 convolution_bitcast_fusion.1
  364.7 10.2 %copy.51 = f32[12,2,320,2,64]{4,3,2,1,0:T(2,128)} copy(f32[12,2,320,2,64]{2,4,1,3,0:T(8,128)} %convolution_bitcast_fusion.1) | data formatting | bytes 7864320 | tf_op jit(solution)/shard_map/skph,scphf->sckpf/transpose | solution.py:100
  374.9 9.1 %copy.52 = f32[12,2,640,64]{2,1,0,3:T(2,128)} copy(f32[12,2,640,64]{3,2,1,0:T(8,128)} %bitcast.96) | data formatting | bytes 7864320 | tf_op jit(solution)/shard_map/reshape | solution.py:104
  386.3 119.7 %all-reduce.3.cloned.1.call-done = f32[12,2,640,64]{2,1,0,3:T(2,128)} async-done(((f32[12,2,640,64]{2,1,0,3:T(2,128)}), f32[12,2,640,64]{2,1,0,3:T(2,128)}) %all-reduce.3.cloned.1.call-update) | async-done | bytes 3932176
  (80 shorter events, 27.8 us)
Async XLA Ops:
  7.2 5.0 copy-start.4
  7.2 6.6 %copy-start.3 = (s32[384]{0:T(512)S(1)}, s32[384]{0:T(512)}, u32[]{:S(2)}) copy-start(s32[384]{0:T(512)} %param.13) | copy-start | bytes 4612
  7.2 52.5 %all-gather.2.cloned.1.call-start = ((), (), s32[]{:S(2)}) async-start(), calls=%async_computation.2 | async-start | bytes 2088960 | tf_op jit(solution)/shard_map/all_gather | solution.py:41
  12.1 63.1 %copy-start.1 = (bf16[12,320,2,48,1]{1,3,4,2,0:T(8,128)(2,1)}, bf16[12,320,2,48,1]{1,3,4,2,0:T(8,128)(2,1)S(1)}, u32[]{:S(2)}) copy-start(bf16[12,320,2,48,1]{1,3,4,2,0:T(8,128)(2,1)S(1)} %copy.54) | copy-start | bytes 2211844
  80.9 21.5 %all-to-all-start = ((bf16[32,2,2304]{2,1,0:T(2,128)(2,1)}), bf16[32,2,2304]{2,1,0:T(2,128)(2,1)S(1)}, u32[]{:S(2)}, u32[]{:S(2)}) async-start(bf16[32,2,2304]{2,1,0:T(2,128)(2,1)} %reshape.290), calls=%async_computation | async-start | bytes 589824 | tf_op jit(solution)/shard_map/all_to_all | solution.py:61
  176.2 2.9 copy-start
  254.2 2.9 copy-start
  332.3 2.9 copy-start
  341.3 20.2 %copy-start.5 = (f32[48]{0:T(128)S(1)}, f32[48]{0:T(128)}, u32[]{:S(2)}) copy-start(f32[48]{0:T(128)} %param.12) | copy-start | bytes 580
  341.7 20.0 %copy-start.2 = (bf16[12,320,2,48,1]{1,3,4,2,0:T(8,128)(2,1)S(1)}, bf16[12,320,2,48,1]{1,3,4,2,0:T(8,128)(2,1)}, u32[]{:S(2)}) copy-start(bf16[12,320,2,48,1]{1,3,4,2,0:T(8,128)(2,1)} %copy-done.1) | copy-start | bytes 2211844
  342.8 15.3 %all-to-all-start.1 = ((bf16[32,2,2304]{2,1,0:T(2,128)(2,1)}), bf16[32,2,2304]{2,1,0:T(2,128)(2,1)S(1)}, u32[]{:S(2)}, u32[]{:S(2)}) async-start(bf16[32,2,2304]{2,1,0:T(2,128)(2,1)} %reshape.292), calls=%async_computation.1 | async-start | bytes 589824 | tf_op jit(solution)/shard_map/all_to_all | solution.py:85
  347.4 158.6 %all-reduce.3.cloned.1.call-start = ((), (), s32[]{:S(2)}) async-start(), calls=%async_computation.3 | async-start | bytes 7864320
Sparse Core Ops, SparseCore 0:
  10.7 48.9 all-gather.1
  384.2 121.7 all-reduce.2
where the time goes:
time: 516 us; the launch traced here: 515 us
  other arithmetic  211 us (41%)
  waiting for transfers between devices  187 us (36%)
  local copies, waits for them, and re-layouts  54.9 us (11%)
  matrix products  24 us (5%)
  between operations  15.1 us (3%)
  starting transfers between devices  13.9 us (3%)
  loops' own time  8.84 us (2%)
    another operation x3, other arithmetic  197 us
    unnamed x3, waiting for transfers between devices  120 us
    all_gather x1, waiting for transfers between devices, shards(): shard_piece = lax.all_gather(spectra, 'field', axis=3, tiled=True)  45.5 us
    all_to_all x1, waiting for transfers between devices, shards(): lax.all_to_all(outgoing, 'wave', split_axis=2, concat_axis=0, tiled=True)  12.1 us
    dot_general x3, matrix products, grid_row(): jnp.einsum('fk,mck->mcf', product, lon_table, preferred_element_type=jnp....  11.7 us
  transfers between devices with their start and end apart: 4, of which 4 were waited for; matrix products, arithmetic and copies ran while one was open for 2% of the time, Pallas kernels for 0%

commit v1 on v0

v1 whole, which is shorter than its diff:
```python
import functools
import math

import jax
import jax.numpy as jnp
from jax import lax
from jax.experimental import pallas as pl
from jax.experimental.pallas import tpu as pltpu
from jax.sharding import PartitionSpec as P

LONPAD = 3200
LANES = 128
BLOCK = 256
BLOCKS = -(-LONPAD // BLOCK)
MESH_VMEM = 56 * 1024 * 1024

NT = (((1,), (1,)), ((), ()))
NN = (((1,), (0,)), ((), ()))
TN = (((0,), (0,)), ((), ()))


def dot(a, b, dims):
    return lax.dot_general(a, b, dims, preferred_element_type=jnp.float32)


def params():
    return pltpu.CompilerParams(vmem_limit_bytes=MESH_VMEM)


def cost(micros):
    return pl.CostEstimate(flops=0, bytes_accessed=int(micros * 3.7e6), transcendentals=0)


def smem():
    return pl.BlockSpec(memory_space=pltpu.SMEM)


def vmem():
    return pl.BlockSpec(memory_space=pltpu.VMEM)


def side_of(core):
    return 1 - 2 * core


def legendre_rows_kernel(wave_id, field_id, wave_of_slot, lat_of_row, legendre, out, pick, south, *, waves, fields):
    slots, band, degrees = legendre.shape
    rows = out.shape[1]
    row_count = rows // waves
    half = lat_of_row.shape[0] // 2
    own, field = wave_id[0], field_id[0]
    lane = lax.broadcasted_iota(jnp.int32, (1, LANES), 1)
    for row in range(rows):
        member, wave = divmod(row, waves)
        lat = lat_of_row[(wave * fields + field) * row_count + member]
        is_south = lat >= half
        hemi = jnp.where(is_south, 2 * half - 1 - lat, lat) - field * band
        pick[row : row + 1, :] = (lane == hemi).astype(jnp.float32)
        south[row : row + 1, :] = jnp.broadcast_to(is_south.astype(jnp.float32), (1, LANES))
    offsets = lax.broadcasted_iota(jnp.int32, (1, degrees), 1)
    odd = (offsets & 1).astype(jnp.float32)
    sign = 1.0 - 2.0 * (south[:, :1] * odd)
    chosen = pick[:, :band].astype(jnp.bfloat16)
    for slot in range(slots):
        table = dot(chosen, legendre[slot], NN) * sign
        live = offsets < degrees - wave_of_slot[own * slots + slot]
        out[slot] = jnp.where(live, table, 0.0).astype(jnp.bfloat16)


def sin_cos(phase, period):
    inverse = 1.0 / period
    turns = (phase - jnp.floor(phase * inverse + 0.5) * period) * inverse
    quarter = jnp.floor(4.0 * turns + 0.5)
    w = (2.0 * math.pi) * (turns - 0.25 * quarter)
    w2 = w * w
    sine = w * (1.0 + w2 * (-1.0 / 6 + w2 * (1.0 / 120 + w2 * (-1.0 / 5040 + w2 * (1.0 / 362880)))))
    cosine = 1.0 + w2 * (-0.5 + w2 * (1.0 / 24 + w2 * (-1.0 / 720 + w2 * (1.0 / 40320))))
    size = jnp.abs(quarter)
    odd = size == 1.0
    flipped = size >= 2.0
    cos_out = jnp.where(odd, sine, cosine)
    sin_out = jnp.where(odd, cosine, sine)
    cos_out = jnp.where(flipped | (quarter == 1.0), -cos_out, cos_out)
    sin_out = jnp.where(flipped | (quarter == -1.0), -sin_out, sin_out)
    return cos_out, sin_out


def fourier_tables_kernel(
    wave_id, field_id, lat_of_row, lon_count, lat_weight, waves_row,
    inner, inner_t, outer_fwd, outer_inv, place, *, fields, zs,
):
    row_count = inner.shape[0]
    band = lat_weight.shape[0]
    half = lon_count.shape[0]
    slots = waves_row.shape[1]
    steps = outer_fwd.shape[1]
    wave, field = wave_id[0], field_id[0]
    for member in range(row_count):
        lat = lat_of_row[(wave * fields + field) * row_count + member]
        hemi = jnp.where(lat >= half, 2 * half - 1 - lat, lat)
        points = lon_count[hemi].astype(jnp.float32)
        period = jnp.broadcast_to(points, (1, LANES))
        weight = lat_weight[hemi - field * band] / jnp.sqrt(period)
        for part in range(slots // LANES):
            m = waves_row[:, part * LANES : (part + 1) * LANES]
            at = part * 2 * LANES
            x = lax.broadcasted_iota(jnp.int32, (BLOCK, LANES), 0).astype(jnp.float32)
            cosine, sine = sin_cos(x * m, period)
            both = jnp.concatenate([cosine, -sine], axis=1)
            inner[member, :, at : at + 2 * LANES] = both.astype(jnp.bfloat16)
            inner_t[member, at : at + 2 * LANES, :] = both.T.astype(jnp.bfloat16)
            x = (BLOCK * lax.broadcasted_iota(jnp.int32, (steps, LANES), 0)).astype(jnp.float32)
            cosine, sine = sin_cos(x * m, period)
            both = jnp.concatenate([cosine, sine], axis=1)
            outer_fwd[member, :, at : at + 2 * LANES] = both * (1.0 / math.sqrt(slots))
            outer_inv[member, :, at : at + 2 * LANES] = both * jnp.concatenate([weight, weight], axis=1)
    at = lax.broadcasted_iota(jnp.int32, (LANES, LANES), 1)
    chunk, part, low = (at >> 3) & 7, (at >> 2) & 1, at & 3
    core = (field & 1) ^ (at >> 6)
    back = (chunk + 1) >> 1
    other = ((chunk & 1) ^ 1) & (chunk > 0).astype(jnp.int32)
    z = ((field >> 1) - side_of(core) * back + zs) & (zs - 1)
    target = part * 64 + (2 * z + (core ^ other)) * 4 + low
    place[...] = (lax.broadcasted_iota(jnp.int32, (LANES, LANES), 0) == target).astype(jnp.bfloat16)


def legendre_forward_kernel(own, one, two, three, four, table, *refs, second):
    swapped, out, held = (None,) * (3 - len(refs)) + refs
    slots, rows, degrees = table.shape
    waves = out.shape[0]
    row_count = rows // waves
    each = slots * row_count
    empty = jnp.zeros((64, degrees), jnp.float32)
    for pair in range(slots // 2):
        at = pl.ds(16 * pair, 16)
        both = [own[at, :]] + [piece[i, at, :] for piece in (one, two, three) for i in range(2)] + [four[at, :]]
        both = [b.astype(jnp.float32) for b in both]
        for half in range(2):
            slot = 2 * pair + half
            spec = [b[8 * half : 8 * half + 8] for b in both]
            spec = [empty] + spec if second else spec + [empty]
            sums = dot(table[slot], jnp.concatenate(spec, axis=0).astype(jnp.bfloat16), NT)
            for member in range(row_count):
                held[pl.ds(slot * row_count + member, waves, stride=each), :] = sums[
                    waves * member : waves * (member + 1)
                ]
    for wave in range(waves):
        lines = held[wave * each : (wave + 1) * each, :]
        if swapped is not None:
            lines = lines + swapped[wave].astype(jnp.float32)
        out[wave] = lines.astype(jnp.bfloat16)


def legendre_inverse_kernel(
    arrived, swapped, table, table_swapped, own, one, one_other, two, two_other, three, four, held, held_swapped
):
    slots, rows, degrees = table.shape
    waves = arrived.shape[0]
    row_count = rows // waves
    each = slots * row_count
    for wave in range(waves):
        held[wave * each : (wave + 1) * each, :] = arrived[wave].astype(jnp.float32)
        held_swapped[wave * each : (wave + 1) * each, :] = pltpu.roll(swapped[wave].astype(jnp.float32), 64, 1)

    def share(ref, slot, legendre):
        weighted = jnp.concatenate(
            [ref[pl.ds(slot * row_count + member, waves, stride=each), :] for member in range(row_count)], axis=0
        )
        return dot(weighted[:, :64].astype(jnp.bfloat16), legendre[slot], TN)

    for pair in range(slots // 2):
        at = pl.ds(16 * pair, 16)
        sums = [
            share(held, slot, table) + share(held_swapped, slot, table_swapped) for slot in (2 * pair, 2 * pair + 1)
        ]
        pieces = [jnp.concatenate([s[8 * chunk : 8 * chunk + 8] for s in sums], axis=0) for chunk in range(8)]
        own[at, :] = pieces[0]
        pieces = [piece.astype(jnp.bfloat16) for piece in pieces]
        one[at, :] = pieces[1]
        one_other[at, :] = pieces[2]
        two[at, :] = pieces[3]
        two_other[at, :] = pieces[4]
        three[0, at, :] = pieces[5]
        three[1, at, :] = pieces[6]
        four[at, :] = pieces[7]


def fourier_kernel(
    wave_id, field_id, lat_of_row, lon_count, arrived, inner, inner_t, outer_fwd, outer_inv, place,
    grid_out, sent, held, back, turned, products, *, fields,
):
    row_count = inner.shape[0]
    waves, each, _ = arrived.shape
    slots = waves * each // row_count
    parts = slots // LANES
    half = lon_count.shape[0]
    levels = grid_out.shape[1]
    wave, field = wave_id[0], field_id[0]
    for source in range(waves):
        held[source * each : (source + 1) * each, :] = arrived[source].astype(jnp.float32)
    for member in range(row_count):
        lat = lat_of_row[(wave * fields + field) * row_count + member]
        hemi = jnp.where(lat >= half, 2 * half - 1 - lat, lat)
        points = lon_count[hemi]
        lines = held[pl.ds(member, slots, stride=row_count), :].astype(jnp.bfloat16)
        coef = dot(place[...], lines, NT)
        for step in range(BLOCKS):
            rows = pl.ds(step * levels, levels)
            for part in range(parts):
                real = coef[:levels, part * LANES : (part + 1) * LANES]
                imag = coef[levels:, part * LANES : (part + 1) * LANES]
                at = part * 2 * LANES
                cosine = outer_fwd[member, step : step + 1, at : at + LANES]
                sine = outer_fwd[member, step : step + 1, at + LANES : at + 2 * LANES]
                turned[rows, at : at + LANES] = (real * cosine - imag * sine).astype(jnp.bfloat16)
                turned[rows, at + LANES : at + 2 * LANES] = (real * sine + imag * cosine).astype(jnp.bfloat16)
        values = dot(turned[...], inner_t[member], NN)
        for step in range(BLOCKS):
            width = min(BLOCK, LONPAD - step * BLOCK)
            line = values[step * levels : (step + 1) * levels]
            x = step * BLOCK + lax.broadcasted_iota(jnp.int32, (1, BLOCK), 1)
            line = jnp.where(x < points, line, 0.0).astype(jnp.bfloat16)
            grid_out[member, :, step * BLOCK : step * BLOCK + width] = line[:, :width]
            line = line.astype(jnp.float32)
            partner = pltpu.roll(line, levels - 1, 0)
            products[step * levels : (step + 1) * levels, :] = (line * partner).astype(jnp.bfloat16)
        reals, imags = [], []
        for part in range(parts):
            at = part * 2 * LANES
            sums = dot(products[...], inner[member, :, at : at + 2 * LANES], NN)
            real = jnp.zeros((levels, LANES), jnp.float32)
            imag = jnp.zeros((levels, LANES), jnp.float32)
            for step in range(BLOCKS):
                rows = slice(step * levels, (step + 1) * levels)
                cosine = outer_inv[member, step : step + 1, at : at + LANES]
                sine = outer_inv[member, step : step + 1, at + LANES : at + 2 * LANES]
                real += sums[rows, :LANES] * cosine + sums[rows, LANES:] * sine
                imag += sums[rows, LANES:] * cosine - sums[rows, :LANES] * sine
            reals.append(real)
            imags.append(imag)
        analysed = jnp.concatenate([jnp.concatenate(reals, axis=1), jnp.concatenate(imags, axis=1)], axis=0)
        back[pl.ds(member, slots, stride=row_count), :] = dot(
            analysed.T.astype(jnp.bfloat16), place[...], NN
        )
    for source in range(waves):
        sent[source] = back[source * each : (source + 1) * each, :].astype(jnp.bfloat16)


def shards(spectra, legendre, lat_weight, wave_of_slot, lat_of_row, lon_count):
    waves = lax.axis_size("wave")
    fields = lax.axis_size("field")
    zs = fields // 2
    wave_id = lax.axis_index("wave").astype(jnp.int32).reshape(1)
    field_id = lax.axis_index("field").astype(jnp.int32).reshape(1)
    slots, _, degrees, cols = spectra.shape
    band = legendre.shape[2]
    rows = 2 * band
    row_count = rows // waves
    all_slots = wave_of_slot.shape[0]
    levels = cols * fields
    each = row_count * slots
    coded = slots * 2 * cols

    def hop(x, by, cross=0):
        pairs = [
            (i, (2 * (i // 2 + side_of(i % 2) * by) + (i % 2 ^ cross)) % fields) for i in range(fields)
        ]
        return lax.ppermute(x, "field", pairs)

    def swap(x):
        return hop(x, 0, 1)

    own = jnp.transpose(spectra, (0, 1, 3, 2)).reshape(coded, degrees)
    four = hop(own, 4)
    legendre = jnp.transpose(legendre, (0, 2, 1))
    legendre_swapped = swap(legendre)
    partner, legendre = lax.optimization_barrier((swap(own), legendre))
    pair = jnp.stack([own, partner])
    two = hop(pair, 2)
    one = hop(pair, 1)
    def order_rows(values, band_of):
        return pl.pallas_call(
            functools.partial(legendre_rows_kernel, waves=waves, fields=fields),
            out_shape=jax.ShapeDtypeStruct((slots, rows, degrees), jnp.bfloat16),
            in_specs=[smem(), smem(), smem(), smem(), vmem()],
            out_specs=vmem(),
            scratch_shapes=[pltpu.VMEM((rows, LANES), jnp.float32)] * 2,
            compiler_params=params(),
            cost_estimate=cost(3),
            name="legendre_rows",
        )(wave_id, band_of, wave_of_slot, lat_of_row, values)

    two, table = lax.optimization_barrier((two, order_rows(legendre, field_id)))
    two, legendre_swapped = lax.optimization_barrier((two, legendre_swapped))
    three = hop(two, 1)
    table_swapped = order_rows(legendre_swapped, field_id ^ 1)

    def forward(legendre_table, second, *swapped):
        return pl.pallas_call(
            functools.partial(legendre_forward_kernel, second=second),
            out_shape=jax.ShapeDtypeStruct((waves, each, LANES), jnp.bfloat16),
            in_specs=[vmem()] * (6 + len(swapped)),
            out_specs=vmem(),
            scratch_shapes=[pltpu.VMEM((waves * each, LANES), jnp.float32)],
            compiler_params=params(),
            cost_estimate=cost(2),
            name="legendre_forward",
        )(own, one, two, three, four, legendre_table, *swapped)

    outgoing = forward(table, False, swap(forward(table_swapped, True)))
    outgoing, lat_weight = lax.optimization_barrier((outgoing, lat_weight))
    arrived = lax.all_to_all(outgoing, "wave", split_axis=0, concat_axis=0, tiled=True)

    steps = 16
    inner, inner_t, outer_fwd, outer_inv, place = pl.pallas_call(
        functools.partial(fourier_tables_kernel, fields=fields, zs=zs),
        out_shape=(
            jax.ShapeDtypeStruct((row_count, BLOCK, 2 * all_slots), jnp.bfloat16),
            jax.ShapeDtypeStruct((row_count, 2 * all_slots, BLOCK), jnp.bfloat16),
            jax.ShapeDtypeStruct((row_count, steps, 2 * all_slots), jnp.float32),
            jax.ShapeDtypeStruct((row_count, steps, 2 * all_slots), jnp.float32),
            jax.ShapeDtypeStruct((LANES, LANES), jnp.bfloat16),
        ),
        in_specs=[smem()] * 5 + [vmem()],
        out_specs=(vmem(),) * 5,
        compiler_params=params(),
        cost_estimate=cost(4),
        name="fourier_tables",
    )(
        wave_id, field_id, lat_of_row, lon_count, lat_weight,
        wave_of_slot.astype(jnp.float32).reshape(1, all_slots),
    )

    grid_field, sent = pl.pallas_call(
        functools.partial(fourier_kernel, fields=fields),
        out_shape=(
            jax.ShapeDtypeStruct((row_count, levels, LONPAD), jnp.bfloat16),
            jax.ShapeDtypeStruct((waves, each, LANES), jnp.bfloat16),
        ),
        in_specs=[smem()] * 4 + [vmem()] * 6,
        out_specs=(vmem(), vmem()),
        scratch_shapes=[
            pltpu.VMEM((waves * each, LANES), jnp.float32),
            pltpu.VMEM((waves * each, LANES), jnp.float32),
            pltpu.VMEM((BLOCKS * levels, 2 * all_slots), jnp.bfloat16),
            pltpu.VMEM((BLOCKS * levels, BLOCK), jnp.bfloat16),
        ],
        compiler_params=params(),
        cost_estimate=cost(7),
        name="fourier",
    )(wave_id, field_id, lat_of_row, lon_count, arrived, inner, inner_t, outer_fwd, outer_inv, place)

    returned = lax.all_to_all(sent, "wave", split_axis=0, concat_axis=0, tiled=True)

    half = jax.ShapeDtypeStruct((coded, degrees), jnp.bfloat16)
    total, one, one_other, two, two_other, three, four = pl.pallas_call(
        legendre_inverse_kernel,
        out_shape=(
            jax.ShapeDtypeStruct((coded, degrees), jnp.float32), half, half, half, half,
            jax.ShapeDtypeStruct((2, coded, degrees), jnp.bfloat16), half,
        ),
        in_specs=[vmem()] * 4,
        out_specs=(vmem(),) * 7,
        scratch_shapes=[pltpu.VMEM((waves * each, LANES), jnp.float32)] * 2,
        compiler_params=params(),
        cost_estimate=cost(3),
        name="legendre_inverse",
    )(returned, swap(returned), table, table_swapped)

    def add(a, b):
        return (a.astype(jnp.float32) + b.astype(jnp.float32)).astype(jnp.bfloat16)

    three = hop(three, -1)
    landed = [hop(four, -4), hop(one, -1), hop(one_other, -1, 1)]
    landed += [hop(add(two, three[0]), -2), hop(add(two_other, three[1]), -2, 1)]
    total = total + sum(x.astype(jnp.float32) for x in landed)
    spectral = jnp.transpose(total.reshape(slots, 2, cols, degrees), (0, 1, 3, 2))
    return grid_field, spectral


def solution(mesh):
    in_specs = (P("wave", None, None, "field"), P("wave", None, "field"), P("field"), P(), P(), P())
    out_specs = (P(("wave", "field"), None, None), P("wave", None, None, "field"))
    return jax.shard_map(shards, mesh=mesh, in_specs=in_specs, out_specs=out_specs, check_vma=False)
```

time: 516 us -> 141 us (0.27)
  other arithmetic: 211 us -> 2.11 us
  waiting for transfers between devices: 187 us -> 20.5 us
  starting transfers between devices: 13.9 us -> 64.6 us
  local copies, waits for them, and re-layouts: 54.9 us -> 6.8 us
  Pallas kernels: 0 us -> 28 us
  matrix products: 24 us -> 0 us
  blocking collectives: 0 us -> 16 us
  between operations: 15.1 us -> 0.87 us
  loops' own time: 8.84 us -> 0 us
    another operation x4 -> x1, other arithmetic: 198 us -> 0.03 us  [shards(): pair = jnp.stack([own, partner])]
    unnamed x3 -> x0, waiting for transfers between devices: 120 us -> none
    ppermute x0 -> x14, starting transfers between devices: none -> 55.2 us  [hop(): return lax.ppermute(x, 'field', pairs)]
    all_gather x1 -> x0, waiting for transfers between devices: 45.5 us -> none  [shards(): shard_piece = lax.all_gather(spectra, 'field', axis=3, tiled=True)]
    pallas_call x0 -> x7, Pallas kernels: none -> 28 us  [the longest x1 7.29 us: shards(): pl.pallas_call(functools.partial(fourier_kernel, fields=fields), out_shap...]
    dot_general x8 -> x0, matrix products: 24 us -> none  [the longest x3 11.7 us: grid_row(): jnp.einsum('fk,mck->mcf', product, lon_table, preferred_element_type=jnp....]
    all_to_all x0 -> x1, blocking collectives: none -> 16 us  [shards(): lax.all_to_all(sent, 'wave', split_axis=0, concat_axis=0, tiled=True)]
    all_to_all x2 -> x1, waiting for transfers between devices: 21.8 us -> 7.93 us  [shards(): lax.all_to_all(outgoing, 'wave', split_axis=0, concat_axis=0, tiled=True)]
  transfers between devices with their start and end apart: 4 -> 15, of which waited for: 4 -> 8; matrix products, arithmetic and copies ran while one was open for 2% -> 3% of each run, Pallas kernels for 0% -> 7%
where the time goes in v1:
time: 141 us; the launch traced here: 139 us
  starting transfers between devices  64.6 us (46%)
  Pallas kernels  28 us (20%)
  waiting for transfers between devices  20.5 us (15%)
  blocking collectives  16 us (11%)
  local copies, waits for them, and re-layouts  6.8 us (5%)
  other arithmetic  2.11 us (1%)
    ppermute x14, starting transfers between devices, hop(): return lax.ppermute(x, 'field', pairs)  55.2 us
    all_to_all x1, blocking collectives, shards(): lax.all_to_all(sent, 'wave', split_axis=0, concat_axis=0, tiled=True)  16 us
    ppermute x14, waiting for transfers between devices, hop(): return lax.ppermute(x, 'field', pairs)  12.6 us
    all_to_all x1, starting transfers between devices, shards(): lax.all_to_all(outgoing, 'wave', split_axis=0, concat_axis=0, tiled=True)  9.32 us
    all_to_all x1, waiting for transfers between devices, shards(): lax.all_to_all(outgoing, 'wave', split_axis=0, concat_axis=0, tiled=True)  7.93 us
    pallas_call x1, Pallas kernels, shards(): pl.pallas_call(functools.partial(fourier_kernel, fields=fields), out_shap...  7.29 us
    pallas_call x2, Pallas kernels, forward(): pl.pallas_call(functools.partial(legendre_forward_kernel, second=second),...  6.52 us
    pallas_call x2, Pallas kernels, order_rows(): pl.pallas_call(functools.partial(legendre_rows_kernel, waves=waves, field...  6.01 us
  transfers between devices with their start and end apart: 15, of which 8 were waited for; matrix products, arithmetic and copies ran while one was open for 3% of the time, Pallas kernels for 7%

profile of v1, /device:TPU:1, one launch (start us, length us, event | category | flops | bytes accessed | tf_op | source)
XLA Modules:
  0.0 138.8 jit_solution(3995708250948893954)
XLA Ops:
  0.6 8.8 %collective-permute-start.3 = (bf16[12,48,640]{2,1,0:T(8,128)(2,1)}, bf16[12,48,640]{2,1,0:T(8,128)(2,1)S(1)}, u32[]{:S(2)}, u32[]{:S(2)}) collective-permute-start(bf16[12,48,640]{2,1,0:T(8,128)(2,1)} %bitcast.16), channel_id=1, source_target_pairs={{0,1},{1,0},{2,3},{3,2},{4,5},{5,4},{6,7},{7,6},{8,9},{9,8},{10,11... | collective-permute-start | bytes 2211848 | tf_op jit(solution)/shard_map/ppermute | solution.py:268
  13.6 5.3 %collective-permute-start.2 = (bf16[2,96,640]{2,1,0:T(8,128)(2,1)S(1)}, bf16[2,96,640]{2,1,0:T(8,128)(2,1)S(1)}, u32[]{:S(2)}, u32[]{:S(2)}) collective-permute-start(bf16[2,96,640]{2,1,0:T(8,128)(2,1)S(1)} %pad_maximum_fusion), channel_id=1, source_target_pairs={{0,4},{1,13},{2,6},{3,15},{4,8},{5,1},{6,10},{7,3},{8,12},{9,5},{1... | collective-permute-start | bytes 737288 | tf_op jit(solution)/shard_map/ppermute | solution.py:268
  18.9 2.2 %collective-permute-start.1 = (bf16[2,96,640]{2,1,0:T(8,128)(2,1)S(1)}, bf16[2,96,640]{2,1,0:T(8,128)(2,1)S(1)}, u32[]{:S(2)}, u32[]{:S(2)}) collective-permute-start(bf16[2,96,640]{2,1,0:T(8,128)(2,1)S(1)} %pad_maximum_fusion), channel_id=1, source_target_pairs={{0,2},{1,15},{2,4},{3,1},{4,6},{5,3},{6,8},{7,5},{8,10},{9,7},{10,... | collective-permute-start | bytes 737288 | tf_op jit(solution)/shard_map/ppermute | solution.py:268
  21.1 3.0 %legendre_rows.2.table = bf16[12,96,640]{2,1,0:T(8,128)(2,1)} custom-call(s32[1]{0:T(128)} %bitcast.wave_id, s32[1]{0:T(128)} %bitcast.1.field_id, s32[384]{0:T(512)} %wave_of_slot.3, s32[1536]{0:T(1024)} %lat_of_row.7, bf16[12,48,640]{2,1,0:T(8,128)(2,1)} %bitcast.17), custom_call_target="tpu_custom_call" | custom-call | bytes 11100000 | tf_op jit(solution)/shard_map/legendre_rows/pallas_call | solution.py:282
  24.7 4.4 %collective-permute-start.4 = (bf16[2,96,640]{2,1,0:T(8,128)(2,1)S(1)}, bf16[2,96,640]{2,1,0:T(8,128)(2,1)S(1)}, u32[]{:S(2)}, u32[]{:S(2)}) collective-permute-start(bf16[2,96,640]{2,1,0:T(8,128)(2,1)S(1)} %collective-permute-done.2.two), channel_id=1, source_target_pairs={{0,2},{1,15},{2,4},{3,1},{4,6},{5,3},{6,8},{7,5},{8,10},{9,7},{10,... | collective-permute-start | bytes 737288 | tf_op jit(solution)/shard_map/ppermute | solution.py:268
  29.2 2.0 %collective-permute-start.5 = (bf16[96,640]{1,0:T(8,128)(2,1)S(1)}, bf16[96,640]{1,0:T(8,128)(2,1)S(1)}, u32[]{:S(2)}, u32[]{:S(2)}) collective-permute-start(bf16[96,640]{1,0:T(8,128)(2,1)S(1)} %reshape.25.own), channel_id=1, source_target_pairs={{0,8},{1,9},{2,10},{3,11},{4,12},{5,13},{6,14},{7,15},{8,0},{9,1},... | collective-permute-start | bytes 368648 | tf_op jit(solution)/shard_map/ppermute | solution.py:268
  31.2 3.0 %legendre_rows.3.table.table_swapped = bf16[12,96,640]{2,1,0:T(8,128)(2,1)} custom-call(s32[1]{0:T(128)} %bitcast.wave_id, s32[1]{0:T(128)S(6)} %xor.3.field_id, s32[384]{0:T(512)} %wave_of_slot.3, s32[1536]{0:T(1024)} %lat_of_row.7, bf16[12,48,640]{2,1,0:T(8,128)(2,1)} %copy-done.6), custom_call_target="tpu_custom_call" | custom-call | bytes 11100000 | tf_op jit(solution)/shard_map/legendre_rows/pallas_call | solution.py:282
  34.2 5.7 %collective-permute-done.5.four = bf16[96,640]{1,0:T(8,128)(2,1)S(1)} collective-permute-done((bf16[96,640]{1,0:T(8,128)(2,1)S(1)}, bf16[96,640]{1,0:T(8,128)(2,1)S(1)}, u32[]{:S(2)}, u32[]{:S(2)}) %collective-permute-start.5) | collective-permute-done | bytes 122912 | tf_op jit(solution)/shard_map/ppermute | solution.py:268
  41.3 3.4 %legendre_forward.2 = bf16[32,36,128]{2,1,0:T(8,128)(2,1)} custom-call(bf16[96,640]{1,0:T(8,128)(2,1)} %copy-done.2, bf16[2,96,640]{2,1,0:T(8,128)(2,1)} %copy-done.4, bf16[2,96,640]{2,1,0:T(8,128)(2,1)} %copy-done.3, bf16[2,96,640]{2,1,0:T(8,128)(2,1)} %copy-done.5, bf16[96,640]{1,0:T(8,128)(2,1)} %copy-done.7, ...), custom_call_target="tpu_custom_call" | custom-call | bytes 7400000 | tf_op jit(solution)/shard_map/legendre_forward/pallas_call | solution.py:299
  44.7 5.5 %collective-permute-start.6 = (bf16[32,36,128]{2,1,0:T(8,128)(2,1)}, bf16[32,36,128]{2,1,0:T(8,128)(2,1)S(1)}, u32[]{:S(2)}, u32[]{:S(2)}) collective-permute-start(bf16[32,36,128]{2,1,0:T(8,128)(2,1)} %legendre_forward.2), channel_id=1, source_target_pairs={{0,1},{1,0},{2,3},{3,2},{4,5},{5,4},{6,7},{7,6},{8,9},{9,8},{10,11... | collective-permute-start | bytes 884744 | tf_op jit(solution)/shard_map/ppermute | solution.py:268
  52.4 3.1 %legendre_forward.3 = bf16[32,36,128]{2,1,0:T(8,128)(2,1)} custom-call(bf16[96,640]{1,0:T(8,128)(2,1)} %copy-done.2, bf16[2,96,640]{2,1,0:T(8,128)(2,1)} %copy-done.4, bf16[2,96,640]{2,1,0:T(8,128)(2,1)} %copy-done.3, bf16[2,96,640]{2,1,0:T(8,128)(2,1)} %copy-done.5, bf16[96,640]{1,0:T(8,128)(2,1)} %copy-done.7, bf16[12,96,640]{2,1,0:T(8,128)(2,1)} %legendre_rows.2.table, ...), custom_call_target="tpu_custom_call" | custom-call | bytes 7400000 | tf_op jit(solution)/shard_map/legendre_forward/pallas_call | solution.py:299
  55.5 9.3 %all-to-all-start = ((bf16[32,36,128]{2,1,0:T(8,128)(2,1)}), bf16[32,36,128]{2,1,0:T(8,128)(2,1)S(1)}, u32[]{:S(2)}, u32[]{:S(2)}) async-start(bf16[32,36,128]{2,1,0:T(8,128)(2,1)} %legendre_forward.3), calls=%async_computation | async-start | bytes 655360 | tf_op jit(solution)/shard_map/all_to_all | solution.py:312
  65.4 4.2 %fourier_tables.1 = (bf16[3,256,768]{2,1,0:T(8,128)(2,1)}, bf16[3,768,256]{2,1,0:T(8,128)(2,1)}, f32[3,16,768]{2,1,0:T(8,128)}, f32[3,16,768]{2,1,0:T(8,128)}, bf16[128,128]{1,0:T(8,128)(2,1)}) custom-call(s32[1]{0:T(128)} %bitcast.wave_id, s32[1]{0:T(128)} %bitcast.1.field_id, s32[1536]{0:T(1024)} %lat_of_row.7, s32[768]{0:T(1024)} %lon_count.3, ...), custom_call_target="tpu_custom_call" | custom-call | bytes 14800000 | tf_op jit(solution)/shard_map/fourier_tables/pallas_call | solution.py:315
  69.6 7.9 %all-to-all-done.arrived = bf16[32,36,128]{2,1,0:T(8,128)(2,1)S(1)} async-done(((bf16[32,36,128]{2,1,0:T(8,128)(2,1)}), bf16[32,36,128]{2,1,0:T(8,128)(2,1)S(1)}, u32[]{:S(2)}, u32[]{:S(2)}) %all-to-all-start) | async-done | bytes 294944 | tf_op jit(solution)/shard_map/all_to_all | solution.py:312
  78.3 7.3 %fourier.1 = (bf16[3,64,3200]{2,1,0:T(8,128)(2,1)}, bf16[32,36,128]{2,1,0:T(8,128)(2,1)}) custom-call(s32[1]{0:T(128)} %bitcast.wave_id, s32[1]{0:T(128)} %bitcast.1.field_id, s32[1536]{0:T(1024)} %lat_of_row.7, s32[768]{0:T(1024)} %lon_count.3, bf16[32,36,128]{2,1,0:T(8,128)(2,1)} %copy-done.1, bf16[3,256,768]{2,1,0:T(8,128)(2,1)} %get-tuple-element.32.inner, ...), custom_call_target="tpu_custom_call" | custom-call | bytes 25900000 | tf_op jit(solution)/shard_map/fourier/pallas_call | solution.py:334
  85.6 16.0 %all_to_all.10.arrived = bf16[32,36,128]{2,1,0:T(8,128)(2,1)S(1)} all-to-all(bf16[32,36,128]{2,1,0:T(8,128)(2,1)} %get-tuple-element.38), channel_id=1, replica_groups=mesh['wave'=32,'field'=16] {'wave'}, dimensions={0} | all-to-all | bytes 589824 | tf_op jit(solution)/shard_map/all_to_all | solution.py:353
  101.6 5.6 %collective-permute-start.7 = (bf16[32,36,128]{2,1,0:T(8,128)(2,1)S(1)}, bf16[32,36,128]{2,1,0:T(8,128)(2,1)S(1)}, u32[]{:S(2)}, u32[]{:S(2)}) collective-permute-start(bf16[32,36,128]{2,1,0:T(8,128)(2,1)S(1)} %all_to_all.10.arrived), channel_id=1, source_target_pairs={{0,1},{1,0},{2,3},{3,2},{4,5},{5,4},{6,7},{7,6},{8,9},{9,8},{10,11... | collective-permute-start | bytes 884744 | tf_op jit(solution)/shard_map/ppermute | solution.py:268
  109.2 3.9 %legendre_inverse.1 = (f32[96,640]{1,0:T(8,128)}, bf16[96,640]{1,0:T(8,128)(2,1)}, bf16[96,640]{1,0:T(8,128)(2,1)}, bf16[96,640]{1,0:T(8,128)(2,1)}, bf16[96,640...) custom-call(bf16[32,36,128]{2,1,0:T(8,128)(2,1)} %copy-done, bf16[32,36,128]{2,1,0:T(8,128)(2,1)} %copy-done.8, ...), custom_call_target="tpu_custom_call" | custom-call | bytes 11100000 | tf_op jit(solution)/shard_map/legendre_inverse/pallas_call | solution.py:356
  115.0 4.1 %collective-permute-start.8 = (bf16[96,640]{1,0:T(8,128)(2,1)}, bf16[96,640]{1,0:T(8,128)(2,1)S(1)}, u32[]{:S(2)}, u32[]{:S(2)}) collective-permute-start(bf16[96,640]{1,0:T(8,128)(2,1)} %get-tuple-element.40), channel_id=1, source_target_pairs={{0,8},{1,9},{2,10},{3,11},{4,12},{5,13},{6,14},{7,15},{8,0},{9,1},... | collective-permute-start | bytes 368648 | tf_op jit(solution)/shard_map/ppermute | solution.py:268
  119.1 2.9 %collective-permute-start.9 = (bf16[96,640]{1,0:T(8,128)(2,1)}, bf16[96,640]{1,0:T(8,128)(2,1)S(1)}, u32[]{:S(2)}, u32[]{:S(2)}) collective-permute-start(bf16[96,640]{1,0:T(8,128)(2,1)} %get-tuple-element.41), channel_id=1, source_target_pairs={{0,14},{1,3},{2,0},{3,5},{4,2},{5,7},{6,4},{7,9},{8,6},{9,11},{10,... | collective-permute-start | bytes 368648 | tf_op jit(solution)/shard_map/ppermute | solution.py:268
  122.0 4.4 %collective-permute-start.10 = (bf16[96,640]{1,0:T(8,128)(2,1)}, bf16[96,640]{1,0:T(8,128)(2,1)S(1)}, u32[]{:S(2)}, u32[]{:S(2)}) collective-permute-start(bf16[96,640]{1,0:T(8,128)(2,1)} %get-tuple-element.42), channel_id=1, source_target_pairs={{0,15},{1,2},{2,1},{3,4},{4,3},{5,6},{6,5},{7,8},{8,7},{9,10},{10,... | collective-permute-start | bytes 368648 | tf_op jit(solution)/shard_map/ppermute | solution.py:268
  127.5 2.2 %collective-permute-start.12 = (bf16[96,640]{1,0:T(8,128)(2,1)S(1)}, bf16[96,640]{1,0:T(8,128)(2,1)S(1)}, u32[]{:S(2)}, u32[]{:S(2)}) collective-permute-start(bf16[96,640]{1,0:T(8,128)(2,1)S(1)} %get-tuple-element.46), channel_id=1, source_target_pairs={{0,12},{1,5},{2,14},{3,7},{4,0},{5,9},{6,2},{7,11},{8,4},{9,13},{1... | collective-permute-start | bytes 368648 | tf_op jit(solution)/shard_map/ppermute | solution.py:268
  129.6 4.0 %collective-permute-start.13 = (bf16[96,640]{1,0:T(8,128)(2,1)S(1)}, bf16[96,640]{1,0:T(8,128)(2,1)S(1)}, u32[]{:S(2)}, u32[]{:S(2)}) collective-permute-start(bf16[96,640]{1,0:T(8,128)(2,1)S(1)} %get-tuple-element.47), channel_id=1, source_target_pairs={{0,13},{1,4},{2,15},{3,6},{4,1},{5,8},{6,3},{7,10},{8,5},{9,12},{1... | collective-permute-start | bytes 368648 | tf_op jit(solution)/shard_map/ppermute | solution.py:268
  133.7 2.9 %collective-permute-done.12 = bf16[96,640]{1,0:T(8,128)(2,1)S(1)} collective-permute-done((bf16[96,640]{1,0:T(8,128)(2,1)S(1)}, bf16[96,640]{1,0:T(8,128)(2,1)S(1)}, u32[]{:S(2)}, u32[]{:S(2)}) %collective-permute-start.12) | collective-permute-done | bytes 122912 | tf_op jit(solution)/shard_map/ppermute | solution.py:268
  (44 shorter events, 16.7 us)
Async XLA Ops:
  0.6 24.1 %collective-permute-start.3 = (bf16[12,48,640]{2,1,0:T(8,128)(2,1)}, bf16[12,48,640]{2,1,0:T(8,128)(2,1)S(1)}, u32[]{:S(2)}, u32[]{:S(2)}) collective-permute-start(bf16[12,48,640]{2,1,0:T(8,128)(2,1)} %bitcast.16), channel_id=1, source_target_pairs={{0,1},{1,0},{2,3},{3,2},{4,5},{5,4},{6,7},{7,6},{8,9},{9,8},{10,11... | collective-permute-start | bytes 2211848 | tf_op jit(solution)/shard_map/ppermute | solution.py:268
  10.4 18.8 %copy-start.2 = (bf16[96,640]{1,0:T(8,128)(2,1)}, bf16[96,640]{1,0:T(8,128)(2,1)S(1)}, u32[]{:S(2)}) copy-start(bf16[96,640]{1,0:T(8,128)(2,1)S(1)} %reshape.25.own) | copy-start | bytes 368644
  10.4 3.2 %collective-permute-start = (bf16[96,640]{1,0:T(8,128)(2,1)S(1)}, bf16[96,640]{1,0:T(8,128)(2,1)S(1)}, u32[]{:S(2)}, u32[]{:S(2)}) collective-permute-start(bf16[96,640]{1,0:T(8,128)(2,1)S(1)} %reshape.25.own), channel_id=1, source_target_pairs={{0,1},{1,0},{2,3},{3,2},{4,5},{5,4},{6,7},{7,6},{8,9},{9,8},{10,11... | collective-permute-start | bytes 368648 | tf_op jit(solution)/shard_map/ppermute | solution.py:268
  13.6 11.0 %collective-permute-start.2 = (bf16[2,96,640]{2,1,0:T(8,128)(2,1)S(1)}, bf16[2,96,640]{2,1,0:T(8,128)(2,1)S(1)}, u32[]{:S(2)}, u32[]{:S(2)}) collective-permute-start(bf16[2,96,640]{2,1,0:T(8,128)(2,1)S(1)} %pad_maximum_fusion), channel_id=1, source_target_pairs={{0,4},{1,13},{2,6},{3,15},{4,8},{5,1},{6,10},{7,3},{8,12},{9,5},{1... | collective-permute-start | bytes 737288 | tf_op jit(solution)/shard_map/ppermute | solution.py:268
  18.9 21.0 %collective-permute-start.1 = (bf16[2,96,640]{2,1,0:T(8,128)(2,1)S(1)}, bf16[2,96,640]{2,1,0:T(8,128)(2,1)S(1)}, u32[]{:S(2)}, u32[]{:S(2)}) collective-permute-start(bf16[2,96,640]{2,1,0:T(8,128)(2,1)S(1)} %pad_maximum_fusion), channel_id=1, source_target_pairs={{0,2},{1,15},{2,4},{3,1},{4,6},{5,3},{6,8},{7,5},{8,10},{9,7},{10,... | collective-permute-start | bytes 737288 | tf_op jit(solution)/shard_map/ppermute | solution.py:268
  24.7 15.2 %copy-start.3 = (bf16[2,96,640]{2,1,0:T(8,128)(2,1)}, bf16[2,96,640]{2,1,0:T(8,128)(2,1)S(1)}, u32[]{:S(2)}) copy-start(bf16[2,96,640]{2,1,0:T(8,128)(2,1)S(1)} %collective-permute-done.2.two) | copy-start | bytes 737284
  24.7 6.5 %copy-start.6 = (bf16[12,48,640]{2,1,0:T(8,128)(2,1)}, bf16[12,48,640]{2,1,0:T(8,128)(2,1)S(1)}, u32[]{:S(2)}) copy-start(bf16[12,48,640]{2,1,0:T(8,128)(2,1)S(1)} %collective-permute-done.3.legendre) | copy-start | bytes 2211844
  24.7 15.2 %collective-permute-start.4 = (bf16[2,96,640]{2,1,0:T(8,128)(2,1)S(1)}, bf16[2,96,640]{2,1,0:T(8,128)(2,1)S(1)}, u32[]{:S(2)}, u32[]{:S(2)}) collective-permute-start(bf16[2,96,640]{2,1,0:T(8,128)(2,1)S(1)} %collective-permute-done.2.two), channel_id=1, source_target_pairs={{0,2},{1,15},{2,4},{3,1},{4,6},{5,3},{6,8},{7,5},{8,10},{9,7},{10,... | collective-permute-start | bytes 737288 | tf_op jit(solution)/shard_map/ppermute | solution.py:268
  29.2 10.7 %collective-permute-start.5 = (bf16[96,640]{1,0:T(8,128)(2,1)S(1)}, bf16[96,640]{1,0:T(8,128)(2,1)S(1)}, u32[]{:S(2)}, u32[]{:S(2)}) collective-permute-start(bf16[96,640]{1,0:T(8,128)(2,1)S(1)} %reshape.25.own), channel_id=1, source_target_pairs={{0,8},{1,9},{2,10},{3,11},{4,12},{5,13},{6,14},{7,15},{8,0},{9,1},... | collective-permute-start | bytes 368648 | tf_op jit(solution)/shard_map/ppermute | solution.py:268
  39.9 0.7 copy-start.4
  44.7 20.1 %copy-start.10 = (s32[384]{0:T(512)S(1)}, s32[384]{0:T(512)}, u32[]{:S(2)}) copy-start(s32[384]{0:T(512)} %wave_of_slot.3) | copy-start | bytes 4612
  44.7 6.9 %collective-permute-start.6 = (bf16[32,36,128]{2,1,0:T(8,128)(2,1)}, bf16[32,36,128]{2,1,0:T(8,128)(2,1)S(1)}, u32[]{:S(2)}, u32[]{:S(2)}) collective-permute-start(bf16[32,36,128]{2,1,0:T(8,128)(2,1)} %legendre_forward.2), channel_id=1, source_target_pairs={{0,1},{1,0},{2,3},{3,2},{4,5},{5,4},{6,7},{7,6},{8,9},{9,8},{10,11... | collective-permute-start | bytes 884744 | tf_op jit(solution)/shard_map/ppermute | solution.py:268
  51.7 0.7 copy-start.9
  55.5 22.1 %all-to-all-start = ((bf16[32,36,128]{2,1,0:T(8,128)(2,1)}), bf16[32,36,128]{2,1,0:T(8,128)(2,1)S(1)}, u32[]{:S(2)}, u32[]{:S(2)}) async-start(bf16[32,36,128]{2,1,0:T(8,128)(2,1)} %legendre_forward.3), calls=%async_computation | async-start | bytes 655360 | tf_op jit(solution)/shard_map/all_to_all | solution.py:312
  77.6 0.7 copy-start.1
  101.6 6.8 %copy-start = (bf16[32,36,128]{2,1,0:T(8,128)(2,1)}, bf16[32,36,128]{2,1,0:T(8,128)(2,1)S(1)}, u32[]{:S(2)}) copy-start(bf16[32,36,128]{2,1,0:T(8,128)(2,1)S(1)} %all_to_all.10.arrived) | copy-start | bytes 884740
  101.6 6.8 %collective-permute-start.7 = (bf16[32,36,128]{2,1,0:T(8,128)(2,1)S(1)}, bf16[32,36,128]{2,1,0:T(8,128)(2,1)S(1)}, u32[]{:S(2)}, u32[]{:S(2)}) collective-permute-start(bf16[32,36,128]{2,1,0:T(8,128)(2,1)S(1)} %all_to_all.10.arrived), channel_id=1, source_target_pairs={{0,1},{1,0},{2,3},{3,2},{4,5},{5,4},{6,7},{7,6},{8,9},{9,8},{10,11... | collective-permute-start | bytes 884744 | tf_op jit(solution)/shard_map/ppermute | solution.py:268
  108.4 0.7 copy-start.8
  113.1 13.4 %collective-permute-start.11 = (bf16[2,96,640]{2,1,0:T(8,128)(2,1)}, bf16[2,96,640]{2,1,0:T(8,128)(2,1)S(1)}, u32[]{:S(2)}, u32[]{:S(2)}) collective-permute-start(bf16[2,96,640]{2,1,0:T(8,128)(2,1)} %get-tuple-element.44), channel_id=1, source_target_pairs={{0,14},{1,3},{2,0},{3,5},{4,2},{5,7},{6,4},{7,9},{8,6},{9,11},{10,... | collective-permute-start | bytes 737288 | tf_op jit(solution)/shard_map/ppermute | solution.py:268
  115.0 18.7 %collective-permute-start.8 = (bf16[96,640]{1,0:T(8,128)(2,1)}, bf16[96,640]{1,0:T(8,128)(2,1)S(1)}, u32[]{:S(2)}, u32[]{:S(2)}) collective-permute-start(bf16[96,640]{1,0:T(8,128)(2,1)} %get-tuple-element.40), channel_id=1, source_target_pairs={{0,8},{1,9},{2,10},{3,11},{4,12},{5,13},{6,14},{7,15},{8,0},{9,1},... | collective-permute-start | bytes 368648 | tf_op jit(solution)/shard_map/ppermute | solution.py:268
  119.1 14.6 %collective-permute-start.9 = (bf16[96,640]{1,0:T(8,128)(2,1)}, bf16[96,640]{1,0:T(8,128)(2,1)S(1)}, u32[]{:S(2)}, u32[]{:S(2)}) collective-permute-start(bf16[96,640]{1,0:T(8,128)(2,1)} %get-tuple-element.41), channel_id=1, source_target_pairs={{0,14},{1,3},{2,0},{3,5},{4,2},{5,7},{6,4},{7,9},{8,6},{9,11},{10,... | collective-permute-start | bytes 368648 | tf_op jit(solution)/shard_map/ppermute | solution.py:268
  122.0 11.7 %collective-permute-start.10 = (bf16[96,640]{1,0:T(8,128)(2,1)}, bf16[96,640]{1,0:T(8,128)(2,1)S(1)}, u32[]{:S(2)}, u32[]{:S(2)}) collective-permute-start(bf16[96,640]{1,0:T(8,128)(2,1)} %get-tuple-element.42), channel_id=1, source_target_pairs={{0,15},{1,2},{2,1},{3,4},{4,3},{5,6},{6,5},{7,8},{8,7},{9,10},{10,... | collective-permute-start | bytes 368648 | tf_op jit(solution)/shard_map/ppermute | solution.py:268
  127.5 9.2 %collective-permute-start.12 = (bf16[96,640]{1,0:T(8,128)(2,1)S(1)}, bf16[96,640]{1,0:T(8,128)(2,1)S(1)}, u32[]{:S(2)}, u32[]{:S(2)}) collective-permute-start(bf16[96,640]{1,0:T(8,128)(2,1)S(1)} %get-tuple-element.46), channel_id=1, source_target_pairs={{0,12},{1,5},{2,14},{3,7},{4,0},{5,9},{6,2},{7,11},{8,4},{9,13},{1... | collective-permute-start | bytes 368648 | tf_op jit(solution)/shard_map/ppermute | solution.py:268
  129.6 7.3 %collective-permute-start.13 = (bf16[96,640]{1,0:T(8,128)(2,1)S(1)}, bf16[96,640]{1,0:T(8,128)(2,1)S(1)}, u32[]{:S(2)}, u32[]{:S(2)}) collective-permute-start(bf16[96,640]{1,0:T(8,128)(2,1)S(1)} %get-tuple-element.47), channel_id=1, source_target_pairs={{0,13},{1,4},{2,15},{3,6},{4,1},{5,8},{6,3},{7,10},{8,5},{9,12},{1... | collective-permute-start | bytes 368648 | tf_op jit(solution)/shard_map/ppermute | solution.py:268
  (2 other events, 1.3 us)

commit v2 on v1

--- a/solution.py
+++ b/solution.py
@@ -12,7 +12,6 @@
 LANES = 128
 BLOCK = 256
 BLOCKS = -(-LONPAD // BLOCK)
-MESH_VMEM = 56 * 1024 * 1024
 
 NT = (((1,), (1,)), ((), ()))
 NN = (((1,), (0,)), ((), ()))
@@ -23,8 +22,8 @@
     return lax.dot_general(a, b, dims, preferred_element_type=jnp.float32)
 
 
-def params():
-    return pltpu.CompilerParams(vmem_limit_bytes=MESH_VMEM)
+def params(mebibytes):
+    return pltpu.CompilerParams(vmem_limit_bytes=mebibytes * 1024 * 1024)
 
 
 def cost(micros):
@@ -124,31 +123,24 @@
     place[...] = (lax.broadcasted_iota(jnp.int32, (LANES, LANES), 0) == target).astype(jnp.bfloat16)
 
 
-def legendre_forward_kernel(own, one, two, three, four, table, *refs, second):
-    swapped, out, held = (None,) * (3 - len(refs)) + refs
+def legendre_forward_kernel(*refs):
+    pieces, (table, table_swapped, out, held) = refs[:-4], refs[-4:]
     slots, rows, degrees = table.shape
     waves = out.shape[0]
     row_count = rows // waves
     each = slots * row_count
-    empty = jnp.zeros((64, degrees), jnp.float32)
     for pair in range(slots // 2):
-        at = pl.ds(16 * pair, 16)
-        both = [own[at, :]] + [piece[i, at, :] for piece in (one, two, three) for i in range(2)] + [four[at, :]]
-        both = [b.astype(jnp.float32) for b in both]
+        both = [piece[16 * pair : 16 * pair + 16, :].astype(jnp.float32) for piece in pieces]
         for half in range(2):
             slot = 2 * pair + half
-            spec = [b[8 * half : 8 * half + 8] for b in both]
-            spec = [empty] + spec if second else spec + [empty]
-            sums = dot(table[slot], jnp.concatenate(spec, axis=0).astype(jnp.bfloat16), NT)
+            spec = jnp.concatenate([b[8 * half : 8 * half + 8] for b in both], axis=0).astype(jnp.bfloat16)
+            sums = jnp.concatenate([dot(table[slot], spec, NT), dot(table_swapped[slot], spec, NT)], axis=1)
             for member in range(row_count):
                 held[pl.ds(slot * row_count + member, waves, stride=each), :] = sums[
                     waves * member : waves * (member + 1)
                 ]
     for wave in range(waves):
-        lines = held[wave * each : (wave + 1) * each, :]
-        if swapped is not None:
-            lines = lines + swapped[wave].astype(jnp.float32)
-        out[wave] = lines.astype(jnp.bfloat16)
+        out[wave] = held[wave * each : (wave + 1) * each, :].astype(jnp.bfloat16)
 
 
 def legendre_inverse_kernel(
@@ -186,7 +178,7 @@
 
 
 def fourier_kernel(
-    wave_id, field_id, lat_of_row, lon_count, arrived, inner, inner_t, outer_fwd, outer_inv, place,
+    wave_id, field_id, lat_of_row, lon_count, arrived, swapped, inner, inner_t, outer_fwd, outer_inv, place,
     grid_out, sent, held, back, turned, products, *, fields,
 ):
     row_count = inner.shape[0]
@@ -196,8 +188,11 @@
     half = lon_count.shape[0]
     levels = grid_out.shape[1]
     wave, field = wave_id[0], field_id[0]
+    mine = lax.broadcasted_iota(jnp.int32, (1, LANES), 1) < 64
     for source in range(waves):
-        held[source * each : (source + 1) * each, :] = arrived[source].astype(jnp.float32)
+        held[source * each : (source + 1) * each, :] = jnp.where(
+            mine, arrived[source].astype(jnp.float32), swapped[source].astype(jnp.float32)
+        )
     for member in range(row_count):
         lat = lat_of_row[(wave * fields + field) * row_count + member]
         hemi = jnp.where(lat >= half, 2 * half - 1 - lat, lat)
@@ -271,13 +266,11 @@
         return hop(x, 0, 1)
 
     own = jnp.transpose(spectra, (0, 1, 3, 2)).reshape(coded, degrees)
-    four = hop(own, 4)
+    two, two_x = hop(own, 2), hop(own, -2, 1)
+    one, one_x = hop(own, 1), hop(own, -1, 1)
     legendre = jnp.transpose(legendre, (0, 2, 1))
     legendre_swapped = swap(legendre)
-    partner, legendre = lax.optimization_barrier((swap(own), legendre))
-    pair = jnp.stack([own, partner])
-    two = hop(pair, 2)
-    one = hop(pair, 1)
+
     def order_rows(values, band_of):
         return pl.pallas_call(
             functools.partial(legendre_rows_kernel, waves=waves, fields=fields),
@@ -285,29 +278,27 @@
             in_specs=[smem(), smem(), smem(), smem(), vmem()],
             out_specs=vmem(),
             scratch_shapes=[pltpu.VMEM((rows, LANES), jnp.float32)] * 2,
-            compiler_params=params(),
+            compiler_params=params(8),
             cost_estimate=cost(3),
             name="legendre_rows",
         )(wave_id, band_of, wave_of_slot, lat_of_row, values)
 
     two, table = lax.optimization_barrier((two, order_rows(legendre, field_id)))
-    two, legendre_swapped = lax.optimization_barrier((two, legendre_swapped))
-    three = hop(two, 1)
+    two_x, legendre_swapped = lax.optimization_barrier((two_x, legendre_swapped))
+    three, three_x = hop(two, 1), hop(two_x, 1)
+    four = hop(two, 2)
     table_swapped = order_rows(legendre_swapped, field_id ^ 1)
 
-    def forward(legendre_table, second, *swapped):
-        return pl.pallas_call(
-            functools.partial(legendre_forward_kernel, second=second),
-            out_shape=jax.ShapeDtypeStruct((waves, each, LANES), jnp.bfloat16),
-            in_specs=[vmem()] * (6 + len(swapped)),
-            out_specs=vmem(),
-            scratch_shapes=[pltpu.VMEM((waves * each, LANES), jnp.float32)],
-            compiler_params=params(),
-            cost_estimate=cost(2),
-            name="legendre_forward",
-        )(own, one, two, three, four, legendre_table, *swapped)
-
-    outgoing = forward(table, False, swap(forward(table_swapped, True)))
+    outgoing = pl.pallas_call(
+        legendre_forward_kernel,
+        out_shape=jax.ShapeDtypeStruct((waves, each, LANES), jnp.bfloat16),
+        in_specs=[vmem()] * 10,
+        out_specs=vmem(),
+        scratch_shapes=[pltpu.VMEM((waves * each, LANES), jnp.float32)],
+        compiler_params=params(16),
+        cost_estimate=cost(4),
+        name="legendre_forward",
+    )(own, one, one_x, two, two_x, three, three_x, four, table, table_swapped)
     outgoing, lat_weight = lax.optimization_barrier((outgoing, lat_weight))
     arrived = lax.all_to_all(outgoing, "wave", split_axis=0, concat_axis=0, tiled=True)
 
@@ -323,7 +314,7 @@
         ),
         in_specs=[smem()] * 5 + [vmem()],
         out_specs=(vmem(),) * 5,
-        compiler_params=params(),
+        compiler_params=params(16),
         cost_estimate=cost(4),
         name="fourier_tables",
     )(
@@ -331,13 +322,14 @@
         wave_of_slot.astype(jnp.float32).reshape(1, all_slots),
     )
 
+    arrived, place = lax.optimization_barrier((arrived, place))
     grid_field, sent = pl.pallas_call(
         functools.partial(fourier_kernel, fields=fields),
         out_shape=(
             jax.ShapeDtypeStruct((row_count, levels, LONPAD), jnp.bfloat16),
             jax.ShapeDtypeStruct((waves, each, LANES), jnp.bfloat16),
         ),
-        in_specs=[smem()] * 4 + [vmem()] * 6,
+        in_specs=[smem()] * 4 + [vmem()] * 7,
         out_specs=(vmem(), vmem()),
         scratch_shapes=[
             pltpu.VMEM((waves * each, LANES), jnp.float32),
@@ -345,10 +337,10 @@
             pltpu.VMEM((BLOCKS * levels, 2 * all_slots), jnp.bfloat16),
             pltpu.VMEM((BLOCKS * levels, BLOCK), jnp.bfloat16),
         ],
-        compiler_params=params(),
+        compiler_params=params(24),
         cost_estimate=cost(7),
         name="fourier",
-    )(wave_id, field_id, lat_of_row, lon_count, arrived, inner, inner_t, outer_fwd, outer_inv, place)
+    )(wave_id, field_id, lat_of_row, lon_count, arrived, swap(arrived), inner, inner_t, outer_fwd, outer_inv, place)
 
     returned = lax.all_to_all(sent, "wave", split_axis=0, concat_axis=0, tiled=True)
 
@@ -362,17 +354,17 @@
         in_specs=[vmem()] * 4,
         out_specs=(vmem(),) * 7,
         scratch_shapes=[pltpu.VMEM((waves * each, LANES), jnp.float32)] * 2,
-        compiler_params=params(),
+        compiler_params=params(16),
         cost_estimate=cost(3),
         name="legendre_inverse",
     )(returned, swap(returned), table, table_swapped)
 
-    def add(a, b):
-        return (a.astype(jnp.float32) + b.astype(jnp.float32)).astype(jnp.bfloat16)
-
-    three = hop(three, -1)
-    landed = [hop(four, -4), hop(one, -1), hop(one_other, -1, 1)]
-    landed += [hop(add(two, three[0]), -2), hop(add(two_other, three[1]), -2, 1)]
+    def add(*terms):
+        return sum(x.astype(jnp.float32) for x in terms).astype(jnp.bfloat16)
+
+    three, four = hop(three, -1), hop(four, -2)
+    landed = [hop(one, -1), hop(one_other, -1, 1)]
+    landed += [hop(add(two, three[0], four), -2), hop(add(two_other, three[1]), -2, 1)]
     total = total + sum(x.astype(jnp.float32) for x in landed)
     spectral = jnp.transpose(total.reshape(slots, 2, cols, degrees), (0, 1, 3, 2))
     return grid_field, spectral

time: 141 us -> 132 us (0.936)
  Pallas kernels: 28 us -> 15.5 us
  waiting for transfers between devices: 20.5 us -> 10.7 us
  local copies, waits for them, and re-layouts: 6.8 us -> 14.4 us
  starting transfers between devices: 64.6 us -> 71.2 us
  other arithmetic: 2.11 us -> 0.17 us
    unnamed x22 -> x32, local copies, waits for them, and re-layouts: 3.6 us -> 12.6 us
    ppermute x14 -> x16, starting transfers between devices: 55.2 us -> 61.5 us  [hop(): return lax.ppermute(x, 'field', pairs)]
    ppermute x14 -> x16, waiting for transfers between devices: 12.6 us -> 6.81 us  [hop(): return lax.ppermute(x, 'field', pairs)]
    all_to_all x1, waiting for transfers between devices: 7.93 us -> 3.91 us  [shards(): lax.all_to_all(outgoing, 'wave', split_axis=0, concat_axis=0, tiled=True)]
    pallas_call x2 -> x1, Pallas kernels: 6.52 us -> 2.69 us  [shards(): pl.pallas_call(legendre_forward_kernel, out_shape=jax.ShapeDtypeStruct((w...]
    pallas_call x2, Pallas kernels: 6.01 us -> 2.87 us  [order_rows(): pl.pallas_call(functools.partial(legendre_rows_kernel, waves=waves, field...]
    pallas_call x1, Pallas kernels: 3.92 us -> 0.92 us  [shards(): pl.pallas_call(legendre_inverse_kernel, out_shape=(jax.ShapeDtypeStruct((...]
    pallas_call x1, Pallas kernels: 4.23 us -> 2.72 us  [shards(): pl.pallas_call(functools.partial(fourier_tables_kernel, fields=fields, zs...]
  transfers between devices with their start and end apart: 15 -> 17, of which waited for: 8 -> 6; matrix products, arithmetic and copies ran while one was open for 3% -> 1% of each run, Pallas kernels for 7% -> 4%
where the time goes in v2:
time: 132 us; the launch traced here: 130 us
  starting transfers between devices  71.2 us (54%)
  blocking collectives  16.9 us (13%)
  Pallas kernels  15.5 us (12%)
  local copies, waits for them, and re-layouts  14.4 us (11%)
  waiting for transfers between devices  10.7 us (8%)
    ppermute x16, starting transfers between devices, hop(): return lax.ppermute(x, 'field', pairs)  61.5 us
    all_to_all x1, blocking collectives, shards(): lax.all_to_all(sent, 'wave', split_axis=0, concat_axis=0, tiled=True)  16.9 us
    unnamed x32, local copies, waits for them, and re-layouts  12.6 us
    all_to_all x1, starting transfers between devices, shards(): lax.all_to_all(outgoing, 'wave', split_axis=0, concat_axis=0, tiled=True)  9.67 us
    ppermute x16, waiting for transfers between devices, hop(): return lax.ppermute(x, 'field', pairs)  6.81 us
    pallas_call x1, Pallas kernels, shards(): pl.pallas_call(functools.partial(fourier_kernel, fields=fields), out_shap...  6.31 us
    all_to_all x1, waiting for transfers between devices, shards(): lax.all_to_all(outgoing, 'wave', split_axis=0, concat_axis=0, tiled=True)  3.91 us
    pallas_call x2, Pallas kernels, order_rows(): pl.pallas_call(functools.partial(legendre_rows_kernel, waves=waves, field...  2.87 us
  transfers between devices with their start and end apart: 17, of which 6 were waited for; matrix products, arithmetic and copies ran while one was open for 1% of the time, Pallas kernels for 4%

profile of v2, /device:TPU:1, one launch (start us, length us, event | category | flops | bytes accessed | tf_op | source)
XLA Modules:
  0.0 129.8 jit_solution(13030999821328976451)
XLA Ops:
  0.6 8.8 %collective-permute-start.4 = (bf16[12,48,640]{2,1,0:T(8,128)(2,1)}, bf16[12,48,640]{2,1,0:T(8,128)(2,1)S(1)}, u32[]{:S(2)}, u32[]{:S(2)}) collective-permute-start(bf16[12,48,640]{2,1,0:T(8,128)(2,1)} %bitcast.15), channel_id=1, source_target_pairs={{0,1},{1,0},{2,3},{3,2},{4,5},{5,4},{6,7},{7,6},{8,9},{9,8},{10,11... | collective-permute-start | bytes 2211848 | tf_op jit(solution)/shard_map/ppermute | solution.py:263
  10.4 5.3 %collective-permute-start.2 = (bf16[96,640]{1,0:T(8,128)(2,1)S(1)}, bf16[96,640]{1,0:T(8,128)(2,1)S(1)}, u32[]{:S(2)}, u32[]{:S(2)}) collective-permute-start(bf16[96,640]{1,0:T(8,128)(2,1)S(1)} %reshape.25.refs_0_), channel_id=1, source_target_pairs={{0,4},{1,13},{2,6},{3,15},{4,8},{5,1},{6,10},{7,3},{8,12},{9,5},{1... | collective-permute-start | bytes 368648 | tf_op jit(solution)/shard_map/ppermute | solution.py:263
  15.7 2.3 %collective-permute-start.3 = (bf16[96,640]{1,0:T(8,128)(2,1)S(1)}, bf16[96,640]{1,0:T(8,128)(2,1)S(1)}, u32[]{:S(2)}, u32[]{:S(2)}) collective-permute-start(bf16[96,640]{1,0:T(8,128)(2,1)S(1)} %reshape.25.refs_0_), channel_id=1, source_target_pairs={{0,13},{1,4},{2,15},{3,6},{4,1},{5,8},{6,3},{7,10},{8,5},{9,12},{1... | collective-permute-start | bytes 368648 | tf_op jit(solution)/shard_map/ppermute | solution.py:263
  18.0 3.2 %collective-permute-start.1 = (bf16[96,640]{1,0:T(8,128)(2,1)S(1)}, bf16[96,640]{1,0:T(8,128)(2,1)S(1)}, u32[]{:S(2)}, u32[]{:S(2)}) collective-permute-start(bf16[96,640]{1,0:T(8,128)(2,1)S(1)} %reshape.25.refs_0_), channel_id=1, source_target_pairs={{0,15},{1,2},{2,1},{3,4},{4,3},{5,6},{6,5},{7,8},{8,7},{9,10},{10,... | collective-permute-start | bytes 368648 | tf_op jit(solution)/shard_map/ppermute | solution.py:263
  21.3 3.4 %collective-permute-start = (bf16[96,640]{1,0:T(8,128)(2,1)S(1)}, bf16[96,640]{1,0:T(8,128)(2,1)}, u32[]{:S(2)}, u32[]{:S(2)}) collective-permute-start(bf16[96,640]{1,0:T(8,128)(2,1)S(1)} %reshape.25.refs_0_), channel_id=1, source_target_pairs={{0,2},{1,15},{2,4},{3,1},{4,6},{5,3},{6,8},{7,5},{8,10},{9,7},{10,... | collective-permute-start | bytes 368648 | tf_op jit(solution)/shard_map/ppermute | solution.py:263
  28.6 1.9 %collective-permute-start.7 = (bf16[96,640]{1,0:T(8,128)(2,1)S(1)}, bf16[96,640]{1,0:T(8,128)(2,1)S(1)}, u32[]{:S(2)}, u32[]{:S(2)}) collective-permute-start(bf16[96,640]{1,0:T(8,128)(2,1)S(1)} %collective-permute-done.2.refs_3_), channel_id=1, source_target_pairs={{0,4},{1,13},{2,6},{3,15},{4,8},{5,1},{6,10},{7,3},{8,12},{9,5},{1... | collective-permute-start | bytes 368648 | tf_op jit(solution)/shard_map/ppermute | solution.py:263
  30.6 2.7 %collective-permute-start.5 = (bf16[96,640]{1,0:T(8,128)(2,1)S(1)}, bf16[96,640]{1,0:T(8,128)(2,1)S(1)}, u32[]{:S(2)}, u32[]{:S(2)}) collective-permute-start(bf16[96,640]{1,0:T(8,128)(2,1)S(1)} %collective-permute-done.2.refs_3_), channel_id=1, source_target_pairs={{0,2},{1,15},{2,4},{3,1},{4,6},{5,3},{6,8},{7,5},{8,10},{9,7},{10,... | collective-permute-start | bytes 368648 | tf_op jit(solution)/shard_map/ppermute | solution.py:263
  34.1 4.3 %collective-permute-start.6 = (bf16[96,640]{1,0:T(8,128)(2,1)S(1)}, bf16[96,640]{1,0:T(8,128)(2,1)S(1)}, u32[]{:S(2)}, u32[]{:S(2)}) collective-permute-start(bf16[96,640]{1,0:T(8,128)(2,1)S(1)} %collective-permute-done.3.refs_4_), channel_id=1, source_target_pairs={{0,2},{1,15},{2,4},{3,1},{4,6},{5,3},{6,8},{7,5},{8,10},{9,7},{10,... | collective-permute-start | bytes 368648 | tf_op jit(solution)/shard_map/ppermute | solution.py:263
  41.1 2.7 %legendre_forward.1 = bf16[32,36,128]{2,1,0:T(8,128)(2,1)} custom-call(bf16[96,640]{1,0:T(8,128)(2,1)S(1)} %reshape.25.refs_0_, bf16[96,640]{1,0:T(8,128)(2,1)} %collective-permute-done.refs_1_, bf16[96,640]{1,0:T(8,128)(2,1)S(1)} %collective-permute-done.1.refs_2_, bf16[96,640]{1,0:T(8,128)(2,1)S(1)} %collective-permute-done.2.refs_3_, ...), custom_call_target="tpu_custom_call" | custom-call | bytes 14800000 | tf_op jit(solution)/shard_map/legendre_forward/pallas_call | solution.py:292
  43.8 9.7 %all-to-all-start = ((bf16[32,36,128]{2,1,0:T(8,128)(2,1)}), bf16[32,36,128]{2,1,0:T(8,128)(2,1)S(1)}, u32[]{:S(2)}, u32[]{:S(2)}) async-start(bf16[32,36,128]{2,1,0:T(8,128)(2,1)} %legendre_forward.1), calls=%async_computation | async-start | bytes 655360 | tf_op jit(solution)/shard_map/all_to_all | solution.py:303
  54.8 2.7 %fourier_tables.1 = (bf16[3,256,768]{2,1,0:T(8,128)(2,1)S(1)}, bf16[3,768,256]{2,1,0:T(8,128)(2,1)S(1)}, f32[3,16,768]{2,1,0:T(8,128)S(1)}, f32[3,16,768]{2,1,0:T(8,128)S(1)}, bf16[128,128]{1,0:T(8,128)(2,1)S(1)}) custom-call(s32[1]{0:T(128)} %bitcast.wave_id, s32[1]{0:T(128)} %bitcast.1.field_id, s32[1536]{0:T(1024)S(1)} %copy-done.10, s32[768]{0:T(1024)S(1)} %copy-done.13, ...), custom_call_target="tpu_custom_call" | custom-call | bytes 14800000 | tf_op jit(solution)/shard_map/fourier_tables/pallas_call | solution.py:306
  60.3 3.9 %all-to-all-done.arrived = bf16[32,36,128]{2,1,0:T(8,128)(2,1)S(1)} async-done(((bf16[32,36,128]{2,1,0:T(8,128)(2,1)}), bf16[32,36,128]{2,1,0:T(8,128)(2,1)S(1)}, u32[]{:S(2)}, u32[]{:S(2)}) %all-to-all-start) | async-done | bytes 294944 | tf_op jit(solution)/shard_map/all_to_all | solution.py:303
  64.2 8.1 %collective-permute-start.8 = (bf16[32,36,128]{2,1,0:T(8,128)(2,1)S(1)}, bf16[32,36,128]{2,1,0:T(8,128)(2,1)S(1)}, u32[]{:S(2)}, u32[]{:S(2)}) collective-permute-start(bf16[32,36,128]{2,1,0:T(8,128)(2,1)S(1)} %all-to-all-done.arrived), channel_id=1, source_target_pairs={{0,1},{1,0},{2,3},{3,2},{4,5},{5,4},{6,7},{7,6},{8,9},{9,8},{10,11... | collective-permute-start | bytes 884744 | tf_op jit(solution)/shard_map/ppermute | solution.py:263
  77.6 6.3 %fourier.1 = (bf16[3,64,3200]{2,1,0:T(8,128)(2,1)}, bf16[32,36,128]{2,1,0:T(8,128)(2,1)S(1)}) custom-call(s32[1]{0:T(128)} %bitcast.wave_id, s32[1]{0:T(128)} %bitcast.1.field_id, s32[1536]{0:T(1024)S(1)} %copy-done.10, s32[768]{0:T(1024)S(1)} %copy-done.14, bf16[32,36,128]{2,1,0:T(8,128)(2,1)S(1)} %all-to-all-done.arrived, ...), custom_call_target="tpu_custom_call" | custom-call | bytes 25900000 | tf_op jit(solution)/shard_map/fourier/pallas_call | solution.py:326
  83.9 16.9 %all_to_all.10.arrived = bf16[32,36,128]{2,1,0:T(8,128)(2,1)S(1)} all-to-all(bf16[32,36,128]{2,1,0:T(8,128)(2,1)S(1)} %get-tuple-element.38), channel_id=1, replica_groups=mesh['wave'=32,'field'=16] {'wave'}, dimensions={0} | all-to-all | bytes 589824 | tf_op jit(solution)/shard_map/all_to_all | solution.py:345
  100.8 4.3 %collective-permute-start.9 = (bf16[32,36,128]{2,1,0:T(8,128)(2,1)S(1)}, bf16[32,36,128]{2,1,0:T(8,128)(2,1)S(1)}, u32[]{:S(2)}, u32[]{:S(2)}) collective-permute-start(bf16[32,36,128]{2,1,0:T(8,128)(2,1)S(1)} %all_to_all.10.arrived), channel_id=1, source_target_pairs={{0,1},{1,0},{2,3},{3,2},{4,5},{5,4},{6,7},{7,6},{8,9},{9,8},{10,11... | collective-permute-start | bytes 884744 | tf_op jit(solution)/shard_map/ppermute | solution.py:263
  107.3 1.9 %collective-permute-start.12 = (bf16[2,96,640]{2,1,0:T(8,128)(2,1)S(1)}, bf16[2,96,640]{2,1,0:T(8,128)(2,1)S(1)}, u32[]{:S(2)}, u32[]{:S(2)}) collective-permute-start(bf16[2,96,640]{2,1,0:T(8,128)(2,1)S(1)} %get-tuple-element.43), channel_id=1, source_target_pairs={{0,14},{1,3},{2,0},{3,5},{4,2},{5,7},{6,4},{7,9},{8,6},{9,11},{10,... | collective-permute-start | bytes 737288 | tf_op jit(solution)/shard_map/ppermute | solution.py:263
  109.2 2.4 %collective-permute-start.13 = (bf16[96,640]{1,0:T(8,128)(2,1)S(1)}, bf16[96,640]{1,0:T(8,128)(2,1)S(1)}, u32[]{:S(2)}, u32[]{:S(2)}) collective-permute-start(bf16[96,640]{1,0:T(8,128)(2,1)S(1)} %get-tuple-element.44), channel_id=1, source_target_pairs={{0,12},{1,5},{2,14},{3,7},{4,0},{5,9},{6,2},{7,11},{8,4},{9,13},{1... | collective-permute-start | bytes 368648 | tf_op jit(solution)/shard_map/ppermute | solution.py:263
  111.6 2.3 %collective-permute-start.10 = (bf16[96,640]{1,0:T(8,128)(2,1)S(1)}, bf16[96,640]{1,0:T(8,128)(2,1)S(1)}, u32[]{:S(2)}, u32[]{:S(2)}) collective-permute-start(bf16[96,640]{1,0:T(8,128)(2,1)S(1)} %get-tuple-element.40), channel_id=1, source_target_pairs={{0,14},{1,3},{2,0},{3,5},{4,2},{5,7},{6,4},{7,9},{8,6},{9,11},{10,... | collective-permute-start | bytes 368648 | tf_op jit(solution)/shard_map/ppermute | solution.py:263
  113.9 4.1 %collective-permute-start.11 = (bf16[96,640]{1,0:T(8,128)(2,1)S(1)}, bf16[96,640]{1,0:T(8,128)(2,1)S(1)}, u32[]{:S(2)}, u32[]{:S(2)}) collective-permute-start(bf16[96,640]{1,0:T(8,128)(2,1)S(1)} %get-tuple-element.41), channel_id=1, source_target_pairs={{0,15},{1,2},{2,1},{3,4},{4,3},{5,6},{6,5},{7,8},{8,7},{9,10},{10,... | collective-permute-start | bytes 368648 | tf_op jit(solution)/shard_map/ppermute | solution.py:263
  118.5 3.3 %collective-permute-start.14 = (bf16[96,640]{1,0:T(8,128)(2,1)S(1)}, bf16[96,640]{1,0:T(8,128)(2,1)S(1)}, u32[]{:S(2)}, u32[]{:S(2)}) collective-permute-start(bf16[96,640]{1,0:T(8,128)(2,1)S(1)} %get-tuple-element.46), channel_id=1, source_target_pairs={{0,12},{1,5},{2,14},{3,7},{4,0},{5,9},{6,2},{7,11},{8,4},{9,13},{1... | collective-permute-start | bytes 368648 | tf_op jit(solution)/shard_map/ppermute | solution.py:263
  121.8 3.2 %collective-permute-start.15 = (bf16[96,640]{1,0:T(8,128)(2,1)S(1)}, bf16[96,640]{1,0:T(8,128)(2,1)S(1)}, u32[]{:S(2)}, u32[]{:S(2)}) collective-permute-start(bf16[96,640]{1,0:T(8,128)(2,1)S(1)} %get-tuple-element.47), channel_id=1, source_target_pairs={{0,13},{1,4},{2,15},{3,6},{4,1},{5,8},{6,3},{7,10},{8,5},{9,12},{1... | collective-permute-start | bytes 368648 | tf_op jit(solution)/shard_map/ppermute | solution.py:263
  125.0 1.9 %collective-permute-done.14 = bf16[96,640]{1,0:T(8,128)(2,1)S(1)} collective-permute-done((bf16[96,640]{1,0:T(8,128)(2,1)S(1)}, bf16[96,640]{1,0:T(8,128)(2,1)S(1)}, u32[]{:S(2)}, u32[]{:S(2)}) %collective-permute-start.14) | collective-permute-done | bytes 122912 | tf_op jit(solution)/shard_map/ppermute | solution.py:263
  127.0 2.0 %collective-permute-done.15 = bf16[96,640]{1,0:T(8,128)(2,1)S(1)} collective-permute-done((bf16[96,640]{1,0:T(8,128)(2,1)S(1)}, bf16[96,640]{1,0:T(8,128)(2,1)S(1)}, u32[]{:S(2)}, u32[]{:S(2)}) %collective-permute-start.15) | collective-permute-done | bytes 122912 | tf_op jit(solution)/shard_map/ppermute | solution.py:263
  (55 shorter events, 21.2 us)
Async XLA Ops:
  0.6 32.6 %collective-permute-start.4 = (bf16[12,48,640]{2,1,0:T(8,128)(2,1)}, bf16[12,48,640]{2,1,0:T(8,128)(2,1)S(1)}, u32[]{:S(2)}, u32[]{:S(2)}) collective-permute-start(bf16[12,48,640]{2,1,0:T(8,128)(2,1)} %bitcast.15), channel_id=1, source_target_pairs={{0,1},{1,0},{2,3},{3,2},{4,5},{5,4},{6,7},{7,6},{8,9},{9,8},{10,11... | collective-permute-start | bytes 2211848 | tf_op jit(solution)/shard_map/ppermute | solution.py:263
  9.4 29.0 %copy-start.10 = (s32[1536]{0:T(1024)S(1)}, s32[1536]{0:T(1024)}, u32[]{:S(2)}) copy-start(s32[1536]{0:T(1024)} %lat_of_row.7) | copy-start | bytes 18436
  9.4 29.0 %copy-start.12 = (s32[384]{0:T(512)S(1)}, s32[384]{0:T(512)}, u32[]{:S(2)}) copy-start(s32[384]{0:T(512)} %wave_of_slot.3) | copy-start | bytes 4612
  10.4 18.2 %collective-permute-start.2 = (bf16[96,640]{1,0:T(8,128)(2,1)S(1)}, bf16[96,640]{1,0:T(8,128)(2,1)S(1)}, u32[]{:S(2)}, u32[]{:S(2)}) collective-permute-start(bf16[96,640]{1,0:T(8,128)(2,1)S(1)} %reshape.25.refs_0_), channel_id=1, source_target_pairs={{0,4},{1,13},{2,6},{3,15},{4,8},{5,1},{6,10},{7,3},{8,12},{9,5},{1... | collective-permute-start | bytes 368648 | tf_op jit(solution)/shard_map/ppermute | solution.py:263
  15.7 14.9 %collective-permute-start.3 = (bf16[96,640]{1,0:T(8,128)(2,1)S(1)}, bf16[96,640]{1,0:T(8,128)(2,1)S(1)}, u32[]{:S(2)}, u32[]{:S(2)}) collective-permute-start(bf16[96,640]{1,0:T(8,128)(2,1)S(1)} %reshape.25.refs_0_), channel_id=1, source_target_pairs={{0,13},{1,4},{2,15},{3,6},{4,1},{5,8},{6,3},{7,10},{8,5},{9,12},{1... | collective-permute-start | bytes 368648 | tf_op jit(solution)/shard_map/ppermute | solution.py:263
  18.0 23.0 %collective-permute-start.1 = (bf16[96,640]{1,0:T(8,128)(2,1)S(1)}, bf16[96,640]{1,0:T(8,128)(2,1)S(1)}, u32[]{:S(2)}, u32[]{:S(2)}) collective-permute-start(bf16[96,640]{1,0:T(8,128)(2,1)S(1)} %reshape.25.refs_0_), channel_id=1, source_target_pairs={{0,15},{1,2},{2,1},{3,4},{4,3},{5,6},{6,5},{7,8},{8,7},{9,10},{10,... | collective-permute-start | bytes 368648 | tf_op jit(solution)/shard_map/ppermute | solution.py:263
  21.3 19.8 %collective-permute-start = (bf16[96,640]{1,0:T(8,128)(2,1)S(1)}, bf16[96,640]{1,0:T(8,128)(2,1)}, u32[]{:S(2)}, u32[]{:S(2)}) collective-permute-start(bf16[96,640]{1,0:T(8,128)(2,1)S(1)} %reshape.25.refs_0_), channel_id=1, source_target_pairs={{0,2},{1,15},{2,4},{3,1},{4,6},{5,3},{6,8},{7,5},{8,10},{9,7},{10,... | collective-permute-start | bytes 368648 | tf_op jit(solution)/shard_map/ppermute | solution.py:263
  24.7 1.1 copy-start.4
  28.6 12.4 %collective-permute-start.7 = (bf16[96,640]{1,0:T(8,128)(2,1)S(1)}, bf16[96,640]{1,0:T(8,128)(2,1)S(1)}, u32[]{:S(2)}, u32[]{:S(2)}) collective-permute-start(bf16[96,640]{1,0:T(8,128)(2,1)S(1)} %collective-permute-done.2.refs_3_), channel_id=1, source_target_pairs={{0,4},{1,13},{2,6},{3,15},{4,8},{5,1},{6,10},{7,3},{8,12},{9,5},{1... | collective-permute-start | bytes 368648 | tf_op jit(solution)/shard_map/ppermute | solution.py:263
  30.6 10.5 %collective-permute-start.5 = (bf16[96,640]{1,0:T(8,128)(2,1)S(1)}, bf16[96,640]{1,0:T(8,128)(2,1)S(1)}, u32[]{:S(2)}, u32[]{:S(2)}) collective-permute-start(bf16[96,640]{1,0:T(8,128)(2,1)S(1)} %collective-permute-done.2.refs_3_), channel_id=1, source_target_pairs={{0,2},{1,15},{2,4},{3,1},{4,6},{5,3},{6,8},{7,5},{8,10},{9,7},{10,... | collective-permute-start | bytes 368648 | tf_op jit(solution)/shard_map/ppermute | solution.py:263
  34.1 6.9 %collective-permute-start.6 = (bf16[96,640]{1,0:T(8,128)(2,1)S(1)}, bf16[96,640]{1,0:T(8,128)(2,1)S(1)}, u32[]{:S(2)}, u32[]{:S(2)}) collective-permute-start(bf16[96,640]{1,0:T(8,128)(2,1)S(1)} %collective-permute-done.3.refs_4_), channel_id=1, source_target_pairs={{0,2},{1,15},{2,4},{3,1},{4,6},{5,3},{6,8},{7,5},{8,10},{9,7},{10,... | collective-permute-start | bytes 368648 | tf_op jit(solution)/shard_map/ppermute | solution.py:263
  38.5 1.1 copy-start.6
  43.8 20.4 %all-to-all-start = ((bf16[32,36,128]{2,1,0:T(8,128)(2,1)}), bf16[32,36,128]{2,1,0:T(8,128)(2,1)S(1)}, u32[]{:S(2)}, u32[]{:S(2)}) async-start(bf16[32,36,128]{2,1,0:T(8,128)(2,1)} %legendre_forward.1), calls=%async_computation | async-start | bytes 655360 | tf_op jit(solution)/shard_map/all_to_all | solution.py:303
  58.6 1.0 copy-start.2
  64.2 9.3 %collective-permute-start.8 = (bf16[32,36,128]{2,1,0:T(8,128)(2,1)S(1)}, bf16[32,36,128]{2,1,0:T(8,128)(2,1)S(1)}, u32[]{:S(2)}, u32[]{:S(2)}) collective-permute-start(bf16[32,36,128]{2,1,0:T(8,128)(2,1)S(1)} %all-to-all-done.arrived), channel_id=1, source_target_pairs={{0,1},{1,0},{2,3},{3,2},{4,5},{5,4},{6,7},{7,6},{8,9},{9,8},{10,11... | collective-permute-start | bytes 884744 | tf_op jit(solution)/shard_map/ppermute | solution.py:263
  73.5 1.3 copy-start.1
  74.8 1.3 copy-start.3
  100.8 5.6 %collective-permute-start.9 = (bf16[32,36,128]{2,1,0:T(8,128)(2,1)S(1)}, bf16[32,36,128]{2,1,0:T(8,128)(2,1)S(1)}, u32[]{:S(2)}, u32[]{:S(2)}) collective-permute-start(bf16[32,36,128]{2,1,0:T(8,128)(2,1)S(1)} %all_to_all.10.arrived), channel_id=1, source_target_pairs={{0,1},{1,0},{2,3},{3,2},{4,5},{5,4},{6,7},{7,6},{8,9},{9,8},{10,11... | collective-permute-start | bytes 884744 | tf_op jit(solution)/shard_map/ppermute | solution.py:263
  107.3 11.1 %collective-permute-start.12 = (bf16[2,96,640]{2,1,0:T(8,128)(2,1)S(1)}, bf16[2,96,640]{2,1,0:T(8,128)(2,1)S(1)}, u32[]{:S(2)}, u32[]{:S(2)}) collective-permute-start(bf16[2,96,640]{2,1,0:T(8,128)(2,1)S(1)} %get-tuple-element.43), channel_id=1, source_target_pairs={{0,14},{1,3},{2,0},{3,5},{4,2},{5,7},{6,4},{7,9},{8,6},{9,11},{10,... | collective-permute-start | bytes 737288 | tf_op jit(solution)/shard_map/ppermute | solution.py:263
  109.2 9.2 %collective-permute-start.13 = (bf16[96,640]{1,0:T(8,128)(2,1)S(1)}, bf16[96,640]{1,0:T(8,128)(2,1)S(1)}, u32[]{:S(2)}, u32[]{:S(2)}) collective-permute-start(bf16[96,640]{1,0:T(8,128)(2,1)S(1)} %get-tuple-element.44), channel_id=1, source_target_pairs={{0,12},{1,5},{2,14},{3,7},{4,0},{5,9},{6,2},{7,11},{8,4},{9,13},{1... | collective-permute-start | bytes 368648 | tf_op jit(solution)/shard_map/ppermute | solution.py:263
  111.6 13.4 %collective-permute-start.10 = (bf16[96,640]{1,0:T(8,128)(2,1)S(1)}, bf16[96,640]{1,0:T(8,128)(2,1)S(1)}, u32[]{:S(2)}, u32[]{:S(2)}) collective-permute-start(bf16[96,640]{1,0:T(8,128)(2,1)S(1)} %get-tuple-element.40), channel_id=1, source_target_pairs={{0,14},{1,3},{2,0},{3,5},{4,2},{5,7},{6,4},{7,9},{8,6},{9,11},{10,... | collective-permute-start | bytes 368648 | tf_op jit(solution)/shard_map/ppermute | solution.py:263
  113.9 11.1 %collective-permute-start.11 = (bf16[96,640]{1,0:T(8,128)(2,1)S(1)}, bf16[96,640]{1,0:T(8,128)(2,1)S(1)}, u32[]{:S(2)}, u32[]{:S(2)}) collective-permute-start(bf16[96,640]{1,0:T(8,128)(2,1)S(1)} %get-tuple-element.41), channel_id=1, source_target_pairs={{0,15},{1,2},{2,1},{3,4},{4,3},{5,6},{6,5},{7,8},{8,7},{9,10},{10,... | collective-permute-start | bytes 368648 | tf_op jit(solution)/shard_map/ppermute | solution.py:263
  118.5 8.5 %collective-permute-start.14 = (bf16[96,640]{1,0:T(8,128)(2,1)S(1)}, bf16[96,640]{1,0:T(8,128)(2,1)S(1)}, u32[]{:S(2)}, u32[]{:S(2)}) collective-permute-start(bf16[96,640]{1,0:T(8,128)(2,1)S(1)} %get-tuple-element.46), channel_id=1, source_target_pairs={{0,12},{1,5},{2,14},{3,7},{4,0},{5,9},{6,2},{7,11},{8,4},{9,13},{1... | collective-permute-start | bytes 368648 | tf_op jit(solution)/shard_map/ppermute | solution.py:263
  121.8 7.2 %collective-permute-start.15 = (bf16[96,640]{1,0:T(8,128)(2,1)S(1)}, bf16[96,640]{1,0:T(8,128)(2,1)S(1)}, u32[]{:S(2)}, u32[]{:S(2)}) collective-permute-start(bf16[96,640]{1,0:T(8,128)(2,1)S(1)} %get-tuple-element.47), channel_id=1, source_target_pairs={{0,13},{1,4},{2,15},{3,6},{4,1},{5,8},{6,3},{7,10},{8,5},{9,12},{1... | collective-permute-start | bytes 368648 | tf_op jit(solution)/shard_map/ppermute | solution.py:263
  (9 other events, 6.9 us)

commit v3 on v2

v3 whole, which is shorter than its diff:
```python
import functools
import math

import jax
import jax.numpy as jnp
from jax import lax
from jax.experimental import pallas as pl
from jax.experimental.pallas import tpu as pltpu
from jax.sharding import PartitionSpec as P

LONPAD = 3200
LANES = 128
BLOCK = 256
BLOCKS = -(-LONPAD // BLOCK)

NT = (((1,), (1,)), ((), ()))
NN = (((1,), (0,)), ((), ()))
TN = (((0,), (0,)), ((), ()))


def dot(a, b, dims):
    return lax.dot_general(a, b, dims, preferred_element_type=jnp.float32)


def params(mebibytes):
    return pltpu.CompilerParams(vmem_limit_bytes=mebibytes * 1024 * 1024)


def in_hbm(x):
    return pltpu.with_memory_space_constraint(x, pltpu.HBM)


def cost(micros):
    return pl.CostEstimate(flops=0, bytes_accessed=int(micros * 3.7e6), transcendentals=0)


def smem():
    return pl.BlockSpec(memory_space=pltpu.SMEM)


def vmem():
    return pl.BlockSpec(memory_space=pltpu.VMEM)


def hbm():
    return pl.BlockSpec(memory_space=pltpu.HBM)


def side_of(core):
    return 1 - 2 * core


def pair_kernel(own, partner, out, mine, held, sem):
    copy = pltpu.make_async_copy(own, mine, sem)
    copy.start()
    slots, parts, cols, _ = mine.shape
    for at, source in ((1, partner), (0, mine)):
        if at == 0:
            copy.wait()
        for slot in range(slots):
            for part in range(parts):
                row = (slot * parts + part) * cols
                held[row : row + cols, :] = source[slot, part].astype(jnp.float32)
        out[at] = held[...].astype(jnp.bfloat16)


def ordered_rows(chosen, south, live, legendre, out):
    slots, band, degrees = legendre.shape
    odd = (lax.broadcasted_iota(jnp.int32, (1, degrees), 1) & 1).astype(jnp.float32)
    sign = 1.0 - 2.0 * (south[:, :1] * odd)
    for slot in range(slots):
        table = dot(chosen[:, :band], legendre[slot], NN) * sign
        out[slot] = (table * live[slot : slot + 1, :]).astype(jnp.bfloat16)


def own_rows_kernel(
    wave_id, field_id, wave_of_slot, lat_of_row, legendre,
    out, chosen_x, south_x, live,
    slot_waves, row_lats, held, pick, south, sems, *, waves, fields,
):
    copies = [
        pltpu.make_async_copy(source, target, sems.at[i])
        for i, (source, target) in enumerate(((lat_of_row, row_lats), (wave_of_slot, slot_waves), (legendre, held)))
    ]
    for copy in copies:
        copy.start()
    slots, band, degrees = held.shape
    rows = out.shape[1]
    row_count = rows // waves
    half = row_lats.shape[0] // 2
    own, field = wave_id[0], field_id[0]
    lane = lax.broadcasted_iota(jnp.int32, (1, LANES), 1)
    copies[0].wait()
    for at in range(2):
        this = field ^ at
        for row in range(rows):
            member, wave = divmod(row, waves)
            lat = row_lats[(wave * fields + this) * row_count + member]
            is_south = lat >= half
            hemi = jnp.where(is_south, 2 * half - 1 - lat, lat) - this * band
            pick[at, row : row + 1, :] = (lane == hemi).astype(jnp.float32)
            south[at, row : row + 1, :] = jnp.broadcast_to(is_south.astype(jnp.float32), (1, LANES))
    chosen_x[...] = pick[1].astype(jnp.bfloat16)
    south_x[...] = south[1]
    offsets = lax.broadcasted_iota(jnp.int32, (1, degrees), 1)
    copies[1].wait()
    live[...] = jnp.zeros(live.shape, jnp.float32)
    for slot in range(slots):
        live[slot : slot + 1, :] = (offsets < degrees - slot_waves[own * slots + slot]).astype(jnp.float32)
    copies[2].wait()
    ordered_rows(pick[0].astype(jnp.bfloat16), south[0], live, held, out)


def partner_rows_kernel(chosen, south, live, legendre, out, held, sem):
    copy = pltpu.make_async_copy(legendre, held, sem)
    copy.start()
    copy.wait()
    ordered_rows(chosen[...], south[...], live, held, out)


def sin_cos(phase, period):
    inverse = 1.0 / period
    turns = (phase - jnp.floor(phase * inverse + 0.5) * period) * inverse
    quarter = jnp.floor(4.0 * turns + 0.5)
    w = (2.0 * math.pi) * (turns - 0.25 * quarter)
    w2 = w * w
    sine = w * (1.0 + w2 * (-1.0 / 6 + w2 * (1.0 / 120 + w2 * (-1.0 / 5040 + w2 * (1.0 / 362880)))))
    cosine = 1.0 + w2 * (-0.5 + w2 * (1.0 / 24 + w2 * (-1.0 / 720 + w2 * (1.0 / 40320))))
    size = jnp.abs(quarter)
    odd = size == 1.0
    flipped = size >= 2.0
    cos_out = jnp.where(odd, sine, cosine)
    sin_out = jnp.where(odd, cosine, sine)
    cos_out = jnp.where(flipped | (quarter == 1.0), -cos_out, cos_out)
    sin_out = jnp.where(flipped | (quarter == -1.0), -sin_out, sin_out)
    return cos_out, sin_out


def fourier_tables_kernel(
    wave_id, field_id, lat_of_row, lon_count, lat_weight, waves_row,
    inner_out, inner_t_out, outer_fwd_out, outer_inv_out, place_out, limits_out,
    inner, inner_t, outer_fwd, outer_inv, place, limits, sems, *, fields, zs,
):
    row_count = inner.shape[0]
    band = lat_weight.shape[0]
    half = lon_count.shape[0]
    slots = waves_row.shape[1]
    steps = outer_fwd.shape[1]
    wave, field = wave_id[0], field_id[0]
    for member in range(row_count):
        lat = lat_of_row[(wave * fields + field) * row_count + member]
        hemi = jnp.where(lat >= half, 2 * half - 1 - lat, lat)
        points = lon_count[hemi].astype(jnp.float32)
        period = jnp.broadcast_to(points, (1, LANES))
        limits[member] = jnp.broadcast_to(points, limits.shape[1:])
        weight = lat_weight[hemi - field * band] / jnp.sqrt(period)
        for part in range(slots // LANES):
            m = waves_row[:, part * LANES : (part + 1) * LANES]
            at = part * 2 * LANES
            x = lax.broadcasted_iota(jnp.int32, (BLOCK, LANES), 0).astype(jnp.float32)
            cosine, sine = sin_cos(x * m, period)
            both = jnp.concatenate([cosine, -sine], axis=1)
            inner[member, :, at : at + 2 * LANES] = both.astype(jnp.bfloat16)
            inner_t[member, at : at + 2 * LANES, :] = both.T.astype(jnp.bfloat16)
            x = (BLOCK * lax.broadcasted_iota(jnp.int32, (steps, LANES), 0)).astype(jnp.float32)
            cosine, sine = sin_cos(x * m, period)
            both = jnp.concatenate([cosine, sine], axis=1)
            outer_fwd[member, :, at : at + 2 * LANES] = both * (1.0 / math.sqrt(slots))
            outer_inv[member, :, at : at + 2 * LANES] = both * jnp.concatenate([weight, weight], axis=1)
    at = lax.broadcasted_iota(jnp.int32, (LANES, LANES), 1)
    chunk, part, low = (at >> 3) & 7, (at >> 2) & 1, at & 3
    core = (field & 1) ^ (at >> 6)
    back = (chunk + 1) >> 1
    other = ((chunk & 1) ^ 1) & (chunk > 0).astype(jnp.int32)
    z = ((field >> 1) - side_of(core) * back + zs) & (zs - 1)
    target = part * 64 + (2 * z + (core ^ other)) * 4 + low
    place[...] = (lax.broadcasted_iota(jnp.int32, (LANES, LANES), 0) == target).astype(jnp.bfloat16)
    results = (
        (inner, inner_out), (inner_t, inner_t_out), (outer_fwd, outer_fwd_out),
        (outer_inv, outer_inv_out), (place, place_out), (limits, limits_out),
    )
    copies = [pltpu.make_async_copy(source, target, sems.at[i]) for i, (source, target) in enumerate(results)]
    for copy in copies:
        copy.start()
    for copy in copies:
        copy.wait()


def legendre_forward_kernel(pair0, one, two, three, four, table, table_swapped, out, held):
    pieces = [pair0.at[0]] + [piece.at[i] for piece in (one, two, three) for i in range(2)] + [four]
    slots, rows, degrees = table.shape
    waves = out.shape[0]
    row_count = rows // waves
    each = slots * row_count
    for pair in range(slots // 2):
        both = [piece[16 * pair : 16 * pair + 16, :].astype(jnp.float32) for piece in pieces]
        for half in range(2):
            slot = 2 * pair + half
            spec = jnp.concatenate([b[8 * half : 8 * half + 8] for b in both], axis=0).astype(jnp.bfloat16)
            sums = jnp.concatenate([dot(table[slot], spec, NT), dot(table_swapped[slot], spec, NT)], axis=1)
            for member in range(row_count):
                held[pl.ds(slot * row_count + member, waves, stride=each), :] = sums[
                    waves * member : waves * (member + 1)
                ]
    for wave in range(waves):
        out[wave] = held[wave * each : (wave + 1) * each, :].astype(jnp.bfloat16)


def legendre_inverse_kernel(
    arrived, swapped, table, table_swapped, own, one, two, three, four, held, held_swapped
):
    slots, rows, degrees = table.shape
    waves = arrived.shape[0]
    row_count = rows // waves
    each = slots * row_count
    for wave in range(waves):
        held[wave * each : (wave + 1) * each, :] = arrived[wave].astype(jnp.float32)
        held_swapped[wave * each : (wave + 1) * each, :] = pltpu.roll(swapped[wave].astype(jnp.float32), 64, 1)

    def share(ref, slot, legendre):
        weighted = jnp.concatenate(
            [ref[pl.ds(slot * row_count + member, waves, stride=each), :] for member in range(row_count)], axis=0
        )
        return dot(weighted[:, :64].astype(jnp.bfloat16), legendre[slot], TN)

    for pair in range(slots // 2):
        at = pl.ds(16 * pair, 16)
        sums = [
            share(held, slot, table) + share(held_swapped, slot, table_swapped) for slot in (2 * pair, 2 * pair + 1)
        ]
        pieces = [jnp.concatenate([s[8 * chunk : 8 * chunk + 8] for s in sums], axis=0) for chunk in range(8)]
        own[at, :] = pieces[0]
        pieces = [piece.astype(jnp.bfloat16) for piece in pieces]
        for target, first in ((one, 1), (two, 3), (three, 5)):
            for i in range(2):
                target[i, at, :] = pieces[first + i]
        four[at, :] = pieces[7]


def fourier_kernel(
    arrived, swapped, inner_in, inner_t_in, outer_fwd_in, outer_inv_in, place_in, limits_in,
    grid_out, sent,
    inner, inner_t, outer_fwd, outer_inv, place, limits, held, back, turned, products, lines_out, sems, out_sems,
):
    inputs = (
        (place_in, place), (outer_fwd_in, outer_fwd), (limits_in, limits),
        (inner_t_in, inner_t), (inner_in, inner), (outer_inv_in, outer_inv),
    )
    copies = [pltpu.make_async_copy(source, target, sems.at[i]) for i, (source, target) in enumerate(inputs)]
    for copy in copies:
        copy.start()
    row_count = inner.shape[0]
    waves, each, _ = arrived.shape
    slots = waves * each // row_count
    parts = slots // LANES
    levels = grid_out.shape[1]
    mine = lax.broadcasted_iota(jnp.int32, (1, LANES), 1) < 64
    for source in range(waves):
        held[source * each : (source + 1) * each, :] = jnp.where(
            mine, arrived[source].astype(jnp.float32), swapped[source].astype(jnp.float32)
        )
    for copy in copies:
        copy.wait()
    column = lax.broadcasted_iota(jnp.int32, (1, BLOCK), 1).astype(jnp.float32)
    results = []
    for member in range(row_count):
        points = jnp.concatenate([limits[member, :1, :]] * (BLOCK // LANES), axis=1)
        lines = held[pl.ds(member, slots, stride=row_count), :].astype(jnp.bfloat16)
        coef = dot(place[...], lines, NT)
        for step in range(BLOCKS):
            rows = pl.ds(step * levels, levels)
            for part in range(parts):
                real = coef[:levels, part * LANES : (part + 1) * LANES]
                imag = coef[levels:, part * LANES : (part + 1) * LANES]
                at = part * 2 * LANES
                cosine = outer_fwd[member, step : step + 1, at : at + LANES]
                sine = outer_fwd[member, step : step + 1, at + LANES : at + 2 * LANES]
                turned[member, rows, at : at + LANES] = (real * cosine - imag * sine).astype(jnp.bfloat16)
                turned[member, rows, at + LANES : at + 2 * LANES] = (real * sine + imag * cosine).astype(jnp.bfloat16)
        values = dot(turned[member], inner_t[member], NN)
        for step in range(BLOCKS):
            width = min(BLOCK, LONPAD - step * BLOCK)
            line = values[step * levels : (step + 1) * levels]
            line = jnp.where(column + step * BLOCK < points, line, 0.0).astype(jnp.bfloat16)
            lines_out[member, :, step * BLOCK : step * BLOCK + width] = line[:, :width]
            line = line.astype(jnp.float32)
            partner = pltpu.roll(line, levels - 1, 0)
            products[member, step * levels : (step + 1) * levels, :] = (line * partner).astype(jnp.bfloat16)
        result = pltpu.make_async_copy(lines_out.at[member], grid_out.at[member], out_sems.at[member])
        result.start()
        results.append(result)
        reals, imags = [], []
        for part in range(parts):
            at = part * 2 * LANES
            sums = dot(products[member], inner[member, :, at : at + 2 * LANES], NN)
            real = jnp.zeros((levels, LANES), jnp.float32)
            imag = jnp.zeros((levels, LANES), jnp.float32)
            for step in range(BLOCKS):
                rows = slice(step * levels, (step + 1) * levels)
                cosine = outer_inv[member, step : step + 1, at : at + LANES]
                sine = outer_inv[member, step : step + 1, at + LANES : at + 2 * LANES]
                real += sums[rows, :LANES] * cosine + sums[rows, LANES:] * sine
                imag += sums[rows, LANES:] * cosine - sums[rows, :LANES] * sine
            reals.append(real)
            imags.append(imag)
        analysed = jnp.concatenate([jnp.concatenate(reals, axis=1), jnp.concatenate(imags, axis=1)], axis=0)
        back[pl.ds(member, slots, stride=row_count), :] = dot(
            analysed.T.astype(jnp.bfloat16), place[...], NN
        )
    for source in range(waves):
        sent[source] = back[source * each : (source + 1) * each, :].astype(jnp.bfloat16)
    for result in results:
        result.wait()


def add_three_kernel(two, three, four, out):
    out[0] = (
        two[0].astype(jnp.float32) + three[0].astype(jnp.float32) + four[...].astype(jnp.float32)
    ).astype(jnp.bfloat16)
    out[1] = (two[1].astype(jnp.float32) + three[1].astype(jnp.float32)).astype(jnp.bfloat16)


def add_two_kernel(one, two, out, out_other):
    for i, target in enumerate((out, out_other)):
        target[...] = (one[i].astype(jnp.float32) + two[i].astype(jnp.float32)).astype(jnp.bfloat16)


def add_own_kernel(own, one, one_other, out):
    total = own[...] + one[...].astype(jnp.float32) + one_other[...].astype(jnp.float32)
    groups, cols, _ = out.shape
    for group in range(groups):
        out[group] = total[group * cols : (group + 1) * cols]


def shards(spectra, legendre, lat_weight, wave_of_slot, lat_of_row, lon_count):
    waves = lax.axis_size("wave")
    fields = lax.axis_size("field")
    zs = fields // 2
    wave_id = lax.axis_index("wave").astype(jnp.int32).reshape(1)
    field_id = lax.axis_index("field").astype(jnp.int32).reshape(1)
    slots, _, degrees, cols = spectra.shape
    band = legendre.shape[2]
    rows = 2 * band
    row_count = rows // waves
    all_slots = wave_of_slot.shape[0]
    levels = cols * fields
    each = row_count * slots
    coded = slots * 2 * cols

    def hop(x, by, cross=0):
        pairs = [
            (i, (2 * (i // 2 + side_of(i % 2) * by) + (i % 2 ^ cross)) % fields) for i in range(fields)
        ]
        return lax.ppermute(x, "field", pairs)

    def swap(x):
        return hop(x, 0, 1)

    def local(kernel, out_shape, name, micros, mebibytes=8, in_specs=None, out_specs=None, scratch=()):
        if in_specs is None:
            in_specs = pl.BlockSpec(memory_space=pltpu.VMEM)
        return pl.pallas_call(
            kernel,
            out_shape=out_shape,
            in_specs=in_specs,
            out_specs=jax.tree.map(lambda _: vmem(), out_shape) if out_specs is None else out_specs,
            scratch_shapes=list(scratch),
            compiler_params=params(mebibytes),
            cost_estimate=cost(micros),
            name=name,
        )

    chunk = jax.ShapeDtypeStruct((coded, degrees), jnp.bfloat16)
    chunk_pair = jax.ShapeDtypeStruct((2, coded, degrees), jnp.bfloat16)
    row_table = jax.ShapeDtypeStruct((slots, rows, degrees), jnp.bfloat16)
    fourier_shape = jax.ShapeDtypeStruct((waves, each, LANES), jnp.bfloat16)
    float_rows = pltpu.VMEM((waves * each, LANES), jnp.float32)

    spectra = jnp.transpose(spectra, (0, 1, 3, 2))
    legendre = jnp.transpose(legendre, (0, 2, 1))
    pair = local(
        pair_kernel,
        chunk_pair,
        "pair",
        1,
        in_specs=[hbm(), vmem()],
        scratch=[
            pltpu.VMEM(spectra.shape, jnp.bfloat16),
            pltpu.VMEM((coded, degrees), jnp.float32),
            pltpu.SemaphoreType.DMA(()),
        ],
    )(in_hbm(spectra), swap(spectra))
    pair, legendre = lax.optimization_barrier((pair, legendre))
    legendre_x = swap(legendre)
    one = hop(pair, 1)
    table, chosen_x, south_x, live = local(
        functools.partial(own_rows_kernel, waves=waves, fields=fields),
        (
            row_table,
            jax.ShapeDtypeStruct((rows, LANES), jnp.bfloat16),
            jax.ShapeDtypeStruct((rows, LANES), jnp.float32),
            jax.ShapeDtypeStruct((-(-slots // 8) * 8, degrees), jnp.float32),
        ),
        "own_rows",
        2,
        in_specs=[smem(), smem(), hbm(), hbm(), hbm()],
        scratch=[
            pltpu.SMEM(wave_of_slot.shape, jnp.int32),
            pltpu.SMEM(lat_of_row.shape, jnp.int32),
            pltpu.VMEM((slots, band, degrees), jnp.bfloat16),
            pltpu.VMEM((2, rows, LANES), jnp.float32),
            pltpu.VMEM((2, rows, LANES), jnp.float32),
            pltpu.SemaphoreType.DMA((3,)),
        ],
    )(wave_id, field_id, in_hbm(wave_of_slot), in_hbm(lat_of_row), in_hbm(legendre))
    one, legendre_x, table = lax.optimization_barrier((one, legendre_x, table))
    two = hop(one, 1)
    table_x = local(
        partner_rows_kernel,
        row_table,
        "partner_rows",
        2,
        in_specs=[vmem(), vmem(), vmem(), hbm()],
        scratch=[pltpu.VMEM((slots, band, degrees), jnp.bfloat16), pltpu.SemaphoreType.DMA(())],
    )(chosen_x, south_x, live, in_hbm(legendre_x))
    two, table_x = lax.optimization_barrier((two, table_x))
    three = hop(two, 1)
    four = hop(three[0], 1)

    outgoing = local(
        legendre_forward_kernel, fourier_shape, "legendre_forward", 4, 16, in_specs=[vmem()] * 7, scratch=[float_rows]
    )(pair, one, two, three, four, table, table_x)
    outgoing, lat_weight = lax.optimization_barrier((outgoing, lat_weight))
    arrived = lax.all_to_all(outgoing, "wave", split_axis=0, concat_axis=0, tiled=True)

    tables = (
        ((row_count, BLOCK, 2 * all_slots), jnp.bfloat16),
        ((row_count, 2 * all_slots, BLOCK), jnp.bfloat16),
        ((row_count, 16, 2 * all_slots), jnp.float32),
        ((row_count, 16, 2 * all_slots), jnp.float32),
        ((LANES, LANES), jnp.bfloat16),
        ((row_count, 8, LANES), jnp.float32),
    )
    tables_vmem = [pltpu.VMEM(shape, kind) for shape, kind in tables]
    prepared = local(
        functools.partial(fourier_tables_kernel, fields=fields, zs=zs),
        [pltpu.HBM(shape, kind) for shape, kind in tables],
        "fourier_tables",
        4,
        16,
        in_specs=[smem()] * 5 + [vmem()],
        out_specs=[hbm()] * 6,
        scratch=tables_vmem + [pltpu.SemaphoreType.DMA((6,))],
    )(
        wave_id, field_id, lat_of_row, lon_count, lat_weight,
        wave_of_slot.astype(jnp.float32).reshape(1, all_slots),
    )
    arrived, prepared = lax.optimization_barrier((arrived, prepared))
    prepared = [in_hbm(x) for x in prepared]

    grid_field, sent = local(
        fourier_kernel,
        (jax.ShapeDtypeStruct((row_count, levels, LONPAD), jnp.bfloat16), fourier_shape),
        "fourier",
        6,
        32,
        in_specs=[vmem()] * 2 + [hbm()] * 6,
        out_specs=(hbm(), vmem()),
        scratch=tables_vmem + [
            float_rows,
            float_rows,
            pltpu.VMEM((row_count, BLOCKS * levels, 2 * all_slots), jnp.bfloat16),
            pltpu.VMEM((row_count, BLOCKS * levels, BLOCK), jnp.bfloat16),
            pltpu.VMEM((row_count, levels, LONPAD), jnp.bfloat16),
            pltpu.SemaphoreType.DMA((6,)),
            pltpu.SemaphoreType.DMA((row_count,)),
        ],
    )(arrived, swap(arrived), *prepared)

    returned = lax.all_to_all(sent, "wave", split_axis=0, concat_axis=0, tiled=True)

    own, one, two, three, four = local(
        legendre_inverse_kernel,
        (jax.ShapeDtypeStruct((coded, degrees), jnp.float32), chunk_pair, chunk_pair, chunk_pair, chunk),
        "legendre_inverse",
        2,
        16,
        in_specs=[vmem()] * 4,
        scratch=[float_rows, float_rows],
    )(returned, swap(returned), table, table_x)
    three, four = hop(three, -1), hop(four, -2)
    two = local(add_three_kernel, chunk_pair, "add_three", 1, in_specs=[vmem()] * 3)(two, three, four)
    one, one_other = local(add_two_kernel, (chunk, chunk), "add_two", 1, in_specs=[vmem()] * 2)(one, hop(two, -1))
    total = local(
        add_own_kernel,
        jax.ShapeDtypeStruct((2 * slots, cols, degrees), jnp.float32),
        "add_own",
        1,
        in_specs=[vmem()] * 3,
    )(own, hop(one, -1), hop(one_other, -1, 1))
    spectral = jnp.transpose(total.reshape(slots, 2, cols, degrees), (0, 1, 3, 2))
    return grid_field, spectral


def solution(mesh):
    in_specs = (P("wave", None, None, "field"), P("wave", None, "field"), P("field"), P(), P(), P())
    out_specs = (P(("wave", "field"), None, None), P("wave", None, None, "field"))
    return jax.shard_map(shards, mesh=mesh, in_specs=in_specs, out_specs=out_specs, check_vma=False)
```

time: 132 us -> 138 us (1.045)
  waiting for transfers between devices: 10.7 us -> 30.3 us
  local copies, waits for them, and re-layouts: 14.4 us -> 0.04 us
  Pallas kernels: 15.5 us -> 18.9 us
    ppermute x16 -> x13, waiting for transfers between devices: 6.81 us -> 23.8 us  [hop(): return lax.ppermute(x, 'field', pairs)]
    unnamed x32 -> x10, local copies, waits for them, and re-layouts: 12.6 us -> 0.03 us
    pallas_call x6 -> x10, Pallas kernels: 15.5 us -> 18.9 us  [the longest x1 6.69 us: shards(): local(fourier_kernel, (jax.ShapeDtypeStruct((row_count, levels, LONPAD),...]
    all_to_all x1, waiting for transfers between devices: 3.91 us -> 6.49 us  [shards(): lax.all_to_all(outgoing, 'wave', split_axis=0, concat_axis=0, tiled=True)]
    reshape x2 -> x0, local copies, waits for them, and re-layouts: 1.71 us -> none  [the longest x1 0.94 us: shards(): own = jnp.transpose(spectra, (0, 1, 3, 2)).reshape(coded, degrees)]
    ppermute x16 -> x13, starting transfers between devices: 61.5 us -> 60.2 us  [hop(): return lax.ppermute(x, 'field', pairs)]
  transfers between devices with their start and end apart: 17 -> 14, of which waited for: 6 -> 11; matrix products, arithmetic and copies ran while one was open for 1% -> 0% of each run, Pallas kernels for 4% -> 6%
where the time goes in v3:
time: 138 us; the launch traced here: 136 us
  starting transfers between devices  69.9 us (51%)
  waiting for transfers between devices  30.3 us (22%)
  Pallas kernels  18.9 us (14%)
  blocking collectives  16.4 us (12%)
    ppermute x13, starting transfers between devices, hop(): return lax.ppermute(x, 'field', pairs)  60.2 us
    ppermute x13, waiting for transfers between devices, hop(): return lax.ppermute(x, 'field', pairs)  23.8 us
    all_to_all x1, blocking collectives, shards(): lax.all_to_all(sent, 'wave', split_axis=0, concat_axis=0, tiled=True)  16.4 us
    all_to_all x1, starting transfers between devices, shards(): lax.all_to_all(outgoing, 'wave', split_axis=0, concat_axis=0, tiled=True)  9.67 us
    pallas_call x1, Pallas kernels, shards(): local(fourier_kernel, (jax.ShapeDtypeStruct((row_count, levels, LONPAD),...  6.69 us
    all_to_all x1, waiting for transfers between devices, shards(): lax.all_to_all(outgoing, 'wave', split_axis=0, concat_axis=0, tiled=True)  6.49 us
    pallas_call x1, Pallas kernels, shards(): local(functools.partial(fourier_tables_kernel, fields=fields, zs=zs), [pl...  4.2 us
  transfers between devices with their start and end apart: 14, of which 11 were waited for; matrix products, arithmetic and copies ran while one was open for 0% of the time, Pallas kernels for 6%

profile of v3, /device:TPU:1, one launch (start us, length us, event | category | flops | bytes accessed | tf_op | source)
XLA Modules:
  0.0 136.4 jit_solution(5468354070124394307)
XLA Ops:
  0.6 8.8 %collective-permute-start = (bf16[12,2,4,640]{3,2,1,0:T(4,128)(2,1)}, bf16[12,2,4,640]{3,2,1,0:T(4,128)(2,1)S(1)}, u32[]{:S(2)}, u32[]{:S(2)}) collective-permute-start(bf16[12,2,4,640]{3,2,1,0:T(4,128)(2,1)} %bitcast.12), channel_id=1, source_target_pairs={{0,1},{1,0},{2,3},{3,2},{4,5},{5,4},{6,7},{7,6},{8,9},{9,8},{10,11... | collective-permute-start | bytes 368648 | tf_op jit(solution)/shard_map/ppermute | solution.py:354
  11.6 2.3 %collective-permute-start.2 = (bf16[12,48,640]{2,1,0:T(8,128)(2,1)}, bf16[12,48,640]{2,1,0:T(8,128)(2,1)S(1)}, u32[]{:S(2)}, u32[]{:S(2)}) collective-permute-start(bf16[12,48,640]{2,1,0:T(8,128)(2,1)} %bitcast.9), channel_id=1, source_target_pairs={{0,1},{1,0},{2,3},{3,2},{4,5},{5,4},{6,7},{7,6},{8,9},{9,8},{10,11... | collective-permute-start | bytes 2211848 | tf_op jit(solution)/shard_map/ppermute | solution.py:354
  13.8 5.3 %collective-permute-start.1 = (bf16[2,96,640]{2,1,0:T(8,128)(2,1)S(1)}, bf16[2,96,640]{2,1,0:T(8,128)(2,1)S(1)}, u32[]{:S(2)}, u32[]{:S(2)}) collective-permute-start(bf16[2,96,640]{2,1,0:T(8,128)(2,1)S(1)} %pair.1.pair0), channel_id=1, source_target_pairs={{0,2},{1,15},{2,4},{3,1},{4,6},{5,3},{6,8},{7,5},{8,10},{9,7},{10,... | collective-permute-start | bytes 737288 | tf_op jit(solution)/shard_map/ppermute | solution.py:354
  19.1 1.9 %own_rows.1 = (bf16[12,96,640]{2,1,0:T(8,128)(2,1)S(1)}, bf16[96,128]{1,0:T(8,128)(2,1)S(1)}, f32[96,128]{1,0:T(8,128)S(1)}, f32[16,640]{1,0:T(8,128)S(1)}) custom-call(s32[1]{0:T(128)} %bitcast.2.wave_id, s32[1]{0:T(128)} %bitcast.3.field_id, s32[384]{0:T(512)} %wave_of_slot.1, s32[1536]{0:T(1024)} %lat_of_row.3, bf16[12,48,640]{2,1,0:T(8,128)(2,1)} %bitcast.10), custom_call_target="tpu_custom_call" | custom-call | bytes 7400000 | tf_op jit(solution)/shard_map/own_rows/pallas_call | solution.py:396
  22.3 5.0 %collective-permute-start.3 = (bf16[2,96,640]{2,1,0:T(8,128)(2,1)S(1)}, bf16[2,96,640]{2,1,0:T(8,128)(2,1)S(1)}, u32[]{:S(2)}, u32[]{:S(2)}) collective-permute-start(bf16[2,96,640]{2,1,0:T(8,128)(2,1)S(1)} %collective-permute-done.1.one), channel_id=1, source_target_pairs={{0,2},{1,15},{2,4},{3,1},{4,6},{5,3},{6,8},{7,5},{8,10},{9,7},{10,... | collective-permute-start | bytes 737288 | tf_op jit(solution)/shard_map/ppermute | solution.py:354
  30.4 5.0 %collective-permute-start.4 = (bf16[2,96,640]{2,1,0:T(8,128)(2,1)S(1)}, bf16[2,96,640]{2,1,0:T(8,128)(2,1)S(1)}, u32[]{:S(2)}, u32[]{:S(2)}) collective-permute-start(bf16[2,96,640]{2,1,0:T(8,128)(2,1)S(1)} %collective-permute-done.3.two), channel_id=1, source_target_pairs={{0,2},{1,15},{2,4},{3,1},{4,6},{5,3},{6,8},{7,5},{8,10},{9,7},{10,... | collective-permute-start | bytes 737288 | tf_op jit(solution)/shard_map/ppermute | solution.py:354
  35.4 3.1 %collective-permute-done.4.three = bf16[2,96,640]{2,1,0:T(8,128)(2,1)S(1)} collective-permute-done((bf16[2,96,640]{2,1,0:T(8,128)(2,1)S(1)}, bf16[2,96,640]{2,1,0:T(8,128)(2,1)S(1)}, u32[]{:S(2)}, u32[]{:S(2)}) %collective-permute-start.4) | collective-permute-done | bytes 245792 | tf_op jit(solution)/shard_map/ppermute | solution.py:354
  38.6 5.2 %collective-permute-start.5 = (bf16[96,640]{1,0:T(8,128)(2,1)S(1)}, bf16[96,640]{1,0:T(8,128)(2,1)S(1)}, u32[]{:S(2)}, u32[]{:S(2)}) collective-permute-start(bf16[96,640]{1,0:T(8,128)(2,1)S(1)} %slice_bitcast_fusion), channel_id=1, source_target_pairs={{0,2},{1,15},{2,4},{3,1},{4,6},{5,3},{6,8},{7,5},{8,10},{9,7},{10,... | collective-permute-start | bytes 368648 | tf_op jit(solution)/shard_map/ppermute | solution.py:354
  43.8 1.8 %collective-permute-done.5.four = bf16[96,640]{1,0:T(8,128)(2,1)S(1)} collective-permute-done((bf16[96,640]{1,0:T(8,128)(2,1)S(1)}, bf16[96,640]{1,0:T(8,128)(2,1)S(1)}, u32[]{:S(2)}, u32[]{:S(2)}) %collective-permute-start.5) | collective-permute-done | bytes 122912 | tf_op jit(solution)/shard_map/ppermute | solution.py:354
  47.4 9.7 %all-to-all-start = ((bf16[32,36,128]{2,1,0:T(8,128)(2,1)}), bf16[32,36,128]{2,1,0:T(8,128)(2,1)S(1)}, u32[]{:S(2)}, u32[]{:S(2)}) async-start(bf16[32,36,128]{2,1,0:T(8,128)(2,1)} %legendre_forward.1), calls=%async_computation | async-start | bytes 655360 | tf_op jit(solution)/shard_map/all_to_all | solution.py:434
  57.1 4.2 %fourier_tables.1 = (bf16[3,256,768]{2,1,0:T(8,128)(2,1)}, bf16[3,768,256]{2,1,0:T(8,128)(2,1)}, f32[3,16,768]{2,1,0:T(8,128)}, f32[3,16,768]{2,1,0:T(8,128)}, b...) custom-call(s32[1]{0:T(128)} %bitcast.2.wave_id, s32[1]{0:T(128)} %bitcast.3.field_id, s32[1536]{0:T(1024)S(1)} %copy-done, ...), custom_call_target="tpu_custom_call" | custom-call | bytes 14800000 | tf_op jit(solution)/shard_map/fourier_tables/pallas_call | solution.py:445
  61.3 6.5 %all-to-all-done.arrived = bf16[32,36,128]{2,1,0:T(8,128)(2,1)S(1)} async-done(((bf16[32,36,128]{2,1,0:T(8,128)(2,1)}), bf16[32,36,128]{2,1,0:T(8,128)(2,1)S(1)}, u32[]{:S(2)}, u32[]{:S(2)}) %all-to-all-start) | async-done | bytes 294944 | tf_op jit(solution)/shard_map/all_to_all | solution.py:434
  67.8 8.3 %collective-permute-start.6 = (bf16[32,36,128]{2,1,0:T(8,128)(2,1)S(1)}, bf16[32,36,128]{2,1,0:T(8,128)(2,1)S(1)}, u32[]{:S(2)}, u32[]{:S(2)}) collective-permute-start(bf16[32,36,128]{2,1,0:T(8,128)(2,1)S(1)} %all-to-all-done.arrived), channel_id=1, source_target_pairs={{0,1},{1,0},{2,3},{3,2},{4,5},{5,4},{6,7},{7,6},{8,9},{9,8},{10,11... | collective-permute-start | bytes 884744 | tf_op jit(solution)/shard_map/ppermute | solution.py:354
  77.3 6.7 %fourier.1 = (bf16[3,64,3200]{2,1,0:T(8,128)(2,1)}, bf16[32,36,128]{2,1,0:T(8,128)(2,1)S(1)}) custom-call(bf16[32,36,128]{2,1,0:T(8,128)(2,1)S(1)} %all-to-all-done.arrived, bf16[32,36,128]{2,1,0:T(8,128)(2,1)S(1)} %collective-permute-done.6.swapped, bf16[3,256,768]{2,1,0:T(8,128)(2,1)} %get-tuple-element.57.inner_in, ...), custom_call_target="tpu_custom_call" | custom-call | bytes 22200000 | tf_op jit(solution)/shard_map/fourier/pallas_call | solution.py:461
  84.0 16.4 %all_to_all.10.arrived = bf16[32,36,128]{2,1,0:T(8,128)(2,1)S(1)} all-to-all(bf16[32,36,128]{2,1,0:T(8,128)(2,1)S(1)} %get-tuple-element.64), channel_id=1, replica_groups=mesh['wave'=32,'field'=16] {'wave'}, dimensions={0} | all-to-all | bytes 589824 | tf_op jit(solution)/shard_map/all_to_all | solution.py:480
  100.4 4.3 %collective-permute-start.7 = (bf16[32,36,128]{2,1,0:T(8,128)(2,1)S(1)}, bf16[32,36,128]{2,1,0:T(8,128)(2,1)S(1)}, u32[]{:S(2)}, u32[]{:S(2)}) collective-permute-start(bf16[32,36,128]{2,1,0:T(8,128)(2,1)S(1)} %all_to_all.10.arrived), channel_id=1, source_target_pairs={{0,1},{1,0},{2,3},{3,2},{4,5},{5,4},{6,7},{7,6},{8,9},{9,8},{10,11... | collective-permute-start | bytes 884744 | tf_op jit(solution)/shard_map/ppermute | solution.py:354
  106.9 1.9 %collective-permute-start.8 = (bf16[2,96,640]{2,1,0:T(8,128)(2,1)S(1)}, bf16[2,96,640]{2,1,0:T(8,128)(2,1)S(1)}, u32[]{:S(2)}, u32[]{:S(2)}) collective-permute-start(bf16[2,96,640]{2,1,0:T(8,128)(2,1)S(1)} %get-tuple-element.68), channel_id=1, source_target_pairs={{0,14},{1,3},{2,0},{3,5},{4,2},{5,7},{6,4},{7,9},{8,6},{9,11},{10,... | collective-permute-start | bytes 737288 | tf_op jit(solution)/shard_map/ppermute | solution.py:354
  108.8 1.9 %collective-permute-start.9 = (bf16[96,640]{1,0:T(8,128)(2,1)S(1)}, bf16[96,640]{1,0:T(8,128)(2,1)S(1)}, u32[]{:S(2)}, u32[]{:S(2)}) collective-permute-start(bf16[96,640]{1,0:T(8,128)(2,1)S(1)} %get-tuple-element.69), channel_id=1, source_target_pairs={{0,12},{1,5},{2,14},{3,7},{4,0},{5,9},{6,2},{7,11},{8,4},{9,13},{1... | collective-permute-start | bytes 368648 | tf_op jit(solution)/shard_map/ppermute | solution.py:354
  110.7 5.9 %collective-permute-done.9.four = bf16[96,640]{1,0:T(8,128)(2,1)S(1)} collective-permute-done((bf16[96,640]{1,0:T(8,128)(2,1)S(1)}, bf16[96,640]{1,0:T(8,128)(2,1)S(1)}, u32[]{:S(2)}, u32[]{:S(2)}) %collective-permute-start.9) | collective-permute-done | bytes 122912 | tf_op jit(solution)/shard_map/ppermute | solution.py:354
  116.7 4.1 %collective-permute-start.10 = (bf16[2,96,640]{2,1,0:T(8,128)(2,1)S(1)}, bf16[2,96,640]{2,1,0:T(8,128)(2,1)S(1)}, u32[]{:S(2)}, u32[]{:S(2)}) collective-permute-start(bf16[2,96,640]{2,1,0:T(8,128)(2,1)S(1)} %add_three.1), channel_id=1, source_target_pairs={{0,14},{1,3},{2,0},{3,5},{4,2},{5,7},{6,4},{7,9},{8,6},{9,11},{10,... | collective-permute-start | bytes 737288 | tf_op jit(solution)/shard_map/ppermute | solution.py:354
  120.9 4.0 %collective-permute-done.10.two = bf16[2,96,640]{2,1,0:T(8,128)(2,1)S(1)} collective-permute-done((bf16[2,96,640]{2,1,0:T(8,128)(2,1)S(1)}, bf16[2,96,640]{2,1,0:T(8,128)(2,1)S(1)}, u32[]{:S(2)}, u32[]{:S(2)}) %collective-permute-start.10) | collective-permute-done | bytes 245792 | tf_op jit(solution)/shard_map/ppermute | solution.py:354
  125.0 3.2 %collective-permute-start.11 = (bf16[96,640]{1,0:T(8,128)(2,1)S(1)}, bf16[96,640]{1,0:T(8,128)(2,1)S(1)}, u32[]{:S(2)}, u32[]{:S(2)}) collective-permute-start(bf16[96,640]{1,0:T(8,128)(2,1)S(1)} %get-tuple-element.70), channel_id=1, source_target_pairs={{0,14},{1,3},{2,0},{3,5},{4,2},{5,7},{6,4},{7,9},{8,6},{9,11},{10,... | collective-permute-start | bytes 368648 | tf_op jit(solution)/shard_map/ppermute | solution.py:354
  128.2 5.0 %collective-permute-start.12 = (bf16[96,640]{1,0:T(8,128)(2,1)S(1)}, bf16[96,640]{1,0:T(8,128)(2,1)S(1)}, u32[]{:S(2)}, u32[]{:S(2)}) collective-permute-start(bf16[96,640]{1,0:T(8,128)(2,1)S(1)} %get-tuple-element.71), channel_id=1, source_target_pairs={{0,15},{1,2},{2,1},{3,4},{4,3},{5,6},{6,5},{7,8},{8,7},{9,10},{10,... | collective-permute-start | bytes 368648 | tf_op jit(solution)/shard_map/ppermute | solution.py:354
  133.1 2.5 %collective-permute-done.12.one_other = bf16[96,640]{1,0:T(8,128)(2,1)S(1)} collective-permute-done((bf16[96,640]{1,0:T(8,128)(2,1)S(1)}, bf16[96,640]{1,0:T(8,128)(2,1)S(1)}, u32[]{:S(2)}, u32[]{:S(2)}) %collective-permute-start.12) | collective-permute-done | bytes 122912 | tf_op jit(solution)/shard_map/ppermute | solution.py:354
  (28 shorter events, 12.5 us)
Async XLA Ops:
  0.6 10.0 %collective-permute-start = (bf16[12,2,4,640]{3,2,1,0:T(4,128)(2,1)}, bf16[12,2,4,640]{3,2,1,0:T(4,128)(2,1)S(1)}, u32[]{:S(2)}, u32[]{:S(2)}) collective-permute-start(bf16[12,2,4,640]{3,2,1,0:T(4,128)(2,1)} %bitcast.12), channel_id=1, source_target_pairs={{0,1},{1,0},{2,3},{3,2},{4,5},{5,4},{6,7},{7,6},{8,9},{9,8},{10,11... | collective-permute-start | bytes 368648 | tf_op jit(solution)/shard_map/ppermute | solution.py:354
  11.6 10.7 %collective-permute-start.2 = (bf16[12,48,640]{2,1,0:T(8,128)(2,1)}, bf16[12,48,640]{2,1,0:T(8,128)(2,1)S(1)}, u32[]{:S(2)}, u32[]{:S(2)}) collective-permute-start(bf16[12,48,640]{2,1,0:T(8,128)(2,1)} %bitcast.9), channel_id=1, source_target_pairs={{0,1},{1,0},{2,3},{3,2},{4,5},{5,4},{6,7},{7,6},{8,9},{9,8},{10,11... | collective-permute-start | bytes 2211848 | tf_op jit(solution)/shard_map/ppermute | solution.py:354
  13.8 8.4 %collective-permute-start.1 = (bf16[2,96,640]{2,1,0:T(8,128)(2,1)S(1)}, bf16[2,96,640]{2,1,0:T(8,128)(2,1)S(1)}, u32[]{:S(2)}, u32[]{:S(2)}) collective-permute-start(bf16[2,96,640]{2,1,0:T(8,128)(2,1)S(1)} %pair.1.pair0), channel_id=1, source_target_pairs={{0,2},{1,15},{2,4},{3,1},{4,6},{5,3},{6,8},{7,5},{8,10},{9,7},{10,... | collective-permute-start | bytes 737288 | tf_op jit(solution)/shard_map/ppermute | solution.py:354
  22.3 5.0 %copy-start.3 = (bf16[12,48,640]{2,1,0:T(8,128)(2,1)}, bf16[12,48,640]{2,1,0:T(8,128)(2,1)S(1)}, u32[]{:S(2)}) copy-start(bf16[12,48,640]{2,1,0:T(8,128)(2,1)S(1)} %collective-permute-done.2.legendre) | copy-start | bytes 2211844
  22.3 8.1 %collective-permute-start.3 = (bf16[2,96,640]{2,1,0:T(8,128)(2,1)S(1)}, bf16[2,96,640]{2,1,0:T(8,128)(2,1)S(1)}, u32[]{:S(2)}, u32[]{:S(2)}) collective-permute-start(bf16[2,96,640]{2,1,0:T(8,128)(2,1)S(1)} %collective-permute-done.1.one), channel_id=1, source_target_pairs={{0,2},{1,15},{2,4},{3,1},{4,6},{5,3},{6,8},{7,5},{8,10},{9,7},{10,... | collective-permute-start | bytes 737288 | tf_op jit(solution)/shard_map/ppermute | solution.py:354
  30.4 8.1 %collective-permute-start.4 = (bf16[2,96,640]{2,1,0:T(8,128)(2,1)S(1)}, bf16[2,96,640]{2,1,0:T(8,128)(2,1)S(1)}, u32[]{:S(2)}, u32[]{:S(2)}) collective-permute-start(bf16[2,96,640]{2,1,0:T(8,128)(2,1)S(1)} %collective-permute-done.3.two), channel_id=1, source_target_pairs={{0,2},{1,15},{2,4},{3,1},{4,6},{5,3},{6,8},{7,5},{8,10},{9,7},{10,... | collective-permute-start | bytes 737288 | tf_op jit(solution)/shard_map/ppermute | solution.py:354
  38.6 18.5 %copy-start.4 = (s32[384]{0:T(512)S(1)}, s32[384]{0:T(512)}, u32[]{:S(2)}) copy-start(s32[384]{0:T(512)} %wave_of_slot.1) | copy-start | bytes 4612
  38.6 18.5 %copy-start = (s32[1536]{0:T(1024)S(1)}, s32[1536]{0:T(1024)}, u32[]{:S(2)}) copy-start(s32[1536]{0:T(1024)} %lat_of_row.3) | copy-start | bytes 18436
  38.6 18.5 %copy-start.1 = (s32[768]{0:T(1024)S(1)}, s32[768]{0:T(1024)}, u32[]{:S(2)}) copy-start(s32[768]{0:T(1024)} %lon_count.1) | copy-start | bytes 9220
  38.6 18.5 %copy-start.2 = (f32[48]{0:T(128)S(1)}, f32[48]{0:T(128)}, u32[]{:S(2)}) copy-start(f32[48]{0:T(128)} %lat_weight) | copy-start | bytes 580
  38.6 7.0 %collective-permute-start.5 = (bf16[96,640]{1,0:T(8,128)(2,1)S(1)}, bf16[96,640]{1,0:T(8,128)(2,1)S(1)}, u32[]{:S(2)}, u32[]{:S(2)}) collective-permute-start(bf16[96,640]{1,0:T(8,128)(2,1)S(1)} %slice_bitcast_fusion), channel_id=1, source_target_pairs={{0,2},{1,15},{2,4},{3,1},{4,6},{5,3},{6,8},{7,5},{8,10},{9,7},{10,... | collective-permute-start | bytes 368648 | tf_op jit(solution)/shard_map/ppermute | solution.py:354
  47.4 20.4 %all-to-all-start = ((bf16[32,36,128]{2,1,0:T(8,128)(2,1)}), bf16[32,36,128]{2,1,0:T(8,128)(2,1)S(1)}, u32[]{:S(2)}, u32[]{:S(2)}) async-start(bf16[32,36,128]{2,1,0:T(8,128)(2,1)} %legendre_forward.1), calls=%async_computation | async-start | bytes 655360 | tf_op jit(solution)/shard_map/all_to_all | solution.py:434
  67.8 9.5 %collective-permute-start.6 = (bf16[32,36,128]{2,1,0:T(8,128)(2,1)S(1)}, bf16[32,36,128]{2,1,0:T(8,128)(2,1)S(1)}, u32[]{:S(2)}, u32[]{:S(2)}) collective-permute-start(bf16[32,36,128]{2,1,0:T(8,128)(2,1)S(1)} %all-to-all-done.arrived), channel_id=1, source_target_pairs={{0,1},{1,0},{2,3},{3,2},{4,5},{5,4},{6,7},{7,6},{8,9},{9,8},{10,11... | collective-permute-start | bytes 884744 | tf_op jit(solution)/shard_map/ppermute | solution.py:354
  100.4 5.5 %collective-permute-start.7 = (bf16[32,36,128]{2,1,0:T(8,128)(2,1)S(1)}, bf16[32,36,128]{2,1,0:T(8,128)(2,1)S(1)}, u32[]{:S(2)}, u32[]{:S(2)}) collective-permute-start(bf16[32,36,128]{2,1,0:T(8,128)(2,1)S(1)} %all_to_all.10.arrived), channel_id=1, source_target_pairs={{0,1},{1,0},{2,3},{3,2},{4,5},{5,4},{6,7},{7,6},{8,9},{9,8},{10,11... | collective-permute-start | bytes 884744 | tf_op jit(solution)/shard_map/ppermute | solution.py:354
  106.9 9.8 %collective-permute-start.8 = (bf16[2,96,640]{2,1,0:T(8,128)(2,1)S(1)}, bf16[2,96,640]{2,1,0:T(8,128)(2,1)S(1)}, u32[]{:S(2)}, u32[]{:S(2)}) collective-permute-start(bf16[2,96,640]{2,1,0:T(8,128)(2,1)S(1)} %get-tuple-element.68), channel_id=1, source_target_pairs={{0,14},{1,3},{2,0},{3,5},{4,2},{5,7},{6,4},{7,9},{8,6},{9,11},{10,... | collective-permute-start | bytes 737288 | tf_op jit(solution)/shard_map/ppermute | solution.py:354
  108.8 7.8 %collective-permute-start.9 = (bf16[96,640]{1,0:T(8,128)(2,1)S(1)}, bf16[96,640]{1,0:T(8,128)(2,1)S(1)}, u32[]{:S(2)}, u32[]{:S(2)}) collective-permute-start(bf16[96,640]{1,0:T(8,128)(2,1)S(1)} %get-tuple-element.69), channel_id=1, source_target_pairs={{0,12},{1,5},{2,14},{3,7},{4,0},{5,9},{6,2},{7,11},{8,4},{9,13},{1... | collective-permute-start | bytes 368648 | tf_op jit(solution)/shard_map/ppermute | solution.py:354
  116.7 8.2 %collective-permute-start.10 = (bf16[2,96,640]{2,1,0:T(8,128)(2,1)S(1)}, bf16[2,96,640]{2,1,0:T(8,128)(2,1)S(1)}, u32[]{:S(2)}, u32[]{:S(2)}) collective-permute-start(bf16[2,96,640]{2,1,0:T(8,128)(2,1)S(1)} %add_three.1), channel_id=1, source_target_pairs={{0,14},{1,3},{2,0},{3,5},{4,2},{5,7},{6,4},{7,9},{8,6},{9,11},{10,... | collective-permute-start | bytes 737288 | tf_op jit(solution)/shard_map/ppermute | solution.py:354
  125.0 8.2 %collective-permute-start.11 = (bf16[96,640]{1,0:T(8,128)(2,1)S(1)}, bf16[96,640]{1,0:T(8,128)(2,1)S(1)}, u32[]{:S(2)}, u32[]{:S(2)}) collective-permute-start(bf16[96,640]{1,0:T(8,128)(2,1)S(1)} %get-tuple-element.70), channel_id=1, source_target_pairs={{0,14},{1,3},{2,0},{3,5},{4,2},{5,7},{6,4},{7,9},{8,6},{9,11},{10,... | collective-permute-start | bytes 368648 | tf_op jit(solution)/shard_map/ppermute | solution.py:354
  128.2 7.5 %collective-permute-start.12 = (bf16[96,640]{1,0:T(8,128)(2,1)S(1)}, bf16[96,640]{1,0:T(8,128)(2,1)S(1)}, u32[]{:S(2)}, u32[]{:S(2)}) collective-permute-start(bf16[96,640]{1,0:T(8,128)(2,1)S(1)} %get-tuple-element.71), channel_id=1, source_target_pairs={{0,15},{1,2},{2,1},{3,4},{4,3},{5,6},{6,5},{7,8},{8,7},{9,10},{10,... | collective-permute-start | bytes 368648 | tf_op jit(solution)/shard_map/ppermute | solution.py:354

commit v4 on v3

--- a/solution.py
+++ b/solution.py
@@ -44,24 +44,6 @@
 
 def hbm():
     return pl.BlockSpec(memory_space=pltpu.HBM)
-
-
-def side_of(core):
-    return 1 - 2 * core
-
-
-def pair_kernel(own, partner, out, mine, held, sem):
-    copy = pltpu.make_async_copy(own, mine, sem)
-    copy.start()
-    slots, parts, cols, _ = mine.shape
-    for at, source in ((1, partner), (0, mine)):
-        if at == 0:
-            copy.wait()
-        for slot in range(slots):
-            for part in range(parts):
-                row = (slot * parts + part) * cols
-                held[row : row + cols, :] = source[slot, part].astype(jnp.float32)
-        out[at] = held[...].astype(jnp.bfloat16)
 
 
 def ordered_rows(chosen, south, live, legendre, out):
@@ -139,7 +121,7 @@
 def fourier_tables_kernel(
     wave_id, field_id, lat_of_row, lon_count, lat_weight, waves_row,
     inner_out, inner_t_out, outer_fwd_out, outer_inv_out, place_out, limits_out,
-    inner, inner_t, outer_fwd, outer_inv, place, limits, sems, *, fields, zs,
+    inner, inner_t, outer_fwd, outer_inv, place, limits, sems, *, fields,
 ):
     row_count = inner.shape[0]
     band = lat_weight.shape[0]
@@ -168,12 +150,8 @@
             outer_fwd[member, :, at : at + 2 * LANES] = both * (1.0 / math.sqrt(slots))
             outer_inv[member, :, at : at + 2 * LANES] = both * jnp.concatenate([weight, weight], axis=1)
     at = lax.broadcasted_iota(jnp.int32, (LANES, LANES), 1)
-    chunk, part, low = (at >> 3) & 7, (at >> 2) & 1, at & 3
-    core = (field & 1) ^ (at >> 6)
-    back = (chunk + 1) >> 1
-    other = ((chunk & 1) ^ 1) & (chunk > 0).astype(jnp.int32)
-    z = ((field >> 1) - side_of(core) * back + zs) & (zs - 1)
-    target = part * 64 + (2 * z + (core ^ other)) * 4 + low
+    core, z, part, low = (field & 1) ^ (at >> 6), (at >> 3) & 7, (at >> 2) & 1, at & 3
+    target = part * 64 + (2 * z + core) * 4 + low
     place[...] = (lax.broadcasted_iota(jnp.int32, (LANES, LANES), 0) == target).astype(jnp.bfloat16)
     results = (
         (inner, inner_out), (inner_t, inner_t_out), (outer_fwd, outer_fwd_out),
@@ -186,14 +164,13 @@
         copy.wait()
 
 
-def legendre_forward_kernel(pair0, one, two, three, four, table, table_swapped, out, held):
-    pieces = [pair0.at[0]] + [piece.at[i] for piece in (one, two, three) for i in range(2)] + [four]
+def legendre_forward_kernel(gathered, table, table_swapped, out, held):
     slots, rows, degrees = table.shape
     waves = out.shape[0]
     row_count = rows // waves
     each = slots * row_count
     for pair in range(slots // 2):
-        both = [piece[16 * pair : 16 * pair + 16, :].astype(jnp.float32) for piece in pieces]
+        both = [gathered[z, 16 * pair : 16 * pair + 16, :].astype(jnp.float32) for z in range(gathered.shape[0])]
         for half in range(2):
             slot = 2 * pair + half
             spec = jnp.concatenate([b[8 * half : 8 * half + 8] for b in both], axis=0).astype(jnp.bfloat16)
@@ -207,7 +184,7 @@
 
 
 def legendre_inverse_kernel(
-    arrived, swapped, table, table_swapped, own, one, two, three, four, held, held_swapped
+    arrived, swapped, table, table_swapped, out, held, held_swapped
 ):
     slots, rows, degrees = table.shape
     waves = arrived.shape[0]
@@ -228,13 +205,9 @@
         sums = [
             share(held, slot, table) + share(held_swapped, slot, table_swapped) for slot in (2 * pair, 2 * pair + 1)
         ]
-        pieces = [jnp.concatenate([s[8 * chunk : 8 * chunk + 8] for s in sums], axis=0) for chunk in range(8)]
-        own[at, :] = pieces[0]
-        pieces = [piece.astype(jnp.bfloat16) for piece in pieces]
-        for target, first in ((one, 1), (two, 3), (three, 5)):
-            for i in range(2):
-                target[i, at, :] = pieces[first + i]
-        four[at, :] = pieces[7]
+        for z in range(out.shape[0]):
+            piece = jnp.concatenate([s[8 * z : 8 * z + 8] for s in sums], axis=0)
+            out[z, at, :] = piece.astype(jnp.bfloat16)
 
 
 def fourier_kernel(
@@ -313,20 +286,8 @@
         result.wait()
 
 
-def add_three_kernel(two, three, four, out):
-    out[0] = (
-        two[0].astype(jnp.float32) + three[0].astype(jnp.float32) + four[...].astype(jnp.float32)
-    ).astype(jnp.bfloat16)
-    out[1] = (two[1].astype(jnp.float32) + three[1].astype(jnp.float32)).astype(jnp.bfloat16)
-
-
-def add_two_kernel(one, two, out, out_other):
-    for i, target in enumerate((out, out_other)):
-        target[...] = (one[i].astype(jnp.float32) + two[i].astype(jnp.float32)).astype(jnp.bfloat16)
-
-
-def add_own_kernel(own, one, one_other, out):
-    total = own[...] + one[...].astype(jnp.float32) + one_other[...].astype(jnp.float32)
+def finish_kernel(summed, out):
+    total = summed[...].astype(jnp.float32)
     groups, cols, _ = out.shape
     for group in range(groups):
         out[group] = total[group * cols : (group + 1) * cols]
@@ -347,14 +308,10 @@
     each = row_count * slots
     coded = slots * 2 * cols
 
-    def hop(x, by, cross=0):
-        pairs = [
-            (i, (2 * (i // 2 + side_of(i % 2) * by) + (i % 2 ^ cross)) % fields) for i in range(fields)
-        ]
-        return lax.ppermute(x, "field", pairs)
+    like_cores = [list(range(core, fields, 2)) for core in range(2)]
 
     def swap(x):
-        return hop(x, 0, 1)
+        return lax.ppermute(x, "field", [(i, i ^ 1) for i in range(fields)])
 
     def local(kernel, out_shape, name, micros, mebibytes=8, in_specs=None, out_specs=None, scratch=()):
         if in_specs is None:
@@ -370,29 +327,14 @@
             name=name,
         )
 
-    chunk = jax.ShapeDtypeStruct((coded, degrees), jnp.bfloat16)
-    chunk_pair = jax.ShapeDtypeStruct((2, coded, degrees), jnp.bfloat16)
     row_table = jax.ShapeDtypeStruct((slots, rows, degrees), jnp.bfloat16)
     fourier_shape = jax.ShapeDtypeStruct((waves, each, LANES), jnp.bfloat16)
     float_rows = pltpu.VMEM((waves * each, LANES), jnp.float32)
 
-    spectra = jnp.transpose(spectra, (0, 1, 3, 2))
-    legendre = jnp.transpose(legendre, (0, 2, 1))
-    pair = local(
-        pair_kernel,
-        chunk_pair,
-        "pair",
-        1,
-        in_specs=[hbm(), vmem()],
-        scratch=[
-            pltpu.VMEM(spectra.shape, jnp.bfloat16),
-            pltpu.VMEM((coded, degrees), jnp.float32),
-            pltpu.SemaphoreType.DMA(()),
-        ],
-    )(in_hbm(spectra), swap(spectra))
-    pair, legendre = lax.optimization_barrier((pair, legendre))
+    own = jnp.transpose(spectra, (0, 1, 3, 2)).reshape(coded, degrees)
+    own, legendre = lax.optimization_barrier((own, jnp.transpose(legendre, (0, 2, 1))))
+    gathered = lax.all_gather(own, "field", axis_index_groups=like_cores)
     legendre_x = swap(legendre)
-    one = hop(pair, 1)
     table, chosen_x, south_x, live = local(
         functools.partial(own_rows_kernel, waves=waves, fields=fields),
         (
@@ -413,8 +355,6 @@
             pltpu.SemaphoreType.DMA((3,)),
         ],
     )(wave_id, field_id, in_hbm(wave_of_slot), in_hbm(lat_of_row), in_hbm(legendre))
-    one, legendre_x, table = lax.optimization_barrier((one, legendre_x, table))
-    two = hop(one, 1)
     table_x = local(
         partner_rows_kernel,
         row_table,
@@ -423,13 +363,9 @@
         in_specs=[vmem(), vmem(), vmem(), hbm()],
         scratch=[pltpu.VMEM((slots, band, degrees), jnp.bfloat16), pltpu.SemaphoreType.DMA(())],
     )(chosen_x, south_x, live, in_hbm(legendre_x))
-    two, table_x = lax.optimization_barrier((two, table_x))
-    three = hop(two, 1)
-    four = hop(three[0], 1)
-
     outgoing = local(
-        legendre_forward_kernel, fourier_shape, "legendre_forward", 4, 16, in_specs=[vmem()] * 7, scratch=[float_rows]
-    )(pair, one, two, three, four, table, table_x)
+        legendre_forward_kernel, fourier_shape, "legendre_forward", 4, 16, in_specs=[vmem()] * 3, scratch=[float_rows]
+    )(gathered, table, table_x)
     outgoing, lat_weight = lax.optimization_barrier((outgoing, lat_weight))
     arrived = lax.all_to_all(outgoing, "wave", split_axis=0, concat_axis=0, tiled=True)
 
@@ -443,7 +379,7 @@
     )
     tables_vmem = [pltpu.VMEM(shape, kind) for shape, kind in tables]
     prepared = local(
-        functools.partial(fourier_tables_kernel, fields=fields, zs=zs),
+        functools.partial(fourier_tables_kernel, fields=fields),
         [pltpu.HBM(shape, kind) for shape, kind in tables],
         "fourier_tables",
         4,
@@ -479,25 +415,29 @@
 
     returned = lax.all_to_all(sent, "wave", split_axis=0, concat_axis=0, tiled=True)
 
-    own, one, two, three, four = local(
+    partial = local(
         legendre_inverse_kernel,
-        (jax.ShapeDtypeStruct((coded, degrees), jnp.float32), chunk_pair, chunk_pair, chunk_pair, chunk),
+        jax.ShapeDtypeStruct((zs, coded, degrees), jnp.bfloat16),
         "legendre_inverse",
         2,
         16,
         in_specs=[vmem()] * 4,
         scratch=[float_rows, float_rows],
     )(returned, swap(returned), table, table_x)
-    three, four = hop(three, -1), hop(four, -2)
-    two = local(add_three_kernel, chunk_pair, "add_three", 1, in_specs=[vmem()] * 3)(two, three, four)
-    one, one_other = local(add_two_kernel, (chunk, chunk), "add_two", 1, in_specs=[vmem()] * 2)(one, hop(two, -1))
+    summed = lax.psum_scatter(
+        partial.reshape(zs * coded, degrees),
+        "field",
+        scatter_dimension=0,
+        axis_index_groups=like_cores,
+        tiled=True,
+    )
     total = local(
-        add_own_kernel,
+        finish_kernel,
         jax.ShapeDtypeStruct((2 * slots, cols, degrees), jnp.float32),
-        "add_own",
+        "finish",
         1,
-        in_specs=[vmem()] * 3,
-    )(own, hop(one, -1), hop(one_other, -1, 1))
+        in_specs=[vmem()],
+    )(summed)
     spectral = jnp.transpose(total.reshape(slots, 2, cols, degrees), (0, 1, 3, 2))
     return grid_field, spectral
 

time: 138 us -> 148 us (1.072)
  the two profiles are of different devices: /device:TPU:1 before, /device:TPU:4 now
where the time goes in v4:
time: 148 us
  blocking collectives  51.3 us (35%)
  waiting for transfers between devices  45 us (30%)
  Pallas kernels  17.8 us (12%)
  starting transfers between devices  16 us (11%)
  between operations  14.2 us (10%)
  local copies, waits for them, and re-layouts  3.67 us (2%)
    reduce_scatter x1, waiting for transfers between devices, shards(): lax.psum_scatter(partial.reshape(zs * coded, degrees), 'field', scatter_d...  35.6 us
    all_gather x1, blocking collectives, shards(): gathered = lax.all_gather(own, 'field', axis_index_groups=like_cores)  33 us
    all_to_all x1, blocking collectives, shards(): lax.all_to_all(sent, 'wave', split_axis=0, concat_axis=0, tiled=True)  18.3 us
    all_to_all x1, starting transfers between devices, shards(): lax.all_to_all(outgoing, 'wave', split_axis=0, concat_axis=0, tiled=True)  10.2 us
    pallas_call x1, Pallas kernels, shards(): local(fourier_kernel, (jax.ShapeDtypeStruct((row_count, levels, LONPAD),...  6.69 us
    all_to_all x1, waiting for transfers between devices, shards(): lax.all_to_all(outgoing, 'wave', split_axis=0, concat_axis=0, tiled=True)  6.21 us
    ppermute x3, starting transfers between devices, swap(): return lax.ppermute(x, 'field', [(i, i ^ 1) for i in range(fields)])  5.74 us
    pallas_call x1, Pallas kernels, shards(): local(functools.partial(fourier_tables_kernel, fields=fields), [pltpu.HBM...  4.19 us
  transfers between devices with their start and end apart: 5, of which 4 were waited for; matrix products, arithmetic and copies ran while one was open for 0% of the time, Pallas kernels for 4%

profile of v4, /device:TPU:4, one launch (start us, length us, event | category | flops | bytes accessed | tf_op | source)
XLA Modules:
  0.0 148.0 jit_solution(6313790536730759267)
XLA Ops:
  7.2 0.9 reshape.22
  8.1 1.9 %collective-permute-start = (bf16[12,48,640]{2,1,0:T(8,128)(2,1)}, bf16[12,48,640]{2,1,0:T(8,128)(2,1)S(1)}, u32[]{:S(2)}, u32[]{:S(2)}) collective-permute-start(bf16[12,48,640]{2,1,0:T(8,128)(2,1)} %bitcast.11), channel_id=1, source_target_pairs={{0,1},{1,0},{2,3},{3,2},{4,5},{5,4},{6,7},{7,6},{8,9},{9,8},{10,11... | collective-permute-start | bytes 2211848 | tf_op jit(solution)/shard_map/ppermute | solution.py:314
  10.0 1.9 %own_rows.1 = (bf16[12,96,640]{2,1,0:T(8,128)(2,1)S(1)}, bf16[96,128]{1,0:T(8,128)(2,1)S(1)}, f32[96,128]{1,0:T(8,128)S(1)}, f32[16,640]{1,0:T(8,128)S(1)}) custom-call(s32[1]{0:T(128)} %bitcast.3.wave_id, s32[1]{0:T(128)} %bitcast.4.field_id, s32[384]{0:T(512)} %wave_of_slot.1, s32[1536]{0:T(1024)} %lat_of_row.3, bf16[12,48,640]{2,1,0:T(8,128)(2,1)} %bitcast.12), custom_call_target="tpu_custom_call" | custom-call | bytes 7400000 | tf_op jit(solution)/shard_map/own_rows/pallas_call | solution.py:338
  11.9 33.0 %all-gather = bf16[768,640]{1,0:T(8,128)(2,1)S(1)} all-gather(bf16[96,640]{1,0:T(8,128)(2,1)S(1)} %reshape.22), channel_id=2, replica_groups={{0,2,4,6,8,10,12,14},{1,3,5,7,9,11,13,15},{16,18,20,22,24,26,28,30},{17..., dimensions={0}, use_global_device_ids=true | all-gather | bytes 1105920 | tf_op jit(solution)/shard_map/all_gather | solution.py:336
  45.0 0.9 copy-done.5
  45.8 1.6 %partner_rows.1.table_swapped = bf16[12,96,640]{2,1,0:T(8,128)(2,1)S(1)} custom-call(bf16[96,128]{1,0:T(8,128)(2,1)S(1)} %get-tuple-element.28.chosen, f32[96,128]{1,0:T(8,128)S(1)} %get-tuple-element.29.south, f32[16,640]{1,0:T(8,128)S(1)} %get-tuple-element.30.live, bf16[12,48,640]{2,1,0:T(8,128)(2,1)} %copy-done.5), custom_call_target="tpu_custom_call" | custom-call | bytes 7400000 | tf_op jit(solution)/shard_map/partner_rows/pallas_call | solution.py:358
  47.5 0.0 copy-start.6
  47.5 1.8 %legendre_forward.1 = bf16[32,36,128]{2,1,0:T(8,128)(2,1)} custom-call(bf16[8,96,640]{2,1,0:T(8,128)(2,1)S(1)} %bitcast.10, bf16[12,96,640]{2,1,0:T(8,128)(2,1)S(1)} %get-tuple-element.27.table, bf16[12,96,640]{2,1,0:T(8,128)(2,1)S(1)} %partner_rows.1.table_swapped), custom_call_target="tpu_custom_call" | custom-call | bytes 14800000 | tf_op jit(solution)/shard_map/legendre_forward/pallas_call | solution.py:366
  49.3 10.2 %all-to-all-start = ((bf16[32,36,128]{2,1,0:T(8,128)(2,1)}), bf16[32,36,128]{2,1,0:T(8,128)(2,1)S(1)}, u32[]{:S(2)}, u32[]{:S(2)}) async-start(bf16[32,36,128]{2,1,0:T(8,128)(2,1)} %legendre_forward.1), calls=%async_computation | async-start | bytes 655360 | tf_op jit(solution)/shard_map/all_to_all | solution.py:370
  59.5 0.0 reduce-scatter.2.cloned.1.call-start
  59.6 4.2 %fourier_tables.1 = (bf16[3,256,768]{2,1,0:T(8,128)(2,1)}, bf16[3,768,256]{2,1,0:T(8,128)(2,1)}, f32[3,16,768]{2,1,0:T(8,128)}, f32[3,16,768]{2,1,0:T(8,128)}, b...) custom-call(s32[1]{0:T(128)} %bitcast.3.wave_id, s32[1]{0:T(128)} %bitcast.4.field_id, s32[1536]{0:T(1024)S(1)} %copy-done.2, ...), custom_call_target="tpu_custom_call" | custom-call | bytes 14800000 | tf_op jit(solution)/shard_map/fourier_tables/pallas_call | solution.py:381
  63.8 6.2 %all-to-all-done.arrived = bf16[32,36,128]{2,1,0:T(8,128)(2,1)S(1)} async-done(((bf16[32,36,128]{2,1,0:T(8,128)(2,1)}), bf16[32,36,128]{2,1,0:T(8,128)(2,1)S(1)}, u32[]{:S(2)}, u32[]{:S(2)}) %all-to-all-start) | async-done | bytes 294944 | tf_op jit(solution)/shard_map/all_to_all | solution.py:370
  70.1 1.9 %collective-permute-start.1 = (bf16[32,36,128]{2,1,0:T(8,128)(2,1)S(1)}, bf16[32,36,128]{2,1,0:T(8,128)(2,1)S(1)}, u32[]{:S(2)}, u32[]{:S(2)}) collective-permute-start(bf16[32,36,128]{2,1,0:T(8,128)(2,1)S(1)} %all-to-all-done.arrived), channel_id=1, source_target_pairs={{0,1},{1,0},{2,3},{3,2},{4,5},{5,4},{6,7},{7,6},{8,9},{9,8},{10,11... | collective-permute-start | bytes 884744 | tf_op jit(solution)/shard_map/ppermute | solution.py:314
  72.0 1.6 %collective-permute-done.1.swapped = bf16[32,36,128]{2,1,0:T(8,128)(2,1)S(1)} collective-permute-done((bf16[32,36,128]{2,1,0:T(8,128)(2,1)S(1)}, bf16[32,36,128]{2,1,0:T(8,128)(2,1)S(1)}, u32[]{:S(2)}, u32[]{:S(2)}) %collective-permute-start.1) | collective-permute-done | bytes 294944 | tf_op jit(solution)/shard_map/ppermute | solution.py:314
  73.6 6.7 %fourier.1 = (bf16[3,64,3200]{2,1,0:T(8,128)(2,1)}, bf16[32,36,128]{2,1,0:T(8,128)(2,1)S(1)}) custom-call(bf16[32,36,128]{2,1,0:T(8,128)(2,1)S(1)} %all-to-all-done.arrived, bf16[32,36,128]{2,1,0:T(8,128)(2,1)S(1)} %collective-permute-done.1.swapped, bf16[3,256,768]{2,1,0:T(8,128)(2,1)} %get-tuple-element.40.inner_in, ...), custom_call_target="tpu_custom_call" | custom-call | bytes 22200000 | tf_op jit(solution)/shard_map/fourier/pallas_call | solution.py:397
  80.3 18.3 %all_to_all.10.arrived = bf16[32,36,128]{2,1,0:T(8,128)(2,1)S(1)} all-to-all(bf16[32,36,128]{2,1,0:T(8,128)(2,1)S(1)} %get-tuple-element.47), channel_id=1, replica_groups=mesh['wave'=32,'field'=16] {'wave'}, dimensions={0} | all-to-all | bytes 589824 | tf_op jit(solution)/shard_map/all_to_all | solution.py:416
  98.6 1.9 %collective-permute-start.2 = (bf16[32,36,128]{2,1,0:T(8,128)(2,1)S(1)}, bf16[32,36,128]{2,1,0:T(8,128)(2,1)S(1)}, u32[]{:S(2)}, u32[]{:S(2)}) collective-permute-start(bf16[32,36,128]{2,1,0:T(8,128)(2,1)S(1)} %all_to_all.10.arrived), channel_id=1, source_target_pairs={{0,1},{1,0},{2,3},{3,2},{4,5},{5,4},{6,7},{7,6},{8,9},{9,8},{10,11... | collective-permute-start | bytes 884744 | tf_op jit(solution)/shard_map/ppermute | solution.py:314
  100.5 1.6 %collective-permute-done.2.swapped = bf16[32,36,128]{2,1,0:T(8,128)(2,1)S(1)} collective-permute-done((bf16[32,36,128]{2,1,0:T(8,128)(2,1)S(1)}, bf16[32,36,128]{2,1,0:T(8,128)(2,1)S(1)}, u32[]{:S(2)}, u32[]{:S(2)}) %collective-permute-start.2) | collective-permute-done | bytes 294944 | tf_op jit(solution)/shard_map/ppermute | solution.py:314
  102.1 0.9 legendre_inverse.1
  103.0 0.9 copy-done
  103.9 0.0 reduce-scatter.2.cloned.1.call-update
  104.0 35.6 %reduce-scatter.2.cloned.1.call-done.summed = bf16[96,640]{1,0:T(8,128)(2,1)} async-done(((bf16[768,640]{1,0:T(8,128)(2,1)}), bf16[96,640]{1,0:T(8,128)(2,1)}) %reduce-scatter.2.cloned.1.call-update) | async-done | bytes 122896 | tf_op jit(solution)/shard_map/reduce_scatter | solution.py:427
  139.6 0.9 copy-done.1
  140.5 0.7 finish.1
  (13 shorter events, 0.0 us)
Async XLA Ops:
  8.1 36.9 %collective-permute-start = (bf16[12,48,640]{2,1,0:T(8,128)(2,1)}, bf16[12,48,640]{2,1,0:T(8,128)(2,1)S(1)}, u32[]{:S(2)}, u32[]{:S(2)}) collective-permute-start(bf16[12,48,640]{2,1,0:T(8,128)(2,1)} %bitcast.11), channel_id=1, source_target_pairs={{0,1},{1,0},{2,3},{3,2},{4,5},{5,4},{6,7},{7,6},{8,9},{9,8},{10,11... | collective-permute-start | bytes 2211848 | tf_op jit(solution)/shard_map/ppermute | solution.py:314
  45.0 0.9 copy-start.5
  47.5 12.1 %copy-start.6 = (s32[384]{0:T(512)S(1)}, s32[384]{0:T(512)}, u32[]{:S(2)}) copy-start(s32[384]{0:T(512)} %wave_of_slot.1) | copy-start | bytes 4612
  47.5 12.1 %copy-start.2 = (s32[1536]{0:T(1024)S(1)}, s32[1536]{0:T(1024)}, u32[]{:S(2)}) copy-start(s32[1536]{0:T(1024)} %lat_of_row.3) | copy-start | bytes 18436
  47.5 12.1 %copy-start.3 = (s32[768]{0:T(1024)S(1)}, s32[768]{0:T(1024)}, u32[]{:S(2)}) copy-start(s32[768]{0:T(1024)} %lon_count.1) | copy-start | bytes 9220
  47.5 12.1 %copy-start.4 = (f32[48]{0:T(128)S(1)}, f32[48]{0:T(128)}, u32[]{:S(2)}) copy-start(f32[48]{0:T(128)} %lat_weight) | copy-start | bytes 580
  49.3 20.7 %all-to-all-start = ((bf16[32,36,128]{2,1,0:T(8,128)(2,1)}), bf16[32,36,128]{2,1,0:T(8,128)(2,1)S(1)}, u32[]{:S(2)}, u32[]{:S(2)}) async-start(bf16[32,36,128]{2,1,0:T(8,128)(2,1)} %legendre_forward.1), calls=%async_computation | async-start | bytes 655360 | tf_op jit(solution)/shard_map/all_to_all | solution.py:370
  59.5 80.0 %reduce-scatter.2.cloned.1.call-start = ((), (), s32[]{:S(2)}) async-start(), calls=%async_computation.3 | async-start | bytes 1105920 | tf_op jit(solution)/shard_map/reduce_scatter | solution.py:427
  70.1 3.5 %collective-permute-start.1 = (bf16[32,36,128]{2,1,0:T(8,128)(2,1)S(1)}, bf16[32,36,128]{2,1,0:T(8,128)(2,1)S(1)}, u32[]{:S(2)}, u32[]{:S(2)}) collective-permute-start(bf16[32,36,128]{2,1,0:T(8,128)(2,1)S(1)} %all-to-all-done.arrived), channel_id=1, source_target_pairs={{0,1},{1,0},{2,3},{3,2},{4,5},{5,4},{6,7},{7,6},{8,9},{9,8},{10,11... | collective-permute-start | bytes 884744 | tf_op jit(solution)/shard_map/ppermute | solution.py:314
  98.6 3.5 %collective-permute-start.2 = (bf16[32,36,128]{2,1,0:T(8,128)(2,1)S(1)}, bf16[32,36,128]{2,1,0:T(8,128)(2,1)S(1)}, u32[]{:S(2)}, u32[]{:S(2)}) collective-permute-start(bf16[32,36,128]{2,1,0:T(8,128)(2,1)S(1)} %all_to_all.10.arrived), channel_id=1, source_target_pairs={{0,1},{1,0},{2,3},{3,2},{4,5},{5,4},{6,7},{7,6},{8,9},{9,8},{10,11... | collective-permute-start | bytes 884744 | tf_op jit(solution)/shard_map/ppermute | solution.py:314
  103.0 0.9 copy-start
  139.5 0.9 copy-start.1
Sparse Core Ops, SparseCore 0:
  104.1 35.4 reduce-scatter.1

commit v5 on v4

--- a/solution.py
+++ b/solution.py
@@ -44,6 +44,10 @@
 
 def hbm():
     return pl.BlockSpec(memory_space=pltpu.HBM)
+
+
+def side_of(core):
+    return 1 - 2 * core
 
 
 def ordered_rows(chosen, south, live, legendre, out):
@@ -121,7 +125,7 @@
 def fourier_tables_kernel(
     wave_id, field_id, lat_of_row, lon_count, lat_weight, waves_row,
     inner_out, inner_t_out, outer_fwd_out, outer_inv_out, place_out, limits_out,
-    inner, inner_t, outer_fwd, outer_inv, place, limits, sems, *, fields,
+    inner, inner_t, outer_fwd, outer_inv, place, limits, sems, *, fields, zs,
 ):
     row_count = inner.shape[0]
     band = lat_weight.shape[0]
@@ -150,9 +154,13 @@
             outer_fwd[member, :, at : at + 2 * LANES] = both * (1.0 / math.sqrt(slots))
             outer_inv[member, :, at : at + 2 * LANES] = both * jnp.concatenate([weight, weight], axis=1)
     at = lax.broadcasted_iota(jnp.int32, (LANES, LANES), 1)
-    core, z, part, low = (field & 1) ^ (at >> 6), (at >> 3) & 7, (at >> 2) & 1, at & 3
-    target = part * 64 + (2 * z + core) * 4 + low
-    place[...] = (lax.broadcasted_iota(jnp.int32, (LANES, LANES), 0) == target).astype(jnp.bfloat16)
+    core, chunk, part, low = (field & 1) ^ (at >> 6), (at >> 3) & 7, (at >> 2) & 1, at & 3
+    away = (chunk + 1) >> 1
+    cross = ((chunk & 1) ^ 1) & (chunk > 0).astype(jnp.int32)
+    z = ((field >> 1) - side_of(core) * away + zs) & (zs - 1)
+    row = lax.broadcasted_iota(jnp.int32, (LANES, LANES), 0)
+    for way, shard in enumerate((2 * chunk + core, 2 * z + (core ^ cross))):
+        place[way] = (row == part * 64 + shard * 4 + low).astype(jnp.bfloat16)
     results = (
         (inner, inner_out), (inner_t, inner_t_out), (outer_fwd, outer_fwd_out),
         (outer_inv, outer_inv_out), (place, place_out), (limits, limits_out),
@@ -184,7 +192,7 @@
 
 
 def legendre_inverse_kernel(
-    arrived, swapped, table, table_swapped, out, held, held_swapped
+    arrived, swapped, table, table_swapped, own, one, one_x, two, two_x, three, four, held, held_swapped
 ):
     slots, rows, degrees = table.shape
     waves = arrived.shape[0]
@@ -205,9 +213,11 @@
         sums = [
             share(held, slot, table) + share(held_swapped, slot, table_swapped) for slot in (2 * pair, 2 * pair + 1)
         ]
-        for z in range(out.shape[0]):
-            piece = jnp.concatenate([s[8 * z : 8 * z + 8] for s in sums], axis=0)
-            out[z, at, :] = piece.astype(jnp.bfloat16)
+        pieces = [jnp.concatenate([s[8 * chunk : 8 * chunk + 8] for s in sums], axis=0) for chunk in range(8)]
+        own[at, :] = pieces[0]
+        targets = (one, one_x, two, two_x, three.at[0], three.at[1], four)
+        for target, piece in zip(targets, pieces[1:]):
+            target[at, :] = piece.astype(jnp.bfloat16)
 
 
 def fourier_kernel(
@@ -239,7 +249,7 @@
     for member in range(row_count):
         points = jnp.concatenate([limits[member, :1, :]] * (BLOCK // LANES), axis=1)
         lines = held[pl.ds(member, slots, stride=row_count), :].astype(jnp.bfloat16)
-        coef = dot(place[...], lines, NT)
+        coef = dot(place[0], lines, NT)
         for step in range(BLOCKS):
             rows = pl.ds(step * levels, levels)
             for part in range(parts):
@@ -278,7 +288,7 @@
             imags.append(imag)
         analysed = jnp.concatenate([jnp.concatenate(reals, axis=1), jnp.concatenate(imags, axis=1)], axis=0)
         back[pl.ds(member, slots, stride=row_count), :] = dot(
-            analysed.T.astype(jnp.bfloat16), place[...], NN
+            analysed.T.astype(jnp.bfloat16), place[1], NN
         )
     for source in range(waves):
         sent[source] = back[source * each : (source + 1) * each, :].astype(jnp.bfloat16)
@@ -286,8 +296,17 @@
         result.wait()
 
 
-def finish_kernel(summed, out):
-    total = summed[...].astype(jnp.float32)
+def add_three_kernel(two, two_x, three, four, out, out_x):
+    out[...] = (
+        two[...].astype(jnp.float32) + three[0].astype(jnp.float32) + four[...].astype(jnp.float32)
+    ).astype(jnp.bfloat16)
+    out_x[...] = (two_x[...].astype(jnp.float32) + three[1].astype(jnp.float32)).astype(jnp.bfloat16)
+
+
+def add_own_kernel(own, one, one_x, two, two_x, out):
+    total = own[...]
+    for landed in (one, one_x, two, two_x):
+        total = total + landed[...].astype(jnp.float32)
     groups, cols, _ = out.shape
     for group in range(groups):
         out[group] = total[group * cols : (group + 1) * cols]
@@ -310,8 +329,14 @@
 
     like_cores = [list(range(core, fields, 2)) for core in range(2)]
 
+    def hop(x, by, cross=0):
+        pairs = [
+            (i, (2 * (i // 2 + side_of(i % 2) * by) + (i % 2 ^ cross)) % fields) for i in range(fields)
+        ]
+        return lax.ppermute(x, "field", pairs)
+
     def swap(x):
-        return lax.ppermute(x, "field", [(i, i ^ 1) for i in range(fields)])
+        return hop(x, 0, 1)
 
     def local(kernel, out_shape, name, micros, mebibytes=8, in_specs=None, out_specs=None, scratch=()):
         if in_specs is None:
@@ -374,12 +399,12 @@
         ((row_count, 2 * all_slots, BLOCK), jnp.bfloat16),
         ((row_count, 16, 2 * all_slots), jnp.float32),
         ((row_count, 16, 2 * all_slots), jnp.float32),
-        ((LANES, LANES), jnp.bfloat16),
+        ((2, LANES, LANES), jnp.bfloat16),
         ((row_count, 8, LANES), jnp.float32),
     )
     tables_vmem = [pltpu.VMEM(shape, kind) for shape, kind in tables]
     prepared = local(
-        functools.partial(fourier_tables_kernel, fields=fields),
+        functools.partial(fourier_tables_kernel, fields=fields, zs=zs),
         [pltpu.HBM(shape, kind) for shape, kind in tables],
         "fourier_tables",
         4,
@@ -415,29 +440,33 @@
 
     returned = lax.all_to_all(sent, "wave", split_axis=0, concat_axis=0, tiled=True)
 
-    partial = local(
+    chunk = jax.ShapeDtypeStruct((coded, degrees), jnp.bfloat16)
+    own, one, one_x, two, two_x, three, four = local(
         legendre_inverse_kernel,
-        jax.ShapeDtypeStruct((zs, coded, degrees), jnp.bfloat16),
+        (
+            jax.ShapeDtypeStruct((coded, degrees), jnp.float32),
+            chunk, chunk, chunk, chunk, jax.ShapeDtypeStruct((2, coded, degrees), jnp.bfloat16), chunk,
+        ),
         "legendre_inverse",
         2,
         16,
         in_specs=[vmem()] * 4,
         scratch=[float_rows, float_rows],
     )(returned, swap(returned), table, table_x)
-    summed = lax.psum_scatter(
-        partial.reshape(zs * coded, degrees),
-        "field",
-        scatter_dimension=0,
-        axis_index_groups=like_cores,
-        tiled=True,
+    three, four = hop(three, -1), hop(four, -2)
+    two, two_x = local(add_three_kernel, (chunk, chunk), "add_three", 1, in_specs=[vmem()] * 4)(
+        two, two_x, three, four
     )
+    two, two_x, one_x = lax.optimization_barrier((two, two_x, one_x))
+    two, two_x = hop(two, -2), hop(two_x, -2, 1)
+    one, one_x = hop(one, -1), hop(one_x, -1, 1)
     total = local(
-        finish_kernel,
+        add_own_kernel,
         jax.ShapeDtypeStruct((2 * slots, cols, degrees), jnp.float32),
-        "finish",
+        "add_own",
         1,
-        in_specs=[vmem()],
-    )(summed)
+        in_specs=[vmem()] * 5,
+    )(own, one, one_x, two, two_x)
     spectral = jnp.transpose(total.reshape(slots, 2, cols, degrees), (0, 1, 3, 2))
     return grid_field, spectral
 

time: 148 us -> 126 us (0.85)
  the two profiles are of different devices: /device:TPU:4 before, /device:TPU:1 now
where the time goes in v5:
time: 126 us; the launch traced here: 124 us
  starting transfers between devices  49.3 us (39%)
  blocking collectives  38.4 us (30%)
  Pallas kernels  18 us (14%)
  waiting for transfers between devices  15.8 us (13%)
  local copies, waits for them, and re-layouts  1.83 us (1%)
    ppermute x9, starting transfers between devices, hop(): return lax.ppermute(x, 'field', pairs)  39.7 us
    all_gather x1, blocking collectives, shards(): gathered = lax.all_gather(own, 'field', axis_index_groups=like_cores)  21.9 us
    all_to_all x1, blocking collectives, shards(): lax.all_to_all(sent, 'wave', split_axis=0, concat_axis=0, tiled=True)  16.5 us
    all_to_all x1, starting transfers between devices, shards(): lax.all_to_all(outgoing, 'wave', split_axis=0, concat_axis=0, tiled=True)  9.64 us
    ppermute x9, waiting for transfers between devices, hop(): return lax.ppermute(x, 'field', pairs)  9.34 us
    pallas_call x1, Pallas kernels, shards(): local(fourier_kernel, (jax.ShapeDtypeStruct((row_count, levels, LONPAD),...  6.7 us
    all_to_all x1, waiting for transfers between devices, shards(): lax.all_to_all(outgoing, 'wave', split_axis=0, concat_axis=0, tiled=True)  6.43 us
    pallas_call x1, Pallas kernels, shards(): local(functools.partial(fourier_tables_kernel, fields=fields, zs=zs), [pl...  4.22 us
  transfers between devices with their start and end apart: 10, of which 6 were waited for; matrix products, arithmetic and copies ran while one was open for 0% of the time, Pallas kernels for 5%

profile of v5, /device:TPU:1, one launch (start us, length us, event | category | flops | bytes accessed | tf_op | source)
XLA Modules:
  0.0 124.1 jit_solution(4877402874045725505)
XLA Ops:
  0.6 0.9 reshape.19
  1.6 8.8 %collective-permute-start = (bf16[12,48,640]{2,1,0:T(8,128)(2,1)}, bf16[12,48,640]{2,1,0:T(8,128)(2,1)S(1)}, u32[]{:S(2)}, u32[]{:S(2)}) collective-permute-start(bf16[12,48,640]{2,1,0:T(8,128)(2,1)} %bitcast.9), channel_id=1, source_target_pairs={{0,1},{1,0},{2,3},{3,2},{4,5},{5,4},{6,7},{7,6},{8,9},{9,8},{10,11... | collective-permute-start | bytes 2211848 | tf_op jit(solution)/shard_map/ppermute | solution.py:336
  10.4 1.9 %own_rows.1 = (bf16[12,96,640]{2,1,0:T(8,128)(2,1)S(1)}, bf16[96,128]{1,0:T(8,128)(2,1)S(1)}, f32[96,128]{1,0:T(8,128)S(1)}, f32[16,640]{1,0:T(8,128)S(1)}) custom-call(s32[1]{0:T(128)} %bitcast.3.wave_id, s32[1]{0:T(128)} %bitcast.4.field_id, s32[384]{0:T(512)} %wave_of_slot.1, s32[1536]{0:T(1024)} %lat_of_row.3, bf16[12,48,640]{2,1,0:T(8,128)(2,1)} %bitcast.10), custom_call_target="tpu_custom_call" | custom-call | bytes 7400000 | tf_op jit(solution)/shard_map/own_rows/pallas_call | solution.py:363
  12.3 21.9 %all-gather = bf16[768,640]{1,0:T(8,128)(2,1)S(1)} all-gather(bf16[96,640]{1,0:T(8,128)(2,1)S(1)} %reshape.19), channel_id=2, replica_groups={{0,2,4,6,8,10,12,14},{1,3,5,7,9,11,13,15},{16,18,20,22,24,26,28,30},{17..., dimensions={0}, use_global_device_ids=true | all-gather | bytes 1105920 | tf_op jit(solution)/shard_map/all_gather | solution.py:361
  35.0 1.6 %partner_rows.1.table_swapped = bf16[12,96,640]{2,1,0:T(8,128)(2,1)S(1)} custom-call(bf16[96,128]{1,0:T(8,128)(2,1)S(1)} %get-tuple-element.40.chosen, f32[96,128]{1,0:T(8,128)S(1)} %get-tuple-element.41.south, f32[16,640]{1,0:T(8,128)S(1)} %get-tuple-element.42.live, bf16[12,48,640]{2,1,0:T(8,128)(2,1)} %copy-done.3), custom_call_target="tpu_custom_call" | custom-call | bytes 7400000 | tf_op jit(solution)/shard_map/partner_rows/pallas_call | solution.py:383
  36.7 1.8 %legendre_forward.1 = bf16[32,36,128]{2,1,0:T(8,128)(2,1)} custom-call(bf16[8,96,640]{2,1,0:T(8,128)(2,1)S(1)} %bitcast.8, bf16[12,96,640]{2,1,0:T(8,128)(2,1)S(1)} %get-tuple-element.39.table, bf16[12,96,640]{2,1,0:T(8,128)(2,1)S(1)} %partner_rows.1.table_swapped), custom_call_target="tpu_custom_call" | custom-call | bytes 14800000 | tf_op jit(solution)/shard_map/legendre_forward/pallas_call | solution.py:391
  38.5 9.6 %all-to-all-start = ((bf16[32,36,128]{2,1,0:T(8,128)(2,1)}), bf16[32,36,128]{2,1,0:T(8,128)(2,1)S(1)}, u32[]{:S(2)}, u32[]{:S(2)}) async-start(bf16[32,36,128]{2,1,0:T(8,128)(2,1)} %legendre_forward.1), calls=%async_computation | async-start | bytes 655360 | tf_op jit(solution)/shard_map/all_to_all | solution.py:395
  48.2 4.2 %fourier_tables.1 = (bf16[3,256,768]{2,1,0:T(8,128)(2,1)}, bf16[3,768,256]{2,1,0:T(8,128)(2,1)}, f32[3,16,768]{2,1,0:T(8,128)}, f32[3,16,768]{2,1,0:T(8,128)}, b...) custom-call(s32[1]{0:T(128)} %bitcast.3.wave_id, s32[1]{0:T(128)} %bitcast.4.field_id, s32[1536]{0:T(1024)S(1)} %copy-done, ...), custom_call_target="tpu_custom_call" | custom-call | bytes 14800000 | tf_op jit(solution)/shard_map/fourier_tables/pallas_call | solution.py:406
  52.4 6.4 %all-to-all-done.arrived = bf16[32,36,128]{2,1,0:T(8,128)(2,1)S(1)} async-done(((bf16[32,36,128]{2,1,0:T(8,128)(2,1)}), bf16[32,36,128]{2,1,0:T(8,128)(2,1)S(1)}, u32[]{:S(2)}, u32[]{:S(2)}) %all-to-all-start) | async-done | bytes 294944 | tf_op jit(solution)/shard_map/all_to_all | solution.py:395
  58.9 9.1 %collective-permute-start.1 = (bf16[32,36,128]{2,1,0:T(8,128)(2,1)S(1)}, bf16[32,36,128]{2,1,0:T(8,128)(2,1)S(1)}, u32[]{:S(2)}, u32[]{:S(2)}) collective-permute-start(bf16[32,36,128]{2,1,0:T(8,128)(2,1)S(1)} %all-to-all-done.arrived), channel_id=1, source_target_pairs={{0,1},{1,0},{2,3},{3,2},{4,5},{5,4},{6,7},{7,6},{8,9},{9,8},{10,11... | collective-permute-start | bytes 884744 | tf_op jit(solution)/shard_map/ppermute | solution.py:336
  68.0 1.2 collective-permute-done.1.swapped
  69.2 6.7 %fourier.1 = (bf16[3,64,3200]{2,1,0:T(8,128)(2,1)}, bf16[32,36,128]{2,1,0:T(8,128)(2,1)S(1)}) custom-call(bf16[32,36,128]{2,1,0:T(8,128)(2,1)S(1)} %all-to-all-done.arrived, bf16[32,36,128]{2,1,0:T(8,128)(2,1)S(1)} %collective-permute-done.1.swapped, bf16[3,256,768]{2,1,0:T(8,128)(2,1)} %get-tuple-element.52.inner_in, ...), custom_call_target="tpu_custom_call" | custom-call | bytes 22200000 | tf_op jit(solution)/shard_map/fourier/pallas_call | solution.py:422
  75.9 16.5 %all_to_all.10.arrived = bf16[32,36,128]{2,1,0:T(8,128)(2,1)S(1)} all-to-all(bf16[32,36,128]{2,1,0:T(8,128)(2,1)S(1)} %get-tuple-element.59), channel_id=1, replica_groups=mesh['wave'=32,'field'=16] {'wave'}, dimensions={0} | all-to-all | bytes 589824 | tf_op jit(solution)/shard_map/all_to_all | solution.py:441
  92.4 4.3 %collective-permute-start.2 = (bf16[32,36,128]{2,1,0:T(8,128)(2,1)S(1)}, bf16[32,36,128]{2,1,0:T(8,128)(2,1)S(1)}, u32[]{:S(2)}, u32[]{:S(2)}) collective-permute-start(bf16[32,36,128]{2,1,0:T(8,128)(2,1)S(1)} %all_to_all.10.arrived), channel_id=1, source_target_pairs={{0,1},{1,0},{2,3},{3,2},{4,5},{5,4},{6,7},{7,6},{8,9},{9,8},{10,11... | collective-permute-start | bytes 884744 | tf_op jit(solution)/shard_map/ppermute | solution.py:336
  96.8 1.2 collective-permute-done.2.swapped
  98.0 0.9 legendre_inverse.1
  98.9 3.1 %collective-permute-start.4 = (bf16[2,96,640]{2,1,0:T(8,128)(2,1)S(1)}, bf16[2,96,640]{2,1,0:T(8,128)(2,1)S(1)}, u32[]{:S(2)}, u32[]{:S(2)}) collective-permute-start(bf16[2,96,640]{2,1,0:T(8,128)(2,1)S(1)} %get-tuple-element.64), channel_id=1, source_target_pairs={{0,14},{1,3},{2,0},{3,5},{4,2},{5,7},{6,4},{7,9},{8,6},{9,11},{10,... | collective-permute-start | bytes 737288 | tf_op jit(solution)/shard_map/ppermute | solution.py:336
  102.1 2.1 %collective-permute-start.5 = (bf16[96,640]{1,0:T(8,128)(2,1)S(1)}, bf16[96,640]{1,0:T(8,128)(2,1)S(1)}, u32[]{:S(2)}, u32[]{:S(2)}) collective-permute-start(bf16[96,640]{1,0:T(8,128)(2,1)S(1)} %get-tuple-element.65), channel_id=1, source_target_pairs={{0,12},{1,5},{2,14},{3,7},{4,0},{5,9},{6,2},{7,11},{8,4},{9,13},{1... | collective-permute-start | bytes 368648 | tf_op jit(solution)/shard_map/ppermute | solution.py:336
  104.2 3.4 %collective-permute-start.3 = (bf16[96,640]{1,0:T(8,128)(2,1)S(1)}, bf16[96,640]{1,0:T(8,128)(2,1)S(1)}, u32[]{:S(2)}, u32[]{:S(2)}) collective-permute-start(bf16[96,640]{1,0:T(8,128)(2,1)S(1)} %get-tuple-element.61), channel_id=1, source_target_pairs={{0,14},{1,3},{2,0},{3,5},{4,2},{5,7},{6,4},{7,9},{8,6},{9,11},{10,... | collective-permute-start | bytes 368648 | tf_op jit(solution)/shard_map/ppermute | solution.py:336
  107.6 3.6 %collective-permute-done.5.four = bf16[96,640]{1,0:T(8,128)(2,1)S(1)} collective-permute-done((bf16[96,640]{1,0:T(8,128)(2,1)S(1)}, bf16[96,640]{1,0:T(8,128)(2,1)S(1)}, u32[]{:S(2)}, u32[]{:S(2)}) %collective-permute-start.5) | collective-permute-done | bytes 122912 | tf_op jit(solution)/shard_map/ppermute | solution.py:336
  111.3 1.9 %collective-permute-start.6 = (bf16[96,640]{1,0:T(8,128)(2,1)S(1)}, bf16[96,640]{1,0:T(8,128)(2,1)S(1)}, u32[]{:S(2)}, u32[]{:S(2)}) collective-permute-start(bf16[96,640]{1,0:T(8,128)(2,1)S(1)} %get-tuple-element.69), channel_id=1, source_target_pairs={{0,15},{1,2},{2,1},{3,4},{4,3},{5,6},{6,5},{7,8},{8,7},{9,10},{10,... | collective-permute-start | bytes 368648 | tf_op jit(solution)/shard_map/ppermute | solution.py:336
  113.2 2.8 %collective-permute-start.7 = (bf16[96,640]{1,0:T(8,128)(2,1)S(1)}, bf16[96,640]{1,0:T(8,128)(2,1)S(1)}, u32[]{:S(2)}, u32[]{:S(2)}) collective-permute-start(bf16[96,640]{1,0:T(8,128)(2,1)S(1)} %get-tuple-element.70), channel_id=1, source_target_pairs={{0,12},{1,5},{2,14},{3,7},{4,0},{5,9},{6,2},{7,11},{8,4},{9,13},{1... | collective-permute-start | bytes 368648 | tf_op jit(solution)/shard_map/ppermute | solution.py:336
  116.0 4.0 %collective-permute-start.8 = (bf16[96,640]{1,0:T(8,128)(2,1)S(1)}, bf16[96,640]{1,0:T(8,128)(2,1)S(1)}, u32[]{:S(2)}, u32[]{:S(2)}) collective-permute-start(bf16[96,640]{1,0:T(8,128)(2,1)S(1)} %get-tuple-element.71), channel_id=1, source_target_pairs={{0,13},{1,4},{2,15},{3,6},{4,1},{5,8},{6,3},{7,10},{8,5},{9,12},{1... | collective-permute-start | bytes 368648 | tf_op jit(solution)/shard_map/ppermute | solution.py:336
  121.0 2.4 %collective-permute-done.8.two_x = bf16[96,640]{1,0:T(8,128)(2,1)S(1)} collective-permute-done((bf16[96,640]{1,0:T(8,128)(2,1)S(1)}, bf16[96,640]{1,0:T(8,128)(2,1)S(1)}, u32[]{:S(2)}, u32[]{:S(2)}) %collective-permute-start.8) | collective-permute-done | bytes 122912 | tf_op jit(solution)/shard_map/ppermute | solution.py:336
  (19 shorter events, 2.7 us)
Async XLA Ops:
  1.6 32.6 %collective-permute-start = (bf16[12,48,640]{2,1,0:T(8,128)(2,1)}, bf16[12,48,640]{2,1,0:T(8,128)(2,1)S(1)}, u32[]{:S(2)}, u32[]{:S(2)}) collective-permute-start(bf16[12,48,640]{2,1,0:T(8,128)(2,1)} %bitcast.9), channel_id=1, source_target_pairs={{0,1},{1,0},{2,3},{3,2},{4,5},{5,4},{6,7},{7,6},{8,9},{9,8},{10,11... | collective-permute-start | bytes 2211848 | tf_op jit(solution)/shard_map/ppermute | solution.py:336
  34.1 0.9 copy-start.3
  36.7 11.5 %copy-start.4 = (s32[384]{0:T(512)S(1)}, s32[384]{0:T(512)}, u32[]{:S(2)}) copy-start(s32[384]{0:T(512)} %wave_of_slot.1) | copy-start | bytes 4612
  36.7 11.5 %copy-start = (s32[1536]{0:T(1024)S(1)}, s32[1536]{0:T(1024)}, u32[]{:S(2)}) copy-start(s32[1536]{0:T(1024)} %lat_of_row.3) | copy-start | bytes 18436
  36.7 11.5 %copy-start.1 = (s32[768]{0:T(1024)S(1)}, s32[768]{0:T(1024)}, u32[]{:S(2)}) copy-start(s32[768]{0:T(1024)} %lon_count.1) | copy-start | bytes 9220
  36.7 11.5 %copy-start.2 = (f32[48]{0:T(128)S(1)}, f32[48]{0:T(128)}, u32[]{:S(2)}) copy-start(f32[48]{0:T(128)} %lat_weight) | copy-start | bytes 580
  38.5 20.4 %all-to-all-start = ((bf16[32,36,128]{2,1,0:T(8,128)(2,1)}), bf16[32,36,128]{2,1,0:T(8,128)(2,1)S(1)}, u32[]{:S(2)}, u32[]{:S(2)}) async-start(bf16[32,36,128]{2,1,0:T(8,128)(2,1)} %legendre_forward.1), calls=%async_computation | async-start | bytes 655360 | tf_op jit(solution)/shard_map/all_to_all | solution.py:395
  58.9 10.4 %collective-permute-start.1 = (bf16[32,36,128]{2,1,0:T(8,128)(2,1)S(1)}, bf16[32,36,128]{2,1,0:T(8,128)(2,1)S(1)}, u32[]{:S(2)}, u32[]{:S(2)}) collective-permute-start(bf16[32,36,128]{2,1,0:T(8,128)(2,1)S(1)} %all-to-all-done.arrived), channel_id=1, source_target_pairs={{0,1},{1,0},{2,3},{3,2},{4,5},{5,4},{6,7},{7,6},{8,9},{9,8},{10,11... | collective-permute-start | bytes 884744 | tf_op jit(solution)/shard_map/ppermute | solution.py:336
  92.4 5.6 %collective-permute-start.2 = (bf16[32,36,128]{2,1,0:T(8,128)(2,1)S(1)}, bf16[32,36,128]{2,1,0:T(8,128)(2,1)S(1)}, u32[]{:S(2)}, u32[]{:S(2)}) collective-permute-start(bf16[32,36,128]{2,1,0:T(8,128)(2,1)S(1)} %all_to_all.10.arrived), channel_id=1, source_target_pairs={{0,1},{1,0},{2,3},{3,2},{4,5},{5,4},{6,7},{7,6},{8,9},{9,8},{10,11... | collective-permute-start | bytes 884744 | tf_op jit(solution)/shard_map/ppermute | solution.py:336
  98.9 12.3 %collective-permute-start.4 = (bf16[2,96,640]{2,1,0:T(8,128)(2,1)S(1)}, bf16[2,96,640]{2,1,0:T(8,128)(2,1)S(1)}, u32[]{:S(2)}, u32[]{:S(2)}) collective-permute-start(bf16[2,96,640]{2,1,0:T(8,128)(2,1)S(1)} %get-tuple-element.64), channel_id=1, source_target_pairs={{0,14},{1,3},{2,0},{3,5},{4,2},{5,7},{6,4},{7,9},{8,6},{9,11},{10,... | collective-permute-start | bytes 737288 | tf_op jit(solution)/shard_map/ppermute | solution.py:336
  102.1 9.1 %collective-permute-start.5 = (bf16[96,640]{1,0:T(8,128)(2,1)S(1)}, bf16[96,640]{1,0:T(8,128)(2,1)S(1)}, u32[]{:S(2)}, u32[]{:S(2)}) collective-permute-start(bf16[96,640]{1,0:T(8,128)(2,1)S(1)} %get-tuple-element.65), channel_id=1, source_target_pairs={{0,12},{1,5},{2,14},{3,7},{4,0},{5,9},{6,2},{7,11},{8,4},{9,13},{1... | collective-permute-start | bytes 368648 | tf_op jit(solution)/shard_map/ppermute | solution.py:336
  104.2 15.9 %collective-permute-start.3 = (bf16[96,640]{1,0:T(8,128)(2,1)S(1)}, bf16[96,640]{1,0:T(8,128)(2,1)S(1)}, u32[]{:S(2)}, u32[]{:S(2)}) collective-permute-start(bf16[96,640]{1,0:T(8,128)(2,1)S(1)} %get-tuple-element.61), channel_id=1, source_target_pairs={{0,14},{1,3},{2,0},{3,5},{4,2},{5,7},{6,4},{7,9},{8,6},{9,11},{10,... | collective-permute-start | bytes 368648 | tf_op jit(solution)/shard_map/ppermute | solution.py:336
  111.3 8.8 %collective-permute-start.6 = (bf16[96,640]{1,0:T(8,128)(2,1)S(1)}, bf16[96,640]{1,0:T(8,128)(2,1)S(1)}, u32[]{:S(2)}, u32[]{:S(2)}) collective-permute-start(bf16[96,640]{1,0:T(8,128)(2,1)S(1)} %get-tuple-element.69), channel_id=1, source_target_pairs={{0,15},{1,2},{2,1},{3,4},{4,3},{5,6},{6,5},{7,8},{8,7},{9,10},{10,... | collective-permute-start | bytes 368648 | tf_op jit(solution)/shard_map/ppermute | solution.py:336
  113.2 7.8 %collective-permute-start.7 = (bf16[96,640]{1,0:T(8,128)(2,1)S(1)}, bf16[96,640]{1,0:T(8,128)(2,1)S(1)}, u32[]{:S(2)}, u32[]{:S(2)}) collective-permute-start(bf16[96,640]{1,0:T(8,128)(2,1)S(1)} %get-tuple-element.70), channel_id=1, source_target_pairs={{0,12},{1,5},{2,14},{3,7},{4,0},{5,9},{6,2},{7,11},{8,4},{9,13},{1... | collective-permute-start | bytes 368648 | tf_op jit(solution)/shard_map/ppermute | solution.py:336
  116.0 7.3 %collective-permute-start.8 = (bf16[96,640]{1,0:T(8,128)(2,1)S(1)}, bf16[96,640]{1,0:T(8,128)(2,1)S(1)}, u32[]{:S(2)}, u32[]{:S(2)}) collective-permute-start(bf16[96,640]{1,0:T(8,128)(2,1)S(1)} %get-tuple-element.71), channel_id=1, source_target_pairs={{0,13},{1,4},{2,15},{3,6},{4,1},{5,8},{6,3},{7,10},{8,5},{9,12},{1... | collective-permute-start | bytes 368648 | tf_op jit(solution)/shard_map/ppermute | solution.py:336

commit v6 on v5

--- a/solution.py
+++ b/solution.py
@@ -159,7 +159,8 @@
     cross = ((chunk & 1) ^ 1) & (chunk > 0).astype(jnp.int32)
     z = ((field >> 1) - side_of(core) * away + zs) & (zs - 1)
     row = lax.broadcasted_iota(jnp.int32, (LANES, LANES), 0)
-    for way, shard in enumerate((2 * chunk + core, 2 * z + (core ^ cross))):
+    gathered_z = chunk + core * (zs - 1 - 2 * chunk)
+    for way, shard in enumerate((2 * gathered_z + core, 2 * z + (core ^ cross))):
         place[way] = (row == part * 64 + shard * 4 + low).astype(jnp.bfloat16)
     results = (
         (inner, inner_out), (inner_t, inner_t_out), (outer_fwd, outer_fwd_out),
@@ -172,17 +173,18 @@
         copy.wait()
 
 
-def legendre_forward_kernel(gathered, table, table_swapped, out, held):
+def legendre_forward_kernel(gathered, gathered_x, table, out, held):
     slots, rows, degrees = table.shape
     waves = out.shape[0]
     row_count = rows // waves
     each = slots * row_count
     for pair in range(slots // 2):
-        both = [gathered[z, 16 * pair : 16 * pair + 16, :].astype(jnp.float32) for z in range(gathered.shape[0])]
+        at = pl.ds(16 * pair, 16)
+        both = [source[z, at, :].astype(jnp.float32) for source in (gathered, gathered_x) for z in range(source.shape[0])]
         for half in range(2):
             slot = 2 * pair + half
             spec = jnp.concatenate([b[8 * half : 8 * half + 8] for b in both], axis=0).astype(jnp.bfloat16)
-            sums = jnp.concatenate([dot(table[slot], spec, NT), dot(table_swapped[slot], spec, NT)], axis=1)
+            sums = dot(table[slot], spec, NT)
             for member in range(row_count):
                 held[pl.ds(slot * row_count + member, waves, stride=each), :] = sums[
                     waves * member : waves * (member + 1)
@@ -221,7 +223,7 @@
 
 
 def fourier_kernel(
-    arrived, swapped, inner_in, inner_t_in, outer_fwd_in, outer_inv_in, place_in, limits_in,
+    arrived, inner_in, inner_t_in, outer_fwd_in, outer_inv_in, place_in, limits_in,
     grid_out, sent,
     inner, inner_t, outer_fwd, outer_inv, place, limits, held, back, turned, products, lines_out, sems, out_sems,
 ):
@@ -237,12 +239,9 @@
     slots = waves * each // row_count
     parts = slots // LANES
     levels = grid_out.shape[1]
-    mine = lax.broadcasted_iota(jnp.int32, (1, LANES), 1) < 64
     for source in range(waves):
-        held[source * each : (source + 1) * each, :] = jnp.where(
-            mine, arrived[source].astype(jnp.float32), swapped[source].astype(jnp.float32)
-        )
-    for copy in copies:
+        held[source * each : (source + 1) * each, :] = arrived[source].astype(jnp.float32)
+    for copy in copies[:3]:
         copy.wait()
     column = lax.broadcasted_iota(jnp.int32, (1, BLOCK), 1).astype(jnp.float32)
     results = []
@@ -260,6 +259,8 @@
                 sine = outer_fwd[member, step : step + 1, at + LANES : at + 2 * LANES]
                 turned[member, rows, at : at + LANES] = (real * cosine - imag * sine).astype(jnp.bfloat16)
                 turned[member, rows, at + LANES : at + 2 * LANES] = (real * sine + imag * cosine).astype(jnp.bfloat16)
+        if member == 0:
+            copies[3].wait()
         values = dot(turned[member], inner_t[member], NN)
         for step in range(BLOCKS):
             width = min(BLOCK, LONPAD - step * BLOCK)
@@ -272,6 +273,9 @@
         result = pltpu.make_async_copy(lines_out.at[member], grid_out.at[member], out_sems.at[member])
         result.start()
         results.append(result)
+        if member == 0:
+            copies[4].wait()
+            copies[5].wait()
         reals, imags = [], []
         for part in range(parts):
             at = part * 2 * LANES
@@ -327,7 +331,7 @@
     each = row_count * slots
     coded = slots * 2 * cols
 
-    like_cores = [list(range(core, fields, 2)) for core in range(2)]
+    like_cores = [list(range(0, fields, 2)), list(range(fields - 1, 0, -2))]
 
     def hop(x, by, cross=0):
         pairs = [
@@ -357,9 +361,9 @@
     float_rows = pltpu.VMEM((waves * each, LANES), jnp.float32)
 
     own = jnp.transpose(spectra, (0, 1, 3, 2)).reshape(coded, degrees)
-    own, legendre = lax.optimization_barrier((own, jnp.transpose(legendre, (0, 2, 1))))
     gathered = lax.all_gather(own, "field", axis_index_groups=like_cores)
-    legendre_x = swap(legendre)
+    gathered, legendre = lax.optimization_barrier((gathered, jnp.transpose(legendre, (0, 2, 1))))
+    gathered_x = swap(gathered)
     table, chosen_x, south_x, live = local(
         functools.partial(own_rows_kernel, waves=waves, fields=fields),
         (
@@ -380,20 +384,11 @@
             pltpu.SemaphoreType.DMA((3,)),
         ],
     )(wave_id, field_id, in_hbm(wave_of_slot), in_hbm(lat_of_row), in_hbm(legendre))
-    table_x = local(
-        partner_rows_kernel,
-        row_table,
-        "partner_rows",
-        2,
-        in_specs=[vmem(), vmem(), vmem(), hbm()],
-        scratch=[pltpu.VMEM((slots, band, degrees), jnp.bfloat16), pltpu.SemaphoreType.DMA(())],
-    )(chosen_x, south_x, live, in_hbm(legendre_x))
     outgoing = local(
         legendre_forward_kernel, fourier_shape, "legendre_forward", 4, 16, in_specs=[vmem()] * 3, scratch=[float_rows]
-    )(gathered, table, table_x)
+    )(gathered, gathered_x, table)
     outgoing, lat_weight = lax.optimization_barrier((outgoing, lat_weight))
     arrived = lax.all_to_all(outgoing, "wave", split_axis=0, concat_axis=0, tiled=True)
-
     tables = (
         ((row_count, BLOCK, 2 * all_slots), jnp.bfloat16),
         ((row_count, 2 * all_slots, BLOCK), jnp.bfloat16),
@@ -416,6 +411,8 @@
         wave_id, field_id, lat_of_row, lon_count, lat_weight,
         wave_of_slot.astype(jnp.float32).reshape(1, all_slots),
     )
+    prepared, legendre = lax.optimization_barrier((prepared, legendre))
+    legendre_x = swap(legendre)
     arrived, prepared = lax.optimization_barrier((arrived, prepared))
     prepared = [in_hbm(x) for x in prepared]
 
@@ -425,7 +422,7 @@
         "fourier",
         6,
         32,
-        in_specs=[vmem()] * 2 + [hbm()] * 6,
+        in_specs=[vmem()] + [hbm()] * 6,
         out_specs=(hbm(), vmem()),
         scratch=tables_vmem + [
             float_rows,
@@ -436,9 +433,20 @@
             pltpu.SemaphoreType.DMA((6,)),
             pltpu.SemaphoreType.DMA((row_count,)),
         ],
-    )(arrived, swap(arrived), *prepared)
-
+    )(arrived, *prepared)
+
+    sent, legendre_x = lax.optimization_barrier((sent, legendre_x))
     returned = lax.all_to_all(sent, "wave", split_axis=0, concat_axis=0, tiled=True)
+
+    table_x = local(
+        partner_rows_kernel,
+        row_table,
+        "partner_rows",
+        2,
+        in_specs=[vmem(), vmem(), vmem(), hbm()],
+        scratch=[pltpu.VMEM((slots, band, degrees), jnp.bfloat16), pltpu.SemaphoreType.DMA(())],
+    )(chosen_x, south_x, live, in_hbm(legendre_x))
+    returned, table_x = lax.optimization_barrier((returned, table_x))
 
     chunk = jax.ShapeDtypeStruct((coded, degrees), jnp.bfloat16)
     own, one, one_x, two, two_x, three, four = local(
@@ -457,9 +465,8 @@
     two, two_x = local(add_three_kernel, (chunk, chunk), "add_three", 1, in_specs=[vmem()] * 4)(
         two, two_x, three, four
     )
-    two, two_x, one_x = lax.optimization_barrier((two, two_x, one_x))
+    one, one_x = hop(one, -1), hop(one_x, -1, 1)
     two, two_x = hop(two, -2), hop(two_x, -2, 1)
-    one, one_x = hop(one, -1), hop(one_x, -1, 1)
     total = local(
         add_own_kernel,
         jax.ShapeDtypeStruct((2 * slots, cols, degrees), jnp.float32),

time: 126 us -> 128 us (1.016)
  blocking collectives: 38.4 us -> 51 us
  starting transfers between devices: 49.3 us -> 39.2 us
  waiting for transfers between devices: 15.8 us -> 17.6 us
    all_gather x1, blocking collectives: 21.9 us -> 28.6 us  [shards(): gathered = lax.all_gather(own, 'field', axis_index_groups=like_cores)]
    all_to_all x1, blocking collectives: 16.5 us -> 22.4 us  [shards(): lax.all_to_all(outgoing, 'wave', split_axis=0, concat_axis=0, tiled=True)]
    all_to_all x1, starting transfers between devices: 9.64 us -> 4.57 us  [shards(): lax.all_to_all(sent, 'wave', split_axis=0, concat_axis=0, tiled=True)]
    ppermute x9, starting transfers between devices: 39.7 us -> 34.7 us  [hop(): return lax.ppermute(x, 'field', pairs)]
    all_to_all x1, waiting for transfers between devices: 6.43 us -> 9.57 us  [shards(): lax.all_to_all(sent, 'wave', split_axis=0, concat_axis=0, tiled=True)]
    ppermute x9, waiting for transfers between devices: 9.34 us -> 8.02 us  [hop(): return lax.ppermute(x, 'field', pairs)]
  transfers between devices with their start and end apart: 10 -> 10, of which waited for: 6 -> 5; matrix products, arithmetic and copies ran while one was open for 0% -> 0% of each run, Pallas kernels for 5% -> 9%
where the time goes in v6:
time: 128 us; the launch traced here: 127 us
  blocking collectives  51 us (40%)
  starting transfers between devices  39.2 us (31%)
  Pallas kernels  17.6 us (14%)
  waiting for transfers between devices  17.6 us (14%)
    ppermute x9, starting transfers between devices, hop(): return lax.ppermute(x, 'field', pairs)  34.7 us
    all_gather x1, blocking collectives, shards(): gathered = lax.all_gather(own, 'field', axis_index_groups=like_cores)  28.6 us
    all_to_all x1, blocking collectives, shards(): lax.all_to_all(outgoing, 'wave', split_axis=0, concat_axis=0, tiled=True)  22.4 us
    all_to_all x1, waiting for transfers between devices, shards(): lax.all_to_all(sent, 'wave', split_axis=0, concat_axis=0, tiled=True)  9.57 us
    ppermute x9, waiting for transfers between devices, hop(): return lax.ppermute(x, 'field', pairs)  8.02 us
    pallas_call x1, Pallas kernels, shards(): local(fourier_kernel, (jax.ShapeDtypeStruct((row_count, levels, LONPAD),...  7.23 us
    all_to_all x1, starting transfers between devices, shards(): lax.all_to_all(sent, 'wave', split_axis=0, concat_axis=0, tiled=True)  4.57 us
    pallas_call x1, Pallas kernels, shards(): local(functools.partial(fourier_tables_kernel, fields=fields, zs=zs), [pl...  4.22 us
  transfers between devices with their start and end apart: 10, of which 5 were waited for; matrix products, arithmetic and copies ran while one was open for 0% of the time, Pallas kernels for 9%

profile of v6, /device:TPU:1, one launch (start us, length us, event | category | flops | bytes accessed | tf_op | source)
XLA Modules:
  0.0 127.3 jit_solution(1166000702717536417)
XLA Ops:
  0.6 0.9 all_gather_reshape.3
  1.6 28.6 %all_gather.3.gathered = bf16[8,96,640]{2,1,0:T(8,128)(2,1)S(1)} all-gather(bf16[1,96,640]{2,1,0:T(8,128)(2,1)S(1)} %all_gather_reshape.3), channel_id=1, replica_groups={{0,2,4,6,8,10,12,14},{15,13,11,9,7,5,3,1},{16,18,20,22,24,26,28,30},{31..., dimensions={0}, use_global_device_ids=true | all-gather | bytes 1105920 | tf_op jit(solution)/shard_map/all_gather | solution.py:364
  30.2 7.7 %collective-permute-start = (bf16[8,96,640]{2,1,0:T(8,128)(2,1)S(1)}, bf16[8,96,640]{2,1,0:T(8,128)(2,1)S(1)}, u32[]{:S(2)}, u32[]{:S(2)}) collective-permute-start(bf16[8,96,640]{2,1,0:T(8,128)(2,1)S(1)} %all_gather.3.gathered), channel_id=1, source_target_pairs={{0,1},{1,0},{2,3},{3,2},{4,5},{5,4},{6,7},{7,6},{8,9},{9,8},{10,11... | collective-permute-start | bytes 2949128 | tf_op jit(solution)/shard_map/ppermute | solution.py:340
  38.0 1.9 %own_rows.1 = (bf16[12,96,640]{2,1,0:T(8,128)(2,1)S(1)}, bf16[96,128]{1,0:T(8,128)(2,1)S(1)}, f32[96,128]{1,0:T(8,128)S(1)}, f32[16,640]{1,0:T(8,128)S(1)}) custom-call(s32[1]{0:T(128)} %bitcast.2.wave_id, s32[1]{0:T(128)} %bitcast.3.field_id, s32[384]{0:T(512)} %wave_of_slot.1, s32[1536]{0:T(1024)} %lat_of_row.3, bf16[12,48,640]{2,1,0:T(8,128)(2,1)} %bitcast.7), custom_call_target="tpu_custom_call" | custom-call | bytes 7400000 | tf_op jit(solution)/shard_map/own_rows/pallas_call | solution.py:367
  40.1 0.9 legendre_forward.1
  41.0 4.2 %fourier_tables.1 = (bf16[3,256,768]{2,1,0:T(8,128)(2,1)}, bf16[3,768,256]{2,1,0:T(8,128)(2,1)}, f32[3,16,768]{2,1,0:T(8,128)}, f32[3,16,768]{2,1,0:T(8,128)}, b...) custom-call(s32[1]{0:T(128)} %bitcast.2.wave_id, s32[1]{0:T(128)} %bitcast.3.field_id, s32[1536]{0:T(1024)S(1)} %copy-done, ...), custom_call_target="tpu_custom_call" | custom-call | bytes 14800000 | tf_op jit(solution)/shard_map/fourier_tables/pallas_call | solution.py:401
  45.3 2.3 %collective-permute-start.1 = (bf16[12,48,640]{2,1,0:T(8,128)(2,1)S(1)}, bf16[12,48,640]{2,1,0:T(8,128)(2,1)S(1)}, u32[]{:S(2)}, u32[]{:S(2)}) collective-permute-start(bf16[12,48,640]{2,1,0:T(8,128)(2,1)S(1)} %bitcast.8), channel_id=1, source_target_pairs={{0,1},{1,0},{2,3},{3,2},{4,5},{5,4},{6,7},{7,6},{8,9},{9,8},{10,11... | collective-permute-start | bytes 2211848 | tf_op jit(solution)/shard_map/ppermute | solution.py:340
  47.6 22.4 %all_to_all.10.arrived = bf16[32,36,128]{2,1,0:T(8,128)(2,1)S(1)} all-to-all(bf16[32,36,128]{2,1,0:T(8,128)(2,1)S(1)} %legendre_forward.1), channel_id=1, replica_groups=mesh['wave'=32,'field'=16] {'wave'}, dimensions={0} | all-to-all | bytes 589824 | tf_op jit(solution)/shard_map/all_to_all | solution.py:391
  70.0 7.2 %fourier.1 = (bf16[3,64,3200]{2,1,0:T(8,128)(2,1)}, bf16[32,36,128]{2,1,0:T(8,128)(2,1)}) custom-call(bf16[32,36,128]{2,1,0:T(8,128)(2,1)S(1)} %all_to_all.10.arrived, bf16[3,256,768]{2,1,0:T(8,128)(2,1)} %get-tuple-element.63.inner_in, bf16[3,768,256]{2,1,0:T(8,128)(2,1)} %get-tuple-element.64.inner_t_in, f32[3,16,768]{2,1,0:T(8,128)} %get-tuple-element.65.outer_fwd_in, ...), custom_call_target="tpu_custom_call" | custom-call | bytes 22200000 | tf_op jit(solution)/shard_map/fourier/pallas_call | solution.py:419
  77.3 4.6 %all-to-all-start.1 = ((bf16[32,36,128]{2,1,0:T(8,128)(2,1)}), bf16[32,36,128]{2,1,0:T(8,128)(2,1)S(1)}, u32[]{:S(2)}, u32[]{:S(2)}) async-start(bf16[32,36,128]{2,1,0:T(8,128)(2,1)} %get-tuple-element.72), calls=%async_computation.1 | async-start | bytes 655360 | tf_op jit(solution)/shard_map/all_to_all | solution.py:439
  81.8 1.7 %partner_rows.1.table_swapped = bf16[12,96,640]{2,1,0:T(8,128)(2,1)S(1)} custom-call(bf16[96,128]{1,0:T(8,128)(2,1)S(1)} %get-tuple-element.73.chosen, f32[96,128]{1,0:T(8,128)S(1)} %get-tuple-element.74.south, f32[16,640]{1,0:T(8,128)S(1)} %get-tuple-element.75.live, bf16[12,48,640]{2,1,0:T(8,128)(2,1)} %copy-done.4), custom_call_target="tpu_custom_call" | custom-call | bytes 7400000 | tf_op jit(solution)/shard_map/partner_rows/pallas_call | solution.py:441
  83.5 9.6 %all-to-all-done.1.arrived = bf16[32,36,128]{2,1,0:T(8,128)(2,1)S(1)} async-done(((bf16[32,36,128]{2,1,0:T(8,128)(2,1)}), bf16[32,36,128]{2,1,0:T(8,128)(2,1)S(1)}, u32[]{:S(2)}, u32[]{:S(2)}) %all-to-all-start.1) | async-done | bytes 294944 | tf_op jit(solution)/shard_map/all_to_all | solution.py:439
  93.1 5.6 %collective-permute-start.2 = (bf16[32,36,128]{2,1,0:T(8,128)(2,1)S(1)}, bf16[32,36,128]{2,1,0:T(8,128)(2,1)S(1)}, u32[]{:S(2)}, u32[]{:S(2)}) collective-permute-start(bf16[32,36,128]{2,1,0:T(8,128)(2,1)S(1)} %all-to-all-done.1.arrived), channel_id=1, source_target_pairs={{0,1},{1,0},{2,3},{3,2},{4,5},{5,4},{6,7},{7,6},{8,9},{9,8},{10,11... | collective-permute-start | bytes 884744 | tf_op jit(solution)/shard_map/ppermute | solution.py:340
  98.6 1.2 collective-permute-done.2.swapped
  99.9 0.9 legendre_inverse.1
  100.8 3.1 %collective-permute-start.5 = (bf16[2,96,640]{2,1,0:T(8,128)(2,1)S(1)}, bf16[2,96,640]{2,1,0:T(8,128)(2,1)S(1)}, u32[]{:S(2)}, u32[]{:S(2)}) collective-permute-start(bf16[2,96,640]{2,1,0:T(8,128)(2,1)S(1)} %get-tuple-element.84), channel_id=1, source_target_pairs={{0,14},{1,3},{2,0},{3,5},{4,2},{5,7},{6,4},{7,9},{8,6},{9,11},{10,... | collective-permute-start | bytes 737288 | tf_op jit(solution)/shard_map/ppermute | solution.py:340
  103.9 2.3 %collective-permute-start.6 = (bf16[96,640]{1,0:T(8,128)(2,1)S(1)}, bf16[96,640]{1,0:T(8,128)(2,1)S(1)}, u32[]{:S(2)}, u32[]{:S(2)}) collective-permute-start(bf16[96,640]{1,0:T(8,128)(2,1)S(1)} %get-tuple-element.85), channel_id=1, source_target_pairs={{0,12},{1,5},{2,14},{3,7},{4,0},{5,9},{6,2},{7,11},{8,4},{9,13},{1... | collective-permute-start | bytes 368648 | tf_op jit(solution)/shard_map/ppermute | solution.py:340
  106.2 3.3 %collective-permute-start.3 = (bf16[96,640]{1,0:T(8,128)(2,1)S(1)}, bf16[96,640]{1,0:T(8,128)(2,1)S(1)}, u32[]{:S(2)}, u32[]{:S(2)}) collective-permute-start(bf16[96,640]{1,0:T(8,128)(2,1)S(1)} %get-tuple-element.80), channel_id=1, source_target_pairs={{0,14},{1,3},{2,0},{3,5},{4,2},{5,7},{6,4},{7,9},{8,6},{9,11},{10,... | collective-permute-start | bytes 368648 | tf_op jit(solution)/shard_map/ppermute | solution.py:340
  109.5 3.9 %collective-permute-start.4 = (bf16[96,640]{1,0:T(8,128)(2,1)S(1)}, bf16[96,640]{1,0:T(8,128)(2,1)S(1)}, u32[]{:S(2)}, u32[]{:S(2)}) collective-permute-start(bf16[96,640]{1,0:T(8,128)(2,1)S(1)} %get-tuple-element.81), channel_id=1, source_target_pairs={{0,15},{1,2},{2,1},{3,4},{4,3},{5,6},{6,5},{7,8},{8,7},{9,10},{10,... | collective-permute-start | bytes 368648 | tf_op jit(solution)/shard_map/ppermute | solution.py:340
  113.5 4.3 %collective-permute-start.7 = (bf16[96,640]{1,0:T(8,128)(2,1)S(1)}, bf16[96,640]{1,0:T(8,128)(2,1)S(1)}, u32[]{:S(2)}, u32[]{:S(2)}) collective-permute-start(bf16[96,640]{1,0:T(8,128)(2,1)S(1)} %get-tuple-element.86), channel_id=1, source_target_pairs={{0,12},{1,5},{2,14},{3,7},{4,0},{5,9},{6,2},{7,11},{8,4},{9,13},{1... | collective-permute-start | bytes 368648 | tf_op jit(solution)/shard_map/ppermute | solution.py:340
  117.8 2.2 %collective-permute-start.8 = (bf16[96,640]{1,0:T(8,128)(2,1)S(1)}, bf16[96,640]{1,0:T(8,128)(2,1)S(1)}, u32[]{:S(2)}, u32[]{:S(2)}) collective-permute-start(bf16[96,640]{1,0:T(8,128)(2,1)S(1)} %get-tuple-element.87), channel_id=1, source_target_pairs={{0,13},{1,4},{2,15},{3,6},{4,1},{5,8},{6,3},{7,10},{8,5},{9,12},{1... | collective-permute-start | bytes 368648 | tf_op jit(solution)/shard_map/ppermute | solution.py:340
  120.0 1.3 %collective-permute-done.7.two = bf16[96,640]{1,0:T(8,128)(2,1)S(1)} collective-permute-done((bf16[96,640]{1,0:T(8,128)(2,1)S(1)}, bf16[96,640]{1,0:T(8,128)(2,1)S(1)}, u32[]{:S(2)}, u32[]{:S(2)}) %collective-permute-start.7) | collective-permute-done | bytes 122912 | tf_op jit(solution)/shard_map/ppermute | solution.py:340
  121.4 5.2 %collective-permute-done.8.two_x = bf16[96,640]{1,0:T(8,128)(2,1)S(1)} collective-permute-done((bf16[96,640]{1,0:T(8,128)(2,1)S(1)}, bf16[96,640]{1,0:T(8,128)(2,1)S(1)}, u32[]{:S(2)}, u32[]{:S(2)}) %collective-permute-start.8) | collective-permute-done | bytes 122912 | tf_op jit(solution)/shard_map/ppermute | solution.py:340
  126.5 0.8 add_own.1
  (21 shorter events, 0.4 us)
Async XLA Ops:
  0.6 37.3 %copy-start.5 = (s32[384]{0:T(512)S(1)}, s32[384]{0:T(512)}, u32[]{:S(2)}) copy-start(s32[384]{0:T(512)} %wave_of_slot.1) | copy-start | bytes 4612
  30.2 9.9 %collective-permute-start = (bf16[8,96,640]{2,1,0:T(8,128)(2,1)S(1)}, bf16[8,96,640]{2,1,0:T(8,128)(2,1)S(1)}, u32[]{:S(2)}, u32[]{:S(2)}) collective-permute-start(bf16[8,96,640]{2,1,0:T(8,128)(2,1)S(1)} %all_gather.3.gathered), channel_id=1, source_target_pairs={{0,1},{1,0},{2,3},{3,2},{4,5},{5,4},{6,7},{7,6},{8,9},{9,8},{10,11... | collective-permute-start | bytes 2949128 | tf_op jit(solution)/shard_map/ppermute | solution.py:340
  40.1 0.9 copy-start
  40.1 0.9 copy-start.1
  40.1 0.9 copy-start.2
  40.1 5.1 %copy-start.3 = (bf16[12,640,48]{1,2,0:T(8,128)(2,1)S(1)}, bf16[12,640,48]{1,2,0:T(8,128)(2,1)}, u32[]{:S(2)}) copy-start(bf16[12,640,48]{1,2,0:T(8,128)(2,1)} %param.7) | copy-start | bytes 2211844
  45.3 32.0 %collective-permute-start.1 = (bf16[12,48,640]{2,1,0:T(8,128)(2,1)S(1)}, bf16[12,48,640]{2,1,0:T(8,128)(2,1)S(1)}, u32[]{:S(2)}, u32[]{:S(2)}) collective-permute-start(bf16[12,48,640]{2,1,0:T(8,128)(2,1)S(1)} %bitcast.8), channel_id=1, source_target_pairs={{0,1},{1,0},{2,3},{3,2},{4,5},{5,4},{6,7},{7,6},{8,9},{9,8},{10,11... | collective-permute-start | bytes 2211848 | tf_op jit(solution)/shard_map/ppermute | solution.py:340
  77.2 4.6 %copy-start.4 = (bf16[12,48,640]{2,1,0:T(8,128)(2,1)}, bf16[12,48,640]{2,1,0:T(8,128)(2,1)S(1)}, u32[]{:S(2)}) copy-start(bf16[12,48,640]{2,1,0:T(8,128)(2,1)S(1)} %collective-permute-done.1.legendre) | copy-start | bytes 2211844
  77.3 15.8 %all-to-all-start.1 = ((bf16[32,36,128]{2,1,0:T(8,128)(2,1)}), bf16[32,36,128]{2,1,0:T(8,128)(2,1)S(1)}, u32[]{:S(2)}, u32[]{:S(2)}) async-start(bf16[32,36,128]{2,1,0:T(8,128)(2,1)} %get-tuple-element.72), calls=%async_computation.1 | async-start | bytes 655360 | tf_op jit(solution)/shard_map/all_to_all | solution.py:439
  93.1 6.8 %collective-permute-start.2 = (bf16[32,36,128]{2,1,0:T(8,128)(2,1)S(1)}, bf16[32,36,128]{2,1,0:T(8,128)(2,1)S(1)}, u32[]{:S(2)}, u32[]{:S(2)}) collective-permute-start(bf16[32,36,128]{2,1,0:T(8,128)(2,1)S(1)} %all-to-all-done.1.arrived), channel_id=1, source_target_pairs={{0,1},{1,0},{2,3},{3,2},{4,5},{5,4},{6,7},{7,6},{8,9},{9,8},{10,11... | collective-permute-start | bytes 884744 | tf_op jit(solution)/shard_map/ppermute | solution.py:340
  100.8 12.6 %collective-permute-start.5 = (bf16[2,96,640]{2,1,0:T(8,128)(2,1)S(1)}, bf16[2,96,640]{2,1,0:T(8,128)(2,1)S(1)}, u32[]{:S(2)}, u32[]{:S(2)}) collective-permute-start(bf16[2,96,640]{2,1,0:T(8,128)(2,1)S(1)} %get-tuple-element.84), channel_id=1, source_target_pairs={{0,14},{1,3},{2,0},{3,5},{4,2},{5,7},{6,4},{7,9},{8,6},{9,11},{10,... | collective-permute-start | bytes 737288 | tf_op jit(solution)/shard_map/ppermute | solution.py:340
  103.9 9.5 %collective-permute-start.6 = (bf16[96,640]{1,0:T(8,128)(2,1)S(1)}, bf16[96,640]{1,0:T(8,128)(2,1)S(1)}, u32[]{:S(2)}, u32[]{:S(2)}) collective-permute-start(bf16[96,640]{1,0:T(8,128)(2,1)S(1)} %get-tuple-element.85), channel_id=1, source_target_pairs={{0,12},{1,5},{2,14},{3,7},{4,0},{5,9},{6,2},{7,11},{8,4},{9,13},{1... | collective-permute-start | bytes 368648 | tf_op jit(solution)/shard_map/ppermute | solution.py:340
  106.2 13.8 %collective-permute-start.3 = (bf16[96,640]{1,0:T(8,128)(2,1)S(1)}, bf16[96,640]{1,0:T(8,128)(2,1)S(1)}, u32[]{:S(2)}, u32[]{:S(2)}) collective-permute-start(bf16[96,640]{1,0:T(8,128)(2,1)S(1)} %get-tuple-element.80), channel_id=1, source_target_pairs={{0,14},{1,3},{2,0},{3,5},{4,2},{5,7},{6,4},{7,9},{8,6},{9,11},{10,... | collective-permute-start | bytes 368648 | tf_op jit(solution)/shard_map/ppermute | solution.py:340
  109.5 10.5 %collective-permute-start.4 = (bf16[96,640]{1,0:T(8,128)(2,1)S(1)}, bf16[96,640]{1,0:T(8,128)(2,1)S(1)}, u32[]{:S(2)}, u32[]{:S(2)}) collective-permute-start(bf16[96,640]{1,0:T(8,128)(2,1)S(1)} %get-tuple-element.81), channel_id=1, source_target_pairs={{0,15},{1,2},{2,1},{3,4},{4,3},{5,6},{6,5},{7,8},{8,7},{9,10},{10,... | collective-permute-start | bytes 368648 | tf_op jit(solution)/shard_map/ppermute | solution.py:340
  113.5 7.8 %collective-permute-start.7 = (bf16[96,640]{1,0:T(8,128)(2,1)S(1)}, bf16[96,640]{1,0:T(8,128)(2,1)S(1)}, u32[]{:S(2)}, u32[]{:S(2)}) collective-permute-start(bf16[96,640]{1,0:T(8,128)(2,1)S(1)} %get-tuple-element.86), channel_id=1, source_target_pairs={{0,12},{1,5},{2,14},{3,7},{4,0},{5,9},{6,2},{7,11},{8,4},{9,13},{1... | collective-permute-start | bytes 368648 | tf_op jit(solution)/shard_map/ppermute | solution.py:340
  117.8 8.7 %collective-permute-start.8 = (bf16[96,640]{1,0:T(8,128)(2,1)S(1)}, bf16[96,640]{1,0:T(8,128)(2,1)S(1)}, u32[]{:S(2)}, u32[]{:S(2)}) collective-permute-start(bf16[96,640]{1,0:T(8,128)(2,1)S(1)} %get-tuple-element.87), channel_id=1, source_target_pairs={{0,13},{1,4},{2,15},{3,6},{4,1},{5,8},{6,3},{7,10},{8,5},{9,12},{1... | collective-permute-start | bytes 368648 | tf_op jit(solution)/shard_map/ppermute | solution.py:340

commit v7 on v6

--- a/solution.py
+++ b/solution.py
@@ -173,6 +173,20 @@
         copy.wait()
 
 
+def unpack_lines(messages, held, each):
+    for at in range(messages.shape[0]):
+        message = messages[at].astype(jnp.float32)
+        for group in range(each // 4):
+            first = at * each + 4 * group
+            held[first : first + 4, :] = message[:, group * LANES : (group + 1) * LANES]
+
+
+def pack_lines(held, messages, each):
+    for at in range(messages.shape[0]):
+        groups = [held[at * each + 4 * group : at * each + 4 * group + 4, :] for group in range(each // 4)]
+        messages[at] = jnp.concatenate(groups, axis=1).astype(jnp.bfloat16)
+
+
 def legendre_forward_kernel(gathered, gathered_x, table, out, held):
     slots, rows, degrees = table.shape
     waves = out.shape[0]
@@ -189,8 +203,7 @@
                 held[pl.ds(slot * row_count + member, waves, stride=each), :] = sums[
                     waves * member : waves * (member + 1)
                 ]
-    for wave in range(waves):
-        out[wave] = held[wave * each : (wave + 1) * each, :].astype(jnp.bfloat16)
+    pack_lines(held, out, each)
 
 
 def legendre_inverse_kernel(
@@ -200,20 +213,21 @@
     waves = arrived.shape[0]
     row_count = rows // waves
     each = slots * row_count
-    for wave in range(waves):
-        held[wave * each : (wave + 1) * each, :] = arrived[wave].astype(jnp.float32)
-        held_swapped[wave * each : (wave + 1) * each, :] = pltpu.roll(swapped[wave].astype(jnp.float32), 64, 1)
-
-    def share(ref, slot, legendre):
+    unpack_lines(arrived, held, each)
+    unpack_lines(swapped, held_swapped, each)
+
+    def share(ref, slot, legendre, turn=0):
         weighted = jnp.concatenate(
             [ref[pl.ds(slot * row_count + member, waves, stride=each), :] for member in range(row_count)], axis=0
         )
+        if turn:
+            weighted = pltpu.roll(weighted, turn, 1)
         return dot(weighted[:, :64].astype(jnp.bfloat16), legendre[slot], TN)
 
     for pair in range(slots // 2):
         at = pl.ds(16 * pair, 16)
         sums = [
-            share(held, slot, table) + share(held_swapped, slot, table_swapped) for slot in (2 * pair, 2 * pair + 1)
+            share(held, slot, table) + share(held_swapped, slot, table_swapped, 64) for slot in (2 * pair, 2 * pair + 1)
         ]
         pieces = [jnp.concatenate([s[8 * chunk : 8 * chunk + 8] for s in sums], axis=0) for chunk in range(8)]
         own[at, :] = pieces[0]
@@ -235,12 +249,11 @@
     for copy in copies:
         copy.start()
     row_count = inner.shape[0]
-    waves, each, _ = arrived.shape
-    slots = waves * each // row_count
+    slots = held.shape[0] // row_count
+    each = held.shape[0] // arrived.shape[0]
     parts = slots // LANES
     levels = grid_out.shape[1]
-    for source in range(waves):
-        held[source * each : (source + 1) * each, :] = arrived[source].astype(jnp.float32)
+    unpack_lines(arrived, held, each)
     for copy in copies[:3]:
         copy.wait()
     column = lax.broadcasted_iota(jnp.int32, (1, BLOCK), 1).astype(jnp.float32)
@@ -294,8 +307,7 @@
         back[pl.ds(member, slots, stride=row_count), :] = dot(
             analysed.T.astype(jnp.bfloat16), place[1], NN
         )
-    for source in range(waves):
-        sent[source] = back[source * each : (source + 1) * each, :].astype(jnp.bfloat16)
+    pack_lines(back, sent, each)
     for result in results:
         result.wait()
 
@@ -357,7 +369,7 @@
         )
 
     row_table = jax.ShapeDtypeStruct((slots, rows, degrees), jnp.bfloat16)
-    fourier_shape = jax.ShapeDtypeStruct((waves, each, LANES), jnp.bfloat16)
+    fourier_shape = jax.ShapeDtypeStruct((waves, 4, each // 4 * LANES), jnp.bfloat16)
     float_rows = pltpu.VMEM((waves * each, LANES), jnp.float32)
 
     own = jnp.transpose(spectra, (0, 1, 3, 2)).reshape(coded, degrees)
@@ -411,8 +423,6 @@
         wave_id, field_id, lat_of_row, lon_count, lat_weight,
         wave_of_slot.astype(jnp.float32).reshape(1, all_slots),
     )
-    prepared, legendre = lax.optimization_barrier((prepared, legendre))
-    legendre_x = swap(legendre)
     arrived, prepared = lax.optimization_barrier((arrived, prepared))
     prepared = [in_hbm(x) for x in prepared]
 
@@ -435,8 +445,9 @@
         ],
     )(arrived, *prepared)
 
-    sent, legendre_x = lax.optimization_barrier((sent, legendre_x))
+    sent, legendre = lax.optimization_barrier((sent, legendre))
     returned = lax.all_to_all(sent, "wave", split_axis=0, concat_axis=0, tiled=True)
+    legendre_x = swap(legendre)
 
     table_x = local(
         partner_rows_kernel,

time: 128 us -> 125 us (0.977)
  blocking collectives: 51 us -> 28.6 us
  waiting for transfers between devices: 17.6 us -> 27.2 us
  starting transfers between devices: 39.2 us -> 47.7 us
    all_to_all x1 -> x0, blocking collectives: 22.4 us -> none  [shards(): lax.all_to_all(outgoing, 'wave', split_axis=0, concat_axis=0, tiled=True)]
    all_to_all x0 -> x1, starting transfers between devices: none -> 9.67 us  [shards(): lax.all_to_all(outgoing, 'wave', split_axis=0, concat_axis=0, tiled=True)]
    all_to_all x0 -> x1, waiting for transfers between devices: none -> 8.37 us  [shards(): lax.all_to_all(outgoing, 'wave', split_axis=0, concat_axis=0, tiled=True)]
    all_to_all x1, waiting for transfers between devices: 9.57 us -> 11.1 us  [shards(): lax.all_to_all(sent, 'wave', split_axis=0, concat_axis=0, tiled=True)]
  transfers between devices with their start and end apart: 10 -> 11, of which waited for: 5 -> 5; matrix products, arithmetic and copies ran while one was open for 0% -> 0% of each run, Pallas kernels for 9% -> 6%
where the time goes in v7:
time: 125 us; the launch traced here: 124 us
  starting transfers between devices  47.7 us (38%)
  blocking collectives  28.6 us (23%)
  waiting for transfers between devices  27.2 us (22%)
  Pallas kernels  18.3 us (15%)
  local copies, waits for them, and re-layouts  1.55 us (1%)
    ppermute x9, starting transfers between devices, hop(): return lax.ppermute(x, 'field', pairs)  34.2 us
    all_gather x1, blocking collectives, shards(): gathered = lax.all_gather(own, 'field', axis_index_groups=like_cores)  28.6 us
    all_to_all x1, waiting for transfers between devices, shards(): lax.all_to_all(sent, 'wave', split_axis=0, concat_axis=0, tiled=True)  11.1 us
    all_to_all x1, starting transfers between devices, shards(): lax.all_to_all(outgoing, 'wave', split_axis=0, concat_axis=0, tiled=True)  9.67 us
    all_to_all x1, waiting for transfers between devices, shards(): lax.all_to_all(outgoing, 'wave', split_axis=0, concat_axis=0, tiled=True)  8.37 us
    ppermute x9, waiting for transfers between devices, hop(): return lax.ppermute(x, 'field', pairs)  7.73 us
    pallas_call x1, Pallas kernels, shards(): local(fourier_kernel, (jax.ShapeDtypeStruct((row_count, levels, LONPAD),...  7.29 us
    pallas_call x1, Pallas kernels, shards(): local(functools.partial(fourier_tables_kernel, fields=fields, zs=zs), [pl...  4.22 us
  transfers between devices with their start and end apart: 11, of which 5 were waited for; matrix products, arithmetic and copies ran while one was open for 0% of the time, Pallas kernels for 6%

profile of v7, /device:TPU:1, one launch (start us, length us, event | category | flops | bytes accessed | tf_op | source)
XLA Modules:
  0.0 124.3 jit_solution(1695683221161507767)
XLA Ops:
  0.6 0.9 all_gather_reshape.3
  1.6 28.6 %all_gather.3.gathered = bf16[8,96,640]{2,1,0:T(8,128)(2,1)S(1)} all-gather(bf16[1,96,640]{2,1,0:T(8,128)(2,1)S(1)} %all_gather_reshape.3), channel_id=1, replica_groups={{0,2,4,6,8,10,12,14},{15,13,11,9,7,5,3,1},{16,18,20,22,24,26,28,30},{31..., dimensions={0}, use_global_device_ids=true | all-gather | bytes 1105920 | tf_op jit(solution)/shard_map/all_gather | solution.py:376
  30.2 7.7 %collective-permute-start = (bf16[8,96,640]{2,1,0:T(8,128)(2,1)S(1)}, bf16[8,96,640]{2,1,0:T(8,128)(2,1)S(1)}, u32[]{:S(2)}, u32[]{:S(2)}) collective-permute-start(bf16[8,96,640]{2,1,0:T(8,128)(2,1)S(1)} %all_gather.3.gathered), channel_id=1, source_target_pairs={{0,1},{1,0},{2,3},{3,2},{4,5},{5,4},{6,7},{7,6},{8,9},{9,8},{10,11... | collective-permute-start | bytes 2949128 | tf_op jit(solution)/shard_map/ppermute | solution.py:352
  37.9 1.9 %own_rows.1 = (bf16[12,96,640]{2,1,0:T(8,128)(2,1)S(1)}, bf16[96,128]{1,0:T(8,128)(2,1)S(1)}, f32[96,128]{1,0:T(8,128)S(1)}, f32[16,640]{1,0:T(8,128)S(1)}) custom-call(s32[1]{0:T(128)} %bitcast.2.wave_id, s32[1]{0:T(128)} %bitcast.3.field_id, s32[384]{0:T(512)} %wave_of_slot.1, s32[1536]{0:T(1024)} %lat_of_row.3, bf16[12,48,640]{2,1,0:T(8,128)(2,1)} %bitcast.7), custom_call_target="tpu_custom_call" | custom-call | bytes 7400000 | tf_op jit(solution)/shard_map/own_rows/pallas_call | solution.py:379
  40.4 1.6 %legendre_forward.1 = bf16[32,4,1152]{2,1,0:T(4,128)(2,1)} custom-call(bf16[8,96,640]{2,1,0:T(8,128)(2,1)S(1)} %all_gather.3.gathered, bf16[8,96,640]{2,1,0:T(8,128)(2,1)S(1)} %collective-permute-done.gathered_x, bf16[12,96,640]{2,1,0:T(8,128)(2,1)S(1)} %get-tuple-element.40.table), custom_call_target="tpu_custom_call" | custom-call | bytes 14800000 | tf_op jit(solution)/shard_map/legendre_forward/pallas_call | solution.py:399
  42.0 9.7 %all-to-all-start = ((bf16[32,4,1152]{2,1,0:T(4,128)(2,1)}), bf16[32,4,1152]{2,1,0:T(4,128)(2,1)S(1)}, u32[]{:S(2)}, u32[]{:S(2)}) async-start(bf16[32,4,1152]{2,1,0:T(4,128)(2,1)} %legendre_forward.1), calls=%async_computation | async-start | bytes 589824 | tf_op jit(solution)/shard_map/all_to_all | solution.py:403
  51.8 4.2 %fourier_tables.1 = (bf16[3,256,768]{2,1,0:T(8,128)(2,1)}, bf16[3,768,256]{2,1,0:T(8,128)(2,1)}, f32[3,16,768]{2,1,0:T(8,128)}, f32[3,16,768]{2,1,0:T(8,128)}, b...) custom-call(s32[1]{0:T(128)} %bitcast.2.wave_id, s32[1]{0:T(128)} %bitcast.3.field_id, s32[1536]{0:T(1024)S(1)} %copy-done, ...), custom_call_target="tpu_custom_call" | custom-call | bytes 14800000 | tf_op jit(solution)/shard_map/fourier_tables/pallas_call | solution.py:413
  56.0 8.4 %all-to-all-done.arrived = bf16[32,4,1152]{2,1,0:T(4,128)(2,1)S(1)} async-done(((bf16[32,4,1152]{2,1,0:T(4,128)(2,1)}), bf16[32,4,1152]{2,1,0:T(4,128)(2,1)S(1)}, u32[]{:S(2)}, u32[]{:S(2)}) %all-to-all-start) | async-done | bytes 294944 | tf_op jit(solution)/shard_map/all_to_all | solution.py:403
  64.4 7.3 %fourier.1 = (bf16[3,64,3200]{2,1,0:T(8,128)(2,1)}, bf16[32,4,1152]{2,1,0:T(4,128)(2,1)}) custom-call(bf16[32,4,1152]{2,1,0:T(4,128)(2,1)S(1)} %all-to-all-done.arrived, bf16[3,256,768]{2,1,0:T(8,128)(2,1)} %get-tuple-element.50.inner_in, bf16[3,768,256]{2,1,0:T(8,128)(2,1)} %get-tuple-element.51.inner_t_in, f32[3,16,768]{2,1,0:T(8,128)} %get-tuple-element.52.outer_fwd_in, ...), custom_call_target="tpu_custom_call" | custom-call | bytes 22200000 | tf_op jit(solution)/shard_map/fourier/pallas_call | solution.py:429
  71.7 3.9 %collective-permute-start.1 = (bf16[12,48,640]{2,1,0:T(8,128)(2,1)S(1)}, bf16[12,48,640]{2,1,0:T(8,128)(2,1)}, u32[]{:S(2)}, u32[]{:S(2)}) collective-permute-start(bf16[12,48,640]{2,1,0:T(8,128)(2,1)S(1)} %bitcast.8), channel_id=1, source_target_pairs={{0,1},{1,0},{2,3},{3,2},{4,5},{5,4},{6,7},{7,6},{8,9},{9,8},{10,11... | collective-permute-start | bytes 2211848 | tf_op jit(solution)/shard_map/ppermute | solution.py:352
  75.5 3.9 %all-to-all-start.1 = ((bf16[32,4,1152]{2,1,0:T(4,128)(2,1)}), bf16[32,4,1152]{2,1,0:T(4,128)(2,1)S(1)}, u32[]{:S(2)}, u32[]{:S(2)}) async-start(bf16[32,4,1152]{2,1,0:T(4,128)(2,1)} %get-tuple-element.58), calls=%async_computation.1 | async-start | bytes 589824 | tf_op jit(solution)/shard_map/all_to_all | solution.py:449
  79.5 1.6 %partner_rows.1.table_swapped = bf16[12,96,640]{2,1,0:T(8,128)(2,1)S(1)} custom-call(bf16[96,128]{1,0:T(8,128)(2,1)S(1)} %copy-done.2, f32[96,128]{1,0:T(8,128)S(1)} %get-tuple-element.60.south, f32[16,640]{1,0:T(8,128)S(1)} %get-tuple-element.61.live, bf16[12,48,640]{2,1,0:T(8,128)(2,1)} %collective-permute-done.1.legendre), custom_call_target="tpu_custom_call" | custom-call | bytes 7400000 | tf_op jit(solution)/shard_map/partner_rows/pallas_call | solution.py:452
  81.1 11.1 %all-to-all-done.1.arrived = bf16[32,4,1152]{2,1,0:T(4,128)(2,1)S(1)} async-done(((bf16[32,4,1152]{2,1,0:T(4,128)(2,1)}), bf16[32,4,1152]{2,1,0:T(4,128)(2,1)S(1)}, u32[]{:S(2)}, u32[]{:S(2)}) %all-to-all-start.1) | async-done | bytes 294944 | tf_op jit(solution)/shard_map/all_to_all | solution.py:449
  92.2 3.5 %collective-permute-start.2 = (bf16[32,4,1152]{2,1,0:T(4,128)(2,1)S(1)}, bf16[32,4,1152]{2,1,0:T(4,128)(2,1)S(1)}, u32[]{:S(2)}, u32[]{:S(2)}) collective-permute-start(bf16[32,4,1152]{2,1,0:T(4,128)(2,1)S(1)} %all-to-all-done.1.arrived), channel_id=1, source_target_pairs={{0,1},{1,0},{2,3},{3,2},{4,5},{5,4},{6,7},{7,6},{8,9},{9,8},{10,11... | collective-permute-start | bytes 884744 | tf_op jit(solution)/shard_map/ppermute | solution.py:352
  95.7 1.2 collective-permute-done.2.swapped
  96.9 0.9 legendre_inverse.1
  97.8 3.1 %collective-permute-start.5 = (bf16[2,96,640]{2,1,0:T(8,128)(2,1)S(1)}, bf16[2,96,640]{2,1,0:T(8,128)(2,1)S(1)}, u32[]{:S(2)}, u32[]{:S(2)}) collective-permute-start(bf16[2,96,640]{2,1,0:T(8,128)(2,1)S(1)} %get-tuple-element.70), channel_id=1, source_target_pairs={{0,14},{1,3},{2,0},{3,5},{4,2},{5,7},{6,4},{7,9},{8,6},{9,11},{10,... | collective-permute-start | bytes 737288 | tf_op jit(solution)/shard_map/ppermute | solution.py:352
  100.9 2.3 %collective-permute-start.6 = (bf16[96,640]{1,0:T(8,128)(2,1)S(1)}, bf16[96,640]{1,0:T(8,128)(2,1)S(1)}, u32[]{:S(2)}, u32[]{:S(2)}) collective-permute-start(bf16[96,640]{1,0:T(8,128)(2,1)S(1)} %get-tuple-element.71), channel_id=1, source_target_pairs={{0,12},{1,5},{2,14},{3,7},{4,0},{5,9},{6,2},{7,11},{8,4},{9,13},{1... | collective-permute-start | bytes 368648 | tf_op jit(solution)/shard_map/ppermute | solution.py:352
  103.2 3.3 %collective-permute-start.3 = (bf16[96,640]{1,0:T(8,128)(2,1)S(1)}, bf16[96,640]{1,0:T(8,128)(2,1)S(1)}, u32[]{:S(2)}, u32[]{:S(2)}) collective-permute-start(bf16[96,640]{1,0:T(8,128)(2,1)S(1)} %get-tuple-element.66), channel_id=1, source_target_pairs={{0,14},{1,3},{2,0},{3,5},{4,2},{5,7},{6,4},{7,9},{8,6},{9,11},{10,... | collective-permute-start | bytes 368648 | tf_op jit(solution)/shard_map/ppermute | solution.py:352
  106.6 3.9 %collective-permute-start.4 = (bf16[96,640]{1,0:T(8,128)(2,1)S(1)}, bf16[96,640]{1,0:T(8,128)(2,1)S(1)}, u32[]{:S(2)}, u32[]{:S(2)}) collective-permute-start(bf16[96,640]{1,0:T(8,128)(2,1)S(1)} %get-tuple-element.67), channel_id=1, source_target_pairs={{0,15},{1,2},{2,1},{3,4},{4,3},{5,6},{6,5},{7,8},{8,7},{9,10},{10,... | collective-permute-start | bytes 368648 | tf_op jit(solution)/shard_map/ppermute | solution.py:352
  110.5 4.3 %collective-permute-start.7 = (bf16[96,640]{1,0:T(8,128)(2,1)S(1)}, bf16[96,640]{1,0:T(8,128)(2,1)S(1)}, u32[]{:S(2)}, u32[]{:S(2)}) collective-permute-start(bf16[96,640]{1,0:T(8,128)(2,1)S(1)} %get-tuple-element.72), channel_id=1, source_target_pairs={{0,12},{1,5},{2,14},{3,7},{4,0},{5,9},{6,2},{7,11},{8,4},{9,13},{1... | collective-permute-start | bytes 368648 | tf_op jit(solution)/shard_map/ppermute | solution.py:352
  114.8 2.1 %collective-permute-start.8 = (bf16[96,640]{1,0:T(8,128)(2,1)S(1)}, bf16[96,640]{1,0:T(8,128)(2,1)S(1)}, u32[]{:S(2)}, u32[]{:S(2)}) collective-permute-start(bf16[96,640]{1,0:T(8,128)(2,1)S(1)} %get-tuple-element.73), channel_id=1, source_target_pairs={{0,13},{1,4},{2,15},{3,6},{4,1},{5,8},{6,3},{7,10},{8,5},{9,12},{1... | collective-permute-start | bytes 368648 | tf_op jit(solution)/shard_map/ppermute | solution.py:352
  117.0 1.4 %collective-permute-done.7.two = bf16[96,640]{1,0:T(8,128)(2,1)S(1)} collective-permute-done((bf16[96,640]{1,0:T(8,128)(2,1)S(1)}, bf16[96,640]{1,0:T(8,128)(2,1)S(1)}, u32[]{:S(2)}, u32[]{:S(2)}) %collective-permute-start.7) | collective-permute-done | bytes 122912 | tf_op jit(solution)/shard_map/ppermute | solution.py:352
  118.4 5.2 %collective-permute-done.8.two_x = bf16[96,640]{1,0:T(8,128)(2,1)S(1)} collective-permute-done((bf16[96,640]{1,0:T(8,128)(2,1)S(1)}, bf16[96,640]{1,0:T(8,128)(2,1)S(1)}, u32[]{:S(2)}, u32[]{:S(2)}) %collective-permute-start.8) | collective-permute-done | bytes 122912 | tf_op jit(solution)/shard_map/ppermute | solution.py:352
  (24 shorter events, 1.5 us)
Async XLA Ops:
  30.2 10.2 %collective-permute-start = (bf16[8,96,640]{2,1,0:T(8,128)(2,1)S(1)}, bf16[8,96,640]{2,1,0:T(8,128)(2,1)S(1)}, u32[]{:S(2)}, u32[]{:S(2)}) collective-permute-start(bf16[8,96,640]{2,1,0:T(8,128)(2,1)S(1)} %all_gather.3.gathered), channel_id=1, source_target_pairs={{0,1},{1,0},{2,3},{3,2},{4,5},{5,4},{6,7},{7,6},{8,9},{9,8},{10,11... | collective-permute-start | bytes 2949128 | tf_op jit(solution)/shard_map/ppermute | solution.py:352
  39.8 0.6 copy-start.1
  40.4 11.3 %copy-start.6 = (s32[384]{0:T(512)S(1)}, s32[384]{0:T(512)}, u32[]{:S(2)}) copy-start(s32[384]{0:T(512)} %wave_of_slot.1) | copy-start | bytes 4612
  40.4 11.3 %copy-start = (s32[1536]{0:T(1024)S(1)}, s32[1536]{0:T(1024)}, u32[]{:S(2)}) copy-start(s32[1536]{0:T(1024)} %lat_of_row.3) | copy-start | bytes 18436
  40.4 11.3 %copy-start.3 = (s32[768]{0:T(1024)S(1)}, s32[768]{0:T(1024)}, u32[]{:S(2)}) copy-start(s32[768]{0:T(1024)} %lon_count.1) | copy-start | bytes 9220
  40.4 11.3 %copy-start.4 = (f32[48]{0:T(128)S(1)}, f32[48]{0:T(128)}, u32[]{:S(2)}) copy-start(f32[48]{0:T(128)} %lat_weight) | copy-start | bytes 580
  42.0 22.3 %all-to-all-start = ((bf16[32,4,1152]{2,1,0:T(4,128)(2,1)}), bf16[32,4,1152]{2,1,0:T(4,128)(2,1)S(1)}, u32[]{:S(2)}, u32[]{:S(2)}) async-start(bf16[32,4,1152]{2,1,0:T(4,128)(2,1)} %legendre_forward.1), calls=%async_computation | async-start | bytes 589824 | tf_op jit(solution)/shard_map/all_to_all | solution.py:403
  64.4 7.3 %copy-start.5 = (bf16[12,640,48]{1,2,0:T(8,128)(2,1)S(1)}, bf16[12,640,48]{1,2,0:T(8,128)(2,1)}, u32[]{:S(2)}) copy-start(bf16[12,640,48]{1,2,0:T(8,128)(2,1)} %param.7) | copy-start | bytes 2211844
  64.4 15.1 %copy-start.2 = (bf16[96,128]{1,0:T(8,128)(2,1)S(1)}, bf16[96,128]{1,0:T(8,128)(2,1)}, u32[]{:S(2)}) copy-start(bf16[96,128]{1,0:T(8,128)(2,1)} %copy-done.1) | copy-start | bytes 73732
  71.7 7.8 %collective-permute-start.1 = (bf16[12,48,640]{2,1,0:T(8,128)(2,1)S(1)}, bf16[12,48,640]{2,1,0:T(8,128)(2,1)}, u32[]{:S(2)}, u32[]{:S(2)}) collective-permute-start(bf16[12,48,640]{2,1,0:T(8,128)(2,1)S(1)} %bitcast.8), channel_id=1, source_target_pairs={{0,1},{1,0},{2,3},{3,2},{4,5},{5,4},{6,7},{7,6},{8,9},{9,8},{10,11... | collective-permute-start | bytes 2211848 | tf_op jit(solution)/shard_map/ppermute | solution.py:352
  75.5 16.7 %all-to-all-start.1 = ((bf16[32,4,1152]{2,1,0:T(4,128)(2,1)}), bf16[32,4,1152]{2,1,0:T(4,128)(2,1)S(1)}, u32[]{:S(2)}, u32[]{:S(2)}) async-start(bf16[32,4,1152]{2,1,0:T(4,128)(2,1)} %get-tuple-element.58), calls=%async_computation.1 | async-start | bytes 589824 | tf_op jit(solution)/shard_map/all_to_all | solution.py:449
  92.2 4.7 %collective-permute-start.2 = (bf16[32,4,1152]{2,1,0:T(4,128)(2,1)S(1)}, bf16[32,4,1152]{2,1,0:T(4,128)(2,1)S(1)}, u32[]{:S(2)}, u32[]{:S(2)}) collective-permute-start(bf16[32,4,1152]{2,1,0:T(4,128)(2,1)S(1)} %all-to-all-done.1.arrived), channel_id=1, source_target_pairs={{0,1},{1,0},{2,3},{3,2},{4,5},{5,4},{6,7},{7,6},{8,9},{9,8},{10,11... | collective-permute-start | bytes 884744 | tf_op jit(solution)/shard_map/ppermute | solution.py:352
  97.8 12.6 %collective-permute-start.5 = (bf16[2,96,640]{2,1,0:T(8,128)(2,1)S(1)}, bf16[2,96,640]{2,1,0:T(8,128)(2,1)S(1)}, u32[]{:S(2)}, u32[]{:S(2)}) collective-permute-start(bf16[2,96,640]{2,1,0:T(8,128)(2,1)S(1)} %get-tuple-element.70), channel_id=1, source_target_pairs={{0,14},{1,3},{2,0},{3,5},{4,2},{5,7},{6,4},{7,9},{8,6},{9,11},{10,... | collective-permute-start | bytes 737288 | tf_op jit(solution)/shard_map/ppermute | solution.py:352
  100.9 9.5 %collective-permute-start.6 = (bf16[96,640]{1,0:T(8,128)(2,1)S(1)}, bf16[96,640]{1,0:T(8,128)(2,1)S(1)}, u32[]{:S(2)}, u32[]{:S(2)}) collective-permute-start(bf16[96,640]{1,0:T(8,128)(2,1)S(1)} %get-tuple-element.71), channel_id=1, source_target_pairs={{0,12},{1,5},{2,14},{3,7},{4,0},{5,9},{6,2},{7,11},{8,4},{9,13},{1... | collective-permute-start | bytes 368648 | tf_op jit(solution)/shard_map/ppermute | solution.py:352
  103.2 13.8 %collective-permute-start.3 = (bf16[96,640]{1,0:T(8,128)(2,1)S(1)}, bf16[96,640]{1,0:T(8,128)(2,1)S(1)}, u32[]{:S(2)}, u32[]{:S(2)}) collective-permute-start(bf16[96,640]{1,0:T(8,128)(2,1)S(1)} %get-tuple-element.66), channel_id=1, source_target_pairs={{0,14},{1,3},{2,0},{3,5},{4,2},{5,7},{6,4},{7,9},{8,6},{9,11},{10,... | collective-permute-start | bytes 368648 | tf_op jit(solution)/shard_map/ppermute | solution.py:352
  106.6 10.5 %collective-permute-start.4 = (bf16[96,640]{1,0:T(8,128)(2,1)S(1)}, bf16[96,640]{1,0:T(8,128)(2,1)S(1)}, u32[]{:S(2)}, u32[]{:S(2)}) collective-permute-start(bf16[96,640]{1,0:T(8,128)(2,1)S(1)} %get-tuple-element.67), channel_id=1, source_target_pairs={{0,15},{1,2},{2,1},{3,4},{4,3},{5,6},{6,5},{7,8},{8,7},{9,10},{10,... | collective-permute-start | bytes 368648 | tf_op jit(solution)/shard_map/ppermute | solution.py:352
  110.5 7.8 %collective-permute-start.7 = (bf16[96,640]{1,0:T(8,128)(2,1)S(1)}, bf16[96,640]{1,0:T(8,128)(2,1)S(1)}, u32[]{:S(2)}, u32[]{:S(2)}) collective-permute-start(bf16[96,640]{1,0:T(8,128)(2,1)S(1)} %get-tuple-element.72), channel_id=1, source_target_pairs={{0,12},{1,5},{2,14},{3,7},{4,0},{5,9},{6,2},{7,11},{8,4},{9,13},{1... | collective-permute-start | bytes 368648 | tf_op jit(solution)/shard_map/ppermute | solution.py:352
  114.8 8.7 %collective-permute-start.8 = (bf16[96,640]{1,0:T(8,128)(2,1)S(1)}, bf16[96,640]{1,0:T(8,128)(2,1)S(1)}, u32[]{:S(2)}, u32[]{:S(2)}) collective-permute-start(bf16[96,640]{1,0:T(8,128)(2,1)S(1)} %get-tuple-element.73), channel_id=1, source_target_pairs={{0,13},{1,4},{2,15},{3,6},{4,1},{5,8},{6,3},{7,10},{8,5},{9,12},{1... | collective-permute-start | bytes 368648 | tf_op jit(solution)/shard_map/ppermute | solution.py:352

commit v8 on v7

--- a/solution.py
+++ b/solution.py
@@ -257,9 +257,8 @@
     for copy in copies[:3]:
         copy.wait()
     column = lax.broadcasted_iota(jnp.int32, (1, BLOCK), 1).astype(jnp.float32)
-    results = []
-    for member in range(row_count):
-        points = jnp.concatenate([limits[member, :1, :]] * (BLOCK // LANES), axis=1)
+
+    def rotate(member):
         lines = held[pl.ds(member, slots, stride=row_count), :].astype(jnp.bfloat16)
         coef = dot(place[0], lines, NT)
         for step in range(BLOCKS):
@@ -272,9 +271,12 @@
                 sine = outer_fwd[member, step : step + 1, at + LANES : at + 2 * LANES]
                 turned[member, rows, at : at + LANES] = (real * cosine - imag * sine).astype(jnp.bfloat16)
                 turned[member, rows, at + LANES : at + 2 * LANES] = (real * sine + imag * cosine).astype(jnp.bfloat16)
-        if member == 0:
-            copies[3].wait()
-        values = dot(turned[member], inner_t[member], NN)
+
+    def spread(member):
+        return dot(turned[member], inner_t[member], NN)
+
+    def multiply(member, values):
+        points = jnp.concatenate([limits[member, :1, :]] * (BLOCK // LANES), axis=1)
         for step in range(BLOCKS):
             width = min(BLOCK, LONPAD - step * BLOCK)
             line = values[step * levels : (step + 1) * levels]
@@ -285,28 +287,45 @@
             products[member, step * levels : (step + 1) * levels, :] = (line * partner).astype(jnp.bfloat16)
         result = pltpu.make_async_copy(lines_out.at[member], grid_out.at[member], out_sems.at[member])
         result.start()
-        results.append(result)
-        if member == 0:
-            copies[4].wait()
-            copies[5].wait()
+        return result
+
+    def analyse(member):
+        return dot(products[member], inner[member], NN)
+
+    def collect(member, sums):
         reals, imags = [], []
         for part in range(parts):
             at = part * 2 * LANES
-            sums = dot(products[member], inner[member, :, at : at + 2 * LANES], NN)
             real = jnp.zeros((levels, LANES), jnp.float32)
             imag = jnp.zeros((levels, LANES), jnp.float32)
             for step in range(BLOCKS):
                 rows = slice(step * levels, (step + 1) * levels)
                 cosine = outer_inv[member, step : step + 1, at : at + LANES]
                 sine = outer_inv[member, step : step + 1, at + LANES : at + 2 * LANES]
-                real += sums[rows, :LANES] * cosine + sums[rows, LANES:] * sine
-                imag += sums[rows, LANES:] * cosine - sums[rows, :LANES] * sine
+                even, odd = sums[rows, at : at + LANES], sums[rows, at + LANES : at + 2 * LANES]
+                real += even * cosine + odd * sine
+                imag += odd * cosine - even * sine
             reals.append(real)
             imags.append(imag)
         analysed = jnp.concatenate([jnp.concatenate(reals, axis=1), jnp.concatenate(imags, axis=1)], axis=0)
-        back[pl.ds(member, slots, stride=row_count), :] = dot(
-            analysed.T.astype(jnp.bfloat16), place[1], NN
-        )
+        back[pl.ds(member, slots, stride=row_count), :] = dot(analysed.T.astype(jnp.bfloat16), place[1], NN)
+
+    rotate(0)
+    copies[3].wait()
+    copies[4].wait()
+    copies[5].wait()
+    values, sums, results = {0: spread(0)}, {}, []
+    for member in range(row_count):
+        if member + 1 < row_count:
+            rotate(member + 1)
+        if member > 0:
+            sums[member - 1] = analyse(member - 1)
+        results.append(multiply(member, values.pop(member)))
+        if member + 1 < row_count:
+            values[member + 1] = spread(member + 1)
+        if member > 0:
+            collect(member - 1, sums.pop(member - 1))
+    collect(row_count - 1, analyse(row_count - 1))
     pack_lines(back, sent, each)
     for result in results:
         result.wait()

time: 125 us -> 124 us (level)
  no operation moved by 1% of the time
where the time goes in v8:
time: 124 us; the launch traced here: 123 us
  starting transfers between devices  47.7 us (38%)
  blocking collectives  28.6 us (23%)
  waiting for transfers between devices  27.2 us (22%)
  Pallas kernels  17.2 us (14%)
  local copies, waits for them, and re-layouts  1.55 us (1%)
    ppermute x9, starting transfers between devices, hop(): return lax.ppermute(x, 'field', pairs)  34.2 us
    all_gather x1, blocking collectives, shards(): gathered = lax.all_gather(own, 'field', axis_index_groups=like_cores)  28.6 us
    all_to_all x1, waiting for transfers between devices, shards(): lax.all_to_all(sent, 'wave', split_axis=0, concat_axis=0, tiled=True)  11.1 us
    all_to_all x1, starting transfers between devices, shards(): lax.all_to_all(outgoing, 'wave', split_axis=0, concat_axis=0, tiled=True)  9.67 us
    all_to_all x1, waiting for transfers between devices, shards(): lax.all_to_all(outgoing, 'wave', split_axis=0, concat_axis=0, tiled=True)  8.37 us
    ppermute x9, waiting for transfers between devices, hop(): return lax.ppermute(x, 'field', pairs)  7.73 us
    pallas_call x1, Pallas kernels, shards(): local(fourier_kernel, (jax.ShapeDtypeStruct((row_count, levels, LONPAD),...  6.18 us
    pallas_call x1, Pallas kernels, shards(): local(functools.partial(fourier_tables_kernel, fields=fields, zs=zs), [pl...  4.22 us
  transfers between devices with their start and end apart: 11, of which 5 were waited for; matrix products, arithmetic and copies ran while one was open for 0% of the time, Pallas kernels for 6%

profile of v8, /device:TPU:1, one launch (start us, length us, event | category | flops | bytes accessed | tf_op | source)
XLA Modules:
  0.0 123.2 jit_solution(7272854227002229257)
XLA Ops:
  0.6 0.9 all_gather_reshape.3
  1.6 28.6 %all_gather.3.gathered = bf16[8,96,640]{2,1,0:T(8,128)(2,1)S(1)} all-gather(bf16[1,96,640]{2,1,0:T(8,128)(2,1)S(1)} %all_gather_reshape.3), channel_id=1, replica_groups={{0,2,4,6,8,10,12,14},{15,13,11,9,7,5,3,1},{16,18,20,22,24,26,28,30},{31..., dimensions={0}, use_global_device_ids=true | all-gather | bytes 1105920 | tf_op jit(solution)/shard_map/all_gather | solution.py:395
  30.2 7.7 %collective-permute-start = (bf16[8,96,640]{2,1,0:T(8,128)(2,1)S(1)}, bf16[8,96,640]{2,1,0:T(8,128)(2,1)S(1)}, u32[]{:S(2)}, u32[]{:S(2)}) collective-permute-start(bf16[8,96,640]{2,1,0:T(8,128)(2,1)S(1)} %all_gather.3.gathered), channel_id=1, source_target_pairs={{0,1},{1,0},{2,3},{3,2},{4,5},{5,4},{6,7},{7,6},{8,9},{9,8},{10,11... | collective-permute-start | bytes 2949128 | tf_op jit(solution)/shard_map/ppermute | solution.py:371
  37.9 1.9 %own_rows.1 = (bf16[12,96,640]{2,1,0:T(8,128)(2,1)S(1)}, bf16[96,128]{1,0:T(8,128)(2,1)S(1)}, f32[96,128]{1,0:T(8,128)S(1)}, f32[16,640]{1,0:T(8,128)S(1)}) custom-call(s32[1]{0:T(128)} %bitcast.2.wave_id, s32[1]{0:T(128)} %bitcast.3.field_id, s32[384]{0:T(512)} %wave_of_slot.1, s32[1536]{0:T(1024)} %lat_of_row.3, bf16[12,48,640]{2,1,0:T(8,128)(2,1)} %bitcast.7), custom_call_target="tpu_custom_call" | custom-call | bytes 7400000 | tf_op jit(solution)/shard_map/own_rows/pallas_call | solution.py:398
  40.4 1.6 %legendre_forward.1 = bf16[32,4,1152]{2,1,0:T(4,128)(2,1)} custom-call(bf16[8,96,640]{2,1,0:T(8,128)(2,1)S(1)} %all_gather.3.gathered, bf16[8,96,640]{2,1,0:T(8,128)(2,1)S(1)} %collective-permute-done.gathered_x, bf16[12,96,640]{2,1,0:T(8,128)(2,1)S(1)} %get-tuple-element.40.table), custom_call_target="tpu_custom_call" | custom-call | bytes 14800000 | tf_op jit(solution)/shard_map/legendre_forward/pallas_call | solution.py:418
  42.0 9.7 %all-to-all-start = ((bf16[32,4,1152]{2,1,0:T(4,128)(2,1)}), bf16[32,4,1152]{2,1,0:T(4,128)(2,1)S(1)}, u32[]{:S(2)}, u32[]{:S(2)}) async-start(bf16[32,4,1152]{2,1,0:T(4,128)(2,1)} %legendre_forward.1), calls=%async_computation | async-start | bytes 589824 | tf_op jit(solution)/shard_map/all_to_all | solution.py:422
  51.8 4.2 %fourier_tables.1 = (bf16[3,256,768]{2,1,0:T(8,128)(2,1)}, bf16[3,768,256]{2,1,0:T(8,128)(2,1)}, f32[3,16,768]{2,1,0:T(8,128)}, f32[3,16,768]{2,1,0:T(8,128)}, b...) custom-call(s32[1]{0:T(128)} %bitcast.2.wave_id, s32[1]{0:T(128)} %bitcast.3.field_id, s32[1536]{0:T(1024)S(1)} %copy-done, ...), custom_call_target="tpu_custom_call" | custom-call | bytes 14800000 | tf_op jit(solution)/shard_map/fourier_tables/pallas_call | solution.py:432
  56.0 8.4 %all-to-all-done.arrived = bf16[32,4,1152]{2,1,0:T(4,128)(2,1)S(1)} async-done(((bf16[32,4,1152]{2,1,0:T(4,128)(2,1)}), bf16[32,4,1152]{2,1,0:T(4,128)(2,1)S(1)}, u32[]{:S(2)}, u32[]{:S(2)}) %all-to-all-start) | async-done | bytes 294944 | tf_op jit(solution)/shard_map/all_to_all | solution.py:422
  64.4 6.2 %fourier.1 = (bf16[3,64,3200]{2,1,0:T(8,128)(2,1)}, bf16[32,4,1152]{2,1,0:T(4,128)(2,1)}) custom-call(bf16[32,4,1152]{2,1,0:T(4,128)(2,1)S(1)} %all-to-all-done.arrived, bf16[3,256,768]{2,1,0:T(8,128)(2,1)} %get-tuple-element.50.inner_in, bf16[3,768,256]{2,1,0:T(8,128)(2,1)} %get-tuple-element.51.inner_t_in, f32[3,16,768]{2,1,0:T(8,128)} %get-tuple-element.52.outer_fwd_in, ...), custom_call_target="tpu_custom_call" | custom-call | bytes 22200000 | tf_op jit(solution)/shard_map/fourier/pallas_call | solution.py:448
  70.6 3.9 %collective-permute-start.1 = (bf16[12,48,640]{2,1,0:T(8,128)(2,1)S(1)}, bf16[12,48,640]{2,1,0:T(8,128)(2,1)}, u32[]{:S(2)}, u32[]{:S(2)}) collective-permute-start(bf16[12,48,640]{2,1,0:T(8,128)(2,1)S(1)} %bitcast.8), channel_id=1, source_target_pairs={{0,1},{1,0},{2,3},{3,2},{4,5},{5,4},{6,7},{7,6},{8,9},{9,8},{10,11... | collective-permute-start | bytes 2211848 | tf_op jit(solution)/shard_map/ppermute | solution.py:371
  74.4 3.9 %all-to-all-start.1 = ((bf16[32,4,1152]{2,1,0:T(4,128)(2,1)}), bf16[32,4,1152]{2,1,0:T(4,128)(2,1)S(1)}, u32[]{:S(2)}, u32[]{:S(2)}) async-start(bf16[32,4,1152]{2,1,0:T(4,128)(2,1)} %get-tuple-element.58), calls=%async_computation.1 | async-start | bytes 589824 | tf_op jit(solution)/shard_map/all_to_all | solution.py:468
  78.3 1.6 %partner_rows.1.table_swapped = bf16[12,96,640]{2,1,0:T(8,128)(2,1)S(1)} custom-call(bf16[96,128]{1,0:T(8,128)(2,1)S(1)} %copy-done.2, f32[96,128]{1,0:T(8,128)S(1)} %get-tuple-element.60.south, f32[16,640]{1,0:T(8,128)S(1)} %get-tuple-element.61.live, bf16[12,48,640]{2,1,0:T(8,128)(2,1)} %collective-permute-done.1.legendre), custom_call_target="tpu_custom_call" | custom-call | bytes 7400000 | tf_op jit(solution)/shard_map/partner_rows/pallas_call | solution.py:471
  80.0 11.1 %all-to-all-done.1.arrived = bf16[32,4,1152]{2,1,0:T(4,128)(2,1)S(1)} async-done(((bf16[32,4,1152]{2,1,0:T(4,128)(2,1)}), bf16[32,4,1152]{2,1,0:T(4,128)(2,1)S(1)}, u32[]{:S(2)}, u32[]{:S(2)}) %all-to-all-start.1) | async-done | bytes 294944 | tf_op jit(solution)/shard_map/all_to_all | solution.py:468
  91.1 3.5 %collective-permute-start.2 = (bf16[32,4,1152]{2,1,0:T(4,128)(2,1)S(1)}, bf16[32,4,1152]{2,1,0:T(4,128)(2,1)S(1)}, u32[]{:S(2)}, u32[]{:S(2)}) collective-permute-start(bf16[32,4,1152]{2,1,0:T(4,128)(2,1)S(1)} %all-to-all-done.1.arrived), channel_id=1, source_target_pairs={{0,1},{1,0},{2,3},{3,2},{4,5},{5,4},{6,7},{7,6},{8,9},{9,8},{10,11... | collective-permute-start | bytes 884744 | tf_op jit(solution)/shard_map/ppermute | solution.py:371
  94.6 1.2 collective-permute-done.2.swapped
  95.8 0.9 legendre_inverse.1
  96.7 3.1 %collective-permute-start.5 = (bf16[2,96,640]{2,1,0:T(8,128)(2,1)S(1)}, bf16[2,96,640]{2,1,0:T(8,128)(2,1)S(1)}, u32[]{:S(2)}, u32[]{:S(2)}) collective-permute-start(bf16[2,96,640]{2,1,0:T(8,128)(2,1)S(1)} %get-tuple-element.70), channel_id=1, source_target_pairs={{0,14},{1,3},{2,0},{3,5},{4,2},{5,7},{6,4},{7,9},{8,6},{9,11},{10,... | collective-permute-start | bytes 737288 | tf_op jit(solution)/shard_map/ppermute | solution.py:371
  99.8 2.3 %collective-permute-start.6 = (bf16[96,640]{1,0:T(8,128)(2,1)S(1)}, bf16[96,640]{1,0:T(8,128)(2,1)S(1)}, u32[]{:S(2)}, u32[]{:S(2)}) collective-permute-start(bf16[96,640]{1,0:T(8,128)(2,1)S(1)} %get-tuple-element.71), channel_id=1, source_target_pairs={{0,12},{1,5},{2,14},{3,7},{4,0},{5,9},{6,2},{7,11},{8,4},{9,13},{1... | collective-permute-start | bytes 368648 | tf_op jit(solution)/shard_map/ppermute | solution.py:371
  102.1 3.3 %collective-permute-start.3 = (bf16[96,640]{1,0:T(8,128)(2,1)S(1)}, bf16[96,640]{1,0:T(8,128)(2,1)S(1)}, u32[]{:S(2)}, u32[]{:S(2)}) collective-permute-start(bf16[96,640]{1,0:T(8,128)(2,1)S(1)} %get-tuple-element.66), channel_id=1, source_target_pairs={{0,14},{1,3},{2,0},{3,5},{4,2},{5,7},{6,4},{7,9},{8,6},{9,11},{10,... | collective-permute-start | bytes 368648 | tf_op jit(solution)/shard_map/ppermute | solution.py:371
  105.4 3.9 %collective-permute-start.4 = (bf16[96,640]{1,0:T(8,128)(2,1)S(1)}, bf16[96,640]{1,0:T(8,128)(2,1)S(1)}, u32[]{:S(2)}, u32[]{:S(2)}) collective-permute-start(bf16[96,640]{1,0:T(8,128)(2,1)S(1)} %get-tuple-element.67), channel_id=1, source_target_pairs={{0,15},{1,2},{2,1},{3,4},{4,3},{5,6},{6,5},{7,8},{8,7},{9,10},{10,... | collective-permute-start | bytes 368648 | tf_op jit(solution)/shard_map/ppermute | solution.py:371
  109.4 4.3 %collective-permute-start.7 = (bf16[96,640]{1,0:T(8,128)(2,1)S(1)}, bf16[96,640]{1,0:T(8,128)(2,1)S(1)}, u32[]{:S(2)}, u32[]{:S(2)}) collective-permute-start(bf16[96,640]{1,0:T(8,128)(2,1)S(1)} %get-tuple-element.72), channel_id=1, source_target_pairs={{0,12},{1,5},{2,14},{3,7},{4,0},{5,9},{6,2},{7,11},{8,4},{9,13},{1... | collective-permute-start | bytes 368648 | tf_op jit(solution)/shard_map/ppermute | solution.py:371
  113.7 2.1 %collective-permute-start.8 = (bf16[96,640]{1,0:T(8,128)(2,1)S(1)}, bf16[96,640]{1,0:T(8,128)(2,1)S(1)}, u32[]{:S(2)}, u32[]{:S(2)}) collective-permute-start(bf16[96,640]{1,0:T(8,128)(2,1)S(1)} %get-tuple-element.73), channel_id=1, source_target_pairs={{0,13},{1,4},{2,15},{3,6},{4,1},{5,8},{6,3},{7,10},{8,5},{9,12},{1... | collective-permute-start | bytes 368648 | tf_op jit(solution)/shard_map/ppermute | solution.py:371
  115.9 1.4 %collective-permute-done.7.two = bf16[96,640]{1,0:T(8,128)(2,1)S(1)} collective-permute-done((bf16[96,640]{1,0:T(8,128)(2,1)S(1)}, bf16[96,640]{1,0:T(8,128)(2,1)S(1)}, u32[]{:S(2)}, u32[]{:S(2)}) %collective-permute-start.7) | collective-permute-done | bytes 122912 | tf_op jit(solution)/shard_map/ppermute | solution.py:371
  117.3 5.2 %collective-permute-done.8.two_x = bf16[96,640]{1,0:T(8,128)(2,1)S(1)} collective-permute-done((bf16[96,640]{1,0:T(8,128)(2,1)S(1)}, bf16[96,640]{1,0:T(8,128)(2,1)S(1)}, u32[]{:S(2)}, u32[]{:S(2)}) %collective-permute-start.8) | collective-permute-done | bytes 122912 | tf_op jit(solution)/shard_map/ppermute | solution.py:371
  (24 shorter events, 1.5 us)
Async XLA Ops:
  30.2 10.2 %collective-permute-start = (bf16[8,96,640]{2,1,0:T(8,128)(2,1)S(1)}, bf16[8,96,640]{2,1,0:T(8,128)(2,1)S(1)}, u32[]{:S(2)}, u32[]{:S(2)}) collective-permute-start(bf16[8,96,640]{2,1,0:T(8,128)(2,1)S(1)} %all_gather.3.gathered), channel_id=1, source_target_pairs={{0,1},{1,0},{2,3},{3,2},{4,5},{5,4},{6,7},{7,6},{8,9},{9,8},{10,11... | collective-permute-start | bytes 2949128 | tf_op jit(solution)/shard_map/ppermute | solution.py:371
  39.8 0.6 copy-start.1
  40.4 11.3 %copy-start.6 = (s32[384]{0:T(512)S(1)}, s32[384]{0:T(512)}, u32[]{:S(2)}) copy-start(s32[384]{0:T(512)} %wave_of_slot.1) | copy-start | bytes 4612
  40.4 11.3 %copy-start = (s32[1536]{0:T(1024)S(1)}, s32[1536]{0:T(1024)}, u32[]{:S(2)}) copy-start(s32[1536]{0:T(1024)} %lat_of_row.3) | copy-start | bytes 18436
  40.4 11.3 %copy-start.3 = (s32[768]{0:T(1024)S(1)}, s32[768]{0:T(1024)}, u32[]{:S(2)}) copy-start(s32[768]{0:T(1024)} %lon_count.1) | copy-start | bytes 9220
  40.4 11.3 %copy-start.4 = (f32[48]{0:T(128)S(1)}, f32[48]{0:T(128)}, u32[]{:S(2)}) copy-start(f32[48]{0:T(128)} %lat_weight) | copy-start | bytes 580
  42.0 22.3 %all-to-all-start = ((bf16[32,4,1152]{2,1,0:T(4,128)(2,1)}), bf16[32,4,1152]{2,1,0:T(4,128)(2,1)S(1)}, u32[]{:S(2)}, u32[]{:S(2)}) async-start(bf16[32,4,1152]{2,1,0:T(4,128)(2,1)} %legendre_forward.1), calls=%async_computation | async-start | bytes 589824 | tf_op jit(solution)/shard_map/all_to_all | solution.py:422
  64.4 6.2 %copy-start.5 = (bf16[12,640,48]{1,2,0:T(8,128)(2,1)S(1)}, bf16[12,640,48]{1,2,0:T(8,128)(2,1)}, u32[]{:S(2)}) copy-start(bf16[12,640,48]{1,2,0:T(8,128)(2,1)} %param.7) | copy-start | bytes 2211844
  64.4 14.0 %copy-start.2 = (bf16[96,128]{1,0:T(8,128)(2,1)S(1)}, bf16[96,128]{1,0:T(8,128)(2,1)}, u32[]{:S(2)}) copy-start(bf16[96,128]{1,0:T(8,128)(2,1)} %copy-done.1) | copy-start | bytes 73732
  70.6 7.8 %collective-permute-start.1 = (bf16[12,48,640]{2,1,0:T(8,128)(2,1)S(1)}, bf16[12,48,640]{2,1,0:T(8,128)(2,1)}, u32[]{:S(2)}, u32[]{:S(2)}) collective-permute-start(bf16[12,48,640]{2,1,0:T(8,128)(2,1)S(1)} %bitcast.8), channel_id=1, source_target_pairs={{0,1},{1,0},{2,3},{3,2},{4,5},{5,4},{6,7},{7,6},{8,9},{9,8},{10,11... | collective-permute-start | bytes 2211848 | tf_op jit(solution)/shard_map/ppermute | solution.py:371
  74.4 16.6 %all-to-all-start.1 = ((bf16[32,4,1152]{2,1,0:T(4,128)(2,1)}), bf16[32,4,1152]{2,1,0:T(4,128)(2,1)S(1)}, u32[]{:S(2)}, u32[]{:S(2)}) async-start(bf16[32,4,1152]{2,1,0:T(4,128)(2,1)} %get-tuple-element.58), calls=%async_computation.1 | async-start | bytes 589824 | tf_op jit(solution)/shard_map/all_to_all | solution.py:468
  91.1 4.7 %collective-permute-start.2 = (bf16[32,4,1152]{2,1,0:T(4,128)(2,1)S(1)}, bf16[32,4,1152]{2,1,0:T(4,128)(2,1)S(1)}, u32[]{:S(2)}, u32[]{:S(2)}) collective-permute-start(bf16[32,4,1152]{2,1,0:T(4,128)(2,1)S(1)} %all-to-all-done.1.arrived), channel_id=1, source_target_pairs={{0,1},{1,0},{2,3},{3,2},{4,5},{5,4},{6,7},{7,6},{8,9},{9,8},{10,11... | collective-permute-start | bytes 884744 | tf_op jit(solution)/shard_map/ppermute | solution.py:371
  96.7 12.6 %collective-permute-start.5 = (bf16[2,96,640]{2,1,0:T(8,128)(2,1)S(1)}, bf16[2,96,640]{2,1,0:T(8,128)(2,1)S(1)}, u32[]{:S(2)}, u32[]{:S(2)}) collective-permute-start(bf16[2,96,640]{2,1,0:T(8,128)(2,1)S(1)} %get-tuple-element.70), channel_id=1, source_target_pairs={{0,14},{1,3},{2,0},{3,5},{4,2},{5,7},{6,4},{7,9},{8,6},{9,11},{10,... | collective-permute-start | bytes 737288 | tf_op jit(solution)/shard_map/ppermute | solution.py:371
  99.8 9.5 %collective-permute-start.6 = (bf16[96,640]{1,0:T(8,128)(2,1)S(1)}, bf16[96,640]{1,0:T(8,128)(2,1)S(1)}, u32[]{:S(2)}, u32[]{:S(2)}) collective-permute-start(bf16[96,640]{1,0:T(8,128)(2,1)S(1)} %get-tuple-element.71), channel_id=1, source_target_pairs={{0,12},{1,5},{2,14},{3,7},{4,0},{5,9},{6,2},{7,11},{8,4},{9,13},{1... | collective-permute-start | bytes 368648 | tf_op jit(solution)/shard_map/ppermute | solution.py:371
  102.1 13.8 %collective-permute-start.3 = (bf16[96,640]{1,0:T(8,128)(2,1)S(1)}, bf16[96,640]{1,0:T(8,128)(2,1)S(1)}, u32[]{:S(2)}, u32[]{:S(2)}) collective-permute-start(bf16[96,640]{1,0:T(8,128)(2,1)S(1)} %get-tuple-element.66), channel_id=1, source_target_pairs={{0,14},{1,3},{2,0},{3,5},{4,2},{5,7},{6,4},{7,9},{8,6},{9,11},{10,... | collective-permute-start | bytes 368648 | tf_op jit(solution)/shard_map/ppermute | solution.py:371
  105.4 10.5 %collective-permute-start.4 = (bf16[96,640]{1,0:T(8,128)(2,1)S(1)}, bf16[96,640]{1,0:T(8,128)(2,1)S(1)}, u32[]{:S(2)}, u32[]{:S(2)}) collective-permute-start(bf16[96,640]{1,0:T(8,128)(2,1)S(1)} %get-tuple-element.67), channel_id=1, source_target_pairs={{0,15},{1,2},{2,1},{3,4},{4,3},{5,6},{6,5},{7,8},{8,7},{9,10},{10,... | collective-permute-start | bytes 368648 | tf_op jit(solution)/shard_map/ppermute | solution.py:371
  109.4 7.8 %collective-permute-start.7 = (bf16[96,640]{1,0:T(8,128)(2,1)S(1)}, bf16[96,640]{1,0:T(8,128)(2,1)S(1)}, u32[]{:S(2)}, u32[]{:S(2)}) collective-permute-start(bf16[96,640]{1,0:T(8,128)(2,1)S(1)} %get-tuple-element.72), channel_id=1, source_target_pairs={{0,12},{1,5},{2,14},{3,7},{4,0},{5,9},{6,2},{7,11},{8,4},{9,13},{1... | collective-permute-start | bytes 368648 | tf_op jit(solution)/shard_map/ppermute | solution.py:371
  113.7 8.7 %collective-permute-start.8 = (bf16[96,640]{1,0:T(8,128)(2,1)S(1)}, bf16[96,640]{1,0:T(8,128)(2,1)S(1)}, u32[]{:S(2)}, u32[]{:S(2)}) collective-permute-start(bf16[96,640]{1,0:T(8,128)(2,1)S(1)} %get-tuple-element.73), channel_id=1, source_target_pairs={{0,13},{1,4},{2,15},{3,6},{4,1},{5,8},{6,3},{7,10},{8,5},{9,12},{1... | collective-permute-start | bytes 368648 | tf_op jit(solution)/shard_map/ppermute | solution.py:371

commit v9 on v8

--- a/solution.py
+++ b/solution.py
@@ -50,24 +50,12 @@
     return 1 - 2 * core
 
 
-def ordered_rows(chosen, south, live, legendre, out):
-    slots, band, degrees = legendre.shape
-    odd = (lax.broadcasted_iota(jnp.int32, (1, degrees), 1) & 1).astype(jnp.float32)
-    sign = 1.0 - 2.0 * (south[:, :1] * odd)
-    for slot in range(slots):
-        table = dot(chosen[:, :band], legendre[slot], NN) * sign
-        out[slot] = (table * live[slot : slot + 1, :]).astype(jnp.bfloat16)
-
-
-def own_rows_kernel(
-    wave_id, field_id, wave_of_slot, lat_of_row, legendre,
-    out, chosen_x, south_x, live,
+def legendre_rows_kernel(
+    wave_id, field_id, wave_of_slot, lat_of_row, legendre, out,
     slot_waves, row_lats, held, pick, south, sems, *, waves, fields,
 ):
-    copies = [
-        pltpu.make_async_copy(source, target, sems.at[i])
-        for i, (source, target) in enumerate(((lat_of_row, row_lats), (wave_of_slot, slot_waves), (legendre, held)))
-    ]
+    sources = ((lat_of_row, row_lats), (wave_of_slot, slot_waves), (legendre, held))
+    copies = [pltpu.make_async_copy(source, target, sems.at[i]) for i, (source, target) in enumerate(sources)]
     for copy in copies:
         copy.start()
     slots, band, degrees = held.shape
@@ -77,31 +65,21 @@
     own, field = wave_id[0], field_id[0]
     lane = lax.broadcasted_iota(jnp.int32, (1, LANES), 1)
     copies[0].wait()
-    for at in range(2):
-        this = field ^ at
-        for row in range(rows):
-            member, wave = divmod(row, waves)
-            lat = row_lats[(wave * fields + this) * row_count + member]
-            is_south = lat >= half
-            hemi = jnp.where(is_south, 2 * half - 1 - lat, lat) - this * band
-            pick[at, row : row + 1, :] = (lane == hemi).astype(jnp.float32)
-            south[at, row : row + 1, :] = jnp.broadcast_to(is_south.astype(jnp.float32), (1, LANES))
-    chosen_x[...] = pick[1].astype(jnp.bfloat16)
-    south_x[...] = south[1]
+    for row in range(rows):
+        member, wave = divmod(row, waves)
+        lat = row_lats[(wave * fields + field) * row_count + member]
+        is_south = lat >= half
+        hemi = jnp.where(is_south, 2 * half - 1 - lat, lat) - field * band
+        pick[row : row + 1, :] = (lane == hemi).astype(jnp.float32)
+        south[row : row + 1, :] = jnp.broadcast_to(is_south.astype(jnp.float32), (1, LANES))
+    copies[1].wait()
+    copies[2].wait()
     offsets = lax.broadcasted_iota(jnp.int32, (1, degrees), 1)
-    copies[1].wait()
-    live[...] = jnp.zeros(live.shape, jnp.float32)
+    sign = 1.0 - 2.0 * (south[:, :1] * (offsets & 1).astype(jnp.float32))
+    chosen = pick[:, :band].astype(jnp.bfloat16)
     for slot in range(slots):
-        live[slot : slot + 1, :] = (offsets < degrees - slot_waves[own * slots + slot]).astype(jnp.float32)
-    copies[2].wait()
-    ordered_rows(pick[0].astype(jnp.bfloat16), south[0], live, held, out)
-
-
-def partner_rows_kernel(chosen, south, live, legendre, out, held, sem):
-    copy = pltpu.make_async_copy(legendre, held, sem)
-    copy.start()
-    copy.wait()
-    ordered_rows(chosen[...], south[...], live, held, out)
+        live = offsets < degrees - slot_waves[own * slots + slot]
+        out[slot] = jnp.where(live, dot(chosen, held[slot], NN) * sign, 0.0).astype(jnp.bfloat16)
 
 
 def sin_cos(phase, period):
@@ -175,16 +153,12 @@
 
 def unpack_lines(messages, held, each):
     for at in range(messages.shape[0]):
-        message = messages[at].astype(jnp.float32)
-        for group in range(each // 4):
-            first = at * each + 4 * group
-            held[first : first + 4, :] = message[:, group * LANES : (group + 1) * LANES]
+        held[at * each : (at + 1) * each, :] = messages[at].astype(jnp.float32)
 
 
 def pack_lines(held, messages, each):
     for at in range(messages.shape[0]):
-        groups = [held[at * each + 4 * group : at * each + 4 * group + 4, :] for group in range(each // 4)]
-        messages[at] = jnp.concatenate(groups, axis=1).astype(jnp.bfloat16)
+        messages[at] = held[at * each : (at + 1) * each, :].astype(jnp.bfloat16)
 
 
 def legendre_forward_kernel(gathered, gathered_x, table, out, held):
@@ -388,33 +362,32 @@
         )
 
     row_table = jax.ShapeDtypeStruct((slots, rows, degrees), jnp.bfloat16)
-    fourier_shape = jax.ShapeDtypeStruct((waves, 4, each // 4 * LANES), jnp.bfloat16)
+    fourier_shape = jax.ShapeDtypeStruct((waves, each, LANES), jnp.bfloat16)
     float_rows = pltpu.VMEM((waves * each, LANES), jnp.float32)
 
     own = jnp.transpose(spectra, (0, 1, 3, 2)).reshape(coded, degrees)
     gathered = lax.all_gather(own, "field", axis_index_groups=like_cores)
     gathered, legendre = lax.optimization_barrier((gathered, jnp.transpose(legendre, (0, 2, 1))))
     gathered_x = swap(gathered)
-    table, chosen_x, south_x, live = local(
-        functools.partial(own_rows_kernel, waves=waves, fields=fields),
-        (
+
+    def ordered_rows(values, band_of):
+        return local(
+            functools.partial(legendre_rows_kernel, waves=waves, fields=fields),
             row_table,
-            jax.ShapeDtypeStruct((rows, LANES), jnp.bfloat16),
-            jax.ShapeDtypeStruct((rows, LANES), jnp.float32),
-            jax.ShapeDtypeStruct((-(-slots // 8) * 8, degrees), jnp.float32),
-        ),
-        "own_rows",
-        2,
-        in_specs=[smem(), smem(), hbm(), hbm(), hbm()],
-        scratch=[
-            pltpu.SMEM(wave_of_slot.shape, jnp.int32),
-            pltpu.SMEM(lat_of_row.shape, jnp.int32),
-            pltpu.VMEM((slots, band, degrees), jnp.bfloat16),
-            pltpu.VMEM((2, rows, LANES), jnp.float32),
-            pltpu.VMEM((2, rows, LANES), jnp.float32),
-            pltpu.SemaphoreType.DMA((3,)),
-        ],
-    )(wave_id, field_id, in_hbm(wave_of_slot), in_hbm(lat_of_row), in_hbm(legendre))
+            "legendre_rows",
+            2,
+            in_specs=[smem(), smem(), hbm(), hbm(), hbm()],
+            scratch=[
+                pltpu.SMEM(wave_of_slot.shape, jnp.int32),
+                pltpu.SMEM(lat_of_row.shape, jnp.int32),
+                pltpu.VMEM((slots, band, degrees), jnp.bfloat16),
+                pltpu.VMEM((rows, LANES), jnp.float32),
+                pltpu.VMEM((rows, LANES), jnp.float32),
+                pltpu.SemaphoreType.DMA((3,)),
+            ],
+        )(wave_id, band_of, in_hbm(wave_of_slot), in_hbm(lat_of_row), in_hbm(values))
+
+    table = ordered_rows(legendre, field_id)
     outgoing = local(
         legendre_forward_kernel, fourier_shape, "legendre_forward", 4, 16, in_specs=[vmem()] * 3, scratch=[float_rows]
     )(gathered, gathered_x, table)
@@ -468,14 +441,7 @@
     returned = lax.all_to_all(sent, "wave", split_axis=0, concat_axis=0, tiled=True)
     legendre_x = swap(legendre)
 
-    table_x = local(
-        partner_rows_kernel,
-        row_table,
-        "partner_rows",
-        2,
-        in_specs=[vmem(), vmem(), vmem(), hbm()],
-        scratch=[pltpu.VMEM((slots, band, degrees), jnp.bfloat16), pltpu.SemaphoreType.DMA(())],
-    )(chosen_x, south_x, live, in_hbm(legendre_x))
+    table_x = ordered_rows(legendre_x, field_id ^ 1)
     returned, table_x = lax.optimization_barrier((returned, table_x))
 
     chunk = jax.ShapeDtypeStruct((coded, degrees), jnp.bfloat16)

time: 124 us -> 125 us (level)
  transfers between devices with their start and end apart: 11 -> 11, of which waited for: 5 -> 6; matrix products, arithmetic and copies ran while one was open for 0% -> 0% of each run, Pallas kernels for 6% -> 6%
where the time goes in v9:
time: 125 us; the launch traced here: 124 us
  starting transfers between devices  48.4 us (39%)
  blocking collectives  28.6 us (23%)
  waiting for transfers between devices  28.2 us (23%)
  Pallas kernels  17 us (14%)
    ppermute x9, starting transfers between devices, hop(): return lax.ppermute(x, 'field', pairs)  34.8 us
    all_gather x1, blocking collectives, shards(): gathered = lax.all_gather(own, 'field', axis_index_groups=like_cores)  28.6 us
    all_to_all x1, waiting for transfers between devices, shards(): lax.all_to_all(sent, 'wave', split_axis=0, concat_axis=0, tiled=True)  11.5 us
    all_to_all x1, starting transfers between devices, shards(): lax.all_to_all(outgoing, 'wave', split_axis=0, concat_axis=0, tiled=True)  9.67 us
    all_to_all x1, waiting for transfers between devices, shards(): lax.all_to_all(outgoing, 'wave', split_axis=0, concat_axis=0, tiled=True)  8.47 us
    ppermute x9, waiting for transfers between devices, hop(): return lax.ppermute(x, 'field', pairs)  8.23 us
    pallas_call x1, Pallas kernels, shards(): local(fourier_kernel, (jax.ShapeDtypeStruct((row_count, levels, LONPAD),...  6.19 us
    pallas_call x1, Pallas kernels, shards(): local(functools.partial(fourier_tables_kernel, fields=fields, zs=zs), [pl...  4.21 us
  transfers between devices with their start and end apart: 11, of which 6 were waited for; matrix products, arithmetic and copies ran while one was open for 0% of the time, Pallas kernels for 6%

profile of v9, /device:TPU:1, one launch (start us, length us, event | category | flops | bytes accessed | tf_op | source)
XLA Modules:
  0.0 124.2 jit_solution(9766957047579143016)
XLA Ops:
  0.6 0.9 all_gather_reshape.3
  1.6 28.6 %all_gather.3.gathered = bf16[8,96,640]{2,1,0:T(8,128)(2,1)S(1)} all-gather(bf16[1,96,640]{2,1,0:T(8,128)(2,1)S(1)} %all_gather_reshape.3), channel_id=1, replica_groups={{0,2,4,6,8,10,12,14},{15,13,11,9,7,5,3,1},{16,18,20,22,24,26,28,30},{31..., dimensions={0}, use_global_device_ids=true | all-gather | bytes 1105920 | tf_op jit(solution)/shard_map/all_gather | solution.py:369
  30.2 7.7 %collective-permute-start = (bf16[8,96,640]{2,1,0:T(8,128)(2,1)S(1)}, bf16[8,96,640]{2,1,0:T(8,128)(2,1)S(1)}, u32[]{:S(2)}, u32[]{:S(2)}) collective-permute-start(bf16[8,96,640]{2,1,0:T(8,128)(2,1)S(1)} %all_gather.3.gathered), channel_id=1, source_target_pairs={{0,1},{1,0},{2,3},{3,2},{4,5},{5,4},{6,7},{7,6},{8,9},{9,8},{10,11... | collective-permute-start | bytes 2949128 | tf_op jit(solution)/shard_map/ppermute | solution.py:345
  37.9 1.7 %legendre_rows.2.table = bf16[12,96,640]{2,1,0:T(8,128)(2,1)S(1)} custom-call(s32[1]{0:T(128)} %bitcast.2.wave_id, s32[1]{0:T(128)} %bitcast.3.field_id, s32[384]{0:T(512)} %wave_of_slot.3, s32[1536]{0:T(1024)} %lat_of_row.5, bf16[12,48,640]{2,1,0:T(8,128)(2,1)} %bitcast.7), custom_call_target="tpu_custom_call" | custom-call | bytes 7400000 | tf_op jit(solution)/shard_map/legendre_rows/pallas_call | solution.py:374
  40.1 1.6 %legendre_forward.1 = bf16[32,36,128]{2,1,0:T(8,128)(2,1)} custom-call(bf16[8,96,640]{2,1,0:T(8,128)(2,1)S(1)} %all_gather.3.gathered, bf16[8,96,640]{2,1,0:T(8,128)(2,1)S(1)} %collective-permute-done.gathered_x, bf16[12,96,640]{2,1,0:T(8,128)(2,1)S(1)} %legendre_rows.2.table), custom_call_target="tpu_custom_call" | custom-call | bytes 14800000 | tf_op jit(solution)/shard_map/legendre_forward/pallas_call | solution.py:391
  41.7 9.7 %all-to-all-start = ((bf16[32,36,128]{2,1,0:T(8,128)(2,1)}), bf16[32,36,128]{2,1,0:T(8,128)(2,1)S(1)}, u32[]{:S(2)}, u32[]{:S(2)}) async-start(bf16[32,36,128]{2,1,0:T(8,128)(2,1)} %legendre_forward.1), calls=%async_computation | async-start | bytes 655360 | tf_op jit(solution)/shard_map/all_to_all | solution.py:395
  51.4 4.2 %fourier_tables.1 = (bf16[3,256,768]{2,1,0:T(8,128)(2,1)}, bf16[3,768,256]{2,1,0:T(8,128)(2,1)}, f32[3,16,768]{2,1,0:T(8,128)}, f32[3,16,768]{2,1,0:T(8,128)}, b...) custom-call(s32[1]{0:T(128)} %bitcast.2.wave_id, s32[1]{0:T(128)} %bitcast.3.field_id, s32[1536]{0:T(1024)S(1)} %copy-done, ...), custom_call_target="tpu_custom_call" | custom-call | bytes 14800000 | tf_op jit(solution)/shard_map/fourier_tables/pallas_call | solution.py:405
  55.7 8.5 %all-to-all-done.arrived = bf16[32,36,128]{2,1,0:T(8,128)(2,1)S(1)} async-done(((bf16[32,36,128]{2,1,0:T(8,128)(2,1)}), bf16[32,36,128]{2,1,0:T(8,128)(2,1)S(1)}, u32[]{:S(2)}, u32[]{:S(2)}) %all-to-all-start) | async-done | bytes 294944 | tf_op jit(solution)/shard_map/all_to_all | solution.py:395
  64.1 6.2 %fourier.1 = (bf16[3,64,3200]{2,1,0:T(8,128)(2,1)}, bf16[32,36,128]{2,1,0:T(8,128)(2,1)}) custom-call(bf16[32,36,128]{2,1,0:T(8,128)(2,1)S(1)} %all-to-all-done.arrived, bf16[3,256,768]{2,1,0:T(8,128)(2,1)} %get-tuple-element.45.inner_in, bf16[3,768,256]{2,1,0:T(8,128)(2,1)} %get-tuple-element.46.inner_t_in, f32[3,16,768]{2,1,0:T(8,128)} %get-tuple-element.47.outer_fwd_in, ...), custom_call_target="tpu_custom_call" | custom-call | bytes 22200000 | tf_op jit(solution)/shard_map/fourier/pallas_call | solution.py:421
  70.3 4.3 %collective-permute-start.1 = (bf16[12,48,640]{2,1,0:T(8,128)(2,1)S(1)}, bf16[12,48,640]{2,1,0:T(8,128)(2,1)}, u32[]{:S(2)}, u32[]{:S(2)}) collective-permute-start(bf16[12,48,640]{2,1,0:T(8,128)(2,1)S(1)} %bitcast.8), channel_id=1, source_target_pairs={{0,1},{1,0},{2,3},{3,2},{4,5},{5,4},{6,7},{7,6},{8,9},{9,8},{10,11... | collective-permute-start | bytes 2211848 | tf_op jit(solution)/shard_map/ppermute | solution.py:345
  74.6 3.9 %all-to-all-start.1 = ((bf16[32,36,128]{2,1,0:T(8,128)(2,1)}), bf16[32,36,128]{2,1,0:T(8,128)(2,1)S(1)}, u32[]{:S(2)}, u32[]{:S(2)}) async-start(bf16[32,36,128]{2,1,0:T(8,128)(2,1)} %get-tuple-element.53), calls=%async_computation.1 | async-start | bytes 655360 | tf_op jit(solution)/shard_map/all_to_all | solution.py:441
  78.6 1.7 %legendre_rows.3.table_swapped = bf16[12,96,640]{2,1,0:T(8,128)(2,1)S(1)} custom-call(s32[1]{0:T(128)} %bitcast.2.wave_id, s32[1]{0:T(128)S(6)} %xor.3.field_id, s32[384]{0:T(512)} %wave_of_slot.3, s32[1536]{0:T(1024)} %lat_of_row.5, bf16[12,48,640]{2,1,0:T(8,128)(2,1)} %collective-permute-done.1.legendre), custom_call_target="tpu_custom_call" | custom-call | bytes 7400000 | tf_op jit(solution)/shard_map/legendre_rows/pallas_call | solution.py:374
  80.2 11.5 %all-to-all-done.1.arrived = bf16[32,36,128]{2,1,0:T(8,128)(2,1)S(1)} async-done(((bf16[32,36,128]{2,1,0:T(8,128)(2,1)}), bf16[32,36,128]{2,1,0:T(8,128)(2,1)S(1)}, u32[]{:S(2)}, u32[]{:S(2)}) %all-to-all-start.1) | async-done | bytes 294944 | tf_op jit(solution)/shard_map/all_to_all | solution.py:441
  91.8 3.7 %collective-permute-start.2 = (bf16[32,36,128]{2,1,0:T(8,128)(2,1)S(1)}, bf16[32,36,128]{2,1,0:T(8,128)(2,1)S(1)}, u32[]{:S(2)}, u32[]{:S(2)}) collective-permute-start(bf16[32,36,128]{2,1,0:T(8,128)(2,1)S(1)} %all-to-all-done.1.arrived), channel_id=1, source_target_pairs={{0,1},{1,0},{2,3},{3,2},{4,5},{5,4},{6,7},{7,6},{8,9},{9,8},{10,11... | collective-permute-start | bytes 884744 | tf_op jit(solution)/shard_map/ppermute | solution.py:345
  95.5 1.2 collective-permute-done.2.swapped
  96.8 0.8 legendre_inverse.1
  97.6 3.1 %collective-permute-start.5 = (bf16[2,96,640]{2,1,0:T(8,128)(2,1)S(1)}, bf16[2,96,640]{2,1,0:T(8,128)(2,1)S(1)}, u32[]{:S(2)}, u32[]{:S(2)}) collective-permute-start(bf16[2,96,640]{2,1,0:T(8,128)(2,1)S(1)} %get-tuple-element.62), channel_id=1, source_target_pairs={{0,14},{1,3},{2,0},{3,5},{4,2},{5,7},{6,4},{7,9},{8,6},{9,11},{10,... | collective-permute-start | bytes 737288 | tf_op jit(solution)/shard_map/ppermute | solution.py:345
  100.7 2.3 %collective-permute-start.6 = (bf16[96,640]{1,0:T(8,128)(2,1)S(1)}, bf16[96,640]{1,0:T(8,128)(2,1)S(1)}, u32[]{:S(2)}, u32[]{:S(2)}) collective-permute-start(bf16[96,640]{1,0:T(8,128)(2,1)S(1)} %get-tuple-element.63), channel_id=1, source_target_pairs={{0,12},{1,5},{2,14},{3,7},{4,0},{5,9},{6,2},{7,11},{8,4},{9,13},{1... | collective-permute-start | bytes 368648 | tf_op jit(solution)/shard_map/ppermute | solution.py:345
  103.0 3.4 %collective-permute-start.3 = (bf16[96,640]{1,0:T(8,128)(2,1)S(1)}, bf16[96,640]{1,0:T(8,128)(2,1)S(1)}, u32[]{:S(2)}, u32[]{:S(2)}) collective-permute-start(bf16[96,640]{1,0:T(8,128)(2,1)S(1)} %get-tuple-element.58), channel_id=1, source_target_pairs={{0,14},{1,3},{2,0},{3,5},{4,2},{5,7},{6,4},{7,9},{8,6},{9,11},{10,... | collective-permute-start | bytes 368648 | tf_op jit(solution)/shard_map/ppermute | solution.py:345
  106.4 3.8 %collective-permute-start.4 = (bf16[96,640]{1,0:T(8,128)(2,1)S(1)}, bf16[96,640]{1,0:T(8,128)(2,1)S(1)}, u32[]{:S(2)}, u32[]{:S(2)}) collective-permute-start(bf16[96,640]{1,0:T(8,128)(2,1)S(1)} %get-tuple-element.59), channel_id=1, source_target_pairs={{0,15},{1,2},{2,1},{3,4},{4,3},{5,6},{6,5},{7,8},{8,7},{9,10},{10,... | collective-permute-start | bytes 368648 | tf_op jit(solution)/shard_map/ppermute | solution.py:345
  110.3 4.4 %collective-permute-start.7 = (bf16[96,640]{1,0:T(8,128)(2,1)S(1)}, bf16[96,640]{1,0:T(8,128)(2,1)S(1)}, u32[]{:S(2)}, u32[]{:S(2)}) collective-permute-start(bf16[96,640]{1,0:T(8,128)(2,1)S(1)} %get-tuple-element.64), channel_id=1, source_target_pairs={{0,12},{1,5},{2,14},{3,7},{4,0},{5,9},{6,2},{7,11},{8,4},{9,13},{1... | collective-permute-start | bytes 368648 | tf_op jit(solution)/shard_map/ppermute | solution.py:345
  114.7 2.1 %collective-permute-start.8 = (bf16[96,640]{1,0:T(8,128)(2,1)S(1)}, bf16[96,640]{1,0:T(8,128)(2,1)S(1)}, u32[]{:S(2)}, u32[]{:S(2)}) collective-permute-start(bf16[96,640]{1,0:T(8,128)(2,1)S(1)} %get-tuple-element.65), channel_id=1, source_target_pairs={{0,13},{1,4},{2,15},{3,6},{4,1},{5,8},{6,3},{7,10},{8,5},{9,12},{1... | collective-permute-start | bytes 368648 | tf_op jit(solution)/shard_map/ppermute | solution.py:345
  116.8 1.3 %collective-permute-done.7.two = bf16[96,640]{1,0:T(8,128)(2,1)S(1)} collective-permute-done((bf16[96,640]{1,0:T(8,128)(2,1)S(1)}, bf16[96,640]{1,0:T(8,128)(2,1)S(1)}, u32[]{:S(2)}, u32[]{:S(2)}) %collective-permute-start.7) | collective-permute-done | bytes 122912 | tf_op jit(solution)/shard_map/ppermute | solution.py:345
  118.1 5.2 %collective-permute-done.8.two_x = bf16[96,640]{1,0:T(8,128)(2,1)S(1)} collective-permute-done((bf16[96,640]{1,0:T(8,128)(2,1)S(1)}, bf16[96,640]{1,0:T(8,128)(2,1)S(1)}, u32[]{:S(2)}, u32[]{:S(2)}) %collective-permute-start.8) | collective-permute-done | bytes 122912 | tf_op jit(solution)/shard_map/ppermute | solution.py:345
  (20 shorter events, 1.4 us)
Async XLA Ops:
  30.2 9.9 %collective-permute-start = (bf16[8,96,640]{2,1,0:T(8,128)(2,1)S(1)}, bf16[8,96,640]{2,1,0:T(8,128)(2,1)S(1)}, u32[]{:S(2)}, u32[]{:S(2)}) collective-permute-start(bf16[8,96,640]{2,1,0:T(8,128)(2,1)S(1)} %all_gather.3.gathered), channel_id=1, source_target_pairs={{0,1},{1,0},{2,3},{3,2},{4,5},{5,4},{6,7},{7,6},{8,9},{9,8},{10,11... | collective-permute-start | bytes 2949128 | tf_op jit(solution)/shard_map/ppermute | solution.py:345
  39.6 11.8 %copy-start.4 = (s32[384]{0:T(512)S(1)}, s32[384]{0:T(512)}, u32[]{:S(2)}) copy-start(s32[384]{0:T(512)} %wave_of_slot.3) | copy-start | bytes 4612
  39.6 11.8 %copy-start = (s32[1536]{0:T(1024)S(1)}, s32[1536]{0:T(1024)}, u32[]{:S(2)}) copy-start(s32[1536]{0:T(1024)} %lat_of_row.5) | copy-start | bytes 18436
  39.6 11.8 %copy-start.1 = (s32[768]{0:T(1024)S(1)}, s32[768]{0:T(1024)}, u32[]{:S(2)}) copy-start(s32[768]{0:T(1024)} %lon_count.1) | copy-start | bytes 9220
  39.6 11.8 %copy-start.2 = (f32[48]{0:T(128)S(1)}, f32[48]{0:T(128)}, u32[]{:S(2)}) copy-start(f32[48]{0:T(128)} %lat_weight) | copy-start | bytes 580
  41.7 22.4 %all-to-all-start = ((bf16[32,36,128]{2,1,0:T(8,128)(2,1)}), bf16[32,36,128]{2,1,0:T(8,128)(2,1)S(1)}, u32[]{:S(2)}, u32[]{:S(2)}) async-start(bf16[32,36,128]{2,1,0:T(8,128)(2,1)} %legendre_forward.1), calls=%async_computation | async-start | bytes 655360 | tf_op jit(solution)/shard_map/all_to_all | solution.py:395
  64.1 6.2 %copy-start.3 = (bf16[12,640,48]{1,2,0:T(8,128)(2,1)S(1)}, bf16[12,640,48]{1,2,0:T(8,128)(2,1)}, u32[]{:S(2)}) copy-start(bf16[12,640,48]{1,2,0:T(8,128)(2,1)} %param.7) | copy-start | bytes 2211844
  70.3 8.2 %collective-permute-start.1 = (bf16[12,48,640]{2,1,0:T(8,128)(2,1)S(1)}, bf16[12,48,640]{2,1,0:T(8,128)(2,1)}, u32[]{:S(2)}, u32[]{:S(2)}) collective-permute-start(bf16[12,48,640]{2,1,0:T(8,128)(2,1)S(1)} %bitcast.8), channel_id=1, source_target_pairs={{0,1},{1,0},{2,3},{3,2},{4,5},{5,4},{6,7},{7,6},{8,9},{9,8},{10,11... | collective-permute-start | bytes 2211848 | tf_op jit(solution)/shard_map/ppermute | solution.py:345
  74.6 17.1 %all-to-all-start.1 = ((bf16[32,36,128]{2,1,0:T(8,128)(2,1)}), bf16[32,36,128]{2,1,0:T(8,128)(2,1)S(1)}, u32[]{:S(2)}, u32[]{:S(2)}) async-start(bf16[32,36,128]{2,1,0:T(8,128)(2,1)} %get-tuple-element.53), calls=%async_computation.1 | async-start | bytes 655360 | tf_op jit(solution)/shard_map/all_to_all | solution.py:441
  91.8 5.0 %collective-permute-start.2 = (bf16[32,36,128]{2,1,0:T(8,128)(2,1)S(1)}, bf16[32,36,128]{2,1,0:T(8,128)(2,1)S(1)}, u32[]{:S(2)}, u32[]{:S(2)}) collective-permute-start(bf16[32,36,128]{2,1,0:T(8,128)(2,1)S(1)} %all-to-all-done.1.arrived), channel_id=1, source_target_pairs={{0,1},{1,0},{2,3},{3,2},{4,5},{5,4},{6,7},{7,6},{8,9},{9,8},{10,11... | collective-permute-start | bytes 884744 | tf_op jit(solution)/shard_map/ppermute | solution.py:345
  97.6 12.6 %collective-permute-start.5 = (bf16[2,96,640]{2,1,0:T(8,128)(2,1)S(1)}, bf16[2,96,640]{2,1,0:T(8,128)(2,1)S(1)}, u32[]{:S(2)}, u32[]{:S(2)}) collective-permute-start(bf16[2,96,640]{2,1,0:T(8,128)(2,1)S(1)} %get-tuple-element.62), channel_id=1, source_target_pairs={{0,14},{1,3},{2,0},{3,5},{4,2},{5,7},{6,4},{7,9},{8,6},{9,11},{10,... | collective-permute-start | bytes 737288 | tf_op jit(solution)/shard_map/ppermute | solution.py:345
  100.7 9.5 %collective-permute-start.6 = (bf16[96,640]{1,0:T(8,128)(2,1)S(1)}, bf16[96,640]{1,0:T(8,128)(2,1)S(1)}, u32[]{:S(2)}, u32[]{:S(2)}) collective-permute-start(bf16[96,640]{1,0:T(8,128)(2,1)S(1)} %get-tuple-element.63), channel_id=1, source_target_pairs={{0,12},{1,5},{2,14},{3,7},{4,0},{5,9},{6,2},{7,11},{8,4},{9,13},{1... | collective-permute-start | bytes 368648 | tf_op jit(solution)/shard_map/ppermute | solution.py:345
  103.0 13.8 %collective-permute-start.3 = (bf16[96,640]{1,0:T(8,128)(2,1)S(1)}, bf16[96,640]{1,0:T(8,128)(2,1)S(1)}, u32[]{:S(2)}, u32[]{:S(2)}) collective-permute-start(bf16[96,640]{1,0:T(8,128)(2,1)S(1)} %get-tuple-element.58), channel_id=1, source_target_pairs={{0,14},{1,3},{2,0},{3,5},{4,2},{5,7},{6,4},{7,9},{8,6},{9,11},{10,... | collective-permute-start | bytes 368648 | tf_op jit(solution)/shard_map/ppermute | solution.py:345
  106.4 10.4 %collective-permute-start.4 = (bf16[96,640]{1,0:T(8,128)(2,1)S(1)}, bf16[96,640]{1,0:T(8,128)(2,1)S(1)}, u32[]{:S(2)}, u32[]{:S(2)}) collective-permute-start(bf16[96,640]{1,0:T(8,128)(2,1)S(1)} %get-tuple-element.59), channel_id=1, source_target_pairs={{0,15},{1,2},{2,1},{3,4},{4,3},{5,6},{6,5},{7,8},{8,7},{9,10},{10,... | collective-permute-start | bytes 368648 | tf_op jit(solution)/shard_map/ppermute | solution.py:345
  110.3 7.8 %collective-permute-start.7 = (bf16[96,640]{1,0:T(8,128)(2,1)S(1)}, bf16[96,640]{1,0:T(8,128)(2,1)S(1)}, u32[]{:S(2)}, u32[]{:S(2)}) collective-permute-start(bf16[96,640]{1,0:T(8,128)(2,1)S(1)} %get-tuple-element.64), channel_id=1, source_target_pairs={{0,12},{1,5},{2,14},{3,7},{4,0},{5,9},{6,2},{7,11},{8,4},{9,13},{1... | collective-permute-start | bytes 368648 | tf_op jit(solution)/shard_map/ppermute | solution.py:345
  114.7 8.7 %collective-permute-start.8 = (bf16[96,640]{1,0:T(8,128)(2,1)S(1)}, bf16[96,640]{1,0:T(8,128)(2,1)S(1)}, u32[]{:S(2)}, u32[]{:S(2)}) collective-permute-start(bf16[96,640]{1,0:T(8,128)(2,1)S(1)} %get-tuple-element.65), channel_id=1, source_target_pairs={{0,13},{1,4},{2,15},{3,6},{4,1},{5,8},{6,3},{7,10},{8,5},{9,12},{1... | collective-permute-start | bytes 368648 | tf_op jit(solution)/shard_map/ppermute | solution.py:345

commit v10 on v9

--- a/solution.py
+++ b/solution.py
@@ -153,12 +153,16 @@
 
 def unpack_lines(messages, held, each):
     for at in range(messages.shape[0]):
-        held[at * each : (at + 1) * each, :] = messages[at].astype(jnp.float32)
+        message = messages[at].astype(jnp.float32)
+        for group in range(each // 4):
+            first = at * each + 4 * group
+            held[first : first + 4, :] = message[:, group * LANES : (group + 1) * LANES]
 
 
 def pack_lines(held, messages, each):
     for at in range(messages.shape[0]):
-        messages[at] = held[at * each : (at + 1) * each, :].astype(jnp.bfloat16)
+        groups = [held[at * each + 4 * group : at * each + 4 * group + 4, :] for group in range(each // 4)]
+        messages[at] = jnp.concatenate(groups, axis=1).astype(jnp.bfloat16)
 
 
 def legendre_forward_kernel(gathered, gathered_x, table, out, held):
@@ -362,13 +366,14 @@
         )
 
     row_table = jax.ShapeDtypeStruct((slots, rows, degrees), jnp.bfloat16)
-    fourier_shape = jax.ShapeDtypeStruct((waves, each, LANES), jnp.bfloat16)
+    fourier_shape = jax.ShapeDtypeStruct((waves, 4, each // 4 * LANES), jnp.bfloat16)
     float_rows = pltpu.VMEM((waves * each, LANES), jnp.float32)
 
     own = jnp.transpose(spectra, (0, 1, 3, 2)).reshape(coded, degrees)
     gathered = lax.all_gather(own, "field", axis_index_groups=like_cores)
     gathered, legendre = lax.optimization_barrier((gathered, jnp.transpose(legendre, (0, 2, 1))))
     gathered_x = swap(gathered)
+    legendre_x = swap(legendre)
 
     def ordered_rows(values, band_of):
         return local(
@@ -388,6 +393,7 @@
         )(wave_id, band_of, in_hbm(wave_of_slot), in_hbm(lat_of_row), in_hbm(values))
 
     table = ordered_rows(legendre, field_id)
+    gathered_x, legendre_x = lax.optimization_barrier((gathered_x, legendre_x))
     outgoing = local(
         legendre_forward_kernel, fourier_shape, "legendre_forward", 4, 16, in_specs=[vmem()] * 3, scratch=[float_rows]
     )(gathered, gathered_x, table)
@@ -437,9 +443,8 @@
         ],
     )(arrived, *prepared)
 
-    sent, legendre = lax.optimization_barrier((sent, legendre))
+    sent, legendre_x = lax.optimization_barrier((sent, legendre_x))
     returned = lax.all_to_all(sent, "wave", split_axis=0, concat_axis=0, tiled=True)
-    legendre_x = swap(legendre)
 
     table_x = ordered_rows(legendre_x, field_id ^ 1)
     returned, table_x = lax.optimization_barrier((returned, table_x))

time: 125 us -> 122 us (0.976)
  waiting for transfers between devices: 28.2 us -> 25.8 us
    all_to_all x1, waiting for transfers between devices: 11.5 us -> 9.1 us  [shards(): lax.all_to_all(sent, 'wave', split_axis=0, concat_axis=0, tiled=True)]
where the time goes in v10:
time: 122 us
  starting transfers between devices  48.4 us (40%)
  blocking collectives  28.6 us (23%)
  waiting for transfers between devices  25.8 us (21%)
  Pallas kernels  17 us (14%)
    ppermute x9, starting transfers between devices, hop(): return lax.ppermute(x, 'field', pairs)  34.3 us
    all_gather x1, blocking collectives, shards(): gathered = lax.all_gather(own, 'field', axis_index_groups=like_cores)  28.6 us
    all_to_all x1, starting transfers between devices, shards(): lax.all_to_all(outgoing, 'wave', split_axis=0, concat_axis=0, tiled=True)  9.67 us
    all_to_all x1, waiting for transfers between devices, shards(): lax.all_to_all(sent, 'wave', split_axis=0, concat_axis=0, tiled=True)  9.1 us
    ppermute x9, waiting for transfers between devices, hop(): return lax.ppermute(x, 'field', pairs)  8.53 us
    all_to_all x1, waiting for transfers between devices, shards(): lax.all_to_all(outgoing, 'wave', split_axis=0, concat_axis=0, tiled=True)  8.13 us
    pallas_call x1, Pallas kernels, shards(): local(fourier_kernel, (jax.ShapeDtypeStruct((row_count, levels, LONPAD),...  6.12 us
    all_to_all x1, starting transfers between devices, shards(): lax.all_to_all(sent, 'wave', split_axis=0, concat_axis=0, tiled=True)  4.45 us
  transfers between devices with their start and end apart: 11, of which 6 were waited for; matrix products, arithmetic and copies ran while one was open for 0% of the time, Pallas kernels for 6%

profile of v10, /device:TPU:1, one launch (start us, length us, event | category | flops | bytes accessed | tf_op | source)
XLA Modules:
  0.0 121.6 jit_solution(13711405579709616968)
XLA Ops:
  0.6 0.9 all_gather_reshape.3
  1.6 28.6 %all_gather.3.gathered = bf16[8,96,640]{2,1,0:T(8,128)(2,1)S(1)} all-gather(bf16[1,96,640]{2,1,0:T(8,128)(2,1)S(1)} %all_gather_reshape.3), channel_id=1, replica_groups={{0,2,4,6,8,10,12,14},{15,13,11,9,7,5,3,1},{16,18,20,22,24,26,28,30},{31..., dimensions={0}, use_global_device_ids=true | all-gather | bytes 1105920 | tf_op jit(solution)/shard_map/all_gather | solution.py:373
  30.2 7.7 %collective-permute-start = (bf16[8,96,640]{2,1,0:T(8,128)(2,1)S(1)}, bf16[8,96,640]{2,1,0:T(8,128)(2,1)S(1)}, u32[]{:S(2)}, u32[]{:S(2)}) collective-permute-start(bf16[8,96,640]{2,1,0:T(8,128)(2,1)S(1)} %all_gather.3.gathered), channel_id=1, source_target_pairs={{0,1},{1,0},{2,3},{3,2},{4,5},{5,4},{6,7},{7,6},{8,9},{9,8},{10,11... | collective-permute-start | bytes 2949128 | tf_op jit(solution)/shard_map/ppermute | solution.py:349
  37.9 1.9 %collective-permute-start.1 = (bf16[12,48,640]{2,1,0:T(8,128)(2,1)}, bf16[12,48,640]{2,1,0:T(8,128)(2,1)}, u32[]{:S(2)}, u32[]{:S(2)}) collective-permute-start(bf16[12,48,640]{2,1,0:T(8,128)(2,1)} %bitcast.1.legendre), channel_id=1, source_target_pairs={{0,1},{1,0},{2,3},{3,2},{4,5},{5,4},{6,7},{7,6},{8,9},{9,8},{10,11... | collective-permute-start | bytes 2211848 | tf_op jit(solution)/shard_map/ppermute | solution.py:349
  39.9 1.7 %legendre_rows.2.table = bf16[12,96,640]{2,1,0:T(8,128)(2,1)S(1)} custom-call(s32[1]{0:T(128)} %bitcast.2.wave_id, s32[1]{0:T(128)} %bitcast.3.field_id, s32[384]{0:T(512)} %wave_of_slot.3, s32[1536]{0:T(1024)} %lat_of_row.5, bf16[12,48,640]{2,1,0:T(8,128)(2,1)} %bitcast.1.legendre), custom_call_target="tpu_custom_call" | custom-call | bytes 7400000 | tf_op jit(solution)/shard_map/legendre_rows/pallas_call | solution.py:379
  42.4 1.6 %legendre_forward.1 = bf16[32,4,1152]{2,1,0:T(4,128)(2,1)} custom-call(bf16[8,96,640]{2,1,0:T(8,128)(2,1)S(1)} %all_gather.3.gathered, bf16[8,96,640]{2,1,0:T(8,128)(2,1)S(1)} %collective-permute-done.gathered_x, bf16[12,96,640]{2,1,0:T(8,128)(2,1)S(1)} %legendre_rows.2.table), custom_call_target="tpu_custom_call" | custom-call | bytes 14800000 | tf_op jit(solution)/shard_map/legendre_forward/pallas_call | solution.py:397
  43.9 9.7 %all-to-all-start = ((bf16[32,4,1152]{2,1,0:T(4,128)(2,1)}), bf16[32,4,1152]{2,1,0:T(4,128)(2,1)S(1)}, u32[]{:S(2)}, u32[]{:S(2)}) async-start(bf16[32,4,1152]{2,1,0:T(4,128)(2,1)} %legendre_forward.1), calls=%async_computation | async-start | bytes 589824 | tf_op jit(solution)/shard_map/all_to_all | solution.py:401
  53.7 4.2 %fourier_tables.1 = (bf16[3,256,768]{2,1,0:T(8,128)(2,1)}, bf16[3,768,256]{2,1,0:T(8,128)(2,1)}, f32[3,16,768]{2,1,0:T(8,128)}, f32[3,16,768]{2,1,0:T(8,128)}, b...) custom-call(s32[1]{0:T(128)} %bitcast.2.wave_id, s32[1]{0:T(128)} %bitcast.3.field_id, s32[1536]{0:T(1024)S(1)} %copy-done, ...), custom_call_target="tpu_custom_call" | custom-call | bytes 14800000 | tf_op jit(solution)/shard_map/fourier_tables/pallas_call | solution.py:411
  57.9 8.1 %all-to-all-done.arrived = bf16[32,4,1152]{2,1,0:T(4,128)(2,1)S(1)} async-done(((bf16[32,4,1152]{2,1,0:T(4,128)(2,1)}), bf16[32,4,1152]{2,1,0:T(4,128)(2,1)S(1)}, u32[]{:S(2)}, u32[]{:S(2)}) %all-to-all-start) | async-done | bytes 294944 | tf_op jit(solution)/shard_map/all_to_all | solution.py:401
  66.0 6.1 %fourier.1 = (bf16[3,64,3200]{2,1,0:T(8,128)(2,1)}, bf16[32,4,1152]{2,1,0:T(4,128)(2,1)}) custom-call(bf16[32,4,1152]{2,1,0:T(4,128)(2,1)S(1)} %all-to-all-done.arrived, bf16[3,256,768]{2,1,0:T(8,128)(2,1)} %get-tuple-element.48.inner_in, bf16[3,768,256]{2,1,0:T(8,128)(2,1)} %get-tuple-element.49.inner_t_in, f32[3,16,768]{2,1,0:T(8,128)} %get-tuple-element.50.outer_fwd_in, ...), custom_call_target="tpu_custom_call" | custom-call | bytes 22200000 | tf_op jit(solution)/shard_map/fourier/pallas_call | solution.py:427
  72.2 4.4 %all-to-all-start.1 = ((bf16[32,4,1152]{2,1,0:T(4,128)(2,1)}), bf16[32,4,1152]{2,1,0:T(4,128)(2,1)S(1)}, u32[]{:S(2)}, u32[]{:S(2)}) async-start(bf16[32,4,1152]{2,1,0:T(4,128)(2,1)} %get-tuple-element.57), calls=%async_computation.1 | async-start | bytes 589824 | tf_op jit(solution)/shard_map/all_to_all | solution.py:447
  76.6 1.7 %legendre_rows.3.table_swapped = bf16[12,96,640]{2,1,0:T(8,128)(2,1)S(1)} custom-call(s32[1]{0:T(128)} %bitcast.2.wave_id, s32[1]{0:T(128)S(6)} %xor.3.field_id, s32[384]{0:T(512)} %wave_of_slot.3, s32[1536]{0:T(1024)} %lat_of_row.5, bf16[12,48,640]{2,1,0:T(8,128)(2,1)} %collective-permute-done.1.legendre), custom_call_target="tpu_custom_call" | custom-call | bytes 7400000 | tf_op jit(solution)/shard_map/legendre_rows/pallas_call | solution.py:379
  78.3 9.1 %all-to-all-done.1.arrived = bf16[32,4,1152]{2,1,0:T(4,128)(2,1)S(1)} async-done(((bf16[32,4,1152]{2,1,0:T(4,128)(2,1)}), bf16[32,4,1152]{2,1,0:T(4,128)(2,1)S(1)}, u32[]{:S(2)}, u32[]{:S(2)}) %all-to-all-start.1) | async-done | bytes 294944 | tf_op jit(solution)/shard_map/all_to_all | solution.py:447
  87.4 5.6 %collective-permute-start.2 = (bf16[32,4,1152]{2,1,0:T(4,128)(2,1)S(1)}, bf16[32,4,1152]{2,1,0:T(4,128)(2,1)S(1)}, u32[]{:S(2)}, u32[]{:S(2)}) collective-permute-start(bf16[32,4,1152]{2,1,0:T(4,128)(2,1)S(1)} %all-to-all-done.1.arrived), channel_id=1, source_target_pairs={{0,1},{1,0},{2,3},{3,2},{4,5},{5,4},{6,7},{7,6},{8,9},{9,8},{10,11... | collective-permute-start | bytes 884744 | tf_op jit(solution)/shard_map/ppermute | solution.py:349
  93.0 1.2 collective-permute-done.2.swapped
  94.2 0.9 legendre_inverse.1
  95.1 3.1 %collective-permute-start.5 = (bf16[2,96,640]{2,1,0:T(8,128)(2,1)S(1)}, bf16[2,96,640]{2,1,0:T(8,128)(2,1)S(1)}, u32[]{:S(2)}, u32[]{:S(2)}) collective-permute-start(bf16[2,96,640]{2,1,0:T(8,128)(2,1)S(1)} %get-tuple-element.66), channel_id=1, source_target_pairs={{0,14},{1,3},{2,0},{3,5},{4,2},{5,7},{6,4},{7,9},{8,6},{9,11},{10,... | collective-permute-start | bytes 737288 | tf_op jit(solution)/shard_map/ppermute | solution.py:349
  98.2 2.3 %collective-permute-start.6 = (bf16[96,640]{1,0:T(8,128)(2,1)S(1)}, bf16[96,640]{1,0:T(8,128)(2,1)S(1)}, u32[]{:S(2)}, u32[]{:S(2)}) collective-permute-start(bf16[96,640]{1,0:T(8,128)(2,1)S(1)} %get-tuple-element.67), channel_id=1, source_target_pairs={{0,12},{1,5},{2,14},{3,7},{4,0},{5,9},{6,2},{7,11},{8,4},{9,13},{1... | collective-permute-start | bytes 368648 | tf_op jit(solution)/shard_map/ppermute | solution.py:349
  100.5 3.3 %collective-permute-start.3 = (bf16[96,640]{1,0:T(8,128)(2,1)S(1)}, bf16[96,640]{1,0:T(8,128)(2,1)S(1)}, u32[]{:S(2)}, u32[]{:S(2)}) collective-permute-start(bf16[96,640]{1,0:T(8,128)(2,1)S(1)} %get-tuple-element.62), channel_id=1, source_target_pairs={{0,14},{1,3},{2,0},{3,5},{4,2},{5,7},{6,4},{7,9},{8,6},{9,11},{10,... | collective-permute-start | bytes 368648 | tf_op jit(solution)/shard_map/ppermute | solution.py:349
  103.9 3.9 %collective-permute-start.4 = (bf16[96,640]{1,0:T(8,128)(2,1)S(1)}, bf16[96,640]{1,0:T(8,128)(2,1)S(1)}, u32[]{:S(2)}, u32[]{:S(2)}) collective-permute-start(bf16[96,640]{1,0:T(8,128)(2,1)S(1)} %get-tuple-element.63), channel_id=1, source_target_pairs={{0,15},{1,2},{2,1},{3,4},{4,3},{5,6},{6,5},{7,8},{8,7},{9,10},{10,... | collective-permute-start | bytes 368648 | tf_op jit(solution)/shard_map/ppermute | solution.py:349
  107.8 4.3 %collective-permute-start.7 = (bf16[96,640]{1,0:T(8,128)(2,1)S(1)}, bf16[96,640]{1,0:T(8,128)(2,1)S(1)}, u32[]{:S(2)}, u32[]{:S(2)}) collective-permute-start(bf16[96,640]{1,0:T(8,128)(2,1)S(1)} %get-tuple-element.68), channel_id=1, source_target_pairs={{0,12},{1,5},{2,14},{3,7},{4,0},{5,9},{6,2},{7,11},{8,4},{9,13},{1... | collective-permute-start | bytes 368648 | tf_op jit(solution)/shard_map/ppermute | solution.py:349
  112.1 2.1 %collective-permute-start.8 = (bf16[96,640]{1,0:T(8,128)(2,1)S(1)}, bf16[96,640]{1,0:T(8,128)(2,1)S(1)}, u32[]{:S(2)}, u32[]{:S(2)}) collective-permute-start(bf16[96,640]{1,0:T(8,128)(2,1)S(1)} %get-tuple-element.69), channel_id=1, source_target_pairs={{0,13},{1,4},{2,15},{3,6},{4,1},{5,8},{6,3},{7,10},{8,5},{9,12},{1... | collective-permute-start | bytes 368648 | tf_op jit(solution)/shard_map/ppermute | solution.py:349
  114.3 1.4 %collective-permute-done.7.two = bf16[96,640]{1,0:T(8,128)(2,1)S(1)} collective-permute-done((bf16[96,640]{1,0:T(8,128)(2,1)S(1)}, bf16[96,640]{1,0:T(8,128)(2,1)S(1)}, u32[]{:S(2)}, u32[]{:S(2)}) %collective-permute-start.7) | collective-permute-done | bytes 122912 | tf_op jit(solution)/shard_map/ppermute | solution.py:349
  115.7 5.2 %collective-permute-done.8.two_x = bf16[96,640]{1,0:T(8,128)(2,1)S(1)} collective-permute-done((bf16[96,640]{1,0:T(8,128)(2,1)S(1)}, bf16[96,640]{1,0:T(8,128)(2,1)S(1)}, u32[]{:S(2)}, u32[]{:S(2)}) %collective-permute-start.8) | collective-permute-done | bytes 122912 | tf_op jit(solution)/shard_map/ppermute | solution.py:349
  (18 shorter events, 1.7 us)
Async XLA Ops:
  30.2 12.2 %collective-permute-start = (bf16[8,96,640]{2,1,0:T(8,128)(2,1)S(1)}, bf16[8,96,640]{2,1,0:T(8,128)(2,1)S(1)}, u32[]{:S(2)}, u32[]{:S(2)}) collective-permute-start(bf16[8,96,640]{2,1,0:T(8,128)(2,1)S(1)} %all_gather.3.gathered), channel_id=1, source_target_pairs={{0,1},{1,0},{2,3},{3,2},{4,5},{5,4},{6,7},{7,6},{8,9},{9,8},{10,11... | collective-permute-start | bytes 2949128 | tf_op jit(solution)/shard_map/ppermute | solution.py:349
  37.9 4.5 %collective-permute-start.1 = (bf16[12,48,640]{2,1,0:T(8,128)(2,1)}, bf16[12,48,640]{2,1,0:T(8,128)(2,1)}, u32[]{:S(2)}, u32[]{:S(2)}) collective-permute-start(bf16[12,48,640]{2,1,0:T(8,128)(2,1)} %bitcast.1.legendre), channel_id=1, source_target_pairs={{0,1},{1,0},{2,3},{3,2},{4,5},{5,4},{6,7},{7,6},{8,9},{9,8},{10,11... | collective-permute-start | bytes 2211848 | tf_op jit(solution)/shard_map/ppermute | solution.py:349
  41.6 12.1 %copy-start.3 = (s32[384]{0:T(512)S(1)}, s32[384]{0:T(512)}, u32[]{:S(2)}) copy-start(s32[384]{0:T(512)} %wave_of_slot.3) | copy-start | bytes 4612
  41.6 12.1 %copy-start = (s32[1536]{0:T(1024)S(1)}, s32[1536]{0:T(1024)}, u32[]{:S(2)}) copy-start(s32[1536]{0:T(1024)} %lat_of_row.5) | copy-start | bytes 18436
  41.6 12.1 %copy-start.1 = (s32[768]{0:T(1024)S(1)}, s32[768]{0:T(1024)}, u32[]{:S(2)}) copy-start(s32[768]{0:T(1024)} %lon_count.1) | copy-start | bytes 9220
  41.6 12.1 %copy-start.2 = (f32[48]{0:T(128)S(1)}, f32[48]{0:T(128)}, u32[]{:S(2)}) copy-start(f32[48]{0:T(128)} %lat_weight) | copy-start | bytes 580
  43.9 22.1 %all-to-all-start = ((bf16[32,4,1152]{2,1,0:T(4,128)(2,1)}), bf16[32,4,1152]{2,1,0:T(4,128)(2,1)S(1)}, u32[]{:S(2)}, u32[]{:S(2)}) async-start(bf16[32,4,1152]{2,1,0:T(4,128)(2,1)} %legendre_forward.1), calls=%async_computation | async-start | bytes 589824 | tf_op jit(solution)/shard_map/all_to_all | solution.py:401
  72.2 15.2 %all-to-all-start.1 = ((bf16[32,4,1152]{2,1,0:T(4,128)(2,1)}), bf16[32,4,1152]{2,1,0:T(4,128)(2,1)S(1)}, u32[]{:S(2)}, u32[]{:S(2)}) async-start(bf16[32,4,1152]{2,1,0:T(4,128)(2,1)} %get-tuple-element.57), calls=%async_computation.1 | async-start | bytes 589824 | tf_op jit(solution)/shard_map/all_to_all | solution.py:447
  87.4 6.8 %collective-permute-start.2 = (bf16[32,4,1152]{2,1,0:T(4,128)(2,1)S(1)}, bf16[32,4,1152]{2,1,0:T(4,128)(2,1)S(1)}, u32[]{:S(2)}, u32[]{:S(2)}) collective-permute-start(bf16[32,4,1152]{2,1,0:T(4,128)(2,1)S(1)} %all-to-all-done.1.arrived), channel_id=1, source_target_pairs={{0,1},{1,0},{2,3},{3,2},{4,5},{5,4},{6,7},{7,6},{8,9},{9,8},{10,11... | collective-permute-start | bytes 884744 | tf_op jit(solution)/shard_map/ppermute | solution.py:349
  95.1 12.6 %collective-permute-start.5 = (bf16[2,96,640]{2,1,0:T(8,128)(2,1)S(1)}, bf16[2,96,640]{2,1,0:T(8,128)(2,1)S(1)}, u32[]{:S(2)}, u32[]{:S(2)}) collective-permute-start(bf16[2,96,640]{2,1,0:T(8,128)(2,1)S(1)} %get-tuple-element.66), channel_id=1, source_target_pairs={{0,14},{1,3},{2,0},{3,5},{4,2},{5,7},{6,4},{7,9},{8,6},{9,11},{10,... | collective-permute-start | bytes 737288 | tf_op jit(solution)/shard_map/ppermute | solution.py:349
  98.2 9.5 %collective-permute-start.6 = (bf16[96,640]{1,0:T(8,128)(2,1)S(1)}, bf16[96,640]{1,0:T(8,128)(2,1)S(1)}, u32[]{:S(2)}, u32[]{:S(2)}) collective-permute-start(bf16[96,640]{1,0:T(8,128)(2,1)S(1)} %get-tuple-element.67), channel_id=1, source_target_pairs={{0,12},{1,5},{2,14},{3,7},{4,0},{5,9},{6,2},{7,11},{8,4},{9,13},{1... | collective-permute-start | bytes 368648 | tf_op jit(solution)/shard_map/ppermute | solution.py:349
  100.5 13.7 %collective-permute-start.3 = (bf16[96,640]{1,0:T(8,128)(2,1)S(1)}, bf16[96,640]{1,0:T(8,128)(2,1)S(1)}, u32[]{:S(2)}, u32[]{:S(2)}) collective-permute-start(bf16[96,640]{1,0:T(8,128)(2,1)S(1)} %get-tuple-element.62), channel_id=1, source_target_pairs={{0,14},{1,3},{2,0},{3,5},{4,2},{5,7},{6,4},{7,9},{8,6},{9,11},{10,... | collective-permute-start | bytes 368648 | tf_op jit(solution)/shard_map/ppermute | solution.py:349
  103.9 10.4 %collective-permute-start.4 = (bf16[96,640]{1,0:T(8,128)(2,1)S(1)}, bf16[96,640]{1,0:T(8,128)(2,1)S(1)}, u32[]{:S(2)}, u32[]{:S(2)}) collective-permute-start(bf16[96,640]{1,0:T(8,128)(2,1)S(1)} %get-tuple-element.63), channel_id=1, source_target_pairs={{0,15},{1,2},{2,1},{3,4},{4,3},{5,6},{6,5},{7,8},{8,7},{9,10},{10,... | collective-permute-start | bytes 368648 | tf_op jit(solution)/shard_map/ppermute | solution.py:349
  107.8 7.8 %collective-permute-start.7 = (bf16[96,640]{1,0:T(8,128)(2,1)S(1)}, bf16[96,640]{1,0:T(8,128)(2,1)S(1)}, u32[]{:S(2)}, u32[]{:S(2)}) collective-permute-start(bf16[96,640]{1,0:T(8,128)(2,1)S(1)} %get-tuple-element.68), channel_id=1, source_target_pairs={{0,12},{1,5},{2,14},{3,7},{4,0},{5,9},{6,2},{7,11},{8,4},{9,13},{1... | collective-permute-start | bytes 368648 | tf_op jit(solution)/shard_map/ppermute | solution.py:349
  112.1 8.7 %collective-permute-start.8 = (bf16[96,640]{1,0:T(8,128)(2,1)S(1)}, bf16[96,640]{1,0:T(8,128)(2,1)S(1)}, u32[]{:S(2)}, u32[]{:S(2)}) collective-permute-start(bf16[96,640]{1,0:T(8,128)(2,1)S(1)} %get-tuple-element.69), channel_id=1, source_target_pairs={{0,13},{1,4},{2,15},{3,6},{4,1},{5,8},{6,3},{7,10},{8,5},{9,12},{1... | collective-permute-start | bytes 368648 | tf_op jit(solution)/shard_map/ppermute | solution.py:349

commit v11 on v10

--- a/solution.py
+++ b/solution.py
@@ -10,7 +10,7 @@
 
 LONPAD = 3200
 LANES = 128
-BLOCK = 256
+BLOCK = 512
 BLOCKS = -(-LONPAD // BLOCK)
 
 NT = (((1,), (1,)), ((), ()))
@@ -290,12 +290,13 @@
 
     rotate(0)
     copies[3].wait()
-    copies[4].wait()
-    copies[5].wait()
     values, sums, results = {0: spread(0)}, {}, []
     for member in range(row_count):
         if member + 1 < row_count:
             rotate(member + 1)
+        if member == 1:
+            copies[4].wait()
+            copies[5].wait()
         if member > 0:
             sums[member - 1] = analyse(member - 1)
         results.append(multiply(member, values.pop(member)))
@@ -413,7 +414,7 @@
         [pltpu.HBM(shape, kind) for shape, kind in tables],
         "fourier_tables",
         4,
-        16,
+        24,
         in_specs=[smem()] * 5 + [vmem()],
         out_specs=[hbm()] * 6,
         scratch=tables_vmem + [pltpu.SemaphoreType.DMA((6,))],
@@ -429,7 +430,7 @@
         (jax.ShapeDtypeStruct((row_count, levels, LONPAD), jnp.bfloat16), fourier_shape),
         "fourier",
         6,
-        32,
+        40,
         in_specs=[vmem()] + [hbm()] * 6,
         out_specs=(hbm(), vmem()),
         scratch=tables_vmem + [

time: 122 us -> 123 us (level)
  Pallas kernels: 17 us -> 19.9 us
  waiting for transfers between devices: 25.8 us -> 23.1 us
    all_to_all x1, waiting for transfers between devices: 8.13 us -> 5.48 us  [shards(): lax.all_to_all(outgoing, 'wave', split_axis=0, concat_axis=0, tiled=True)]
    pallas_call x1, Pallas kernels: 4.21 us -> 6.86 us  [shards(): local(functools.partial(fourier_tables_kernel, fields=fields, zs=zs), [pl...]
  transfers between devices with their start and end apart: 11 -> 11, of which waited for: 6 -> 6; matrix products, arithmetic and copies ran while one was open for 0% -> 0% of each run, Pallas kernels for 6% -> 8%
where the time goes in v11:
time: 123 us; the launch traced here: 122 us
  starting transfers between devices  48.4 us (39%)
  blocking collectives  28.6 us (23%)
  waiting for transfers between devices  23.1 us (19%)
  Pallas kernels  19.9 us (16%)
    ppermute x9, starting transfers between devices, hop(): return lax.ppermute(x, 'field', pairs)  34.3 us
    all_gather x1, blocking collectives, shards(): gathered = lax.all_gather(own, 'field', axis_index_groups=like_cores)  28.6 us
    all_to_all x1, starting transfers between devices, shards(): lax.all_to_all(outgoing, 'wave', split_axis=0, concat_axis=0, tiled=True)  9.67 us
    all_to_all x1, waiting for transfers between devices, shards(): lax.all_to_all(sent, 'wave', split_axis=0, concat_axis=0, tiled=True)  9.09 us
    ppermute x9, waiting for transfers between devices, hop(): return lax.ppermute(x, 'field', pairs)  8.53 us
    pallas_call x1, Pallas kernels, shards(): local(functools.partial(fourier_tables_kernel, fields=fields, zs=zs), [pl...  6.86 us
    pallas_call x1, Pallas kernels, shards(): local(fourier_kernel, (jax.ShapeDtypeStruct((row_count, levels, LONPAD),...  6.45 us
    all_to_all x1, waiting for transfers between devices, shards(): lax.all_to_all(outgoing, 'wave', split_axis=0, concat_axis=0, tiled=True)  5.48 us
  transfers between devices with their start and end apart: 11, of which 6 were waited for; matrix products, arithmetic and copies ran while one was open for 0% of the time, Pallas kernels for 8%

profile of v11, /device:TPU:1, one launch (start us, length us, event | category | flops | bytes accessed | tf_op | source)
XLA Modules:
  0.0 122.0 jit_solution(11784425148416265178)
XLA Ops:
  0.6 0.9 all_gather_reshape.3
  1.6 28.6 %all_gather.3.gathered = bf16[8,96,640]{2,1,0:T(8,128)(2,1)S(1)} all-gather(bf16[1,96,640]{2,1,0:T(8,128)(2,1)S(1)} %all_gather_reshape.3), channel_id=1, replica_groups={{0,2,4,6,8,10,12,14},{15,13,11,9,7,5,3,1},{16,18,20,22,24,26,28,30},{31..., dimensions={0}, use_global_device_ids=true | all-gather | bytes 1105920 | tf_op jit(solution)/shard_map/all_gather | solution.py:374
  30.2 7.7 %collective-permute-start = (bf16[8,96,640]{2,1,0:T(8,128)(2,1)S(1)}, bf16[8,96,640]{2,1,0:T(8,128)(2,1)S(1)}, u32[]{:S(2)}, u32[]{:S(2)}) collective-permute-start(bf16[8,96,640]{2,1,0:T(8,128)(2,1)S(1)} %all_gather.3.gathered), channel_id=1, source_target_pairs={{0,1},{1,0},{2,3},{3,2},{4,5},{5,4},{6,7},{7,6},{8,9},{9,8},{10,11... | collective-permute-start | bytes 2949128 | tf_op jit(solution)/shard_map/ppermute | solution.py:350
  37.9 1.9 %collective-permute-start.1 = (bf16[12,48,640]{2,1,0:T(8,128)(2,1)}, bf16[12,48,640]{2,1,0:T(8,128)(2,1)}, u32[]{:S(2)}, u32[]{:S(2)}) collective-permute-start(bf16[12,48,640]{2,1,0:T(8,128)(2,1)} %bitcast.7), channel_id=1, source_target_pairs={{0,1},{1,0},{2,3},{3,2},{4,5},{5,4},{6,7},{7,6},{8,9},{9,8},{10,11... | collective-permute-start | bytes 2211848 | tf_op jit(solution)/shard_map/ppermute | solution.py:350
  39.9 1.7 %legendre_rows.2.table = bf16[12,96,640]{2,1,0:T(8,128)(2,1)S(1)} custom-call(s32[1]{0:T(128)} %bitcast.2.wave_id, s32[1]{0:T(128)} %bitcast.3.field_id, s32[384]{0:T(512)} %wave_of_slot.3, s32[1536]{0:T(1024)} %lat_of_row.5, bf16[12,48,640]{2,1,0:T(8,128)(2,1)} %bitcast.8), custom_call_target="tpu_custom_call" | custom-call | bytes 7400000 | tf_op jit(solution)/shard_map/legendre_rows/pallas_call | solution.py:380
  42.4 1.6 %legendre_forward.1 = bf16[32,4,1152]{2,1,0:T(4,128)(2,1)} custom-call(bf16[8,96,640]{2,1,0:T(8,128)(2,1)S(1)} %all_gather.3.gathered, bf16[8,96,640]{2,1,0:T(8,128)(2,1)S(1)} %collective-permute-done.gathered_x, bf16[12,96,640]{2,1,0:T(8,128)(2,1)S(1)} %legendre_rows.2.table), custom_call_target="tpu_custom_call" | custom-call | bytes 14800000 | tf_op jit(solution)/shard_map/legendre_forward/pallas_call | solution.py:398
  43.9 9.7 %all-to-all-start = ((bf16[32,4,1152]{2,1,0:T(4,128)(2,1)}), bf16[32,4,1152]{2,1,0:T(4,128)(2,1)S(1)}, u32[]{:S(2)}, u32[]{:S(2)}) async-start(bf16[32,4,1152]{2,1,0:T(4,128)(2,1)} %legendre_forward.1), calls=%async_computation | async-start | bytes 589824 | tf_op jit(solution)/shard_map/all_to_all | solution.py:402
  53.7 6.9 %fourier_tables.1 = (bf16[3,512,768]{2,1,0:T(8,128)(2,1)}, bf16[3,768,512]{2,1,0:T(8,128)(2,1)}, f32[3,16,768]{2,1,0:T(8,128)}, f32[3,16,768]{2,1,0:T(8,128)}, b...) custom-call(s32[1]{0:T(128)} %bitcast.2.wave_id, s32[1]{0:T(128)} %bitcast.3.field_id, s32[1536]{0:T(1024)S(1)} %copy-done, ...), custom_call_target="tpu_custom_call" | custom-call | bytes 14800000 | tf_op jit(solution)/shard_map/fourier_tables/pallas_call | solution.py:412
  60.6 5.5 %all-to-all-done.arrived = bf16[32,4,1152]{2,1,0:T(4,128)(2,1)S(1)} async-done(((bf16[32,4,1152]{2,1,0:T(4,128)(2,1)}), bf16[32,4,1152]{2,1,0:T(4,128)(2,1)S(1)}, u32[]{:S(2)}, u32[]{:S(2)}) %all-to-all-start) | async-done | bytes 294944 | tf_op jit(solution)/shard_map/all_to_all | solution.py:402
  66.0 6.5 %fourier.1 = (bf16[3,64,3200]{2,1,0:T(8,128)(2,1)}, bf16[32,4,1152]{2,1,0:T(4,128)(2,1)}) custom-call(bf16[32,4,1152]{2,1,0:T(4,128)(2,1)S(1)} %all-to-all-done.arrived, bf16[3,512,768]{2,1,0:T(8,128)(2,1)} %get-tuple-element.48.inner_in, bf16[3,768,512]{2,1,0:T(8,128)(2,1)} %get-tuple-element.49.inner_t_in, f32[3,16,768]{2,1,0:T(8,128)} %get-tuple-element.50.outer_fwd_in, ...), custom_call_target="tpu_custom_call" | custom-call | bytes 22200000 | tf_op jit(solution)/shard_map/fourier/pallas_call | solution.py:428
  72.5 4.4 %all-to-all-start.1 = ((bf16[32,4,1152]{2,1,0:T(4,128)(2,1)}), bf16[32,4,1152]{2,1,0:T(4,128)(2,1)S(1)}, u32[]{:S(2)}, u32[]{:S(2)}) async-start(bf16[32,4,1152]{2,1,0:T(4,128)(2,1)} %get-tuple-element.57), calls=%async_computation.1 | async-start | bytes 589824 | tf_op jit(solution)/shard_map/all_to_all | solution.py:448
  77.0 1.7 %legendre_rows.3.table_swapped = bf16[12,96,640]{2,1,0:T(8,128)(2,1)S(1)} custom-call(s32[1]{0:T(128)} %bitcast.2.wave_id, s32[1]{0:T(128)S(6)} %xor.3.field_id, s32[384]{0:T(512)} %wave_of_slot.3, s32[1536]{0:T(1024)} %lat_of_row.5, bf16[12,48,640]{2,1,0:T(8,128)(2,1)} %collective-permute-done.1.legendre), custom_call_target="tpu_custom_call" | custom-call | bytes 7400000 | tf_op jit(solution)/shard_map/legendre_rows/pallas_call | solution.py:380
  78.6 9.1 %all-to-all-done.1.arrived = bf16[32,4,1152]{2,1,0:T(4,128)(2,1)S(1)} async-done(((bf16[32,4,1152]{2,1,0:T(4,128)(2,1)}), bf16[32,4,1152]{2,1,0:T(4,128)(2,1)S(1)}, u32[]{:S(2)}, u32[]{:S(2)}) %all-to-all-start.1) | async-done | bytes 294944 | tf_op jit(solution)/shard_map/all_to_all | solution.py:448
  87.7 5.6 %collective-permute-start.2 = (bf16[32,4,1152]{2,1,0:T(4,128)(2,1)S(1)}, bf16[32,4,1152]{2,1,0:T(4,128)(2,1)S(1)}, u32[]{:S(2)}, u32[]{:S(2)}) collective-permute-start(bf16[32,4,1152]{2,1,0:T(4,128)(2,1)S(1)} %all-to-all-done.1.arrived), channel_id=1, source_target_pairs={{0,1},{1,0},{2,3},{3,2},{4,5},{5,4},{6,7},{7,6},{8,9},{9,8},{10,11... | collective-permute-start | bytes 884744 | tf_op jit(solution)/shard_map/ppermute | solution.py:350
  93.3 1.2 collective-permute-done.2.swapped
  94.5 0.9 legendre_inverse.1
  95.4 3.1 %collective-permute-start.5 = (bf16[2,96,640]{2,1,0:T(8,128)(2,1)S(1)}, bf16[2,96,640]{2,1,0:T(8,128)(2,1)S(1)}, u32[]{:S(2)}, u32[]{:S(2)}) collective-permute-start(bf16[2,96,640]{2,1,0:T(8,128)(2,1)S(1)} %get-tuple-element.66), channel_id=1, source_target_pairs={{0,14},{1,3},{2,0},{3,5},{4,2},{5,7},{6,4},{7,9},{8,6},{9,11},{10,... | collective-permute-start | bytes 737288 | tf_op jit(solution)/shard_map/ppermute | solution.py:350
  98.6 2.3 %collective-permute-start.6 = (bf16[96,640]{1,0:T(8,128)(2,1)S(1)}, bf16[96,640]{1,0:T(8,128)(2,1)S(1)}, u32[]{:S(2)}, u32[]{:S(2)}) collective-permute-start(bf16[96,640]{1,0:T(8,128)(2,1)S(1)} %get-tuple-element.67), channel_id=1, source_target_pairs={{0,12},{1,5},{2,14},{3,7},{4,0},{5,9},{6,2},{7,11},{8,4},{9,13},{1... | collective-permute-start | bytes 368648 | tf_op jit(solution)/shard_map/ppermute | solution.py:350
  100.9 3.3 %collective-permute-start.3 = (bf16[96,640]{1,0:T(8,128)(2,1)S(1)}, bf16[96,640]{1,0:T(8,128)(2,1)S(1)}, u32[]{:S(2)}, u32[]{:S(2)}) collective-permute-start(bf16[96,640]{1,0:T(8,128)(2,1)S(1)} %get-tuple-element.62), channel_id=1, source_target_pairs={{0,14},{1,3},{2,0},{3,5},{4,2},{5,7},{6,4},{7,9},{8,6},{9,11},{10,... | collective-permute-start | bytes 368648 | tf_op jit(solution)/shard_map/ppermute | solution.py:350
  104.2 3.9 %collective-permute-start.4 = (bf16[96,640]{1,0:T(8,128)(2,1)S(1)}, bf16[96,640]{1,0:T(8,128)(2,1)S(1)}, u32[]{:S(2)}, u32[]{:S(2)}) collective-permute-start(bf16[96,640]{1,0:T(8,128)(2,1)S(1)} %get-tuple-element.63), channel_id=1, source_target_pairs={{0,15},{1,2},{2,1},{3,4},{4,3},{5,6},{6,5},{7,8},{8,7},{9,10},{10,... | collective-permute-start | bytes 368648 | tf_op jit(solution)/shard_map/ppermute | solution.py:350
  108.2 4.3 %collective-permute-start.7 = (bf16[96,640]{1,0:T(8,128)(2,1)S(1)}, bf16[96,640]{1,0:T(8,128)(2,1)S(1)}, u32[]{:S(2)}, u32[]{:S(2)}) collective-permute-start(bf16[96,640]{1,0:T(8,128)(2,1)S(1)} %get-tuple-element.68), channel_id=1, source_target_pairs={{0,12},{1,5},{2,14},{3,7},{4,0},{5,9},{6,2},{7,11},{8,4},{9,13},{1... | collective-permute-start | bytes 368648 | tf_op jit(solution)/shard_map/ppermute | solution.py:350
  112.5 2.1 %collective-permute-start.8 = (bf16[96,640]{1,0:T(8,128)(2,1)S(1)}, bf16[96,640]{1,0:T(8,128)(2,1)S(1)}, u32[]{:S(2)}, u32[]{:S(2)}) collective-permute-start(bf16[96,640]{1,0:T(8,128)(2,1)S(1)} %get-tuple-element.69), channel_id=1, source_target_pairs={{0,13},{1,4},{2,15},{3,6},{4,1},{5,8},{6,3},{7,10},{8,5},{9,12},{1... | collective-permute-start | bytes 368648 | tf_op jit(solution)/shard_map/ppermute | solution.py:350
  114.6 1.4 %collective-permute-done.7.two = bf16[96,640]{1,0:T(8,128)(2,1)S(1)} collective-permute-done((bf16[96,640]{1,0:T(8,128)(2,1)S(1)}, bf16[96,640]{1,0:T(8,128)(2,1)S(1)}, u32[]{:S(2)}, u32[]{:S(2)}) %collective-permute-start.7) | collective-permute-done | bytes 122912 | tf_op jit(solution)/shard_map/ppermute | solution.py:350
  116.0 5.2 %collective-permute-done.8.two_x = bf16[96,640]{1,0:T(8,128)(2,1)S(1)} collective-permute-done((bf16[96,640]{1,0:T(8,128)(2,1)S(1)}, bf16[96,640]{1,0:T(8,128)(2,1)S(1)}, u32[]{:S(2)}, u32[]{:S(2)}) %collective-permute-start.8) | collective-permute-done | bytes 122912 | tf_op jit(solution)/shard_map/ppermute | solution.py:350
  (18 shorter events, 1.7 us)
Async XLA Ops:
  30.2 12.2 %collective-permute-start = (bf16[8,96,640]{2,1,0:T(8,128)(2,1)S(1)}, bf16[8,96,640]{2,1,0:T(8,128)(2,1)S(1)}, u32[]{:S(2)}, u32[]{:S(2)}) collective-permute-start(bf16[8,96,640]{2,1,0:T(8,128)(2,1)S(1)} %all_gather.3.gathered), channel_id=1, source_target_pairs={{0,1},{1,0},{2,3},{3,2},{4,5},{5,4},{6,7},{7,6},{8,9},{9,8},{10,11... | collective-permute-start | bytes 2949128 | tf_op jit(solution)/shard_map/ppermute | solution.py:350
  37.9 4.5 %collective-permute-start.1 = (bf16[12,48,640]{2,1,0:T(8,128)(2,1)}, bf16[12,48,640]{2,1,0:T(8,128)(2,1)}, u32[]{:S(2)}, u32[]{:S(2)}) collective-permute-start(bf16[12,48,640]{2,1,0:T(8,128)(2,1)} %bitcast.7), channel_id=1, source_target_pairs={{0,1},{1,0},{2,3},{3,2},{4,5},{5,4},{6,7},{7,6},{8,9},{9,8},{10,11... | collective-permute-start | bytes 2211848 | tf_op jit(solution)/shard_map/ppermute | solution.py:350
  41.6 12.1 %copy-start.3 = (s32[384]{0:T(512)S(1)}, s32[384]{0:T(512)}, u32[]{:S(2)}) copy-start(s32[384]{0:T(512)} %wave_of_slot.3) | copy-start | bytes 4612
  41.6 12.1 %copy-start = (s32[1536]{0:T(1024)S(1)}, s32[1536]{0:T(1024)}, u32[]{:S(2)}) copy-start(s32[1536]{0:T(1024)} %lat_of_row.5) | copy-start | bytes 18436
  41.6 12.1 %copy-start.1 = (s32[768]{0:T(1024)S(1)}, s32[768]{0:T(1024)}, u32[]{:S(2)}) copy-start(s32[768]{0:T(1024)} %lon_count.1) | copy-start | bytes 9220
  41.6 12.1 %copy-start.2 = (f32[48]{0:T(128)S(1)}, f32[48]{0:T(128)}, u32[]{:S(2)}) copy-start(f32[48]{0:T(128)} %lat_weight) | copy-start | bytes 580
  43.9 22.1 %all-to-all-start = ((bf16[32,4,1152]{2,1,0:T(4,128)(2,1)}), bf16[32,4,1152]{2,1,0:T(4,128)(2,1)S(1)}, u32[]{:S(2)}, u32[]{:S(2)}) async-start(bf16[32,4,1152]{2,1,0:T(4,128)(2,1)} %legendre_forward.1), calls=%async_computation | async-start | bytes 589824 | tf_op jit(solution)/shard_map/all_to_all | solution.py:402
  72.5 15.2 %all-to-all-start.1 = ((bf16[32,4,1152]{2,1,0:T(4,128)(2,1)}), bf16[32,4,1152]{2,1,0:T(4,128)(2,1)S(1)}, u32[]{:S(2)}, u32[]{:S(2)}) async-start(bf16[32,4,1152]{2,1,0:T(4,128)(2,1)} %get-tuple-element.57), calls=%async_computation.1 | async-start | bytes 589824 | tf_op jit(solution)/shard_map/all_to_all | solution.py:448
  87.7 6.8 %collective-permute-start.2 = (bf16[32,4,1152]{2,1,0:T(4,128)(2,1)S(1)}, bf16[32,4,1152]{2,1,0:T(4,128)(2,1)S(1)}, u32[]{:S(2)}, u32[]{:S(2)}) collective-permute-start(bf16[32,4,1152]{2,1,0:T(4,128)(2,1)S(1)} %all-to-all-done.1.arrived), channel_id=1, source_target_pairs={{0,1},{1,0},{2,3},{3,2},{4,5},{5,4},{6,7},{7,6},{8,9},{9,8},{10,11... | collective-permute-start | bytes 884744 | tf_op jit(solution)/shard_map/ppermute | solution.py:350
  95.4 12.6 %collective-permute-start.5 = (bf16[2,96,640]{2,1,0:T(8,128)(2,1)S(1)}, bf16[2,96,640]{2,1,0:T(8,128)(2,1)S(1)}, u32[]{:S(2)}, u32[]{:S(2)}) collective-permute-start(bf16[2,96,640]{2,1,0:T(8,128)(2,1)S(1)} %get-tuple-element.66), channel_id=1, source_target_pairs={{0,14},{1,3},{2,0},{3,5},{4,2},{5,7},{6,4},{7,9},{8,6},{9,11},{10,... | collective-permute-start | bytes 737288 | tf_op jit(solution)/shard_map/ppermute | solution.py:350
  98.6 9.5 %collective-permute-start.6 = (bf16[96,640]{1,0:T(8,128)(2,1)S(1)}, bf16[96,640]{1,0:T(8,128)(2,1)S(1)}, u32[]{:S(2)}, u32[]{:S(2)}) collective-permute-start(bf16[96,640]{1,0:T(8,128)(2,1)S(1)} %get-tuple-element.67), channel_id=1, source_target_pairs={{0,12},{1,5},{2,14},{3,7},{4,0},{5,9},{6,2},{7,11},{8,4},{9,13},{1... | collective-permute-start | bytes 368648 | tf_op jit(solution)/shard_map/ppermute | solution.py:350
  100.9 13.7 %collective-permute-start.3 = (bf16[96,640]{1,0:T(8,128)(2,1)S(1)}, bf16[96,640]{1,0:T(8,128)(2,1)S(1)}, u32[]{:S(2)}, u32[]{:S(2)}) collective-permute-start(bf16[96,640]{1,0:T(8,128)(2,1)S(1)} %get-tuple-element.62), channel_id=1, source_target_pairs={{0,14},{1,3},{2,0},{3,5},{4,2},{5,7},{6,4},{7,9},{8,6},{9,11},{10,... | collective-permute-start | bytes 368648 | tf_op jit(solution)/shard_map/ppermute | solution.py:350
  104.2 10.4 %collective-permute-start.4 = (bf16[96,640]{1,0:T(8,128)(2,1)S(1)}, bf16[96,640]{1,0:T(8,128)(2,1)S(1)}, u32[]{:S(2)}, u32[]{:S(2)}) collective-permute-start(bf16[96,640]{1,0:T(8,128)(2,1)S(1)} %get-tuple-element.63), channel_id=1, source_target_pairs={{0,15},{1,2},{2,1},{3,4},{4,3},{5,6},{6,5},{7,8},{8,7},{9,10},{10,... | collective-permute-start | bytes 368648 | tf_op jit(solution)/shard_map/ppermute | solution.py:350
  108.2 7.8 %collective-permute-start.7 = (bf16[96,640]{1,0:T(8,128)(2,1)S(1)}, bf16[96,640]{1,0:T(8,128)(2,1)S(1)}, u32[]{:S(2)}, u32[]{:S(2)}) collective-permute-start(bf16[96,640]{1,0:T(8,128)(2,1)S(1)} %get-tuple-element.68), channel_id=1, source_target_pairs={{0,12},{1,5},{2,14},{3,7},{4,0},{5,9},{6,2},{7,11},{8,4},{9,13},{1... | collective-permute-start | bytes 368648 | tf_op jit(solution)/shard_map/ppermute | solution.py:350
  112.5 8.7 %collective-permute-start.8 = (bf16[96,640]{1,0:T(8,128)(2,1)S(1)}, bf16[96,640]{1,0:T(8,128)(2,1)S(1)}, u32[]{:S(2)}, u32[]{:S(2)}) collective-permute-start(bf16[96,640]{1,0:T(8,128)(2,1)S(1)} %get-tuple-element.69), channel_id=1, source_target_pairs={{0,13},{1,4},{2,15},{3,6},{4,1},{5,8},{6,3},{7,10},{8,5},{9,12},{1... | collective-permute-start | bytes 368648 | tf_op jit(solution)/shard_map/ppermute | solution.py:350

commit v12 on v10

--- a/solution.py
+++ b/solution.py
@@ -227,8 +227,8 @@
     for copy in copies:
         copy.start()
     row_count = inner.shape[0]
-    slots = held.shape[0] // row_count
-    each = held.shape[0] // arrived.shape[0]
+    each = arrived.shape[1] * arrived.shape[2] // LANES
+    slots = arrived.shape[0] * each // row_count
     parts = slots // LANES
     levels = grid_out.shape[1]
     unpack_lines(arrived, held, each)
@@ -290,12 +290,13 @@
 
     rotate(0)
     copies[3].wait()
-    copies[4].wait()
-    copies[5].wait()
     values, sums, results = {0: spread(0)}, {}, []
     for member in range(row_count):
         if member + 1 < row_count:
             rotate(member + 1)
+        if member == 1:
+            copies[4].wait()
+            copies[5].wait()
         if member > 0:
             sums[member - 1] = analyse(member - 1)
         results.append(multiply(member, values.pop(member)))
@@ -367,7 +368,7 @@
 
     row_table = jax.ShapeDtypeStruct((slots, rows, degrees), jnp.bfloat16)
     fourier_shape = jax.ShapeDtypeStruct((waves, 4, each // 4 * LANES), jnp.bfloat16)
-    float_rows = pltpu.VMEM((waves * each, LANES), jnp.float32)
+    float_rows = pltpu.VMEM(((waves + 1) * each, LANES), jnp.float32)
 
     own = jnp.transpose(spectra, (0, 1, 3, 2)).reshape(coded, degrees)
     gathered = lax.all_gather(own, "field", axis_index_groups=like_cores)

time: 122 us -> 122 us (level)
  no operation moved by 1% of the time
where the time goes in v12:
time: 122 us
  starting transfers between devices  48.4 us (40%)
  blocking collectives  28.6 us (23%)
  waiting for transfers between devices  25.8 us (21%)
  Pallas kernels  16.9 us (14%)
    ppermute x9, starting transfers between devices, hop(): return lax.ppermute(x, 'field', pairs)  34.3 us
    all_gather x1, blocking collectives, shards(): gathered = lax.all_gather(own, 'field', axis_index_groups=like_cores)  28.6 us
    all_to_all x1, starting transfers between devices, shards(): lax.all_to_all(outgoing, 'wave', split_axis=0, concat_axis=0, tiled=True)  9.67 us
    all_to_all x1, waiting for transfers between devices, shards(): lax.all_to_all(sent, 'wave', split_axis=0, concat_axis=0, tiled=True)  9.09 us
    ppermute x9, waiting for transfers between devices, hop(): return lax.ppermute(x, 'field', pairs)  8.53 us
    all_to_all x1, waiting for transfers between devices, shards(): lax.all_to_all(outgoing, 'wave', split_axis=0, concat_axis=0, tiled=True)  8.13 us
    pallas_call x1, Pallas kernels, shards(): local(fourier_kernel, (jax.ShapeDtypeStruct((row_count, levels, LONPAD),...  6.08 us
    all_to_all x1, starting transfers between devices, shards(): lax.all_to_all(sent, 'wave', split_axis=0, concat_axis=0, tiled=True)  4.45 us
  transfers between devices with their start and end apart: 11, of which 6 were waited for; matrix products, arithmetic and copies ran while one was open for 0% of the time, Pallas kernels for 6%

profile of v12, /device:TPU:1, one launch (start us, length us, event | category | flops | bytes accessed | tf_op | source)
XLA Modules:
  0.0 121.6 jit_solution(2266914794717290517)
XLA Ops:
  0.6 0.9 all_gather_reshape.3
  1.6 28.6 %all_gather.3.gathered = bf16[8,96,640]{2,1,0:T(8,128)(2,1)S(1)} all-gather(bf16[1,96,640]{2,1,0:T(8,128)(2,1)S(1)} %all_gather_reshape.3), channel_id=1, replica_groups={{0,2,4,6,8,10,12,14},{15,13,11,9,7,5,3,1},{16,18,20,22,24,26,28,30},{31..., dimensions={0}, use_global_device_ids=true | all-gather | bytes 1105920 | tf_op jit(solution)/shard_map/all_gather | solution.py:374
  30.2 7.7 %collective-permute-start = (bf16[8,96,640]{2,1,0:T(8,128)(2,1)S(1)}, bf16[8,96,640]{2,1,0:T(8,128)(2,1)S(1)}, u32[]{:S(2)}, u32[]{:S(2)}) collective-permute-start(bf16[8,96,640]{2,1,0:T(8,128)(2,1)S(1)} %all_gather.3.gathered), channel_id=1, source_target_pairs={{0,1},{1,0},{2,3},{3,2},{4,5},{5,4},{6,7},{7,6},{8,9},{9,8},{10,11... | collective-permute-start | bytes 2949128 | tf_op jit(solution)/shard_map/ppermute | solution.py:350
  37.9 1.9 %collective-permute-start.1 = (bf16[12,48,640]{2,1,0:T(8,128)(2,1)}, bf16[12,48,640]{2,1,0:T(8,128)(2,1)}, u32[]{:S(2)}, u32[]{:S(2)}) collective-permute-start(bf16[12,48,640]{2,1,0:T(8,128)(2,1)} %bitcast.1.legendre), channel_id=1, source_target_pairs={{0,1},{1,0},{2,3},{3,2},{4,5},{5,4},{6,7},{7,6},{8,9},{9,8},{10,11... | collective-permute-start | bytes 2211848 | tf_op jit(solution)/shard_map/ppermute | solution.py:350
  39.9 1.7 %legendre_rows.2.table = bf16[12,96,640]{2,1,0:T(8,128)(2,1)S(1)} custom-call(s32[1]{0:T(128)} %bitcast.2.wave_id, s32[1]{0:T(128)} %bitcast.3.field_id, s32[384]{0:T(512)} %wave_of_slot.3, s32[1536]{0:T(1024)} %lat_of_row.5, bf16[12,48,640]{2,1,0:T(8,128)(2,1)} %bitcast.1.legendre), custom_call_target="tpu_custom_call" | custom-call | bytes 7400000 | tf_op jit(solution)/shard_map/legendre_rows/pallas_call | solution.py:380
  42.4 1.6 %legendre_forward.1 = bf16[32,4,1152]{2,1,0:T(4,128)(2,1)} custom-call(bf16[8,96,640]{2,1,0:T(8,128)(2,1)S(1)} %all_gather.3.gathered, bf16[8,96,640]{2,1,0:T(8,128)(2,1)S(1)} %collective-permute-done.gathered_x, bf16[12,96,640]{2,1,0:T(8,128)(2,1)S(1)} %legendre_rows.2.table), custom_call_target="tpu_custom_call" | custom-call | bytes 14800000 | tf_op jit(solution)/shard_map/legendre_forward/pallas_call | solution.py:398
  43.9 9.7 %all-to-all-start = ((bf16[32,4,1152]{2,1,0:T(4,128)(2,1)}), bf16[32,4,1152]{2,1,0:T(4,128)(2,1)S(1)}, u32[]{:S(2)}, u32[]{:S(2)}) async-start(bf16[32,4,1152]{2,1,0:T(4,128)(2,1)} %legendre_forward.1), calls=%async_computation | async-start | bytes 589824 | tf_op jit(solution)/shard_map/all_to_all | solution.py:402
  53.7 4.2 %fourier_tables.1 = (bf16[3,256,768]{2,1,0:T(8,128)(2,1)}, bf16[3,768,256]{2,1,0:T(8,128)(2,1)}, f32[3,16,768]{2,1,0:T(8,128)}, f32[3,16,768]{2,1,0:T(8,128)}, b...) custom-call(s32[1]{0:T(128)} %bitcast.2.wave_id, s32[1]{0:T(128)} %bitcast.3.field_id, s32[1536]{0:T(1024)S(1)} %copy-done, ...), custom_call_target="tpu_custom_call" | custom-call | bytes 14800000 | tf_op jit(solution)/shard_map/fourier_tables/pallas_call | solution.py:412
  57.9 8.1 %all-to-all-done.arrived = bf16[32,4,1152]{2,1,0:T(4,128)(2,1)S(1)} async-done(((bf16[32,4,1152]{2,1,0:T(4,128)(2,1)}), bf16[32,4,1152]{2,1,0:T(4,128)(2,1)S(1)}, u32[]{:S(2)}, u32[]{:S(2)}) %all-to-all-start) | async-done | bytes 294944 | tf_op jit(solution)/shard_map/all_to_all | solution.py:402
  66.0 6.1 %fourier.1 = (bf16[3,64,3200]{2,1,0:T(8,128)(2,1)}, bf16[32,4,1152]{2,1,0:T(4,128)(2,1)}) custom-call(bf16[32,4,1152]{2,1,0:T(4,128)(2,1)S(1)} %all-to-all-done.arrived, bf16[3,256,768]{2,1,0:T(8,128)(2,1)} %get-tuple-element.48.inner_in, bf16[3,768,256]{2,1,0:T(8,128)(2,1)} %get-tuple-element.49.inner_t_in, f32[3,16,768]{2,1,0:T(8,128)} %get-tuple-element.50.outer_fwd_in, ...), custom_call_target="tpu_custom_call" | custom-call | bytes 22200000 | tf_op jit(solution)/shard_map/fourier/pallas_call | solution.py:428
  72.1 4.4 %all-to-all-start.1 = ((bf16[32,4,1152]{2,1,0:T(4,128)(2,1)}), bf16[32,4,1152]{2,1,0:T(4,128)(2,1)S(1)}, u32[]{:S(2)}, u32[]{:S(2)}) async-start(bf16[32,4,1152]{2,1,0:T(4,128)(2,1)} %get-tuple-element.57), calls=%async_computation.1 | async-start | bytes 589824 | tf_op jit(solution)/shard_map/all_to_all | solution.py:448
  76.6 1.7 %legendre_rows.3.table_swapped = bf16[12,96,640]{2,1,0:T(8,128)(2,1)S(1)} custom-call(s32[1]{0:T(128)} %bitcast.2.wave_id, s32[1]{0:T(128)S(6)} %xor.3.field_id, s32[384]{0:T(512)} %wave_of_slot.3, s32[1536]{0:T(1024)} %lat_of_row.5, bf16[12,48,640]{2,1,0:T(8,128)(2,1)} %collective-permute-done.1.legendre), custom_call_target="tpu_custom_call" | custom-call | bytes 7400000 | tf_op jit(solution)/shard_map/legendre_rows/pallas_call | solution.py:380
  78.3 9.1 %all-to-all-done.1.arrived = bf16[32,4,1152]{2,1,0:T(4,128)(2,1)S(1)} async-done(((bf16[32,4,1152]{2,1,0:T(4,128)(2,1)}), bf16[32,4,1152]{2,1,0:T(4,128)(2,1)S(1)}, u32[]{:S(2)}, u32[]{:S(2)}) %all-to-all-start.1) | async-done | bytes 294944 | tf_op jit(solution)/shard_map/all_to_all | solution.py:448
  87.4 5.6 %collective-permute-start.2 = (bf16[32,4,1152]{2,1,0:T(4,128)(2,1)S(1)}, bf16[32,4,1152]{2,1,0:T(4,128)(2,1)S(1)}, u32[]{:S(2)}, u32[]{:S(2)}) collective-permute-start(bf16[32,4,1152]{2,1,0:T(4,128)(2,1)S(1)} %all-to-all-done.1.arrived), channel_id=1, source_target_pairs={{0,1},{1,0},{2,3},{3,2},{4,5},{5,4},{6,7},{7,6},{8,9},{9,8},{10,11... | collective-permute-start | bytes 884744 | tf_op jit(solution)/shard_map/ppermute | solution.py:350
  93.0 1.2 collective-permute-done.2.swapped
  94.2 0.9 legendre_inverse.1
  95.0 3.1 %collective-permute-start.5 = (bf16[2,96,640]{2,1,0:T(8,128)(2,1)S(1)}, bf16[2,96,640]{2,1,0:T(8,128)(2,1)S(1)}, u32[]{:S(2)}, u32[]{:S(2)}) collective-permute-start(bf16[2,96,640]{2,1,0:T(8,128)(2,1)S(1)} %get-tuple-element.66), channel_id=1, source_target_pairs={{0,14},{1,3},{2,0},{3,5},{4,2},{5,7},{6,4},{7,9},{8,6},{9,11},{10,... | collective-permute-start | bytes 737288 | tf_op jit(solution)/shard_map/ppermute | solution.py:350
  98.2 2.3 %collective-permute-start.6 = (bf16[96,640]{1,0:T(8,128)(2,1)S(1)}, bf16[96,640]{1,0:T(8,128)(2,1)S(1)}, u32[]{:S(2)}, u32[]{:S(2)}) collective-permute-start(bf16[96,640]{1,0:T(8,128)(2,1)S(1)} %get-tuple-element.67), channel_id=1, source_target_pairs={{0,12},{1,5},{2,14},{3,7},{4,0},{5,9},{6,2},{7,11},{8,4},{9,13},{1... | collective-permute-start | bytes 368648 | tf_op jit(solution)/shard_map/ppermute | solution.py:350
  100.5 3.3 %collective-permute-start.3 = (bf16[96,640]{1,0:T(8,128)(2,1)S(1)}, bf16[96,640]{1,0:T(8,128)(2,1)S(1)}, u32[]{:S(2)}, u32[]{:S(2)}) collective-permute-start(bf16[96,640]{1,0:T(8,128)(2,1)S(1)} %get-tuple-element.62), channel_id=1, source_target_pairs={{0,14},{1,3},{2,0},{3,5},{4,2},{5,7},{6,4},{7,9},{8,6},{9,11},{10,... | collective-permute-start | bytes 368648 | tf_op jit(solution)/shard_map/ppermute | solution.py:350
  103.8 3.9 %collective-permute-start.4 = (bf16[96,640]{1,0:T(8,128)(2,1)S(1)}, bf16[96,640]{1,0:T(8,128)(2,1)S(1)}, u32[]{:S(2)}, u32[]{:S(2)}) collective-permute-start(bf16[96,640]{1,0:T(8,128)(2,1)S(1)} %get-tuple-element.63), channel_id=1, source_target_pairs={{0,15},{1,2},{2,1},{3,4},{4,3},{5,6},{6,5},{7,8},{8,7},{9,10},{10,... | collective-permute-start | bytes 368648 | tf_op jit(solution)/shard_map/ppermute | solution.py:350
  107.8 4.3 %collective-permute-start.7 = (bf16[96,640]{1,0:T(8,128)(2,1)S(1)}, bf16[96,640]{1,0:T(8,128)(2,1)S(1)}, u32[]{:S(2)}, u32[]{:S(2)}) collective-permute-start(bf16[96,640]{1,0:T(8,128)(2,1)S(1)} %get-tuple-element.68), channel_id=1, source_target_pairs={{0,12},{1,5},{2,14},{3,7},{4,0},{5,9},{6,2},{7,11},{8,4},{9,13},{1... | collective-permute-start | bytes 368648 | tf_op jit(solution)/shard_map/ppermute | solution.py:350
  112.1 2.1 %collective-permute-start.8 = (bf16[96,640]{1,0:T(8,128)(2,1)S(1)}, bf16[96,640]{1,0:T(8,128)(2,1)S(1)}, u32[]{:S(2)}, u32[]{:S(2)}) collective-permute-start(bf16[96,640]{1,0:T(8,128)(2,1)S(1)} %get-tuple-element.69), channel_id=1, source_target_pairs={{0,13},{1,4},{2,15},{3,6},{4,1},{5,8},{6,3},{7,10},{8,5},{9,12},{1... | collective-permute-start | bytes 368648 | tf_op jit(solution)/shard_map/ppermute | solution.py:350
  114.3 1.4 %collective-permute-done.7.two = bf16[96,640]{1,0:T(8,128)(2,1)S(1)} collective-permute-done((bf16[96,640]{1,0:T(8,128)(2,1)S(1)}, bf16[96,640]{1,0:T(8,128)(2,1)S(1)}, u32[]{:S(2)}, u32[]{:S(2)}) %collective-permute-start.7) | collective-permute-done | bytes 122912 | tf_op jit(solution)/shard_map/ppermute | solution.py:350
  115.6 5.2 %collective-permute-done.8.two_x = bf16[96,640]{1,0:T(8,128)(2,1)S(1)} collective-permute-done((bf16[96,640]{1,0:T(8,128)(2,1)S(1)}, bf16[96,640]{1,0:T(8,128)(2,1)S(1)}, u32[]{:S(2)}, u32[]{:S(2)}) %collective-permute-start.8) | collective-permute-done | bytes 122912 | tf_op jit(solution)/shard_map/ppermute | solution.py:350
  (18 shorter events, 1.7 us)
Async XLA Ops:
  30.2 12.2 %collective-permute-start = (bf16[8,96,640]{2,1,0:T(8,128)(2,1)S(1)}, bf16[8,96,640]{2,1,0:T(8,128)(2,1)S(1)}, u32[]{:S(2)}, u32[]{:S(2)}) collective-permute-start(bf16[8,96,640]{2,1,0:T(8,128)(2,1)S(1)} %all_gather.3.gathered), channel_id=1, source_target_pairs={{0,1},{1,0},{2,3},{3,2},{4,5},{5,4},{6,7},{7,6},{8,9},{9,8},{10,11... | collective-permute-start | bytes 2949128 | tf_op jit(solution)/shard_map/ppermute | solution.py:350
  37.9 4.5 %collective-permute-start.1 = (bf16[12,48,640]{2,1,0:T(8,128)(2,1)}, bf16[12,48,640]{2,1,0:T(8,128)(2,1)}, u32[]{:S(2)}, u32[]{:S(2)}) collective-permute-start(bf16[12,48,640]{2,1,0:T(8,128)(2,1)} %bitcast.1.legendre), channel_id=1, source_target_pairs={{0,1},{1,0},{2,3},{3,2},{4,5},{5,4},{6,7},{7,6},{8,9},{9,8},{10,11... | collective-permute-start | bytes 2211848 | tf_op jit(solution)/shard_map/ppermute | solution.py:350
  41.6 12.1 %copy-start.3 = (s32[384]{0:T(512)S(1)}, s32[384]{0:T(512)}, u32[]{:S(2)}) copy-start(s32[384]{0:T(512)} %wave_of_slot.3) | copy-start | bytes 4612
  41.6 12.1 %copy-start = (s32[1536]{0:T(1024)S(1)}, s32[1536]{0:T(1024)}, u32[]{:S(2)}) copy-start(s32[1536]{0:T(1024)} %lat_of_row.5) | copy-start | bytes 18436
  41.6 12.1 %copy-start.1 = (s32[768]{0:T(1024)S(1)}, s32[768]{0:T(1024)}, u32[]{:S(2)}) copy-start(s32[768]{0:T(1024)} %lon_count.1) | copy-start | bytes 9220
  41.6 12.1 %copy-start.2 = (f32[48]{0:T(128)S(1)}, f32[48]{0:T(128)}, u32[]{:S(2)}) copy-start(f32[48]{0:T(128)} %lat_weight) | copy-start | bytes 580
  43.9 22.1 %all-to-all-start = ((bf16[32,4,1152]{2,1,0:T(4,128)(2,1)}), bf16[32,4,1152]{2,1,0:T(4,128)(2,1)S(1)}, u32[]{:S(2)}, u32[]{:S(2)}) async-start(bf16[32,4,1152]{2,1,0:T(4,128)(2,1)} %legendre_forward.1), calls=%async_computation | async-start | bytes 589824 | tf_op jit(solution)/shard_map/all_to_all | solution.py:402
  72.1 15.2 %all-to-all-start.1 = ((bf16[32,4,1152]{2,1,0:T(4,128)(2,1)}), bf16[32,4,1152]{2,1,0:T(4,128)(2,1)S(1)}, u32[]{:S(2)}, u32[]{:S(2)}) async-start(bf16[32,4,1152]{2,1,0:T(4,128)(2,1)} %get-tuple-element.57), calls=%async_computation.1 | async-start | bytes 589824 | tf_op jit(solution)/shard_map/all_to_all | solution.py:448
  87.4 6.8 %collective-permute-start.2 = (bf16[32,4,1152]{2,1,0:T(4,128)(2,1)S(1)}, bf16[32,4,1152]{2,1,0:T(4,128)(2,1)S(1)}, u32[]{:S(2)}, u32[]{:S(2)}) collective-permute-start(bf16[32,4,1152]{2,1,0:T(4,128)(2,1)S(1)} %all-to-all-done.1.arrived), channel_id=1, source_target_pairs={{0,1},{1,0},{2,3},{3,2},{4,5},{5,4},{6,7},{7,6},{8,9},{9,8},{10,11... | collective-permute-start | bytes 884744 | tf_op jit(solution)/shard_map/ppermute | solution.py:350
  95.0 12.6 %collective-permute-start.5 = (bf16[2,96,640]{2,1,0:T(8,128)(2,1)S(1)}, bf16[2,96,640]{2,1,0:T(8,128)(2,1)S(1)}, u32[]{:S(2)}, u32[]{:S(2)}) collective-permute-start(bf16[2,96,640]{2,1,0:T(8,128)(2,1)S(1)} %get-tuple-element.66), channel_id=1, source_target_pairs={{0,14},{1,3},{2,0},{3,5},{4,2},{5,7},{6,4},{7,9},{8,6},{9,11},{10,... | collective-permute-start | bytes 737288 | tf_op jit(solution)/shard_map/ppermute | solution.py:350
  98.2 9.5 %collective-permute-start.6 = (bf16[96,640]{1,0:T(8,128)(2,1)S(1)}, bf16[96,640]{1,0:T(8,128)(2,1)S(1)}, u32[]{:S(2)}, u32[]{:S(2)}) collective-permute-start(bf16[96,640]{1,0:T(8,128)(2,1)S(1)} %get-tuple-element.67), channel_id=1, source_target_pairs={{0,12},{1,5},{2,14},{3,7},{4,0},{5,9},{6,2},{7,11},{8,4},{9,13},{1... | collective-permute-start | bytes 368648 | tf_op jit(solution)/shard_map/ppermute | solution.py:350
  100.5 13.7 %collective-permute-start.3 = (bf16[96,640]{1,0:T(8,128)(2,1)S(1)}, bf16[96,640]{1,0:T(8,128)(2,1)S(1)}, u32[]{:S(2)}, u32[]{:S(2)}) collective-permute-start(bf16[96,640]{1,0:T(8,128)(2,1)S(1)} %get-tuple-element.62), channel_id=1, source_target_pairs={{0,14},{1,3},{2,0},{3,5},{4,2},{5,7},{6,4},{7,9},{8,6},{9,11},{10,... | collective-permute-start | bytes 368648 | tf_op jit(solution)/shard_map/ppermute | solution.py:350
  103.8 10.4 %collective-permute-start.4 = (bf16[96,640]{1,0:T(8,128)(2,1)S(1)}, bf16[96,640]{1,0:T(8,128)(2,1)S(1)}, u32[]{:S(2)}, u32[]{:S(2)}) collective-permute-start(bf16[96,640]{1,0:T(8,128)(2,1)S(1)} %get-tuple-element.63), channel_id=1, source_target_pairs={{0,15},{1,2},{2,1},{3,4},{4,3},{5,6},{6,5},{7,8},{8,7},{9,10},{10,... | collective-permute-start | bytes 368648 | tf_op jit(solution)/shard_map/ppermute | solution.py:350
  107.8 7.8 %collective-permute-start.7 = (bf16[96,640]{1,0:T(8,128)(2,1)S(1)}, bf16[96,640]{1,0:T(8,128)(2,1)S(1)}, u32[]{:S(2)}, u32[]{:S(2)}) collective-permute-start(bf16[96,640]{1,0:T(8,128)(2,1)S(1)} %get-tuple-element.68), channel_id=1, source_target_pairs={{0,12},{1,5},{2,14},{3,7},{4,0},{5,9},{6,2},{7,11},{8,4},{9,13},{1... | collective-permute-start | bytes 368648 | tf_op jit(solution)/shard_map/ppermute | solution.py:350
  112.1 8.7 %collective-permute-start.8 = (bf16[96,640]{1,0:T(8,128)(2,1)S(1)}, bf16[96,640]{1,0:T(8,128)(2,1)S(1)}, u32[]{:S(2)}, u32[]{:S(2)}) collective-permute-start(bf16[96,640]{1,0:T(8,128)(2,1)S(1)} %get-tuple-element.69), channel_id=1, source_target_pairs={{0,13},{1,4},{2,15},{3,6},{4,1},{5,8},{6,3},{7,10},{8,5},{9,12},{1... | collective-permute-start | bytes 368648 | tf_op jit(solution)/shard_map/ppermute | solution.py:350

commit v13 on v12

--- a/solution.py
+++ b/solution.py
@@ -394,11 +394,10 @@
         )(wave_id, band_of, in_hbm(wave_of_slot), in_hbm(lat_of_row), in_hbm(values))
 
     table = ordered_rows(legendre, field_id)
-    gathered_x, legendre_x = lax.optimization_barrier((gathered_x, legendre_x))
     outgoing = local(
         legendre_forward_kernel, fourier_shape, "legendre_forward", 4, 16, in_specs=[vmem()] * 3, scratch=[float_rows]
     )(gathered, gathered_x, table)
-    outgoing, lat_weight = lax.optimization_barrier((outgoing, lat_weight))
+    outgoing, lat_weight, legendre_x = lax.optimization_barrier((outgoing, lat_weight, legendre_x))
     arrived = lax.all_to_all(outgoing, "wave", split_axis=0, concat_axis=0, tiled=True)
     tables = (
         ((row_count, BLOCK, 2 * all_slots), jnp.bfloat16),

time: 122 us -> 121 us (level)
  transfers between devices with their start and end apart: 11 -> 11, of which waited for: 6 -> 5; matrix products, arithmetic and copies ran while one was open for 0% -> 0% of each run, Pallas kernels for 6% -> 8%
where the time goes in v13:
time: 121 us
  starting transfers between devices  48.7 us (40%)
  blocking collectives  28.6 us (24%)
  waiting for transfers between devices  24.7 us (20%)
  Pallas kernels  16.9 us (14%)
    ppermute x9, starting transfers between devices, hop(): return lax.ppermute(x, 'field', pairs)  34.2 us
    all_gather x1, blocking collectives, shards(): gathered = lax.all_gather(own, 'field', axis_index_groups=like_cores)  28.6 us
    all_to_all x1, starting transfers between devices, shards(): lax.all_to_all(outgoing, 'wave', split_axis=0, concat_axis=0, tiled=True)  9.65 us
    all_to_all x1, waiting for transfers between devices, shards(): lax.all_to_all(sent, 'wave', split_axis=0, concat_axis=0, tiled=True)  9.21 us
    all_to_all x1, waiting for transfers between devices, shards(): lax.all_to_all(outgoing, 'wave', split_axis=0, concat_axis=0, tiled=True)  7.76 us
    ppermute x9, waiting for transfers between devices, hop(): return lax.ppermute(x, 'field', pairs)  7.72 us
    pallas_call x1, Pallas kernels, shards(): local(fourier_kernel, (jax.ShapeDtypeStruct((row_count, levels, LONPAD),...  6.09 us
    all_to_all x1, starting transfers between devices, shards(): lax.all_to_all(sent, 'wave', split_axis=0, concat_axis=0, tiled=True)  4.82 us
  transfers between devices with their start and end apart: 11, of which 5 were waited for; matrix products, arithmetic and copies ran while one was open for 0% of the time, Pallas kernels for 8%

profile of v13, /device:TPU:1, one launch (start us, length us, event | category | flops | bytes accessed | tf_op | source)
XLA Modules:
  0.0 120.8 jit_solution(10628908055745736437)
XLA Ops:
  0.6 0.9 all_gather_reshape.3
  1.6 28.6 %all_gather.3.gathered = bf16[8,96,640]{2,1,0:T(8,128)(2,1)S(1)} all-gather(bf16[1,96,640]{2,1,0:T(8,128)(2,1)S(1)} %all_gather_reshape.3), channel_id=1, replica_groups={{0,2,4,6,8,10,12,14},{15,13,11,9,7,5,3,1},{16,18,20,22,24,26,28,30},{31..., dimensions={0}, use_global_device_ids=true | all-gather | bytes 1105920 | tf_op jit(solution)/shard_map/all_gather | solution.py:374
  30.2 7.7 %collective-permute-start = (bf16[8,96,640]{2,1,0:T(8,128)(2,1)S(1)}, bf16[8,96,640]{2,1,0:T(8,128)(2,1)S(1)}, u32[]{:S(2)}, u32[]{:S(2)}) collective-permute-start(bf16[8,96,640]{2,1,0:T(8,128)(2,1)S(1)} %all_gather.3.gathered), channel_id=1, source_target_pairs={{0,1},{1,0},{2,3},{3,2},{4,5},{5,4},{6,7},{7,6},{8,9},{9,8},{10,11... | collective-permute-start | bytes 2949128 | tf_op jit(solution)/shard_map/ppermute | solution.py:350
  37.9 1.9 %collective-permute-start.1 = (bf16[12,48,640]{2,1,0:T(8,128)(2,1)}, bf16[12,48,640]{2,1,0:T(8,128)(2,1)}, u32[]{:S(2)}, u32[]{:S(2)}) collective-permute-start(bf16[12,48,640]{2,1,0:T(8,128)(2,1)} %bitcast.1.legendre), channel_id=1, source_target_pairs={{0,1},{1,0},{2,3},{3,2},{4,5},{5,4},{6,7},{7,6},{8,9},{9,8},{10,11... | collective-permute-start | bytes 2211848 | tf_op jit(solution)/shard_map/ppermute | solution.py:350
  39.9 1.7 %legendre_rows.2.table = bf16[12,96,640]{2,1,0:T(8,128)(2,1)S(1)} custom-call(s32[1]{0:T(128)} %bitcast.2.wave_id, s32[1]{0:T(128)} %bitcast.3.field_id, s32[384]{0:T(512)} %wave_of_slot.3, s32[1536]{0:T(1024)} %lat_of_row.5, bf16[12,48,640]{2,1,0:T(8,128)(2,1)} %bitcast.1.legendre), custom_call_target="tpu_custom_call" | custom-call | bytes 7400000 | tf_op jit(solution)/shard_map/legendre_rows/pallas_call | solution.py:380
  41.6 1.6 %legendre_forward.1 = bf16[32,4,1152]{2,1,0:T(4,128)(2,1)} custom-call(bf16[8,96,640]{2,1,0:T(8,128)(2,1)S(1)} %all_gather.3.gathered, bf16[8,96,640]{2,1,0:T(8,128)(2,1)S(1)} %collective-permute-done.gathered_x, bf16[12,96,640]{2,1,0:T(8,128)(2,1)S(1)} %legendre_rows.2.table), custom_call_target="tpu_custom_call" | custom-call | bytes 14800000 | tf_op jit(solution)/shard_map/legendre_forward/pallas_call | solution.py:397
  43.2 9.6 %all-to-all-start = ((bf16[32,4,1152]{2,1,0:T(4,128)(2,1)}), bf16[32,4,1152]{2,1,0:T(4,128)(2,1)S(1)}, u32[]{:S(2)}, u32[]{:S(2)}) async-start(bf16[32,4,1152]{2,1,0:T(4,128)(2,1)} %legendre_forward.1), calls=%async_computation | async-start | bytes 589824 | tf_op jit(solution)/shard_map/all_to_all | solution.py:401
  52.9 4.2 %fourier_tables.1 = (bf16[3,256,768]{2,1,0:T(8,128)(2,1)}, bf16[3,768,256]{2,1,0:T(8,128)(2,1)}, f32[3,16,768]{2,1,0:T(8,128)}, f32[3,16,768]{2,1,0:T(8,128)}, b...) custom-call(s32[1]{0:T(128)} %bitcast.2.wave_id, s32[1]{0:T(128)} %bitcast.3.field_id, s32[1536]{0:T(1024)S(1)} %copy-done, ...), custom_call_target="tpu_custom_call" | custom-call | bytes 14800000 | tf_op jit(solution)/shard_map/fourier_tables/pallas_call | solution.py:411
  57.1 7.8 %all-to-all-done.arrived = bf16[32,4,1152]{2,1,0:T(4,128)(2,1)S(1)} async-done(((bf16[32,4,1152]{2,1,0:T(4,128)(2,1)}), bf16[32,4,1152]{2,1,0:T(4,128)(2,1)S(1)}, u32[]{:S(2)}, u32[]{:S(2)}) %all-to-all-start) | async-done | bytes 294944 | tf_op jit(solution)/shard_map/all_to_all | solution.py:401
  64.9 6.1 %fourier.1 = (bf16[3,64,3200]{2,1,0:T(8,128)(2,1)}, bf16[32,4,1152]{2,1,0:T(4,128)(2,1)}) custom-call(bf16[32,4,1152]{2,1,0:T(4,128)(2,1)S(1)} %all-to-all-done.arrived, bf16[3,256,768]{2,1,0:T(8,128)(2,1)} %get-tuple-element.46.inner_in, bf16[3,768,256]{2,1,0:T(8,128)(2,1)} %get-tuple-element.47.inner_t_in, f32[3,16,768]{2,1,0:T(8,128)} %get-tuple-element.48.outer_fwd_in, ...), custom_call_target="tpu_custom_call" | custom-call | bytes 22200000 | tf_op jit(solution)/shard_map/fourier/pallas_call | solution.py:427
  71.0 4.8 %all-to-all-start.1 = ((bf16[32,4,1152]{2,1,0:T(4,128)(2,1)}), bf16[32,4,1152]{2,1,0:T(4,128)(2,1)S(1)}, u32[]{:S(2)}, u32[]{:S(2)}) async-start(bf16[32,4,1152]{2,1,0:T(4,128)(2,1)} %get-tuple-element.55), calls=%async_computation.1 | async-start | bytes 589824 | tf_op jit(solution)/shard_map/all_to_all | solution.py:447
  75.8 1.7 %legendre_rows.3.table_swapped = bf16[12,96,640]{2,1,0:T(8,128)(2,1)S(1)} custom-call(s32[1]{0:T(128)} %bitcast.2.wave_id, s32[1]{0:T(128)S(6)} %xor.3.field_id, s32[384]{0:T(512)} %wave_of_slot.3, s32[1536]{0:T(1024)} %lat_of_row.5, bf16[12,48,640]{2,1,0:T(8,128)(2,1)} %collective-permute-done.1.legendre), custom_call_target="tpu_custom_call" | custom-call | bytes 7400000 | tf_op jit(solution)/shard_map/legendre_rows/pallas_call | solution.py:380
  77.5 9.2 %all-to-all-done.1.arrived = bf16[32,4,1152]{2,1,0:T(4,128)(2,1)S(1)} async-done(((bf16[32,4,1152]{2,1,0:T(4,128)(2,1)}), bf16[32,4,1152]{2,1,0:T(4,128)(2,1)S(1)}, u32[]{:S(2)}, u32[]{:S(2)}) %all-to-all-start.1) | async-done | bytes 294944 | tf_op jit(solution)/shard_map/all_to_all | solution.py:447
  86.7 5.5 %collective-permute-start.2 = (bf16[32,4,1152]{2,1,0:T(4,128)(2,1)S(1)}, bf16[32,4,1152]{2,1,0:T(4,128)(2,1)S(1)}, u32[]{:S(2)}, u32[]{:S(2)}) collective-permute-start(bf16[32,4,1152]{2,1,0:T(4,128)(2,1)S(1)} %all-to-all-done.1.arrived), channel_id=1, source_target_pairs={{0,1},{1,0},{2,3},{3,2},{4,5},{5,4},{6,7},{7,6},{8,9},{9,8},{10,11... | collective-permute-start | bytes 884744 | tf_op jit(solution)/shard_map/ppermute | solution.py:350
  92.2 1.2 collective-permute-done.2.swapped
  93.4 0.9 legendre_inverse.1
  94.3 3.2 %collective-permute-start.5 = (bf16[2,96,640]{2,1,0:T(8,128)(2,1)S(1)}, bf16[2,96,640]{2,1,0:T(8,128)(2,1)S(1)}, u32[]{:S(2)}, u32[]{:S(2)}) collective-permute-start(bf16[2,96,640]{2,1,0:T(8,128)(2,1)S(1)} %get-tuple-element.64), channel_id=1, source_target_pairs={{0,14},{1,3},{2,0},{3,5},{4,2},{5,7},{6,4},{7,9},{8,6},{9,11},{10,... | collective-permute-start | bytes 737288 | tf_op jit(solution)/shard_map/ppermute | solution.py:350
  97.4 2.3 %collective-permute-start.6 = (bf16[96,640]{1,0:T(8,128)(2,1)S(1)}, bf16[96,640]{1,0:T(8,128)(2,1)S(1)}, u32[]{:S(2)}, u32[]{:S(2)}) collective-permute-start(bf16[96,640]{1,0:T(8,128)(2,1)S(1)} %get-tuple-element.65), channel_id=1, source_target_pairs={{0,12},{1,5},{2,14},{3,7},{4,0},{5,9},{6,2},{7,11},{8,4},{9,13},{1... | collective-permute-start | bytes 368648 | tf_op jit(solution)/shard_map/ppermute | solution.py:350
  99.7 3.3 %collective-permute-start.3 = (bf16[96,640]{1,0:T(8,128)(2,1)S(1)}, bf16[96,640]{1,0:T(8,128)(2,1)S(1)}, u32[]{:S(2)}, u32[]{:S(2)}) collective-permute-start(bf16[96,640]{1,0:T(8,128)(2,1)S(1)} %get-tuple-element.60), channel_id=1, source_target_pairs={{0,14},{1,3},{2,0},{3,5},{4,2},{5,7},{6,4},{7,9},{8,6},{9,11},{10,... | collective-permute-start | bytes 368648 | tf_op jit(solution)/shard_map/ppermute | solution.py:350
  103.0 3.9 %collective-permute-start.4 = (bf16[96,640]{1,0:T(8,128)(2,1)S(1)}, bf16[96,640]{1,0:T(8,128)(2,1)S(1)}, u32[]{:S(2)}, u32[]{:S(2)}) collective-permute-start(bf16[96,640]{1,0:T(8,128)(2,1)S(1)} %get-tuple-element.61), channel_id=1, source_target_pairs={{0,15},{1,2},{2,1},{3,4},{4,3},{5,6},{6,5},{7,8},{8,7},{9,10},{10,... | collective-permute-start | bytes 368648 | tf_op jit(solution)/shard_map/ppermute | solution.py:350
  107.0 4.3 %collective-permute-start.7 = (bf16[96,640]{1,0:T(8,128)(2,1)S(1)}, bf16[96,640]{1,0:T(8,128)(2,1)S(1)}, u32[]{:S(2)}, u32[]{:S(2)}) collective-permute-start(bf16[96,640]{1,0:T(8,128)(2,1)S(1)} %get-tuple-element.66), channel_id=1, source_target_pairs={{0,12},{1,5},{2,14},{3,7},{4,0},{5,9},{6,2},{7,11},{8,4},{9,13},{1... | collective-permute-start | bytes 368648 | tf_op jit(solution)/shard_map/ppermute | solution.py:350
  111.3 2.1 %collective-permute-start.8 = (bf16[96,640]{1,0:T(8,128)(2,1)S(1)}, bf16[96,640]{1,0:T(8,128)(2,1)S(1)}, u32[]{:S(2)}, u32[]{:S(2)}) collective-permute-start(bf16[96,640]{1,0:T(8,128)(2,1)S(1)} %get-tuple-element.67), channel_id=1, source_target_pairs={{0,13},{1,4},{2,15},{3,6},{4,1},{5,8},{6,3},{7,10},{8,5},{9,12},{1... | collective-permute-start | bytes 368648 | tf_op jit(solution)/shard_map/ppermute | solution.py:350
  113.5 1.4 %collective-permute-done.7.two = bf16[96,640]{1,0:T(8,128)(2,1)S(1)} collective-permute-done((bf16[96,640]{1,0:T(8,128)(2,1)S(1)}, bf16[96,640]{1,0:T(8,128)(2,1)S(1)}, u32[]{:S(2)}, u32[]{:S(2)}) %collective-permute-start.7) | collective-permute-done | bytes 122912 | tf_op jit(solution)/shard_map/ppermute | solution.py:350
  114.9 5.1 %collective-permute-done.8.two_x = bf16[96,640]{1,0:T(8,128)(2,1)S(1)} collective-permute-done((bf16[96,640]{1,0:T(8,128)(2,1)S(1)}, bf16[96,640]{1,0:T(8,128)(2,1)S(1)}, u32[]{:S(2)}, u32[]{:S(2)}) %collective-permute-start.8) | collective-permute-done | bytes 122912 | tf_op jit(solution)/shard_map/ppermute | solution.py:350
  (18 shorter events, 0.9 us)
Async XLA Ops:
  30.2 11.4 %collective-permute-start = (bf16[8,96,640]{2,1,0:T(8,128)(2,1)S(1)}, bf16[8,96,640]{2,1,0:T(8,128)(2,1)S(1)}, u32[]{:S(2)}, u32[]{:S(2)}) collective-permute-start(bf16[8,96,640]{2,1,0:T(8,128)(2,1)S(1)} %all_gather.3.gathered), channel_id=1, source_target_pairs={{0,1},{1,0},{2,3},{3,2},{4,5},{5,4},{6,7},{7,6},{8,9},{9,8},{10,11... | collective-permute-start | bytes 2949128 | tf_op jit(solution)/shard_map/ppermute | solution.py:350
  37.9 5.3 %collective-permute-start.1 = (bf16[12,48,640]{2,1,0:T(8,128)(2,1)}, bf16[12,48,640]{2,1,0:T(8,128)(2,1)}, u32[]{:S(2)}, u32[]{:S(2)}) collective-permute-start(bf16[12,48,640]{2,1,0:T(8,128)(2,1)} %bitcast.1.legendre), channel_id=1, source_target_pairs={{0,1},{1,0},{2,3},{3,2},{4,5},{5,4},{6,7},{7,6},{8,9},{9,8},{10,11... | collective-permute-start | bytes 2211848 | tf_op jit(solution)/shard_map/ppermute | solution.py:350
  41.6 11.3 %copy-start.3 = (s32[384]{0:T(512)S(1)}, s32[384]{0:T(512)}, u32[]{:S(2)}) copy-start(s32[384]{0:T(512)} %wave_of_slot.3) | copy-start | bytes 4612
  41.6 11.3 %copy-start = (s32[1536]{0:T(1024)S(1)}, s32[1536]{0:T(1024)}, u32[]{:S(2)}) copy-start(s32[1536]{0:T(1024)} %lat_of_row.5) | copy-start | bytes 18436
  41.6 11.3 %copy-start.1 = (s32[768]{0:T(1024)S(1)}, s32[768]{0:T(1024)}, u32[]{:S(2)}) copy-start(s32[768]{0:T(1024)} %lon_count.1) | copy-start | bytes 9220
  41.6 11.3 %copy-start.2 = (f32[48]{0:T(128)S(1)}, f32[48]{0:T(128)}, u32[]{:S(2)}) copy-start(f32[48]{0:T(128)} %lat_weight) | copy-start | bytes 580
  43.2 21.7 %all-to-all-start = ((bf16[32,4,1152]{2,1,0:T(4,128)(2,1)}), bf16[32,4,1152]{2,1,0:T(4,128)(2,1)S(1)}, u32[]{:S(2)}, u32[]{:S(2)}) async-start(bf16[32,4,1152]{2,1,0:T(4,128)(2,1)} %legendre_forward.1), calls=%async_computation | async-start | bytes 589824 | tf_op jit(solution)/shard_map/all_to_all | solution.py:401
  71.0 15.7 %all-to-all-start.1 = ((bf16[32,4,1152]{2,1,0:T(4,128)(2,1)}), bf16[32,4,1152]{2,1,0:T(4,128)(2,1)S(1)}, u32[]{:S(2)}, u32[]{:S(2)}) async-start(bf16[32,4,1152]{2,1,0:T(4,128)(2,1)} %get-tuple-element.55), calls=%async_computation.1 | async-start | bytes 589824 | tf_op jit(solution)/shard_map/all_to_all | solution.py:447
  86.7 6.7 %collective-permute-start.2 = (bf16[32,4,1152]{2,1,0:T(4,128)(2,1)S(1)}, bf16[32,4,1152]{2,1,0:T(4,128)(2,1)S(1)}, u32[]{:S(2)}, u32[]{:S(2)}) collective-permute-start(bf16[32,4,1152]{2,1,0:T(4,128)(2,1)S(1)} %all-to-all-done.1.arrived), channel_id=1, source_target_pairs={{0,1},{1,0},{2,3},{3,2},{4,5},{5,4},{6,7},{7,6},{8,9},{9,8},{10,11... | collective-permute-start | bytes 884744 | tf_op jit(solution)/shard_map/ppermute | solution.py:350
  94.3 12.7 %collective-permute-start.5 = (bf16[2,96,640]{2,1,0:T(8,128)(2,1)S(1)}, bf16[2,96,640]{2,1,0:T(8,128)(2,1)S(1)}, u32[]{:S(2)}, u32[]{:S(2)}) collective-permute-start(bf16[2,96,640]{2,1,0:T(8,128)(2,1)S(1)} %get-tuple-element.64), channel_id=1, source_target_pairs={{0,14},{1,3},{2,0},{3,5},{4,2},{5,7},{6,4},{7,9},{8,6},{9,11},{10,... | collective-permute-start | bytes 737288 | tf_op jit(solution)/shard_map/ppermute | solution.py:350
  97.4 9.5 %collective-permute-start.6 = (bf16[96,640]{1,0:T(8,128)(2,1)S(1)}, bf16[96,640]{1,0:T(8,128)(2,1)S(1)}, u32[]{:S(2)}, u32[]{:S(2)}) collective-permute-start(bf16[96,640]{1,0:T(8,128)(2,1)S(1)} %get-tuple-element.65), channel_id=1, source_target_pairs={{0,12},{1,5},{2,14},{3,7},{4,0},{5,9},{6,2},{7,11},{8,4},{9,13},{1... | collective-permute-start | bytes 368648 | tf_op jit(solution)/shard_map/ppermute | solution.py:350
  99.7 13.7 %collective-permute-start.3 = (bf16[96,640]{1,0:T(8,128)(2,1)S(1)}, bf16[96,640]{1,0:T(8,128)(2,1)S(1)}, u32[]{:S(2)}, u32[]{:S(2)}) collective-permute-start(bf16[96,640]{1,0:T(8,128)(2,1)S(1)} %get-tuple-element.60), channel_id=1, source_target_pairs={{0,14},{1,3},{2,0},{3,5},{4,2},{5,7},{6,4},{7,9},{8,6},{9,11},{10,... | collective-permute-start | bytes 368648 | tf_op jit(solution)/shard_map/ppermute | solution.py:350
  103.0 10.4 %collective-permute-start.4 = (bf16[96,640]{1,0:T(8,128)(2,1)S(1)}, bf16[96,640]{1,0:T(8,128)(2,1)S(1)}, u32[]{:S(2)}, u32[]{:S(2)}) collective-permute-start(bf16[96,640]{1,0:T(8,128)(2,1)S(1)} %get-tuple-element.61), channel_id=1, source_target_pairs={{0,15},{1,2},{2,1},{3,4},{4,3},{5,6},{6,5},{7,8},{8,7},{9,10},{10,... | collective-permute-start | bytes 368648 | tf_op jit(solution)/shard_map/ppermute | solution.py:350
  107.0 7.8 %collective-permute-start.7 = (bf16[96,640]{1,0:T(8,128)(2,1)S(1)}, bf16[96,640]{1,0:T(8,128)(2,1)S(1)}, u32[]{:S(2)}, u32[]{:S(2)}) collective-permute-start(bf16[96,640]{1,0:T(8,128)(2,1)S(1)} %get-tuple-element.66), channel_id=1, source_target_pairs={{0,12},{1,5},{2,14},{3,7},{4,0},{5,9},{6,2},{7,11},{8,4},{9,13},{1... | collective-permute-start | bytes 368648 | tf_op jit(solution)/shard_map/ppermute | solution.py:350
  111.3 8.7 %collective-permute-start.8 = (bf16[96,640]{1,0:T(8,128)(2,1)S(1)}, bf16[96,640]{1,0:T(8,128)(2,1)S(1)}, u32[]{:S(2)}, u32[]{:S(2)}) collective-permute-start(bf16[96,640]{1,0:T(8,128)(2,1)S(1)} %get-tuple-element.67), channel_id=1, source_target_pairs={{0,13},{1,4},{2,15},{3,6},{4,1},{5,8},{6,3},{7,10},{8,5},{9,12},{1... | collective-permute-start | bytes 368648 | tf_op jit(solution)/shard_map/ppermute | solution.py:350
